TPU v7x, 256 devices: a whole 4x4x8 slice. The times are simulated.
256 devices in a mesh: dp: 64 (over x_hi, y, z), tensor: 4 (over x_lo, core).
Axes of the slice: x: 4 (x_hi: 2, x_lo: 2; x = x_hi * 2 + x_lo), y: 4, z: 8, core: 2. Of those that a mesh axis runs over, the one named last changes fastest.
Arguments:
- queries: bfloat16 [32768, 4096], P('dp', 'tensor'), may hold values from -64 to 64
- key_proj: bfloat16 [32768, 512], P('dp', 'tensor'), may hold values from -6 to 6
- value_proj: bfloat16 [32768, 512], P('dp', 'tensor'), may hold values from -6 to 6
- out_weight: bfloat16 [4096, 5120], P(None, 'tensor'), may hold values from -0.375 to 0.375
- parents: int32 [128], replicated, may hold values from -1 to 126, as said below
Outputs:
- projected: bfloat16 [32768, 5120], P('dp', 'tensor')
Inputs may be any that keep to these rules, and one draw needn't show every extreme that they name: `parents`: the segments form binary trees of depth at most 4; each tree's segments stand in depth-first preorder, so a segment follows its parent and a subtree's segments stand together; the first 5 segments of each tree form a path from its root to depth 4.
All inputs are finite; a program needn't handle non-finite values.
Results may differ from a plain program's by a relative error of at most 0.0053.
Values may be sent and summed in bfloat16 or wider, within the bound.
No kernel may reach another device: no remote copies, remote signals or barrier semaphores. Data moves between devices by JAX's collectives and lax.ppermute only.
A program may use at most 128 MiB of HBM per device.

v0:
```python
import jax
import jax.numpy as jnp
from jax import lax
from jax.sharding import PartitionSpec as P

HEAD_DIM = 128
SEG_LEN = 256
LEVELS = 4


def entering(shard, axis, combine, identity):
    size, position = (lax.axis_size(axis), lax.axis_index(axis))
    everything = jax.tree.map(
        lambda part, kind: lax.all_gather(part.astype(kind), axis),
        shard,
        jax.tree.map(lambda a: jnp.bfloat16 if a.dtype == jnp.float32 else a.dtype, shard),
    )
    start = jax.tree.map(
        lambda part, zero: jnp.broadcast_to(jnp.asarray(zero, part.dtype), part.shape),
        shard,
        identity,
    )

    def hop(k, before):
        reached = k < position
        new = combine(
            before, jax.tree.map(lambda part, own: part[k].astype(own.dtype), everything, shard)
        )
        return jax.tree.map(lambda a, b: jnp.where(reached, a, b), new, before)

    return lax.fori_loop(0, size, hop, start)


def tree_levels(parents):
    seg_count = parents.shape[0]
    safe_parent = jnp.maximum(parents, 0)
    depths = jnp.zeros((seg_count,), jnp.int32)
    for sweep_idx in range(LEVELS + 1):
        depths = jnp.where(parents >= 0, depths[safe_parent] + 1, 0)
    return depths


def score_block(query_seg, key_block):
    row_count = query_seg.shape[0]
    key_count = key_block.shape[0]
    kv_count = key_block.shape[1] // HEAD_DIM
    group_size = query_seg.shape[1] // (kv_count * HEAD_DIM)
    query_heads = query_seg.reshape(row_count, kv_count, group_size, HEAD_DIM)
    key_heads = key_block.reshape(key_count, kv_count, HEAD_DIM)
    return jnp.einsum(
        "tjgd,kjd->jgtk", query_heads, key_heads, preferred_element_type=jnp.float32
    ) * HEAD_DIM ** (-0.5)


def finish(scores, value_block, seg_depth):
    row_count = scores.shape[2]
    key_count = value_block.shape[0]
    kv_count = value_block.shape[1] // HEAD_DIM
    value_heads = value_block.reshape(key_count, kv_count, HEAD_DIM)
    key_ids = jnp.arange(key_count, dtype=jnp.int32)
    slot_ids = key_ids // row_count
    within = key_ids % row_count
    row_ids = jnp.arange(row_count, dtype=jnp.int32)
    allowed = jnp.where(
        slot_ids[None, :] < LEVELS,
        slot_ids[None, :] < seg_depth,
        within[None, :] <= row_ids[:, None],
    )
    scores = jnp.where(allowed[None, None], scores, -jnp.inf)
    row_max = jnp.max(scores, axis=-1, keepdims=True)
    exponent = jnp.exp(scores - row_max)
    totals = jnp.sum(exponent, axis=-1)
    weights = exponent.astype(jnp.bfloat16)
    mixture = jnp.einsum("jgtk,kjd->tjgd", weights, value_heads, preferred_element_type=jnp.float32)
    mixture = mixture / jnp.transpose(totals, (2, 0, 1))[..., None]
    return mixture.astype(jnp.bfloat16).reshape(row_count, -1)


def per_device(queries, key_proj, value_proj, out_weight, parents):
    local_rows = queries.shape[0]
    local_segs = local_rows // SEG_LEN
    first_seg = lax.axis_index("dp") * local_segs
    depths = tree_levels(parents)
    local_depth = lax.dynamic_slice_in_dim(depths, first_seg, local_segs, 0)
    key_width = key_proj.shape[1]
    own_keys = key_proj.reshape(local_segs, SEG_LEN, key_width)
    own_values = value_proj.reshape(local_segs, SEG_LEN, key_width)
    query_segs = queries.reshape(local_segs, SEG_LEN, queries.shape[1])
    level_ids = jnp.arange(LEVELS, dtype=jnp.int32)
    blank_slots = jnp.zeros((LEVELS, SEG_LEN, key_width), jnp.bfloat16)
    identity = (blank_slots, blank_slots, jnp.zeros((LEVELS,), jnp.bfloat16))

    def combine(earlier, later):
        chosen = later[2] > 0
        return (
            jnp.where(chosen[:, None, None], later[0], earlier[0]),
            jnp.where(chosen[:, None, None], later[1], earlier[1]),
            jnp.maximum(earlier[2], later[2]),
        )

    def element(seg_idx):
        seg_depth = local_depth[seg_idx]
        level_marks = (level_ids >= seg_depth).astype(jnp.bfloat16)
        placed = (level_ids == seg_depth)[:, None, None]
        return (
            jnp.where(placed, own_keys[seg_idx][None], blank_slots),
            jnp.where(placed, own_values[seg_idx][None], blank_slots),
            level_marks,
        )

    summary = identity
    for seg_idx in range(local_segs):
        summary = combine(summary, element(seg_idx))
    running = entering(summary, "dp", combine, identity)
    outputs = []
    for seg_idx in range(local_segs):
        stack_keys = running[0].reshape(LEVELS * SEG_LEN, key_width)
        value_block = jnp.concatenate(
            [running[1].reshape(LEVELS * SEG_LEN, key_width), own_values[seg_idx]], axis=0
        )
        key_block = jnp.concatenate([stack_keys, own_keys[seg_idx]], axis=0)
        scores = score_block(query_segs[seg_idx], key_block)
        outputs.append(finish(scores, value_block, local_depth[seg_idx]))
        running = combine(running, element(seg_idx))
    attended = jnp.concatenate(outputs, axis=0)
    summed = jnp.dot(
        lax.all_gather(attended, "tensor", axis=1, tiled=True),
        out_weight,
        preferred_element_type=jnp.float32,
    )
    return summed.astype(jnp.bfloat16)


def solution(mesh):
    placed = (P("dp", "tensor"), P("dp", "tensor"), P("dp", "tensor"), P(None, "tensor"), P())
    return jax.shard_map(
        per_device, mesh=mesh, in_specs=placed, out_specs=P("dp", "tensor"), check_vma=False
    )
```

profile of v0, /device:TPU:1, one launch (start us, length us, event | category | flops | bytes accessed | tf_op | source)
XLA Modules:
  0.0 603.7 jit_solution(13973408038722428486)
XLA Ops:
  7.2 1.2 gather_fusion
  9.1 1.2 gather_fusion.1
  11.0 1.2 gather_fusion.2
  12.9 1.2 gather_fusion.3
  14.8 1.2 gather_fusion.4
  23.6 1.3 fusion.50
  24.9 156.7 %all-gather = bf16[64,1,4]{2,1,0:T(2,128)(2,1)S(1)} all-gather(bf16[1,1,4]{2,1,0:T(2,128)(2,1)S(1)} %fusion.50), channel_id=1, replica_groups=mesh['dp'=64,'tensor'=4] {'dp'}, dimensions={0}, use_global_device_ids=true | all-gather | bytes 520 | tf_op jit(solution)/shard_map/all_gather | solution.py:14
  181.8 1.3 fusion.59
  183.5 1.3 fusion.43
  184.9 1.4 fusion.21
  186.3 48.1 %all-gather.5.cloned.1.call-done = bf16[64,4,256,128]{3,2,1,0:T(8,128)(2,1)} async-done(((bf16[1,4,256,128]{3,2,1,0:T(8,128)(2,1)}), bf16[64,4,256,128]{3,2,1,0:T(8,128)(2,1)}) %all-gather.5.cloned.1.call-update) | async-done | bytes 16777232 | tf_op jit(solution)/shard_map/all_gather | solution.py:14
  234.4 209.4 %all-gather.7.cloned.1.call-done = bf16[64,4,256,128]{3,2,1,0:T(8,128)(2,1)} async-done(((bf16[1,4,256,128]{3,2,1,0:T(8,128)(2,1)}), bf16[64,4,256,128]{3,2,1,0:T(8,128)(2,1)}) %all-gather.7.cloned.1.call-update) | async-done | bytes 16777232 | tf_op jit(solution)/shard_map/all_gather | solution.py:14
  443.8 78.9 %while.16 = (s32[]{:T(128)}, bf16[4,256,128]{2,1,0:T(8,128)(2,1)S(1)}, bf16[4,256,128]{2,1,0:T(8,128)(2,1)S(1)}, s32[]{:T(128)}, bf16[64,4]{1,0:T(8,128)(2,1)S(1...) while((s32[]{:T(128)}, ...), condition=%wide.region_1.2_spmd.clone, body=%wide.region_0.1_spmd.clone.sunk | while | flops 786448 | bytes 1573001 | solution.py:31
  445.0 1.2 select_select_fusion.7
  446.2 1.2 select_select_fusion.7
  447.5 1.2 select_select_fusion.7
  448.7 1.2 select_select_fusion.7
  449.9 1.2 select_select_fusion.7
  451.1 1.2 select_select_fusion.7
  452.4 1.2 select_select_fusion.7
  453.6 1.2 select_select_fusion.7
  454.8 1.2 select_select_fusion.7
  456.1 1.2 select_select_fusion.7
  457.3 1.2 select_select_fusion.7
  524.5 1.6 fusion.4
  526.1 2.1 fusion
  528.2 1.6 fusion.5
  529.9 2.2 fusion.2
  532.1 2.8 divide_convert_fusion.1
  534.9 3.0 divide_convert_fusion
  538.9 46.9 %all-gather.9.cloned.1.call-done = bf16[512,4096]{0,1:T(8,128)(2,1)} async-done(((bf16[512,1024]{0,1:T(8,128)(2,1)}), bf16[512,4096]{0,1:T(8,128)(2,1)}) %all-gather.9.cloned.1.call-update) | async-done | bytes 4194320 | tf_op jit(solution)/shard_map/all_gather | solution.py:127
  585.8 11.3 %convolution_convert_fusion = bf16[512,1280]{1,0:T(8,128)(2,1)} fusion(bf16[512,4096]{0,1:T(8,128)(2,1)} %all-gather.9.cloned.1.call-done, bf16[4096,1280]{1,0:T(8,128)(2,1)} %param.10), kind=kOutput, calls=%fused_computation.25 | convolution fusion | flops 5369364480 | bytes 15990784 | tf_op jit(solution)/shard_map/dot_general | solution.py:126
  (163 shorter events, 78.1 us)
Async XLA Ops:
  6.5 227.8 %all-gather.5.cloned.1.call-start = ((), (), s32[]{:S(2)}) async-start(), calls=%async_computation | async-start | bytes 17039360 | tf_op jit(solution)/shard_map/all_gather | solution.py:14
  19.7 0.6 copy-start
  21.3 422.4 %all-gather.7.cloned.1.call-start = ((), (), s32[]{:S(2)}) async-start(), calls=%async_computation.1 | async-start | bytes 17039360 | tf_op jit(solution)/shard_map/all_gather | solution.py:14
  22.1 563.8 %all-gather.9.cloned.1.call-start = ((), (), s32[]{:S(2)}) async-start(), calls=%async_computation.2 | async-start | bytes 5242880 | tf_op jit(solution)/shard_map/all_gather | solution.py:127
  524.4 3.8 copy-start.1
  528.2 3.8 copy-start.5
  529.9 2.2 copy-start.2
  532.0 2.8 copy-start.3
  532.1 2.8 copy-start.4
Sparse Core Ops, SparseCore 0:
  21.4 212.8 all-gather.4
  237.9 205.8 all-gather.6
  539.0 46.7 all-gather.8
where the time goes:
time: 605 us; the launch traced here: 604 us
  waiting for transfers between devices  305 us (50%)
  blocking collectives  157 us (26%)
  other arithmetic  92.6 us (15%)
  matrix products  20.3 us (3%)
  local copies, waits for them, and re-layouts  13.5 us (2%)
  between operations  13.4 us (2%)
    all_gather x2, waiting for transfers between devices, entering(): lax.all_gather(part.astype(kind), axis)  257 us
    all_gather x1, blocking collectives, entering(): lax.all_gather(part.astype(kind), axis)  157 us
    select_n x64, other arithmetic, hop(): return jax.tree.map(lambda a, b: jnp.where(reached, a, b), new, before)  75.9 us
    all_gather x1, waiting for transfers between devices, per_device(): lax.all_gather(attended, 'tensor', axis=1, tiled=True)  46.9 us
  transfers between devices with their start and end apart: 3, of which 3 were waited for; matrix products, arithmetic and copies ran while one was open for 1% of the time, Pallas kernels for 0%

commit v1 on v0

v1 whole, which is shorter than its diff:
```python
import functools
import math

import jax
import jax.numpy as jnp
from jax import lax
from jax.experimental import pallas as pl
from jax.experimental.pallas import tpu as pltpu
from jax.sharding import PartitionSpec as P

HEAD_DIM = 128
SEG_LEN = 256
LEVELS = 4
PIECE = 8
MASKED = -1e30
EXP2_SCALE = math.log2(math.e) * HEAD_DIM ** (-0.5)
VMEM_LIMIT = 40 * 1024 * 1024


def path_of(parents_ref, seg):
    path = [parents_ref[seg]]
    for _ in range(LEVELS - 1):
        up = parents_ref[jnp.maximum(path[-1], 0)]
        path.append(jnp.where(path[-1] >= 0, up, -1))
    depth = sum((p >= 0).astype(jnp.int32) for p in path)
    return path, depth


def ancestry_kernel(first_ref, parents_ref, table_ref, limits_ref):
    targets = table_ref.shape[0] // LEVELS

    @pl.loop(0, targets)
    def _(target):
        path, depth = path_of(parents_ref, 2 * target)
        for level in range(LEVELS):
            found = jnp.int32(0)
            for up in range(LEVELS):
                found = jnp.where(depth - 1 - up == level, path[up], found)
            table_ref[target * LEVELS + level] = found

    first = first_ref[0]
    _, depth0 = path_of(parents_ref, first)
    _, depth1 = path_of(parents_ref, first + 1)
    limits_ref[0] = depth0
    limits_ref[1] = jnp.minimum(depth0, depth1)
    limits_ref[2] = (parents_ref[first + 1] == first).astype(jnp.int32)


def ancestry(first, parents, targets):
    smem = pl.BlockSpec(memory_space=pltpu.SMEM)
    return pl.pallas_call(
        ancestry_kernel,
        out_shape=(
            jax.ShapeDtypeStruct((targets * LEVELS,), jnp.int32),
            jax.ShapeDtypeStruct((3,), jnp.int32),
        ),
        in_specs=[smem, smem],
        out_specs=(smem, smem),
        cost_estimate=pl.CostEstimate(flops=8000, bytes_accessed=2000, transcendentals=0),
        name="ancestry",
    )(first, parents)


def pick_kernel(table_ref, pieces_ref, picked_ref):
    @pl.loop(0, picked_ref.shape[0], unroll=8)
    def _(slot):
        picked_ref[slot] = pieces_ref[table_ref[slot]]


def pick(table, pieces):
    slots = table.shape[0]
    vmem = pl.BlockSpec(memory_space=pltpu.VMEM)
    return pl.pallas_call(
        pick_kernel,
        out_shape=jax.ShapeDtypeStruct((slots,) + pieces.shape[1:], pieces.dtype),
        in_specs=[pl.BlockSpec(memory_space=pltpu.SMEM), vmem],
        out_specs=vmem,
        cost_estimate=pl.CostEstimate(flops=0, bytes_accessed=1 << 20, transcendentals=0),
        name="pick",
    )(table, pieces)


def attend_kernel(limits_ref, query_ref, path_key_ref, path_value_ref, key_ref, value_ref, out_ref):
    def scores_of(query, keys):
        return lax.dot_general(
            query, keys, (((1,), (1,)), ((), ())), preferred_element_type=jnp.float32
        )

    def with_ones(values):
        return jnp.concatenate([values, jnp.ones_like(values)], axis=1)

    path_keys, path_values = path_key_ref[...], with_ones(path_value_ref[...])
    level = (lax.broadcasted_iota(jnp.int32, (1, path_keys.shape[0]), 1) // PIECE) % LEVELS
    rows = lax.broadcasted_iota(jnp.int32, (SEG_LEN, SEG_LEN), 0)
    columns = lax.broadcasted_iota(jnp.int32, (SEG_LEN, SEG_LEN), 1)
    for seg in range(2):
        here = slice(seg * SEG_LEN, (seg + 1) * SEG_LEN)
        query = query_ref[here]
        path_scores = scores_of(query, path_keys)
        path_scores = path_scores + jnp.where(level < limits_ref[seg], 0.0, MASKED)
        own_scores = jnp.where(columns <= rows, scores_of(query, key_ref[here]), MASKED)
        blocks = [(path_scores, path_values), (own_scores, with_ones(value_ref[here]))]
        if seg == 1:
            before = scores_of(query, key_ref[:SEG_LEN])
            before = before + jnp.where(limits_ref[2] > 0, 0.0, MASKED)
            blocks.append((before, with_ones(value_ref[:SEG_LEN])))
        row_max = functools.reduce(
            jnp.maximum, [jnp.max(s, axis=1, keepdims=True) for s, _ in blocks]
        )
        total = None
        for scores, values in blocks:
            weights = jnp.exp2((scores - row_max) * EXP2_SCALE).astype(jnp.bfloat16)
            part = jnp.dot(weights, values, preferred_element_type=jnp.float32)
            total = part if total is None else total + part
        out_ref[here] = (total[:, :HEAD_DIM] / total[:, HEAD_DIM:]).astype(out_ref.dtype)


def attend(limits, queries, path_keys, path_values, keys, values, first_head, heads):
    rows = queries.shape[0]
    whole = lambda a: pl.BlockSpec(a.shape, lambda h, limits: (0, 0))
    key_count = path_keys.shape[0] + SEG_LEN + SEG_LEN // 2
    return pl.pallas_call(
        attend_kernel,
        grid_spec=pltpu.PrefetchScalarGridSpec(
            num_scalar_prefetch=1,
            grid=(heads,),
            in_specs=[
                pl.BlockSpec((rows, HEAD_DIM), lambda h, limits: (0, first_head + h)),
                whole(path_keys),
                whole(path_values),
                whole(keys),
                whole(values),
            ],
            out_specs=pl.BlockSpec((rows, HEAD_DIM), lambda h, limits: (0, h)),
        ),
        out_shape=jax.ShapeDtypeStruct((rows, heads * HEAD_DIM), jnp.bfloat16),
        compiler_params=pltpu.CompilerParams(vmem_limit_bytes=VMEM_LIMIT),
        cost_estimate=pl.CostEstimate(
            flops=heads * rows * key_count * HEAD_DIM * 6,
            bytes_accessed=heads * rows * HEAD_DIM * 4 + 4 * path_keys.size,
            transcendentals=heads * rows * key_count,
        ),
        name="attend",
    )(limits, queries, path_keys, path_values, keys, values)


def project_kernel(count, has_base, blocks_ref, *refs):
    parts, weight_ref, rest = refs[:count], refs[count], refs[count + 1 :]
    base_ref = rest[0] if has_base else None
    out_ref, total_ref = rest[-2:]
    step = pl.program_id(0)

    for i in range(count):

        @pl.when(step == i)
        def _(i=i):
            product = jnp.dot(parts[i][...], weight_ref[...], preferred_element_type=jnp.float32)
            if i == 0:
                before = base_ref[...] if has_base else None
            else:
                before = total_ref[...]
            total = product if before is None else before + product
            if i == count - 1:
                out_ref[...] = total.astype(out_ref.dtype)
            else:
                total_ref[...] = total


def project(parts, blocks, weight, base, dtype):
    rows, depth = parts[0].shape
    width = weight.shape[1]
    count = len(parts)
    whole = lambda shape: pl.BlockSpec(shape, lambda k, blocks: (0, 0))
    in_specs = [whole(p.shape) for p in parts]
    in_specs.append(pl.BlockSpec((depth, width), lambda k, blocks: (blocks[k], 0)))
    args = list(parts) + [weight]
    if base is not None:
        in_specs.append(whole(base.shape))
        args.append(base)
    return pl.pallas_call(
        functools.partial(project_kernel, count, base is not None),
        grid_spec=pltpu.PrefetchScalarGridSpec(
            num_scalar_prefetch=1,
            grid=(count,),
            in_specs=in_specs,
            out_specs=whole((rows, width)),
            scratch_shapes=[pltpu.VMEM((rows, width), jnp.float32)],
        ),
        out_shape=jax.ShapeDtypeStruct((rows, width), dtype),
        compiler_params=pltpu.CompilerParams(vmem_limit_bytes=VMEM_LIMIT),
        cost_estimate=pl.CostEstimate(
            flops=2 * count * rows * depth * width,
            bytes_accessed=2 * count * depth * (rows + width) + 4 * rows * width,
            transcendentals=0,
        ),
        name="project",
    )(blocks, *args)


def swap(part, bit):
    size = lax.axis_size("tensor")
    return lax.ppermute(part, "tensor", [(i, i ^ bit) for i in range(size)])


def per_device(queries, key_proj, value_proj, out_weight, parents):
    devices = lax.axis_size("dp")
    me = lax.axis_index("tensor")
    segs = queries.shape[0] // SEG_LEN
    first = (lax.axis_index("dp") * segs).astype(jnp.int32).reshape(1)
    table, limits = ancestry(first, parents, devices)

    half = devices // 2
    cut = lambda a: a.reshape(segs, half, PIECE, HEAD_DIM)
    pieces = jnp.concatenate([cut(key_proj), cut(value_proj)], axis=1).transpose(1, 0, 2, 3)
    pieces = lax.all_to_all(pieces, "dp", 0, 0, tiled=True)
    picked = pick(table, pieces.reshape(devices * segs, PIECE, HEAD_DIM))
    picked = picked.reshape(devices, LEVELS, PIECE, HEAD_DIM)
    picked = lax.all_to_all(picked, "dp", 0, 0, tiled=True)
    path = picked.reshape(2, half * LEVELS * PIECE, HEAD_DIM)

    heads = queries.shape[1] // HEAD_DIM
    chunk = 2
    chunks = heads // chunk
    own = [
        attend(limits, queries, path[0], path[1], key_proj, value_proj, c * chunk, chunk)
        for c in range(chunks)
    ]
    across = [swap(part, 2) for part in own]
    beside = [swap(part, 1) for part in own]
    corner = [swap(part, 1) for part in across]
    where = lambda bit: (me ^ bit) * chunks + jnp.arange(chunks, dtype=jnp.int32)
    near = project(
        own + beside, jnp.concatenate([where(0), where(1)]), out_weight, None, jnp.float32
    )
    far = jnp.stack([where(2), where(3)], axis=1).reshape(-1)
    far_parts = [part for pair in zip(across, corner) for part in pair]
    split = 2 * (chunks - 1)
    near = project(far_parts[:split], far[:split], out_weight, near, jnp.float32)
    return project(far_parts[split:], far[split:], out_weight, near, jnp.bfloat16)


def solution(mesh):
    placed = (P("dp", "tensor"), P("dp", "tensor"), P("dp", "tensor"), P(None, "tensor"), P())
    return jax.shard_map(
        per_device, mesh=mesh, in_specs=placed, out_specs=P("dp", "tensor"), check_vma=False
    )
```

time: 605 us -> 117 us (0.19)
  waiting for transfers between devices: 305 us -> 38.7 us
  blocking collectives: 157 us -> 0 us
  other arithmetic: 92.6 us -> 1.98 us
  Pallas kernels: 0 us -> 40 us
  starting transfers between devices: 0.08 us -> 34.7 us
  matrix products: 20.3 us -> 0 us
  between operations: 13.4 us -> 0.24 us
  local copies, waits for them, and re-layouts: 13.5 us -> 0.86 us
    all_gather x3 -> x0, waiting for transfers between devices: 304 us -> none  [the longest x2 257 us: entering(): lax.all_gather(part.astype(kind), axis)]
    all_gather x1 -> x0, blocking collectives: 157 us -> none  [entering(): lax.all_gather(part.astype(kind), axis)]
    select_n x73 -> x0, other arithmetic: 81.7 us -> none  [the longest x64 75.9 us: hop(): return jax.tree.map(lambda a, b: jnp.where(reached, a, b), new, before)]
    pallas_call x0 -> x9, Pallas kernels: none -> 40 us  [the longest x3 18.4 us: project(): pl.pallas_call(functools.partial(project_kernel, count, base is not None)...]
    all_to_all x0 -> x2, waiting for transfers between devices: none -> 25.9 us  [the longest x1 16.7 us: per_device(): picked = lax.all_to_all(picked, 'dp', 0, 0, tiled=True)]
    all_to_all x0 -> x2, starting transfers between devices: none -> 21.1 us  [the longest x1 15.1 us: per_device(): pieces = lax.all_to_all(pieces, 'dp', 0, 0, tiled=True)]
    dot_general x5 -> x0, matrix products: 20.3 us -> none  [the longest x1 11.3 us: per_device(): jnp.dot(lax.all_gather(attended, 'tensor', axis=1, tiled=True), out_weigh...]
    ppermute x0 -> x12, starting transfers between devices: none -> 13.6 us  [swap(): return lax.ppermute(part, 'tensor', [(i, i ^ bit) for i in range(size)])]
  transfers between devices with their start and end apart: 3 -> 14, of which waited for: 3 -> 5; matrix products, arithmetic and copies ran while one was open for 1% -> 0% of each run, Pallas kernels for 0% -> 19%
where the time goes in v1:
time: 117 us; the launch traced here: 116 us
  Pallas kernels  40 us (34%)
  waiting for transfers between devices  38.7 us (33%)
  starting transfers between devices  34.7 us (30%)
  other arithmetic  1.98 us (2%)
    pallas_call x3, Pallas kernels, project(): pl.pallas_call(functools.partial(project_kernel, count, base is not None)...  18.4 us
    all_to_all x1, waiting for transfers between devices, per_device(): picked = lax.all_to_all(picked, 'dp', 0, 0, tiled=True)  16.7 us
    pallas_call x4, Pallas kernels, attend(): pl.pallas_call(attend_kernel, grid_spec=pltpu.PrefetchScalarGridSpec(num_...  15.6 us
    all_to_all x1, starting transfers between devices, per_device(): pieces = lax.all_to_all(pieces, 'dp', 0, 0, tiled=True)  15.1 us
    ppermute x12, starting transfers between devices, swap(): return lax.ppermute(part, 'tensor', [(i, i ^ bit) for i in range(size)])  13.6 us
    ppermute x12, waiting for transfers between devices, swap(): return lax.ppermute(part, 'tensor', [(i, i ^ bit) for i in range(size)])  12.8 us
    all_to_all x1, waiting for transfers between devices, per_device(): pieces = lax.all_to_all(pieces, 'dp', 0, 0, tiled=True)  9.19 us
    all_to_all x1, starting transfers between devices, per_device(): picked = lax.all_to_all(picked, 'dp', 0, 0, tiled=True)  6 us
  transfers between devices with their start and end apart: 14, of which 5 were waited for; matrix products, arithmetic and copies ran while one was open for 0% of the time, Pallas kernels for 19%

profile of v1, /device:TPU:1, one launch (start us, length us, event | category | flops | bytes accessed | tf_op | source)
XLA Modules:
  0.0 116.4 jit_solution(4617837899249329720)
XLA Ops:
  0.0 1.8 %copy_bitcast_fusion = bf16[64,2,8,128]{3,2,1,0:T(8,128)(2,1)} fusion(bf16[2,32,8,128]{3,2,1,0:T(8,128)(2,1)} %bitcast.22, bf16[2,32,8,128]{3,2,1,0:T(8,128)(2,1)} %bitcast.23), kind=kLoop, calls=%fused_computation.1 | loop fusion | flops 131072 | bytes 524288 | tf_op jit(solution)/shard_map/transpose | solution.py:214
  1.8 15.1 %all-to-all-start = ((bf16[64,2,8,128]{3,2,1,0:T(8,128)(2,1)}), bf16[64,2,8,128]{3,2,1,0:T(8,128)(2,1)S(1)}, u32[]{:S(2)}, u32[]{:S(2)}) async-start(bf16[64,2,8,128]{3,2,1,0:T(8,128)(2,1)} %copy_bitcast_fusion), calls=%async_computation | async-start | bytes 524288 | tf_op jit(solution)/shard_map/all_to_all | solution.py:215
  17.0 3.8 %ancestry.1 = (s32[256]{0:T(256)}, s32[3]{0:T(128)}) custom-call(s32[1]{0:T(128)} %bitcast.1.first_ref, s32[128]{0:T(128)} %parents_ref.1), custom_call_target="tpu_custom_call" | custom-call | flops 8000 | bytes 2000 | tf_op jit(solution)/shard_map/ancestry/pallas_call | solution.py:51
  20.8 9.2 %all-to-all-done = bf16[64,2,8,128]{3,2,1,0:T(8,128)(2,1)S(1)} async-done(((bf16[64,2,8,128]{3,2,1,0:T(8,128)(2,1)}), bf16[64,2,8,128]{3,2,1,0:T(8,128)(2,1)S(1)}, u32[]{:S(2)}, u32[]{:S(2)}) %all-to-all-start) | async-done | bytes 262176 | tf_op jit(solution)/shard_map/all_to_all | solution.py:215
  30.0 0.7 copy-done.5
  30.7 2.2 %pick.1 = bf16[256,8,128]{2,1,0:T(8,128)(2,1)} custom-call(s32[256]{0:T(256)} %get-tuple-element.8.table_ref, bf16[128,8,128]{2,1,0:T(8,128)(2,1)} %bitcast.25), custom_call_target="tpu_custom_call" | custom-call | bytes 1048576 | tf_op jit(solution)/shard_map/pick/pallas_call | solution.py:73
  32.9 6.0 %all-to-all-start.1 = ((bf16[64,4,8,128]{3,2,1,0:T(8,128)(2,1)}), bf16[64,4,8,128]{3,2,1,0:T(8,128)(2,1)S(1)}, u32[]{:S(2)}, u32[]{:S(2)}) async-start(bf16[64,4,8,128]{3,2,1,0:T(8,128)(2,1)} %bitcast.24), calls=%async_computation.1 | async-start | bytes 1048576 | tf_op jit(solution)/shard_map/all_to_all | solution.py:218
  38.9 16.7 %all-to-all-done.1 = bf16[64,4,8,128]{3,2,1,0:T(8,128)(2,1)S(1)} async-done(((bf16[64,4,8,128]{3,2,1,0:T(8,128)(2,1)}), bf16[64,4,8,128]{3,2,1,0:T(8,128)(2,1)S(1)}, u32[]{:S(2)}, u32[]{:S(2)}) %all-to-all-start.1) | async-done | bytes 524320 | tf_op jit(solution)/shard_map/all_to_all | solution.py:218
  55.6 3.9 %attend.7.refs_2_ = bf16[512,256]{1,0:T(8,128)(2,1)S(1)} custom-call(s32[3]{0:T(128)S(1)} %copy-done.4, bf16[512,1024]{1,0:T(8,128)(2,1)S(1)} %copy-done.2, bf16[1024,128]{1,0:T(8,128)(2,1)S(1)} %bitcast.18, bf16[1024,128]{1,0:T(8,128)(2,1)S(1)} %bitcast.14, bf16[512,128]{1,0:T(8,128)(2,1)S(1)} %copy-done.1, bf16[512,128]{1,0:T(8,128)(2,1)S(1)} %copy-done), custom_call_target="tpu_custom_call" | custom-call | flops 1107296256 | bytes 1048576 | tf_op jit(solution)/shard_map/attend/pallas_call | solution.py:122
  59.6 3.9 %attend.6.refs_1_ = bf16[512,256]{1,0:T(8,128)(2,1)S(1)} custom-call(s32[3]{0:T(128)S(1)} %copy-done.4, bf16[512,1024]{1,0:T(8,128)(2,1)S(1)} %copy-done.2, bf16[1024,128]{1,0:T(8,128)(2,1)S(1)} %bitcast.19, bf16[1024,128]{1,0:T(8,128)(2,1)S(1)} %bitcast.15, bf16[512,128]{1,0:T(8,128)(2,1)S(1)} %copy-done.1, bf16[512,128]{1,0:T(8,128)(2,1)S(1)} %copy-done), custom_call_target="tpu_custom_call" | custom-call | flops 1107296256 | bytes 1048576 | tf_op jit(solution)/shard_map/attend/pallas_call | solution.py:122
  63.5 3.9 %attend.5.refs_0_ = bf16[512,256]{1,0:T(8,128)(2,1)S(1)} custom-call(s32[3]{0:T(128)S(1)} %copy-done.4, bf16[512,1024]{1,0:T(8,128)(2,1)S(1)} %copy-done.2, bf16[1024,128]{1,0:T(8,128)(2,1)S(1)} %bitcast.20, bf16[1024,128]{1,0:T(8,128)(2,1)S(1)} %bitcast.16, bf16[512,128]{1,0:T(8,128)(2,1)S(1)} %copy-done.1, bf16[512,128]{1,0:T(8,128)(2,1)S(1)} %copy-done), custom_call_target="tpu_custom_call" | custom-call | flops 1107296256 | bytes 1048576 | tf_op jit(solution)/shard_map/attend/pallas_call | solution.py:122
  67.4 4.2 %collective-permute-start.10 = (bf16[512,256]{1,0:T(8,128)(2,1)S(1)}, bf16[512,256]{1,0:T(8,128)(2,1)S(1)}, u32[]{:S(2)}, u32[]{:S(2)}) collective-permute-start(bf16[512,256]{1,0:T(8,128)(2,1)S(1)} %attend.7.refs_2_), channel_id=1, source_target_pairs={{0,1},{1,0},{2,3},{3,2},{4,5},{5,4},{6,7},{7,6},{8,9},{9,8},{10,11... | collective-permute-start | bytes 786440 | tf_op jit(solution)/shard_map/ppermute | solution.py:202
  71.6 0.1 collective-permute-start.9
  71.7 0.4 collective-permute-start.8
  72.1 0.1 pad_add_fusion
  72.2 0.3 collective-permute-start.4
  72.6 1.2 collective-permute-start.6
  73.7 3.9 %attend.4.refs_3_ = bf16[512,256]{1,0:T(8,128)(2,1)S(1)} custom-call(s32[3]{0:T(128)S(1)} %copy-done.4, bf16[512,1024]{1,0:T(8,128)(2,1)S(1)} %copy-done.3, bf16[1024,128]{1,0:T(8,128)(2,1)S(1)} %bitcast.21, bf16[1024,128]{1,0:T(8,128)(2,1)S(1)} %bitcast.17, bf16[512,128]{1,0:T(8,128)(2,1)S(1)} %copy-done.1, bf16[512,128]{1,0:T(8,128)(2,1)S(1)} %copy-done), custom_call_target="tpu_custom_call" | custom-call | flops 1107296256 | bytes 1048576 | tf_op jit(solution)/shard_map/attend/pallas_call | solution.py:122
  77.6 0.4 collective-permute-start.2
  78.0 0.9 collective-permute-start.11
  79.0 1.2 %collective-permute-start = (bf16[512,256]{1,0:T(8,128)(2,1)S(1)}, bf16[512,256]{1,0:T(8,128)(2,1)}, u32[]{:S(2)}, u32[]{:S(2)}) collective-permute-start(bf16[512,256]{1,0:T(8,128)(2,1)S(1)} %attend.4.refs_3_), channel_id=1, source_target_pairs={{0,2},{1,3},{2,0},{3,1},{4,6},{5,7},{6,4},{7,5},{8,10},{9,11},{10,... | collective-permute-start | bytes 786440 | tf_op jit(solution)/shard_map/ppermute | solution.py:202
  80.2 1.3 %collective-permute-start.5 = (bf16[512,256]{1,0:T(8,128)(2,1)S(1)}, bf16[512,256]{1,0:T(8,128)(2,1)}, u32[]{:S(2)}, u32[]{:S(2)}) collective-permute-start(bf16[512,256]{1,0:T(8,128)(2,1)S(1)} %collective-permute-done.4.refs_2_), channel_id=1, source_target_pairs={{0,1},{1,0},{2,3},{3,2},{4,5},{5,4},{6,7},{7,6},{8,9},{9,8},{10,11... | collective-permute-start | bytes 786440 | tf_op jit(solution)/shard_map/ppermute | solution.py:202
  81.4 4.3 %collective-permute-done.6.refs_4_ = bf16[512,256]{1,0:T(8,128)(2,1)S(1)} collective-permute-done((bf16[512,256]{1,0:T(8,128)(2,1)S(1)}, bf16[512,256]{1,0:T(8,128)(2,1)S(1)}, u32[]{:S(2)}, u32[]{:S(2)}) %collective-permute-start.6) | collective-permute-done | bytes 262176 | tf_op jit(solution)/shard_map/ppermute | solution.py:202
  85.7 1.3 %collective-permute-start.7 = (bf16[512,256]{1,0:T(8,128)(2,1)S(1)}, bf16[512,256]{1,0:T(8,128)(2,1)}, u32[]{:S(2)}, u32[]{:S(2)}) collective-permute-start(bf16[512,256]{1,0:T(8,128)(2,1)S(1)} %collective-permute-done.6.refs_4_), channel_id=1, source_target_pairs={{0,1},{1,0},{2,3},{3,2},{4,5},{5,4},{6,7},{7,6},{8,9},{9,8},{10,11... | collective-permute-start | bytes 786440 | tf_op jit(solution)/shard_map/ppermute | solution.py:202
  87.1 4.3 %collective-permute-done.2.refs_0_ = bf16[512,256]{1,0:T(8,128)(2,1)S(1)} collective-permute-done((bf16[512,256]{1,0:T(8,128)(2,1)S(1)}, bf16[512,256]{1,0:T(8,128)(2,1)S(1)}, u32[]{:S(2)}, u32[]{:S(2)}) %collective-permute-start.2) | collective-permute-done | bytes 262176 | tf_op jit(solution)/shard_map/ppermute | solution.py:202
  91.3 1.3 %collective-permute-start.3 = (bf16[512,256]{1,0:T(8,128)(2,1)S(1)}, bf16[512,256]{1,0:T(8,128)(2,1)}, u32[]{:S(2)}, u32[]{:S(2)}) collective-permute-start(bf16[512,256]{1,0:T(8,128)(2,1)S(1)} %collective-permute-done.2.refs_0_), channel_id=1, source_target_pairs={{0,1},{1,0},{2,3},{3,2},{4,5},{5,4},{6,7},{7,6},{8,9},{9,8},{10,11... | collective-permute-start | bytes 786440 | tf_op jit(solution)/shard_map/ppermute | solution.py:202
  92.7 0.1 slice.31.blocks_ref
  92.8 4.2 %collective-permute-done.refs_0_ = bf16[512,256]{1,0:T(8,128)(2,1)} collective-permute-done((bf16[512,256]{1,0:T(8,128)(2,1)S(1)}, bf16[512,256]{1,0:T(8,128)(2,1)}, u32[]{:S(2)}, u32[]{:S(2)}) %collective-permute-start) | collective-permute-done | bytes 262176 | tf_op jit(solution)/shard_map/ppermute | solution.py:202
  97.1 0.9 collective-permute-start.1
  97.9 8.4 %project.3.refs_7_ = f32[512,1280]{1,0:T(8,128)S(1)} custom-call(s32[8]{0:T(128)S(1)} %pad_add_fusion.1.blocks_ref, bf16[512,256]{1,0:T(8,128)(2,1)S(1)} %attend.5.refs_0_, bf16[512,256]{1,0:T(8,128)(2,1)S(1)} %attend.6.refs_1_, bf16[512,256]{1,0:T(8,128)(2,1)S(1)} %attend.7.refs_2_, bf16[512,256]{1,0:T(8,128)(2,1)S(1)} %attend.4.refs_3_, ...), custom_call_target="tpu_custom_call" | custom-call | flops 2684354560 | bytes 9961472 | tf_op jit(solution)/shard_map/project/pallas_call | solution.py:180
  106.4 6.3 %project.4.refs_3_ = f32[512,1280]{1,0:T(8,128)S(1)} custom-call(s32[6]{0:T(128)S(1)} %slice.31.blocks_ref, bf16[512,256]{1,0:T(8,128)(2,1)S(1)} %collective-permute-done.2.refs_0_, bf16[512,256]{1,0:T(8,128)(2,1)} %collective-permute-done.3.refs_1_, bf16[512,256]{1,0:T(8,128)(2,1)S(1)} %collective-permute-done.4.refs_2_, ...), custom_call_target="tpu_custom_call" | custom-call | flops 2013265920 | bytes 8126464 | tf_op jit(solution)/shard_map/project/pallas_call | solution.py:180
  112.8 3.6 %project.5 = bf16[512,1280]{1,0:T(8,128)(2,1)} custom-call(s32[2]{0:T(128)S(1)} %slice_bitcast_fusion.blocks_ref, bf16[512,256]{1,0:T(8,128)(2,1)} %collective-permute-done.refs_0_, bf16[512,256]{1,0:T(8,128)(2,1)S(1)} %collective-permute-done.1.refs_1_, bf16[4096,1280]{1,0:T(8,128)(2,1)S(1)} %bitcast.13, f32[512,1280]{1,0:T(8,128)S(1)} %project.4.refs_3_), custom_call_target="tpu_custom_call" | custom-call | flops 671088640 | bytes 4456448 | tf_op jit(solution)/shard_map/project/pallas_call | solution.py:180
  (32 shorter events, 0.2 us)
Async XLA Ops:
  0.0 55.6 %copy-start.1 = (bf16[512,128]{1,0:T(8,128)(2,1)S(1)}, bf16[512,128]{1,0:T(8,128)(2,1)}, u32[]{:S(2)}) copy-start(bf16[512,128]{1,0:T(8,128)(2,1)} %key_ref.7) | copy-start | bytes 393220
  0.0 55.6 %copy-start = (bf16[512,128]{1,0:T(8,128)(2,1)S(1)}, bf16[512,128]{1,0:T(8,128)(2,1)}, u32[]{:S(2)}) copy-start(bf16[512,128]{1,0:T(8,128)(2,1)} %value_ref.7) | copy-start | bytes 393220
  0.0 55.6 %copy-start.2 = (bf16[512,1024]{1,0:T(8,128)(2,1)S(1)}, bf16[512,1024]{1,0:T(8,128)(2,1)}, u32[]{:S(2)}) copy-start(bf16[512,1024]{1,0:T(8,128)(2,1)} %query_ref.7) | copy-start | bytes 3145732
  1.8 28.1 %all-to-all-start = ((bf16[64,2,8,128]{3,2,1,0:T(8,128)(2,1)}), bf16[64,2,8,128]{3,2,1,0:T(8,128)(2,1)S(1)}, u32[]{:S(2)}, u32[]{:S(2)}) async-start(bf16[64,2,8,128]{3,2,1,0:T(8,128)(2,1)} %copy_bitcast_fusion), calls=%async_computation | async-start | bytes 524288 | tf_op jit(solution)/shard_map/all_to_all | solution.py:215
  20.8 34.9 %copy-start.4 = (s32[3]{0:T(128)S(1)}, s32[3]{0:T(128)}, u32[]{:S(2)}) copy-start(s32[3]{0:T(128)} %get-tuple-element.7.limits_ref) | copy-start | bytes 40
  30.0 0.7 copy-start.5
  32.9 22.7 %all-to-all-start.1 = ((bf16[64,4,8,128]{3,2,1,0:T(8,128)(2,1)}), bf16[64,4,8,128]{3,2,1,0:T(8,128)(2,1)S(1)}, u32[]{:S(2)}, u32[]{:S(2)}) async-start(bf16[64,4,8,128]{3,2,1,0:T(8,128)(2,1)} %bitcast.24), calls=%async_computation.1 | async-start | bytes 1048576 | tf_op jit(solution)/shard_map/all_to_all | solution.py:218
  63.5 10.2 %copy-start.3 = (bf16[512,1024]{1,0:T(8,128)(2,1)S(1)}, bf16[512,1024]{1,0:T(8,128)(2,1)}, u32[]{:S(2)}) copy-start(bf16[512,1024]{1,0:T(8,128)(2,1)} %query_ref.7) | copy-start | bytes 3145732
  67.4 10.2 %collective-permute-start.10 = (bf16[512,256]{1,0:T(8,128)(2,1)S(1)}, bf16[512,256]{1,0:T(8,128)(2,1)S(1)}, u32[]{:S(2)}, u32[]{:S(2)}) collective-permute-start(bf16[512,256]{1,0:T(8,128)(2,1)S(1)} %attend.7.refs_2_), channel_id=1, source_target_pairs={{0,1},{1,0},{2,3},{3,2},{4,5},{5,4},{6,7},{7,6},{8,9},{9,8},{10,11... | collective-permute-start | bytes 786440 | tf_op jit(solution)/shard_map/ppermute | solution.py:202
  71.6 6.4 %collective-permute-start.9 = (bf16[512,256]{1,0:T(8,128)(2,1)S(1)}, bf16[512,256]{1,0:T(8,128)(2,1)S(1)}, u32[]{:S(2)}, u32[]{:S(2)}) collective-permute-start(bf16[512,256]{1,0:T(8,128)(2,1)S(1)} %attend.6.refs_1_), channel_id=1, source_target_pairs={{0,1},{1,0},{2,3},{3,2},{4,5},{5,4},{6,7},{7,6},{8,9},{9,8},{10,11... | collective-permute-start | bytes 786440 | tf_op jit(solution)/shard_map/ppermute | solution.py:202
  71.7 7.3 %collective-permute-start.8 = (bf16[512,256]{1,0:T(8,128)(2,1)S(1)}, bf16[512,256]{1,0:T(8,128)(2,1)S(1)}, u32[]{:S(2)}, u32[]{:S(2)}) collective-permute-start(bf16[512,256]{1,0:T(8,128)(2,1)S(1)} %attend.5.refs_0_), channel_id=1, source_target_pairs={{0,1},{1,0},{2,3},{3,2},{4,5},{5,4},{6,7},{7,6},{8,9},{9,8},{10,11... | collective-permute-start | bytes 786440 | tf_op jit(solution)/shard_map/ppermute | solution.py:202
  72.2 7.9 %collective-permute-start.4 = (bf16[512,256]{1,0:T(8,128)(2,1)S(1)}, bf16[512,256]{1,0:T(8,128)(2,1)S(1)}, u32[]{:S(2)}, u32[]{:S(2)}) collective-permute-start(bf16[512,256]{1,0:T(8,128)(2,1)S(1)} %attend.6.refs_1_), channel_id=1, source_target_pairs={{0,2},{1,3},{2,0},{3,1},{4,6},{5,7},{6,4},{7,5},{8,10},{9,11},{10,... | collective-permute-start | bytes 786440 | tf_op jit(solution)/shard_map/ppermute | solution.py:202
  72.6 13.2 %collective-permute-start.6 = (bf16[512,256]{1,0:T(8,128)(2,1)S(1)}, bf16[512,256]{1,0:T(8,128)(2,1)S(1)}, u32[]{:S(2)}, u32[]{:S(2)}) collective-permute-start(bf16[512,256]{1,0:T(8,128)(2,1)S(1)} %attend.7.refs_2_), channel_id=1, source_target_pairs={{0,2},{1,3},{2,0},{3,1},{4,6},{5,7},{6,4},{7,5},{8,10},{9,11},{10,... | collective-permute-start | bytes 786440 | tf_op jit(solution)/shard_map/ppermute | solution.py:202
  77.6 13.7 %collective-permute-start.2 = (bf16[512,256]{1,0:T(8,128)(2,1)S(1)}, bf16[512,256]{1,0:T(8,128)(2,1)S(1)}, u32[]{:S(2)}, u32[]{:S(2)}) collective-permute-start(bf16[512,256]{1,0:T(8,128)(2,1)S(1)} %attend.5.refs_0_), channel_id=1, source_target_pairs={{0,2},{1,3},{2,0},{3,1},{4,6},{5,7},{6,4},{7,5},{8,10},{9,11},{10,... | collective-permute-start | bytes 786440 | tf_op jit(solution)/shard_map/ppermute | solution.py:202
  78.0 19.9 %collective-permute-start.11 = (bf16[512,256]{1,0:T(8,128)(2,1)S(1)}, bf16[512,256]{1,0:T(8,128)(2,1)S(1)}, u32[]{:S(2)}, u32[]{:S(2)}) collective-permute-start(bf16[512,256]{1,0:T(8,128)(2,1)S(1)} %attend.4.refs_3_), channel_id=1, source_target_pairs={{0,1},{1,0},{2,3},{3,2},{4,5},{5,4},{6,7},{7,6},{8,9},{9,8},{10,11... | collective-permute-start | bytes 786440 | tf_op jit(solution)/shard_map/ppermute | solution.py:202
  79.0 18.1 %collective-permute-start = (bf16[512,256]{1,0:T(8,128)(2,1)S(1)}, bf16[512,256]{1,0:T(8,128)(2,1)}, u32[]{:S(2)}, u32[]{:S(2)}) collective-permute-start(bf16[512,256]{1,0:T(8,128)(2,1)S(1)} %attend.4.refs_3_), channel_id=1, source_target_pairs={{0,2},{1,3},{2,0},{3,1},{4,6},{5,7},{6,4},{7,5},{8,10},{9,11},{10,... | collective-permute-start | bytes 786440 | tf_op jit(solution)/shard_map/ppermute | solution.py:202
  80.2 26.2 %collective-permute-start.5 = (bf16[512,256]{1,0:T(8,128)(2,1)S(1)}, bf16[512,256]{1,0:T(8,128)(2,1)}, u32[]{:S(2)}, u32[]{:S(2)}) collective-permute-start(bf16[512,256]{1,0:T(8,128)(2,1)S(1)} %collective-permute-done.4.refs_2_), channel_id=1, source_target_pairs={{0,1},{1,0},{2,3},{3,2},{4,5},{5,4},{6,7},{7,6},{8,9},{9,8},{10,11... | collective-permute-start | bytes 786440 | tf_op jit(solution)/shard_map/ppermute | solution.py:202
  85.7 20.7 %collective-permute-start.7 = (bf16[512,256]{1,0:T(8,128)(2,1)S(1)}, bf16[512,256]{1,0:T(8,128)(2,1)}, u32[]{:S(2)}, u32[]{:S(2)}) collective-permute-start(bf16[512,256]{1,0:T(8,128)(2,1)S(1)} %collective-permute-done.6.refs_4_), channel_id=1, source_target_pairs={{0,1},{1,0},{2,3},{3,2},{4,5},{5,4},{6,7},{7,6},{8,9},{9,8},{10,11... | collective-permute-start | bytes 786440 | tf_op jit(solution)/shard_map/ppermute | solution.py:202
  91.3 15.1 %collective-permute-start.3 = (bf16[512,256]{1,0:T(8,128)(2,1)S(1)}, bf16[512,256]{1,0:T(8,128)(2,1)}, u32[]{:S(2)}, u32[]{:S(2)}) collective-permute-start(bf16[512,256]{1,0:T(8,128)(2,1)S(1)} %collective-permute-done.2.refs_0_), channel_id=1, source_target_pairs={{0,1},{1,0},{2,3},{3,2},{4,5},{5,4},{6,7},{7,6},{8,9},{9,8},{10,11... | collective-permute-start | bytes 786440 | tf_op jit(solution)/shard_map/ppermute | solution.py:202
  97.1 15.7 %collective-permute-start.1 = (bf16[512,256]{1,0:T(8,128)(2,1)}, bf16[512,256]{1,0:T(8,128)(2,1)S(1)}, u32[]{:S(2)}, u32[]{:S(2)}) collective-permute-start(bf16[512,256]{1,0:T(8,128)(2,1)} %collective-permute-done.refs_0_), channel_id=1, source_target_pairs={{0,1},{1,0},{2,3},{3,2},{4,5},{5,4},{6,7},{7,6},{8,9},{9,8},{10,11... | collective-permute-start | bytes 786440 | tf_op jit(solution)/shard_map/ppermute | solution.py:202
  97.9 14.9 %slice-start = ((s8[10485760]{0:T(1024)(128)(4,1)}), s8[4194304]{0:T(1024)(128)(4,1)S(1)}, s32[]{:S(2)}) async-start(s8[10485760]{0:T(1024)(128)(4,1)} %bitcast.12), calls=%async_computation.2 | async-start | bytes 8388608
  97.9 14.9 %slice-start.1 = ((s8[10485760]{0:T(1024)(128)(4,1)}), s8[4194304]{0:T(1024)(128)(4,1)S(1)}, s32[]{:S(2)}) async-start(s8[10485760]{0:T(1024)(128)(4,1)} %bitcast.12), calls=%async_computation.3 | async-start | bytes 8388608
  106.4 6.4 %slice-start.2 = ((s8[10485760]{0:T(1024)(128)(4,1)}), s8[2097152]{0:T(1024)(128)(4,1)S(1)}, s32[]{:S(2)}) async-start(s8[10485760]{0:T(1024)(128)(4,1)} %bitcast.12), calls=%async_computation.4 | async-start | bytes 4194304

commit v2 on v1

v2 whole, which is shorter than its diff:
```python
import functools
import math

import jax
import jax.numpy as jnp
from jax import lax
from jax.experimental import pallas as pl
from jax.experimental.pallas import tpu as pltpu
from jax.sharding import PartitionSpec as P

HEAD_DIM = 128
SEG_LEN = 256
LEVELS = 4
FAR = LEVELS - 1
ROW = 8
ROW_SEGS = 2 * ROW
PIECE = SEG_LEN // ROW
PATH = LEVELS * SEG_LEN
FAR_ROWS = FAR * PIECE
MASKED = -1e30
EXP2_SCALE = math.log2(math.e) * HEAD_DIM ** (-0.5)
ATTEND_VMEM = 20 * 1024 * 1024
PROJECT_VMEM = 28 * 1024 * 1024

VMEM = pl.BlockSpec(memory_space=pltpu.VMEM)
SMEM = pl.BlockSpec(memory_space=pltpu.SMEM)
ANY = pl.BlockSpec(memory_space=pl.ANY)


def path_of(parents_ref, seg):
    path = [parents_ref[seg]]
    for _ in range(LEVELS - 1):
        up = parents_ref[jnp.maximum(path[-1], 0)]
        path.append(jnp.where(path[-1] >= 0, up, -1))
    depth = sum((p >= 0).astype(jnp.int32) for p in path)
    return path, depth


def level_of(path, depth, level):
    found = jnp.int32(0)
    for up in range(LEVELS):
        found = jnp.where(depth - 1 - up == level, path[up], found)
    return found


def ancestry_kernel(first_ref, parents_ref, table_ref, carry_ref, limits_ref):
    first = first_ref[0]
    base = (first // ROW_SEGS) * ROW_SEGS
    place = (first - base) // 2

    for shift in range(ROW):
        target = lax.rem(place + shift, ROW)
        path, depth = path_of(parents_ref, base + 2 * target)
        for level in range(FAR):
            seg = level_of(path, depth, level)
            slot = jnp.where(seg >= base - ROW_SEGS, ROW_SEGS + level, ROW_SEGS + FAR)
            table_ref[shift * FAR + level] = jnp.where(seg >= base, seg - base, slot)

    last = parents_ref.shape[0] - 1
    path, depth = path_of(parents_ref, jnp.minimum(base + ROW_SEGS, last))
    for level in range(FAR):
        carry_ref[level] = jnp.clip(level_of(path, depth, level) - base, 0, ROW_SEGS - 1)
    path, depth = path_of(parents_ref, jnp.minimum(base + 2 * ROW_SEGS, last))
    carry_ref[FAR] = jnp.clip(level_of(path, depth, 0) - base, 0, ROW_SEGS - 1)
    carry_ref[FAR + 1] = place

    _, depth0 = path_of(parents_ref, first)
    _, depth1 = path_of(parents_ref, first + 1)
    limits_ref[0] = depth0
    limits_ref[1] = jnp.minimum(depth0, depth1)
    limits_ref[2] = (parents_ref[first + 1] == first).astype(jnp.int32)


def ancestry(first, parents):
    shape = lambda n: jax.ShapeDtypeStruct((n,), jnp.int32)
    return pl.pallas_call(
        ancestry_kernel,
        out_shape=(shape(ROW * FAR), shape(FAR + 2), shape(3)),
        in_specs=[SMEM, SMEM],
        out_specs=(SMEM, SMEM, SMEM),
        cost_estimate=pl.CostEstimate(flops=8000, bytes_accessed=2000, transcendentals=0),
        name="ancestry",
    )(first, parents)


def pack_kernel(first_ref, parents_ref, key_ref, value_ref, deep_ref, *piece_refs):
    place = lax.rem(first_ref[0] // 2, ROW)
    for shift, piece_ref in enumerate(piece_refs):
        piece = lax.rem(place + shift, ROW)
        for seg in range(2):
            rows = pl.ds(pl.multiple_of(seg * SEG_LEN + piece * PIECE, PIECE), PIECE)
            piece_ref[seg, :PIECE] = key_ref[rows]
            piece_ref[seg, PIECE:] = value_ref[rows]
    _, depth = path_of(parents_ref, first_ref[0] + 1)
    start = jnp.where(depth == FAR, SEG_LEN, 0)
    rows = pl.ds(pl.multiple_of(start, SEG_LEN), SEG_LEN)
    deep_ref[:SEG_LEN] = key_ref[rows]
    deep_ref[SEG_LEN:] = value_ref[rows]


def pack(first, parents, keys, values):
    shape = lambda *dims: jax.ShapeDtypeStruct(dims, keys.dtype)
    return pl.pallas_call(
        pack_kernel,
        out_shape=(shape(2 * SEG_LEN, HEAD_DIM),) + (shape(2, 2 * PIECE, HEAD_DIM),) * ROW,
        in_specs=[SMEM, SMEM, VMEM, VMEM],
        out_specs=(VMEM,) * (ROW + 1),
        cost_estimate=pl.CostEstimate(flops=0, bytes_accessed=1 << 19, transcendentals=0),
        name="pack",
    )(first, parents, keys, values)


def carry_kernel(carry_ref, *refs):
    pieces, (held_ref, next_ref, second_ref) = refs[:ROW], refs[ROW:]
    place = carry_ref[FAR + 1]
    for shift, piece in enumerate(pieces):
        source = lax.rem(place + ROW - shift, ROW)
        held_ref[pl.ds(2 * source, 2)] = piece[...]
    for level in range(FAR):
        next_ref[level] = held_ref[carry_ref[level]]
    second_ref[0] = held_ref[carry_ref[FAR]]


def carry_out(carry, pieces):
    shape = lambda n: jax.ShapeDtypeStruct((n,) + pieces[0].shape[1:], pieces[0].dtype)
    return pl.pallas_call(
        carry_kernel,
        out_shape=(shape(ROW_SEGS), shape(FAR), shape(1)),
        in_specs=[SMEM] + [VMEM] * ROW,
        out_specs=(VMEM, VMEM, VMEM),
        cost_estimate=pl.CostEstimate(flops=0, bytes_accessed=1 << 18, transcendentals=0),
        name="carry_out",
    )(carry, *pieces)


def pick_kernel(table_ref, pieces_ref, next_ref, second_ref, *refs):
    picked, held_ref = refs[:ROW], refs[ROW]
    held_ref[:ROW_SEGS] = pieces_ref[...]
    held_ref[ROW_SEGS : ROW_SEGS + FAR] = next_ref[...]
    held_ref[ROW_SEGS + FAR :] = second_ref[...]
    for shift, picked_ref in enumerate(picked):
        for level in range(FAR):
            picked_ref[level] = held_ref[table_ref[shift * FAR + level]]


def pick(table, held, carried, second):
    dims = held.shape[1:]
    return pl.pallas_call(
        pick_kernel,
        out_shape=(jax.ShapeDtypeStruct((FAR,) + dims, held.dtype),) * ROW,
        in_specs=[SMEM, VMEM, VMEM, VMEM],
        out_specs=(VMEM,) * ROW,
        scratch_shapes=[pltpu.VMEM((ROW_SEGS + FAR + 1,) + dims, held.dtype)],
        cost_estimate=pl.CostEstimate(flops=0, bytes_accessed=1 << 20, transcendentals=0),
        name="pick",
    )(table, held, carried, second)


def attend_kernel(first_head, heads, limits_ref, query_ref, key_ref, value_ref, deep_ref, *refs):
    pieces = refs[:ROW]
    out_ref, path_key_ref, path_value_ref = refs[-3:]

    def scores_of(query, keys):
        return lax.dot_general(
            query, keys, (((1,), (1,)), ((), ())), preferred_element_type=jnp.float32
        )

    def with_ones(values):
        return jnp.concatenate([values, jnp.ones_like(values)], axis=1)

    for at, piece in enumerate(pieces):
        for level in range(FAR):
            rows = pl.ds(at * FAR_ROWS + level * PIECE, PIECE)
            path_key_ref[rows, :HEAD_DIM] = piece[level, :PIECE]
            path_value_ref[rows, :HEAD_DIM] = piece[level, PIECE:]
    path_key_ref[FAR * SEG_LEN :, :HEAD_DIM] = deep_ref[:SEG_LEN]
    path_value_ref[FAR * SEG_LEN :, :HEAD_DIM] = deep_ref[SEG_LEN:]
    path_value_ref[:, HEAD_DIM:] = jnp.ones((PATH, HEAD_DIM), jnp.bfloat16)
    row = lax.broadcasted_iota(jnp.int32, (PATH, HEAD_DIM), 0)
    lane = lax.broadcasted_iota(jnp.int32, (PATH, HEAD_DIM), 1)
    level = jnp.where(row < FAR * SEG_LEN, lax.rem(row // PIECE, FAR), FAR)
    limit = jnp.where(lane == 0, limits_ref[0], jnp.where(lane == 1, limits_ref[1], LEVELS))
    path_key_ref[:, HEAD_DIM:] = jnp.where(level < limit, 0.0, MASKED).astype(jnp.bfloat16)
    path_keys, path_values = path_key_ref[...], path_value_ref[...]

    rows = lax.broadcasted_iota(jnp.int32, (2 * SEG_LEN, HEAD_DIM), 0)
    lanes = lax.broadcasted_iota(jnp.int32, (2 * SEG_LEN, HEAD_DIM), 1)
    marks = (lanes == rows // SEG_LEN).astype(jnp.float32).astype(jnp.bfloat16)
    causal = lax.broadcasted_iota(jnp.int32, (SEG_LEN, SEG_LEN), 1) <= lax.broadcasted_iota(
        jnp.int32, (SEG_LEN, SEG_LEN), 0
    )
    follows = jnp.where(limits_ref[2] > 0, 0.0, MASKED)
    halves = [slice(0, SEG_LEN), slice(SEG_LEN, 2 * SEG_LEN)]
    own_values = [with_ones(value_ref[half]) for half in halves]
    for head in range(heads):
        at = (first_head + head) * HEAD_DIM
        query = query_ref[:, at : at + HEAD_DIM]
        path_scores = scores_of(jnp.concatenate([query, marks], axis=1), path_keys)
        own = [
            [(jnp.where(causal, scores_of(query[half], key_ref[half]), MASKED), values)]
            for half, values in zip(halves, own_values)
        ]
        own[1].append((scores_of(query[halves[1]], key_ref[halves[0]]) + follows, own_values[0]))
        path_weights, own_parts = [], []
        for half, blocks in zip(halves, own):
            row_max = functools.reduce(
                jnp.maximum,
                [jnp.max(s, axis=1, keepdims=True) for s, _ in blocks]
                + [jnp.max(path_scores[half], axis=1, keepdims=True)],
            )
            weigh = lambda s: jnp.exp2((s - row_max) * EXP2_SCALE).astype(jnp.bfloat16)
            path_weights.append(weigh(path_scores[half]))
            own_parts.append(
                sum(
                    jnp.dot(weigh(s), values, preferred_element_type=jnp.float32)
                    for s, values in blocks
                )
            )
        total = jnp.dot(
            jnp.concatenate(path_weights, axis=0), path_values, preferred_element_type=jnp.float32
        ) + jnp.concatenate(own_parts, axis=0)
        mixture = total[:, :HEAD_DIM] / total[:, HEAD_DIM:]
        out_ref[:, head * HEAD_DIM : (head + 1) * HEAD_DIM] = mixture.astype(out_ref.dtype)


def attend(limits, queries, keys, values, deep, pieces, first_head, heads, after):
    rows = queries.shape[0]
    key_count = PATH + SEG_LEN + SEG_LEN // 2
    return pl.pallas_call(
        functools.partial(attend_kernel, first_head, heads),
        out_shape=jax.ShapeDtypeStruct((rows, heads * HEAD_DIM), jnp.bfloat16),
        in_specs=[SMEM] + [VMEM] * (4 + ROW) + [ANY] * len(after),
        out_specs=VMEM,
        scratch_shapes=[pltpu.VMEM((PATH, 2 * HEAD_DIM), jnp.bfloat16)] * 2,
        compiler_params=pltpu.CompilerParams(vmem_limit_bytes=ATTEND_VMEM),
        cost_estimate=pl.CostEstimate(
            flops=heads * rows * key_count * HEAD_DIM * 10,
            bytes_accessed=heads * rows * HEAD_DIM * 4 + 8 * PATH * HEAD_DIM,
            transcendentals=heads * rows * key_count,
        ),
        name="attend",
    )(limits, queries, keys, values, deep, *pieces, *after)


def project_kernel(groups, tile, has_base, starts_ref, weight_ref, *refs):
    count = sum(groups)
    parts, rest = refs[:count], refs[count:]
    out_ref, held_ref = rest[-2:]
    at = 0
    for part in parts:
        held_ref[:, at : at + part.shape[1]] = part[...]
        at += part.shape[1]

    for column in range(0, out_ref.shape[1], tile):
        columns = slice(column, column + tile)
        total = rest[0][:, columns] if has_base else None
        at, left = 0, parts
        for g, group in enumerate(groups):
            depth = sum(part.shape[1] for part in left[:group])
            left = left[group:]
            rows = pl.ds(pl.multiple_of(starts_ref[g], 2 * HEAD_DIM), depth)
            product = jnp.dot(
                held_ref[:, at : at + depth],
                weight_ref[rows, columns],
                preferred_element_type=jnp.float32,
            )
            total = product if total is None else total + product
            at += depth
        out_ref[:, columns] = total.astype(out_ref.dtype)


def project(groups, starts, weight, base, dtype):
    parts = [part for group in groups for part in group]
    rows = parts[0].shape[0]
    depth = sum(part.shape[1] for part in parts)
    width = weight.shape[1]
    bases = [] if base is None else [base]
    return pl.pallas_call(
        functools.partial(project_kernel, [len(g) for g in groups], 256, base is not None),
        out_shape=jax.ShapeDtypeStruct((rows, width), dtype),
        in_specs=[SMEM] + [VMEM] * (1 + len(parts) + len(bases)),
        out_specs=VMEM,
        scratch_shapes=[pltpu.VMEM((rows, depth), parts[0].dtype)],
        compiler_params=pltpu.CompilerParams(vmem_limit_bytes=PROJECT_VMEM),
        cost_estimate=pl.CostEstimate(
            flops=2 * rows * depth * width,
            bytes_accessed=2 * depth * (rows + width) + 4 * rows * width,
            transcendentals=0,
        ),
        name="project",
    )(starts, weight, *parts, *bases)


def swap(part, bit):
    size = lax.axis_size("tensor")
    return lax.ppermute(part, "tensor", [(i, i ^ bit) for i in range(size)])


def around(pieces):
    devices = lax.axis_size("dp")
    moved = [
        lax.ppermute(
            piece, "dp", [(i, i - i % ROW + (i + shift) % ROW) for i in range(devices)]
        )
        for shift, piece in enumerate(pieces)
        if shift
    ]
    return [pieces[0]] + moved


def onward(piece, step):
    devices = lax.axis_size("dp")
    return lax.ppermute(piece, "dp", [(i, i + step) for i in range(devices - step)])


def per_device(queries, key_proj, value_proj, out_weight, parents):
    me = lax.axis_index("tensor")
    first = (lax.axis_index("dp") * 2).astype(jnp.int32).reshape(1)
    deep, *pieces = pack(first, parents, key_proj, value_proj)
    pieces = around(pieces)
    deep = onward(deep, 1)
    table, carry, limits = ancestry(first, parents)
    held, to_next, to_second = carry_out(carry, pieces)
    picked = pick(table, held, onward(to_next, ROW), onward(to_second, 2 * ROW))
    picked = around(picked)

    width = queries.shape[1]
    chunk = 2
    chunks = width // HEAD_DIM // chunk
    own, across = [], []
    for c in range(chunks):
        after = across[c - 2 : c - 1] if c >= 2 else []
        own.append(
            attend(
                limits, queries, key_proj, value_proj, deep, picked, c * chunk, chunk, after
            )
        )
        across.append(swap(own[c], 2))
    beside = [swap(part, 1) for part in own]
    split = chunks - 1
    corner = [swap(part, 1) for part in across[:split]]
    starts = jnp.stack([me, me ^ 1, me ^ 2, me ^ 3]) * width
    near = project(
        [own, beside, across[:split], corner], starts, out_weight, None, jnp.float32
    )
    last, near = lax.optimization_barrier((across[split], near))
    return project(
        [[last], [swap(last, 1)]],
        starts[2:] + split * chunk * HEAD_DIM,
        out_weight,
        near,
        jnp.bfloat16,
    )


def solution(mesh):
    placed = (P("dp", "tensor"), P("dp", "tensor"), P("dp", "tensor"), P(None, "tensor"), P())
    return jax.shard_map(
        per_device, mesh=mesh, in_specs=placed, out_specs=P("dp", "tensor"), check_vma=False
    )
```

time: 117 us -> 104 us (0.89)
  the two profiles are of different devices: /device:TPU:1 before, /device:TPU:7 now
where the time goes in v2:
time: 104 us; the launch traced here: 103 us
  starting transfers between devices  53.3 us (51%)
  Pallas kernels  28.1 us (27%)
  waiting for transfers between devices  11.9 us (11%)
  local copies, waits for them, and re-layouts  9.7 us (9%)
    ppermute x14, starting transfers between devices, around(): lax.ppermute(piece, 'dp', [(i, i - i % ROW + (i + shift) % ROW) for i in...  28.4 us
    ppermute x12, starting transfers between devices, swap(): return lax.ppermute(part, 'tensor', [(i, i ^ bit) for i in range(size)])  14.6 us
    pallas_call x4, Pallas kernels, attend(): pl.pallas_call(functools.partial(attend_kernel, first_head, heads), out_s...  12.9 us
    ppermute x3, starting transfers between devices, onward(): lax.ppermute(piece, 'dp', [(i, i + step) for i in range(devices - step)])  10.3 us
    unnamed x32, local copies, waits for them, and re-layouts  9.7 us
    pallas_call x2, Pallas kernels, project(): pl.pallas_call(functools.partial(project_kernel, [len(g) for g in groups]...  8.48 us
    ppermute x14, waiting for transfers between devices, around(): lax.ppermute(piece, 'dp', [(i, i - i % ROW + (i + shift) % ROW) for i in...  4.86 us
    ppermute x3, waiting for transfers between devices, onward(): lax.ppermute(piece, 'dp', [(i, i + step) for i in range(devices - step)])  4.33 us
  transfers between devices with their start and end apart: 29, of which 10 were waited for; matrix products, arithmetic and copies ran while one was open for 0% of the time, Pallas kernels for 18%

profile of v2, /device:TPU:7, one launch (start us, length us, event | category | flops | bytes accessed | tf_op | source)
XLA Modules:
  0.0 103.4 jit_solution(10695014871711795425)
XLA Ops:
  0.0 1.8 %pack.1 = (bf16[512,128]{1,0:T(8,128)(2,1)}, bf16[2,64,128]{2,1,0:T(8,128)(2,1)}, bf16[2,64,128]{2,1,0:T(8,128)(2,1)}, bf16[2,64,128]{2,1,0:T(8,128)(2,1)}, bf16...) custom-call(s32[1]{0:T(128)} %bitcast.4.first_ref, ...), custom_call_target="tpu_custom_call" | custom-call | bytes 524288 | tf_op jit(solution)/shard_map/pack/pallas_call | solution.py:103
  1.8 1.7 %collective-permute-start.1 = (bf16[2,64,128]{2,1,0:T(8,128)(2,1)}, bf16[2,64,128]{2,1,0:T(8,128)(2,1)S(1)}, u32[]{:S(2)}, u32[]{:S(2)}) collective-permute-start(bf16[2,64,128]{2,1,0:T(8,128)(2,1)} %get-tuple-element.35), channel_id=1, source_target_pairs={{0,4},{4,8},{8,12},{12,16},{16,20},{20,24},{24,28},{28,0},{32,36},... | collective-permute-start | bytes 98312 | tf_op jit(solution)/shard_map/ppermute | solution.py:302
  3.5 3.0 %collective-permute-start.2 = (bf16[2,64,128]{2,1,0:T(8,128)(2,1)}, bf16[2,64,128]{2,1,0:T(8,128)(2,1)S(1)}, u32[]{:S(2)}, u32[]{:S(2)}) collective-permute-start(bf16[2,64,128]{2,1,0:T(8,128)(2,1)} %get-tuple-element.36), channel_id=1, source_target_pairs={{0,8},{4,12},{8,16},{12,20},{16,24},{20,28},{24,0},{28,4},{32,40},... | collective-permute-start | bytes 98312 | tf_op jit(solution)/shard_map/ppermute | solution.py:302
  6.5 3.8 %collective-permute-start.3 = (bf16[2,64,128]{2,1,0:T(8,128)(2,1)}, bf16[2,64,128]{2,1,0:T(8,128)(2,1)S(1)}, u32[]{:S(2)}, u32[]{:S(2)}) collective-permute-start(bf16[2,64,128]{2,1,0:T(8,128)(2,1)} %get-tuple-element.37), channel_id=1, source_target_pairs={{0,12},{4,16},{8,20},{12,24},{16,28},{20,0},{24,4},{28,8},{32,44},... | collective-permute-start | bytes 98312 | tf_op jit(solution)/shard_map/ppermute | solution.py:302
  10.7 4.5 %collective-permute-start.5 = (bf16[2,64,128]{2,1,0:T(8,128)(2,1)}, bf16[2,64,128]{2,1,0:T(8,128)(2,1)S(1)}, u32[]{:S(2)}, u32[]{:S(2)}) collective-permute-start(bf16[2,64,128]{2,1,0:T(8,128)(2,1)} %get-tuple-element.39), channel_id=1, source_target_pairs={{0,20},{4,24},{8,28},{12,0},{16,4},{20,8},{24,12},{28,16},{32,52},... | collective-permute-start | bytes 98312 | tf_op jit(solution)/shard_map/ppermute | solution.py:302
  15.2 2.4 %collective-permute-start.6 = (bf16[2,64,128]{2,1,0:T(8,128)(2,1)}, bf16[2,64,128]{2,1,0:T(8,128)(2,1)S(1)}, u32[]{:S(2)}, u32[]{:S(2)}) collective-permute-start(bf16[2,64,128]{2,1,0:T(8,128)(2,1)} %get-tuple-element.40), channel_id=1, source_target_pairs={{0,24},{4,28},{8,0},{12,4},{16,8},{20,12},{24,16},{28,20},{32,56},... | collective-permute-start | bytes 98312 | tf_op jit(solution)/shard_map/ppermute | solution.py:302
  18.3 1.5 %ancestry.1 = (s32[24]{0:T(128)}, s32[5]{0:T(128)}, s32[3]{0:T(128)}) custom-call(s32[1]{0:T(128)} %bitcast.4.first_ref, s32[128]{0:T(128)} %parents_ref.3), custom_call_target="tpu_custom_call" | custom-call | flops 8000 | bytes 2000 | tf_op jit(solution)/shard_map/ancestry/pallas_call | solution.py:76
  21.7 1.6 %carry_out.1 = (bf16[16,64,128]{2,1,0:T(8,128)(2,1)}, bf16[3,64,128]{2,1,0:T(8,128)(2,1)}, bf16[1,64,128]{2,1,0:T(8,128)(2,1)}) custom-call(s32[5]{0:T(128)} %get-tuple-element.33.carry_ref, bf16[2,64,128]{2,1,0:T(8,128)(2,1)} %get-tuple-element.34.refs_0_, bf16[2,64,128]{2,1,0:T(8,128)(2,1)} %copy-done.8, bf16[2,64,128]{2,1,0:T(8,128)(2,1)} %copy-done.9, ...), custom_call_target="tpu_custom_call" | custom-call | bytes 262144 | tf_op jit(solution)/shard_map/carry_out/pallas_call | solution.py:126
  23.3 3.2 %collective-permute-start.8 = (bf16[3,64,128]{2,1,0:T(8,128)(2,1)}, bf16[3,64,128]{2,1,0:T(8,128)(2,1)S(1)}, u32[]{:S(2)}, u32[]{:S(2)}) collective-permute-start(bf16[3,64,128]{2,1,0:T(8,128)(2,1)} %get-tuple-element.43), channel_id=1, source_target_pairs={{0,32},{4,36},{8,40},{12,44},{16,48},{20,52},{24,56},{28,60},{32,6... | collective-permute-start | bytes 147464 | tf_op jit(solution)/shard_map/ppermute | solution.py:313
  26.5 2.6 %collective-permute-start = (bf16[512,128]{1,0:T(8,128)(2,1)}, bf16[512,128]{1,0:T(8,128)(2,1)S(1)}, u32[]{:S(2)}, u32[]{:S(2)}) collective-permute-start(bf16[512,128]{1,0:T(8,128)(2,1)} %get-tuple-element.31), channel_id=1, source_target_pairs={{0,4},{4,8},{8,12},{12,16},{16,20},{20,24},{24,28},{28,32},{32,36}... | collective-permute-start | bytes 393224 | tf_op jit(solution)/shard_map/ppermute | solution.py:313
  29.1 4.5 %collective-permute-start.9 = (bf16[1,64,128]{2,1,0:T(8,128)(2,1)}, bf16[1,64,128]{2,1,0:T(8,128)(2,1)S(1)}, u32[]{:S(2)}, u32[]{:S(2)}) collective-permute-start(bf16[1,64,128]{2,1,0:T(8,128)(2,1)} %get-tuple-element.44), channel_id=1, source_target_pairs={{0,64},{4,68},{8,72},{12,76},{16,80},{20,84},{24,88},{28,92},{32,9... | collective-permute-start | bytes 49160 | tf_op jit(solution)/shard_map/ppermute | solution.py:313
  33.7 4.3 %collective-permute-done.9.second_ref = bf16[1,64,128]{2,1,0:T(8,128)(2,1)S(1)} collective-permute-done((bf16[1,64,128]{2,1,0:T(8,128)(2,1)}, bf16[1,64,128]{2,1,0:T(8,128)(2,1)S(1)}, u32[]{:S(2)}, u32[]{:S(2)}) %collective-permute-start.9) | collective-permute-done | bytes 16416 | tf_op jit(solution)/shard_map/ppermute | solution.py:313
  38.6 1.8 %pick.1 = (bf16[3,64,128]{2,1,0:T(8,128)(2,1)}, bf16[3,64,128]{2,1,0:T(8,128)(2,1)}, bf16[3,64,128]{2,1,0:T(8,128)(2,1)}, bf16[3,64,128]{2,1,0:T(8,128)(2,1)}, b...) custom-call(s32[24]{0:T(128)} %get-tuple-element.32.table_ref, ...), custom_call_target="tpu_custom_call" | custom-call | bytes 1048576 | tf_op jit(solution)/shard_map/pick/pallas_call | solution.py:148
  41.1 4.1 %collective-permute-start.12 = (bf16[3,64,128]{2,1,0:T(8,128)(2,1)}, bf16[3,64,128]{2,1,0:T(8,128)(2,1)S(1)}, u32[]{:S(2)}, u32[]{:S(2)}) collective-permute-start(bf16[3,64,128]{2,1,0:T(8,128)(2,1)} %get-tuple-element.48), channel_id=1, source_target_pairs={{0,12},{4,16},{8,20},{12,24},{16,28},{20,0},{24,4},{28,8},{32,44},... | collective-permute-start | bytes 147464 | tf_op jit(solution)/shard_map/ppermute | solution.py:302
  45.2 1.2 %collective-permute-start.13 = (bf16[3,64,128]{2,1,0:T(8,128)(2,1)}, bf16[3,64,128]{2,1,0:T(8,128)(2,1)S(1)}, u32[]{:S(2)}, u32[]{:S(2)}) collective-permute-start(bf16[3,64,128]{2,1,0:T(8,128)(2,1)} %get-tuple-element.49), channel_id=1, source_target_pairs={{0,16},{4,20},{8,24},{12,28},{16,0},{20,4},{24,8},{28,12},{32,48},... | collective-permute-start | bytes 147464 | tf_op jit(solution)/shard_map/ppermute | solution.py:302
  46.4 4.5 %collective-permute-start.14 = (bf16[3,64,128]{2,1,0:T(8,128)(2,1)}, bf16[3,64,128]{2,1,0:T(8,128)(2,1)S(1)}, u32[]{:S(2)}, u32[]{:S(2)}) collective-permute-start(bf16[3,64,128]{2,1,0:T(8,128)(2,1)} %get-tuple-element.50), channel_id=1, source_target_pairs={{0,20},{4,24},{8,28},{12,0},{16,4},{20,8},{24,12},{28,16},{32,52},... | collective-permute-start | bytes 147464 | tf_op jit(solution)/shard_map/ppermute | solution.py:302
  50.9 1.5 %collective-permute-start.15 = (bf16[3,64,128]{2,1,0:T(8,128)(2,1)}, bf16[3,64,128]{2,1,0:T(8,128)(2,1)S(1)}, u32[]{:S(2)}, u32[]{:S(2)}) collective-permute-start(bf16[3,64,128]{2,1,0:T(8,128)(2,1)} %get-tuple-element.51), channel_id=1, source_target_pairs={{0,24},{4,28},{8,0},{12,4},{16,8},{20,12},{24,16},{28,20},{32,56},... | collective-permute-start | bytes 147464 | tf_op jit(solution)/shard_map/ppermute | solution.py:302
  52.4 1.8 %collective-permute-done.14.refs_5_ = bf16[3,64,128]{2,1,0:T(8,128)(2,1)S(1)} collective-permute-done((bf16[3,64,128]{2,1,0:T(8,128)(2,1)}, bf16[3,64,128]{2,1,0:T(8,128)(2,1)S(1)}, u32[]{:S(2)}, u32[]{:S(2)}) %collective-permute-start.14) | collective-permute-done | bytes 49184 | tf_op jit(solution)/shard_map/ppermute | solution.py:302
  54.2 1.2 %collective-permute-done.15.refs_6_ = bf16[3,64,128]{2,1,0:T(8,128)(2,1)S(1)} collective-permute-done((bf16[3,64,128]{2,1,0:T(8,128)(2,1)}, bf16[3,64,128]{2,1,0:T(8,128)(2,1)S(1)}, u32[]{:S(2)}, u32[]{:S(2)}) %collective-permute-start.15) | collective-permute-done | bytes 49184 | tf_op jit(solution)/shard_map/ppermute | solution.py:302
  57.7 1.2 %copy-done.4 = bf16[512,1024]{1,0:T(8,128)(2,1)S(1)} copy-done((bf16[512,1024]{1,0:T(8,128)(2,1)S(1)}, bf16[512,1024]{1,0:T(8,128)(2,1)}, u32[]{:S(2)}) %copy-start.4) | copy-done | bytes 1048600
  60.4 3.2 %attend.6.refs_0_ = bf16[512,256]{1,0:T(8,128)(2,1)S(1)} custom-call(s32[3]{0:T(128)S(1)} %copy-done.6, bf16[512,1024]{1,0:T(8,128)(2,1)S(1)} %copy-done.4, bf16[512,128]{1,0:T(8,128)(2,1)S(1)} %copy-done.2, bf16[512,128]{1,0:T(8,128)(2,1)S(1)} %copy-done.3, bf16[512,128]{1,0:T(8,128)(2,1)S(1)} %collective-permute-done.deep_ref, ...), custom_call_target="tpu_custom_call" | custom-call | flops 1845493760 | bytes 1572864 | tf_op jit(solution)/shard_map/attend/pallas_call | solution.py:229
  64.3 3.2 %attend.4.refs_1_ = bf16[512,256]{1,0:T(8,128)(2,1)S(1)} custom-call(s32[3]{0:T(128)S(1)} %copy-done.6, bf16[512,1024]{1,0:T(8,128)(2,1)S(1)} %copy-done.4, bf16[512,128]{1,0:T(8,128)(2,1)S(1)} %copy-done.2, bf16[512,128]{1,0:T(8,128)(2,1)S(1)} %copy-done.3, bf16[512,128]{1,0:T(8,128)(2,1)S(1)} %collective-permute-done.deep_ref, ...), custom_call_target="tpu_custom_call" | custom-call | flops 1845493760 | bytes 1572864 | tf_op jit(solution)/shard_map/attend/pallas_call | solution.py:229
  68.6 7.4 %collective-permute-start.20 = (bf16[512,256]{1,0:T(8,128)(2,1)S(1)}, bf16[512,256]{1,0:T(8,128)(2,1)S(1)}, u32[]{:S(2)}, u32[]{:S(2)}) collective-permute-start(bf16[512,256]{1,0:T(8,128)(2,1)S(1)} %attend.6.refs_0_), channel_id=1, source_target_pairs={{0,1},{1,0},{2,3},{3,2},{4,5},{5,4},{6,7},{7,6},{8,9},{9,8},{10,11... | collective-permute-start | bytes 786440 | tf_op jit(solution)/shard_map/ppermute | solution.py:296
  75.9 3.2 %attend.7.refs_2_ = bf16[512,256]{1,0:T(8,128)(2,1)S(1)} custom-call(s32[3]{0:T(128)S(1)} %copy-done.6, bf16[512,1024]{1,0:T(8,128)(2,1)S(1)} %copy-done.4, bf16[512,128]{1,0:T(8,128)(2,1)S(1)} %copy-done.2, bf16[512,128]{1,0:T(8,128)(2,1)S(1)} %copy-done.3, bf16[512,128]{1,0:T(8,128)(2,1)S(1)} %collective-permute-done.deep_ref, ...), custom_call_target="tpu_custom_call" | custom-call | flops 1845493760 | bytes 1572864 | tf_op jit(solution)/shard_map/attend/pallas_call | solution.py:229
  79.8 1.3 %collective-permute-start.22 = (bf16[512,256]{1,0:T(8,128)(2,1)S(1)}, bf16[512,256]{1,0:T(8,128)(2,1)S(1)}, u32[]{:S(2)}, u32[]{:S(2)}) collective-permute-start(bf16[512,256]{1,0:T(8,128)(2,1)S(1)} %attend.7.refs_2_), channel_id=1, source_target_pairs={{0,1},{1,0},{2,3},{3,2},{4,5},{5,4},{6,7},{7,6},{8,9},{9,8},{10,11... | collective-permute-start | bytes 786440 | tf_op jit(solution)/shard_map/ppermute | solution.py:296
  81.1 3.2 %attend.5.refs_3_ = bf16[512,256]{1,0:T(8,128)(2,1)S(1)} custom-call(s32[3]{0:T(128)S(1)} %copy-done.6, bf16[512,1024]{1,0:T(8,128)(2,1)S(1)} %copy-done.4, bf16[512,128]{1,0:T(8,128)(2,1)S(1)} %copy-done.2, bf16[512,128]{1,0:T(8,128)(2,1)S(1)} %copy-done.3, bf16[512,128]{1,0:T(8,128)(2,1)S(1)} %collective-permute-done.deep_ref, ...), custom_call_target="tpu_custom_call" | custom-call | flops 1845493760 | bytes 1572864 | tf_op jit(solution)/shard_map/attend/pallas_call | solution.py:229
  85.0 1.0 collective-permute-done.24.refs_10_
  86.0 1.9 %collective-permute-start.27 = (bf16[512,256]{1,0:T(8,128)(2,1)S(1)}, bf16[512,256]{1,0:T(8,128)(2,1)}, u32[]{:S(2)}, u32[]{:S(2)}) collective-permute-start(bf16[512,256]{1,0:T(8,128)(2,1)S(1)} %collective-permute-done.24.refs_10_), channel_id=1, source_target_pairs={{0,1},{1,0},{2,3},{3,2},{4,5},{5,4},{6,7},{7,6},{8,9},{9,8},{10,11... | collective-permute-start | bytes 786440 | tf_op jit(solution)/shard_map/ppermute | solution.py:296
  89.3 4.0 %copy-done = bf16[4096,1280]{1,0:T(8,128)(2,1)S(1)} copy-done((bf16[4096,1280]{1,0:T(8,128)(2,1)S(1)}, bf16[4096,1280]{1,0:T(8,128)(2,1)}, u32[]{:S(2)}) %copy-start) | copy-done | bytes 10485784
  93.2 6.0 %project.2.refs_2_ = f32[512,1280]{1,0:T(8,128)S(1)} custom-call(s32[4]{0:T(128)S(1)} %add_multiply_fusion.starts_ref, bf16[4096,1280]{1,0:T(8,128)(2,1)S(1)} %copy-done, bf16[512,256]{1,0:T(8,128)(2,1)S(1)} %attend.6.refs_0_, bf16[512,256]{1,0:T(8,128)(2,1)S(1)} %attend.4.refs_1_, bf16[512,256]{1,0:T(8,128)(2,1)S(1)} %attend.7.refs_2_, ...), custom_call_target="tpu_custom_call" | custom-call | flops 4697620480 | bytes 15466496 | tf_op jit(solution)/shard_map/project/pallas_call | solution.py:278
  99.8 1.1 %collective-permute-done.28.refs_1_ = bf16[512,256]{1,0:T(8,128)(2,1)S(1)} collective-permute-done((bf16[512,256]{1,0:T(8,128)(2,1)S(1)}, bf16[512,256]{1,0:T(8,128)(2,1)S(1)}, u32[]{:S(2)}, u32[]{:S(2)}) %collective-permute-start.28) | collective-permute-done | bytes 262176 | tf_op jit(solution)/shard_map/ppermute | solution.py:296
  100.9 2.5 %project.3 = bf16[512,1280]{1,0:T(8,128)(2,1)} custom-call(s32[2]{0:T(128)S(1)} %slice_add_fusion.starts_ref, bf16[4096,1280]{1,0:T(8,128)(2,1)S(1)} %copy-done.1, bf16[512,256]{1,0:T(8,128)(2,1)S(1)} %collective-permute-done.18.refs_0_, bf16[512,256]{1,0:T(8,128)(2,1)S(1)} %collective-permute-done.28.refs_1_, f32[512,1280]{1,0:T(8,128)S(1)} %project.2.refs_2_), custom_call_target="tpu_custom_call" | custom-call | flops 671088640 | bytes 4456448 | tf_op jit(solution)/shard_map/project/pallas_call | solution.py:278
  (70 shorter events, 13.0 us)
Async XLA Ops:
  1.8 13.4 %collective-permute-start.1 = (bf16[2,64,128]{2,1,0:T(8,128)(2,1)}, bf16[2,64,128]{2,1,0:T(8,128)(2,1)S(1)}, u32[]{:S(2)}, u32[]{:S(2)}) collective-permute-start(bf16[2,64,128]{2,1,0:T(8,128)(2,1)} %get-tuple-element.35), channel_id=1, source_target_pairs={{0,4},{4,8},{8,12},{12,16},{16,20},{20,24},{24,28},{28,0},{32,36},... | collective-permute-start | bytes 98312 | tf_op jit(solution)/shard_map/ppermute | solution.py:302
  3.5 14.1 %collective-permute-start.2 = (bf16[2,64,128]{2,1,0:T(8,128)(2,1)}, bf16[2,64,128]{2,1,0:T(8,128)(2,1)S(1)}, u32[]{:S(2)}, u32[]{:S(2)}) collective-permute-start(bf16[2,64,128]{2,1,0:T(8,128)(2,1)} %get-tuple-element.36), channel_id=1, source_target_pairs={{0,8},{4,12},{8,16},{12,20},{16,24},{20,28},{24,0},{28,4},{32,40},... | collective-permute-start | bytes 98312 | tf_op jit(solution)/shard_map/ppermute | solution.py:302
  6.5 13.3 %collective-permute-start.3 = (bf16[2,64,128]{2,1,0:T(8,128)(2,1)}, bf16[2,64,128]{2,1,0:T(8,128)(2,1)S(1)}, u32[]{:S(2)}, u32[]{:S(2)}) collective-permute-start(bf16[2,64,128]{2,1,0:T(8,128)(2,1)} %get-tuple-element.37), channel_id=1, source_target_pairs={{0,12},{4,16},{8,20},{12,24},{16,28},{20,0},{24,4},{28,8},{32,44},... | collective-permute-start | bytes 98312 | tf_op jit(solution)/shard_map/ppermute | solution.py:302
  10.2 9.5 %collective-permute-start.4 = (bf16[2,64,128]{2,1,0:T(8,128)(2,1)}, bf16[2,64,128]{2,1,0:T(8,128)(2,1)S(1)}, u32[]{:S(2)}, u32[]{:S(2)}) collective-permute-start(bf16[2,64,128]{2,1,0:T(8,128)(2,1)} %get-tuple-element.38), channel_id=1, source_target_pairs={{0,16},{4,20},{8,24},{12,28},{16,0},{20,4},{24,8},{28,12},{32,48},... | collective-permute-start | bytes 98312 | tf_op jit(solution)/shard_map/ppermute | solution.py:302
  10.7 9.1 %collective-permute-start.5 = (bf16[2,64,128]{2,1,0:T(8,128)(2,1)}, bf16[2,64,128]{2,1,0:T(8,128)(2,1)S(1)}, u32[]{:S(2)}, u32[]{:S(2)}) collective-permute-start(bf16[2,64,128]{2,1,0:T(8,128)(2,1)} %get-tuple-element.39), channel_id=1, source_target_pairs={{0,20},{4,24},{8,28},{12,0},{16,4},{20,8},{24,12},{28,16},{32,52},... | collective-permute-start | bytes 98312 | tf_op jit(solution)/shard_map/ppermute | solution.py:302
  15.2 5.9 %copy-start.8 = (bf16[2,64,128]{2,1,0:T(8,128)(2,1)}, bf16[2,64,128]{2,1,0:T(8,128)(2,1)S(1)}, u32[]{:S(2)}) copy-start(bf16[2,64,128]{2,1,0:T(8,128)(2,1)S(1)} %collective-permute-done.1.refs_1_) | copy-start | bytes 98308
  15.2 5.6 %collective-permute-start.6 = (bf16[2,64,128]{2,1,0:T(8,128)(2,1)}, bf16[2,64,128]{2,1,0:T(8,128)(2,1)S(1)}, u32[]{:S(2)}, u32[]{:S(2)}) collective-permute-start(bf16[2,64,128]{2,1,0:T(8,128)(2,1)} %get-tuple-element.40), channel_id=1, source_target_pairs={{0,24},{4,28},{8,0},{12,4},{16,8},{20,12},{24,16},{28,20},{32,56},... | collective-permute-start | bytes 98312 | tf_op jit(solution)/shard_map/ppermute | solution.py:302
  17.6 3.5 %collective-permute-start.7 = (bf16[2,64,128]{2,1,0:T(8,128)(2,1)}, bf16[2,64,128]{2,1,0:T(8,128)(2,1)S(1)}, u32[]{:S(2)}, u32[]{:S(2)}) collective-permute-start(bf16[2,64,128]{2,1,0:T(8,128)(2,1)} %get-tuple-element.41), channel_id=1, source_target_pairs={{0,28},{4,0},{8,4},{12,8},{16,12},{20,16},{24,20},{28,24},{32,60},... | collective-permute-start | bytes 98312 | tf_op jit(solution)/shard_map/ppermute | solution.py:302
  23.3 14.7 %collective-permute-start.8 = (bf16[3,64,128]{2,1,0:T(8,128)(2,1)}, bf16[3,64,128]{2,1,0:T(8,128)(2,1)S(1)}, u32[]{:S(2)}, u32[]{:S(2)}) collective-permute-start(bf16[3,64,128]{2,1,0:T(8,128)(2,1)} %get-tuple-element.43), channel_id=1, source_target_pairs={{0,32},{4,36},{8,40},{12,44},{16,48},{20,52},{24,56},{28,60},{32,6... | collective-permute-start | bytes 147464 | tf_op jit(solution)/shard_map/ppermute | solution.py:313
  26.5 29.4 %collective-permute-start = (bf16[512,128]{1,0:T(8,128)(2,1)}, bf16[512,128]{1,0:T(8,128)(2,1)S(1)}, u32[]{:S(2)}, u32[]{:S(2)}) collective-permute-start(bf16[512,128]{1,0:T(8,128)(2,1)} %get-tuple-element.31), channel_id=1, source_target_pairs={{0,4},{4,8},{8,12},{12,16},{16,20},{20,24},{24,28},{28,32},{32,36}... | collective-permute-start | bytes 393224 | tf_op jit(solution)/shard_map/ppermute | solution.py:313
  29.1 8.9 %collective-permute-start.9 = (bf16[1,64,128]{2,1,0:T(8,128)(2,1)}, bf16[1,64,128]{2,1,0:T(8,128)(2,1)S(1)}, u32[]{:S(2)}, u32[]{:S(2)}) collective-permute-start(bf16[1,64,128]{2,1,0:T(8,128)(2,1)} %get-tuple-element.44), channel_id=1, source_target_pairs={{0,64},{4,68},{8,72},{12,76},{16,80},{20,84},{24,88},{28,92},{32,9... | collective-permute-start | bytes 49160 | tf_op jit(solution)/shard_map/ppermute | solution.py:313
  40.4 6.0 %collective-permute-start.10 = (bf16[3,64,128]{2,1,0:T(8,128)(2,1)}, bf16[3,64,128]{2,1,0:T(8,128)(2,1)S(1)}, u32[]{:S(2)}, u32[]{:S(2)}) collective-permute-start(bf16[3,64,128]{2,1,0:T(8,128)(2,1)} %get-tuple-element.46), channel_id=1, source_target_pairs={{0,4},{4,8},{8,12},{12,16},{16,20},{20,24},{24,28},{28,0},{32,36},... | collective-permute-start | bytes 147464 | tf_op jit(solution)/shard_map/ppermute | solution.py:302
  40.4 10.4 %collective-permute-start.11 = (bf16[3,64,128]{2,1,0:T(8,128)(2,1)}, bf16[3,64,128]{2,1,0:T(8,128)(2,1)S(1)}, u32[]{:S(2)}, u32[]{:S(2)}) collective-permute-start(bf16[3,64,128]{2,1,0:T(8,128)(2,1)} %get-tuple-element.47), channel_id=1, source_target_pairs={{0,8},{4,12},{8,16},{12,20},{16,24},{20,28},{24,0},{28,4},{32,40},... | collective-permute-start | bytes 147464 | tf_op jit(solution)/shard_map/ppermute | solution.py:302
  41.1 11.3 %collective-permute-start.12 = (bf16[3,64,128]{2,1,0:T(8,128)(2,1)}, bf16[3,64,128]{2,1,0:T(8,128)(2,1)S(1)}, u32[]{:S(2)}, u32[]{:S(2)}) collective-permute-start(bf16[3,64,128]{2,1,0:T(8,128)(2,1)} %get-tuple-element.48), channel_id=1, source_target_pairs={{0,12},{4,16},{8,20},{12,24},{16,28},{20,0},{24,4},{28,8},{32,44},... | collective-permute-start | bytes 147464 | tf_op jit(solution)/shard_map/ppermute | solution.py:302
  45.2 7.3 %collective-permute-start.13 = (bf16[3,64,128]{2,1,0:T(8,128)(2,1)}, bf16[3,64,128]{2,1,0:T(8,128)(2,1)S(1)}, u32[]{:S(2)}, u32[]{:S(2)}) collective-permute-start(bf16[3,64,128]{2,1,0:T(8,128)(2,1)} %get-tuple-element.49), channel_id=1, source_target_pairs={{0,16},{4,20},{8,24},{12,28},{16,0},{20,4},{24,8},{28,12},{32,48},... | collective-permute-start | bytes 147464 | tf_op jit(solution)/shard_map/ppermute | solution.py:302
  46.4 7.8 %collective-permute-start.14 = (bf16[3,64,128]{2,1,0:T(8,128)(2,1)}, bf16[3,64,128]{2,1,0:T(8,128)(2,1)S(1)}, u32[]{:S(2)}, u32[]{:S(2)}) collective-permute-start(bf16[3,64,128]{2,1,0:T(8,128)(2,1)} %get-tuple-element.50), channel_id=1, source_target_pairs={{0,20},{4,24},{8,28},{12,0},{16,4},{20,8},{24,12},{28,16},{32,52},... | collective-permute-start | bytes 147464 | tf_op jit(solution)/shard_map/ppermute | solution.py:302
  50.9 4.6 %collective-permute-start.15 = (bf16[3,64,128]{2,1,0:T(8,128)(2,1)}, bf16[3,64,128]{2,1,0:T(8,128)(2,1)S(1)}, u32[]{:S(2)}, u32[]{:S(2)}) collective-permute-start(bf16[3,64,128]{2,1,0:T(8,128)(2,1)} %get-tuple-element.51), channel_id=1, source_target_pairs={{0,24},{4,28},{8,0},{12,4},{16,8},{20,12},{24,16},{28,20},{32,56},... | collective-permute-start | bytes 147464 | tf_op jit(solution)/shard_map/ppermute | solution.py:302
  52.3 3.6 %collective-permute-start.16 = (bf16[3,64,128]{2,1,0:T(8,128)(2,1)}, bf16[3,64,128]{2,1,0:T(8,128)(2,1)S(1)}, u32[]{:S(2)}, u32[]{:S(2)}) collective-permute-start(bf16[3,64,128]{2,1,0:T(8,128)(2,1)} %get-tuple-element.52), channel_id=1, source_target_pairs={{0,28},{4,0},{8,4},{12,8},{16,12},{20,16},{24,20},{28,24},{32,60},... | collective-permute-start | bytes 147464 | tf_op jit(solution)/shard_map/ppermute | solution.py:302
  63.7 12.2 %collective-permute-start.19 = (bf16[512,256]{1,0:T(8,128)(2,1)S(1)}, bf16[512,256]{1,0:T(8,128)(2,1)S(1)}, u32[]{:S(2)}, u32[]{:S(2)}) collective-permute-start(bf16[512,256]{1,0:T(8,128)(2,1)S(1)} %attend.6.refs_0_), channel_id=1, source_target_pairs={{0,2},{1,3},{2,0},{3,1},{4,6},{5,7},{6,4},{7,5},{8,10},{9,11},{10,... | collective-permute-start | bytes 786440 | tf_op jit(solution)/shard_map/ppermute | solution.py:296
  67.6 13.5 %collective-permute-start.17 = (bf16[512,256]{1,0:T(8,128)(2,1)S(1)}, bf16[512,256]{1,0:T(8,128)(2,1)S(1)}, u32[]{:S(2)}, u32[]{:S(2)}) collective-permute-start(bf16[512,256]{1,0:T(8,128)(2,1)S(1)} %attend.4.refs_1_), channel_id=1, source_target_pairs={{0,2},{1,3},{2,0},{3,1},{4,6},{5,7},{6,4},{7,5},{8,10},{9,11},{10,... | collective-permute-start | bytes 786440 | tf_op jit(solution)/shard_map/ppermute | solution.py:296
  68.6 15.9 %collective-permute-start.20 = (bf16[512,256]{1,0:T(8,128)(2,1)S(1)}, bf16[512,256]{1,0:T(8,128)(2,1)S(1)}, u32[]{:S(2)}, u32[]{:S(2)}) collective-permute-start(bf16[512,256]{1,0:T(8,128)(2,1)S(1)} %attend.6.refs_0_), channel_id=1, source_target_pairs={{0,1},{1,0},{2,3},{3,2},{4,5},{5,4},{6,7},{7,6},{8,9},{9,8},{10,11... | collective-permute-start | bytes 786440 | tf_op jit(solution)/shard_map/ppermute | solution.py:296
  75.9 9.0 %collective-permute-start.21 = (bf16[512,256]{1,0:T(8,128)(2,1)S(1)}, bf16[512,256]{1,0:T(8,128)(2,1)S(1)}, u32[]{:S(2)}, u32[]{:S(2)}) collective-permute-start(bf16[512,256]{1,0:T(8,128)(2,1)S(1)} %attend.4.refs_1_), channel_id=1, source_target_pairs={{0,1},{1,0},{2,3},{3,2},{4,5},{5,4},{6,7},{7,6},{8,9},{9,8},{10,11... | collective-permute-start | bytes 786440 | tf_op jit(solution)/shard_map/ppermute | solution.py:296
  79.2 6.9 %collective-permute-start.24 = (bf16[512,256]{1,0:T(8,128)(2,1)S(1)}, bf16[512,256]{1,0:T(8,128)(2,1)S(1)}, u32[]{:S(2)}, u32[]{:S(2)}) collective-permute-start(bf16[512,256]{1,0:T(8,128)(2,1)S(1)} %attend.7.refs_2_), channel_id=1, source_target_pairs={{0,2},{1,3},{2,0},{3,1},{4,6},{5,7},{6,4},{7,5},{8,10},{9,11},{10,... | collective-permute-start | bytes 786440 | tf_op jit(solution)/shard_map/ppermute | solution.py:296
  79.8 8.3 %collective-permute-start.22 = (bf16[512,256]{1,0:T(8,128)(2,1)S(1)}, bf16[512,256]{1,0:T(8,128)(2,1)S(1)}, u32[]{:S(2)}, u32[]{:S(2)}) collective-permute-start(bf16[512,256]{1,0:T(8,128)(2,1)S(1)} %attend.7.refs_2_), channel_id=1, source_target_pairs={{0,1},{1,0},{2,3},{3,2},{4,5},{5,4},{6,7},{7,6},{8,9},{9,8},{10,11... | collective-permute-start | bytes 786440 | tf_op jit(solution)/shard_map/ppermute | solution.py:296
  84.3 4.3 %collective-permute-start.23 = (bf16[512,256]{1,0:T(8,128)(2,1)S(1)}, bf16[512,256]{1,0:T(8,128)(2,1)S(1)}, u32[]{:S(2)}, u32[]{:S(2)}) collective-permute-start(bf16[512,256]{1,0:T(8,128)(2,1)S(1)} %attend.5.refs_3_), channel_id=1, source_target_pairs={{0,1},{1,0},{2,3},{3,2},{4,5},{5,4},{6,7},{7,6},{8,9},{9,8},{10,11... | collective-permute-start | bytes 786440 | tf_op jit(solution)/shard_map/ppermute | solution.py:296
  84.4 4.2 %collective-permute-start.25 = (bf16[512,256]{1,0:T(8,128)(2,1)S(1)}, bf16[512,256]{1,0:T(8,128)(2,1)S(1)}, u32[]{:S(2)}, u32[]{:S(2)}) collective-permute-start(bf16[512,256]{1,0:T(8,128)(2,1)S(1)} %collective-permute-done.19.refs_8_), channel_id=1, source_target_pairs={{0,1},{1,0},{2,3},{3,2},{4,5},{5,4},{6,7},{7,6},{8,9},{9,8},{10,11... | collective-permute-start | bytes 786440 | tf_op jit(solution)/shard_map/ppermute | solution.py:296
  84.9 3.7 %collective-permute-start.26 = (bf16[512,256]{1,0:T(8,128)(2,1)S(1)}, bf16[512,256]{1,0:T(8,128)(2,1)S(1)}, u32[]{:S(2)}, u32[]{:S(2)}) collective-permute-start(bf16[512,256]{1,0:T(8,128)(2,1)S(1)} %collective-permute-done.17.refs_8_.refs_9_), channel_id=1, source_target_pairs={{0,1},{1,0},{2,3},{3,2},{4,5},{5,4},{6,7},{7,6},{8,9},{9,8},{10,11... | collective-permute-start | bytes 786440 | tf_op jit(solution)/shard_map/ppermute | solution.py:296
  86.0 3.2 %collective-permute-start.27 = (bf16[512,256]{1,0:T(8,128)(2,1)S(1)}, bf16[512,256]{1,0:T(8,128)(2,1)}, u32[]{:S(2)}, u32[]{:S(2)}) collective-permute-start(bf16[512,256]{1,0:T(8,128)(2,1)S(1)} %collective-permute-done.24.refs_10_), channel_id=1, source_target_pairs={{0,1},{1,0},{2,3},{3,2},{4,5},{5,4},{6,7},{7,6},{8,9},{9,8},{10,11... | collective-permute-start | bytes 786440 | tf_op jit(solution)/shard_map/ppermute | solution.py:296
  88.1 11.2 %collective-permute-start.18 = (bf16[512,256]{1,0:T(8,128)(2,1)S(1)}, bf16[512,256]{1,0:T(8,128)(2,1)S(1)}, u32[]{:S(2)}, u32[]{:S(2)}) collective-permute-start(bf16[512,256]{1,0:T(8,128)(2,1)S(1)} %attend.5.refs_3_), channel_id=1, source_target_pairs={{0,2},{1,3},{2,0},{3,1},{4,6},{5,7},{6,4},{7,5},{8,10},{9,11},{10,... | collective-permute-start | bytes 786440 | tf_op jit(solution)/shard_map/ppermute | solution.py:296
  89.3 4.0 %copy-start = (bf16[4096,1280]{1,0:T(8,128)(2,1)S(1)}, bf16[4096,1280]{1,0:T(8,128)(2,1)}, u32[]{:S(2)}) copy-start(bf16[4096,1280]{1,0:T(8,128)(2,1)} %weight_ref.3) | copy-start | bytes 31457284
  93.2 7.7 %copy-start.1 = (bf16[4096,1280]{1,0:T(8,128)(2,1)S(1)}, bf16[4096,1280]{1,0:T(8,128)(2,1)}, u32[]{:S(2)}) copy-start(bf16[4096,1280]{1,0:T(8,128)(2,1)} %weight_ref.3) | copy-start | bytes 31457284
  99.3 1.6 %collective-permute-start.28 = (bf16[512,256]{1,0:T(8,128)(2,1)S(1)}, bf16[512,256]{1,0:T(8,128)(2,1)S(1)}, u32[]{:S(2)}, u32[]{:S(2)}) collective-permute-start(bf16[512,256]{1,0:T(8,128)(2,1)S(1)} %collective-permute-done.18.refs_0_), channel_id=1, source_target_pairs={{0,1},{1,0},{2,3},{3,2},{4,5},{5,4},{6,7},{7,6},{8,9},{9,8},{10,11... | collective-permute-start | bytes 786440 | tf_op jit(solution)/shard_map/ppermute | solution.py:296
  (13 other events, 14.4 us)

commit v3 on v2

v3 whole, which is shorter than its diff:
```python
import functools
import math

import jax
import jax.numpy as jnp
from jax import lax
from jax.experimental import pallas as pl
from jax.experimental.pallas import tpu as pltpu
from jax.sharding import PartitionSpec as P

HEAD_DIM = 128
SEG_LEN = 256
LEVELS = 4
ROW = 8
ROW_SEGS = 2 * ROW
PIECE = SEG_LEN // ROW
PATH = LEVELS * SEG_LEN
STACK = LEVELS * PIECE
MASKED = -1e30
EXP2_SCALE = math.log2(math.e) * HEAD_DIM ** (-0.5)
SMALL_VMEM = 6 * 1024 * 1024
ATTEND_VMEM = 20 * 1024 * 1024
PROJECT_VMEM = 28 * 1024 * 1024
LAST_VMEM = 16 * 1024 * 1024
TILE = 256

VMEM = pl.BlockSpec(memory_space=pltpu.VMEM)
SMEM = pl.BlockSpec(memory_space=pltpu.SMEM)
ANY = pl.BlockSpec(memory_space=pl.ANY)
HBM = pl.BlockSpec(memory_space=pltpu.HBM)
FLAG_ROWS = 16


def in_hbm(array):
    return pltpu.with_memory_space_constraint(array, pltpu.HBM)


def path_of(parents_ref, seg):
    path = [parents_ref[seg]]
    for _ in range(LEVELS - 1):
        up = parents_ref[jnp.maximum(path[-1], 0)]
        path.append(jnp.where(path[-1] >= 0, up, -1))
    depth = sum((p >= 0).astype(jnp.int32) for p in path)
    return path, depth


def level_of(path, depth, level):
    found = jnp.int32(0)
    for up in range(LEVELS):
        found = jnp.where(depth - 1 - up == level, path[up], found)
    return found


def pack_kernel(key_ref, value_ref, piece_ref, held_ref, sem):
    copies = [
        pltpu.make_async_copy(source, held_ref.at[i], sem.at[i])
        for i, source in enumerate([key_ref, value_ref])
    ]
    for copy in copies:
        copy.start()
    for i, copy in enumerate(copies):
        copy.wait()
        for piece in range(ROW):
            for seg in range(2):
                rows = pl.ds(seg * SEG_LEN + piece * PIECE, PIECE)
                piece_ref[piece, seg, i * PIECE : (i + 1) * PIECE] = held_ref[i, rows]


def pack(keys, values):
    return pl.pallas_call(
        pack_kernel,
        out_shape=jax.ShapeDtypeStruct((ROW, 2, 2 * PIECE, HEAD_DIM), keys.dtype),
        in_specs=[HBM, HBM],
        out_specs=VMEM,
        scratch_shapes=[pltpu.VMEM((2,) + keys.shape, keys.dtype), pltpu.SemaphoreType.DMA((2,))],
        compiler_params=pltpu.CompilerParams(vmem_limit_bytes=SMALL_VMEM),
        cost_estimate=pl.CostEstimate(flops=0, bytes_accessed=1 << 19, transcendentals=0),
        name="pack",
    )(in_hbm(keys), in_hbm(values))


def row_start(first_ref):
    return (first_ref[0] // ROW_SEGS) * ROW_SEGS


def carry_kernel(first_ref, parents_ref, pieces_ref, next_ref, second_ref):
    base = row_start(first_ref)
    last = parents_ref.shape[0] - 1

    def held(path, depth, level):
        return pieces_ref[jnp.clip(level_of(path, depth, level) - base, 0, ROW_SEGS - 1)]

    path, depth = path_of(parents_ref, jnp.minimum(base + ROW_SEGS, last))
    for level in range(LEVELS):
        next_ref[level] = held(path, depth, level)
    path, depth = path_of(parents_ref, jnp.minimum(base + 2 * ROW_SEGS, last))
    second_ref[0] = held(path, depth, 0)


def carry_out(first, parents, pieces):
    shape = lambda n: jax.ShapeDtypeStruct((n,) + pieces.shape[1:], pieces.dtype)
    return pl.pallas_call(
        carry_kernel,
        out_shape=(shape(LEVELS), shape(1)),
        in_specs=[SMEM, SMEM, VMEM],
        out_specs=(VMEM, VMEM),
        compiler_params=pltpu.CompilerParams(vmem_limit_bytes=SMALL_VMEM),
        cost_estimate=pl.CostEstimate(flops=0, bytes_accessed=1 << 18, transcendentals=0),
        name="carry_out",
    )(first, parents, pieces)


def pick_kernel(first_ref, parents_ref, pieces_ref, inside_ref, next_ref, second_ref):
    base = row_start(first_ref)
    ones = lambda on: jnp.full((FLAG_ROWS, HEAD_DIM), on, jnp.float32).astype(jnp.bfloat16)
    for target in range(ROW):
        path, depth = path_of(parents_ref, base + 2 * target)
        for level in range(LEVELS):
            seg = level_of(path, depth, level)
            within = seg >= base
            piece = pieces_ref[jnp.maximum(seg - base, 0)]
            inside_ref[target, level] = jnp.where(within, piece, jnp.zeros_like(piece))
            before = jnp.logical_and(seg < base, seg >= base - ROW_SEGS)
            next_ref[target, level] = ones(jnp.where(before, 1.0, 0.0))
            if level == 0:
                second_ref[target] = ones(jnp.where(seg < base - ROW_SEGS, 1.0, 0.0))


def pick(first, parents, pieces):
    shape = lambda *dims: jax.ShapeDtypeStruct(dims, pieces.dtype)
    return pl.pallas_call(
        pick_kernel,
        out_shape=(
            shape(ROW, LEVELS, *pieces.shape[1:]),
            shape(ROW, LEVELS, FLAG_ROWS, HEAD_DIM),
            shape(ROW, FLAG_ROWS, HEAD_DIM),
        ),
        in_specs=[SMEM, SMEM, VMEM],
        out_specs=(VMEM, VMEM, VMEM),
        compiler_params=pltpu.CompilerParams(vmem_limit_bytes=SMALL_VMEM),
        cost_estimate=pl.CostEstimate(flops=0, bytes_accessed=1 << 20, transcendentals=0),
        name="pick",
    )(first, parents, pieces)


def merge_kernel(inside_ref, on_next_ref, on_second_ref, next_ref, second_ref, picked_ref):
    for level in range(LEVELS):
        for at in range(0, 2 * PIECE, FLAG_ROWS):
            rows = pl.ds(at, FLAG_ROWS)
            carried = next_ref[level, rows]
            older = second_ref[0, rows]
            for target in range(ROW):
                total = inside_ref[target, level, rows] + carried * on_next_ref[target, level]
                if level == 0:
                    total = total + older * on_second_ref[target]
                picked_ref[target, level, rows] = total


def merge(inside, on_next, on_second, carried, second):
    return pl.pallas_call(
        merge_kernel,
        out_shape=jax.ShapeDtypeStruct(inside.shape, inside.dtype),
        in_specs=[VMEM] * 5,
        out_specs=VMEM,
        compiler_params=pltpu.CompilerParams(vmem_limit_bytes=SMALL_VMEM),
        cost_estimate=pl.CostEstimate(flops=0, bytes_accessed=1 << 20, transcendentals=0),
        name="merge",
    )(inside, on_next, on_second, carried, second)


def attend_kernel(
    first_head, heads, first_ref, parents_ref, query_ref, key_ref, value_ref, far_ref, *refs
):
    out_ref, path_key_ref, path_value_ref = refs[-3:]
    first = first_ref[0]
    _, depth0 = path_of(parents_ref, first)
    _, depth1 = path_of(parents_ref, first + 1)
    follows = jnp.where(parents_ref[first + 1] == first, 0.0, MASKED)

    def scores_of(query, keys):
        return lax.dot_general(
            query, keys, (((1,), (1,)), ((), ())), preferred_element_type=jnp.float32
        )

    def with_ones(values):
        return jnp.concatenate([values, jnp.ones_like(values)], axis=1)

    for piece in range(ROW):
        for level in range(LEVELS):
            rows = pl.ds(piece * STACK + level * PIECE, PIECE)
            path_key_ref[rows, :HEAD_DIM] = far_ref[piece, level, :PIECE]
            path_value_ref[rows, :HEAD_DIM] = far_ref[piece, level, PIECE:]
    path_value_ref[:, HEAD_DIM:] = jnp.ones((PATH, HEAD_DIM), jnp.bfloat16)
    row = lax.broadcasted_iota(jnp.int32, (PATH, HEAD_DIM), 0)
    lane = lax.broadcasted_iota(jnp.int32, (PATH, HEAD_DIM), 1)
    level = lax.rem(row // PIECE, LEVELS)
    limit = jnp.where(lane == 0, depth0, jnp.where(lane == 1, jnp.minimum(depth0, depth1), LEVELS))
    path_key_ref[:, HEAD_DIM:] = jnp.where(level < limit, 0.0, MASKED).astype(jnp.bfloat16)
    path_keys, path_values = path_key_ref[...], path_value_ref[...]

    rows = lax.broadcasted_iota(jnp.int32, (2 * SEG_LEN, HEAD_DIM), 0)
    lanes = lax.broadcasted_iota(jnp.int32, (2 * SEG_LEN, HEAD_DIM), 1)
    marks = (lanes == rows // SEG_LEN).astype(jnp.float32).astype(jnp.bfloat16)
    causal = lax.broadcasted_iota(jnp.int32, (SEG_LEN, SEG_LEN), 1) <= lax.broadcasted_iota(
        jnp.int32, (SEG_LEN, SEG_LEN), 0
    )
    halves = [slice(0, SEG_LEN), slice(SEG_LEN, 2 * SEG_LEN)]
    own_values = [with_ones(value_ref[half]) for half in halves]
    for head in range(heads):
        at = (first_head + head) * HEAD_DIM
        query = query_ref[:, at : at + HEAD_DIM]
        path_scores = scores_of(jnp.concatenate([query, marks], axis=1), path_keys)
        own = [
            [(jnp.where(causal, scores_of(query[half], key_ref[half]), MASKED), values)]
            for half, values in zip(halves, own_values)
        ]
        own[1].append((scores_of(query[halves[1]], key_ref[halves[0]]) + follows, own_values[0]))
        path_weights, own_parts = [], []
        for half, blocks in zip(halves, own):
            row_max = functools.reduce(
                jnp.maximum,
                [jnp.max(s, axis=1, keepdims=True) for s, _ in blocks]
                + [jnp.max(path_scores[half], axis=1, keepdims=True)],
            )
            weigh = lambda s: jnp.exp2((s - row_max) * EXP2_SCALE).astype(jnp.bfloat16)
            path_weights.append(weigh(path_scores[half]))
            own_parts.append(
                sum(
                    jnp.dot(weigh(s), values, preferred_element_type=jnp.float32)
                    for s, values in blocks
                )
            )
        total = jnp.dot(
            jnp.concatenate(path_weights, axis=0), path_values, preferred_element_type=jnp.float32
        ) + jnp.concatenate(own_parts, axis=0)
        mixture = total[:, :HEAD_DIM] / total[:, HEAD_DIM:]
        out_ref[:, head * HEAD_DIM : (head + 1) * HEAD_DIM] = mixture.astype(out_ref.dtype)


def attend(first, parents, queries, keys, values, far, first_head, heads, after):
    rows = queries.shape[0]
    key_count = PATH + SEG_LEN + SEG_LEN // 2
    return pl.pallas_call(
        functools.partial(attend_kernel, first_head, heads),
        out_shape=jax.ShapeDtypeStruct((rows, heads * HEAD_DIM), jnp.bfloat16),
        in_specs=[SMEM, SMEM] + [VMEM] * 4 + [ANY] * len(after),
        out_specs=VMEM,
        scratch_shapes=[pltpu.VMEM((PATH, 2 * HEAD_DIM), jnp.bfloat16)] * 2,
        compiler_params=pltpu.CompilerParams(vmem_limit_bytes=ATTEND_VMEM),
        cost_estimate=pl.CostEstimate(
            flops=heads * rows * key_count * HEAD_DIM * 10,
            bytes_accessed=heads * rows * HEAD_DIM * 4 + 8 * PATH * HEAD_DIM,
            transcendentals=heads * rows * key_count,
        ),
        name="attend",
    )(first, parents, queries, keys, values, far, *after)


def near_kernel(
    depths, counts, starts_ref, weight_ref, *refs
):
    count = sum(counts)
    parts = refs[:count]
    out_ref, last_ref, held_ref, tile_ref, sem, last_sem = refs[count:]
    width = out_ref.shape[1]
    tiles = width // TILE

    def fetch(n, g):
        columns = pl.ds(n * TILE, TILE)
        rows = pl.ds(pl.multiple_of(starts_ref[g], 2 * HEAD_DIM), depths[g])
        at = sum(depths[:g])
        return pltpu.make_async_copy(
            weight_ref.at[rows, columns], tile_ref.at[n, pl.ds(at, depths[g])], sem.at[n, g]
        )

    def fetch_last(i):
        depth = last_ref.shape[0] // 2
        at = starts_ref[2 + i] + depths[2]
        rows = pl.ds(pl.multiple_of(at, HEAD_DIM), depth)
        return pltpu.make_async_copy(
            weight_ref.at[rows], last_ref.at[pl.ds(i * depth, depth)], last_sem.at[i]
        )

    groups = range(len(depths))
    for n in range(tiles):
        for g in groups:
            fetch(n, g).start()
    for i in range(2):
        fetch_last(i).start()
    at = 0
    for part in parts:
        held_ref[:, at : at + part.shape[1]] = part[...]
        at += part.shape[1]
    for n in range(tiles):
        for g in groups:
            fetch(n, g).wait()
        out_ref[:, n * TILE : (n + 1) * TILE] = jnp.dot(
            held_ref[...], tile_ref[n], preferred_element_type=jnp.float32
        )
    for i in range(2):
        fetch_last(i).wait()


def near_project(groups, starts, weight):
    parts = [part for group in groups for part in group]
    rows = parts[0].shape[0]
    depths = [sum(part.shape[1] for part in group) for group in groups]
    depth = sum(depths)
    full, width = weight.shape
    left = 2 * (depths[0] - depths[2])
    return pl.pallas_call(
        functools.partial(near_kernel, depths, [len(group) for group in groups]),
        out_shape=(
            jax.ShapeDtypeStruct((rows, width), jnp.float32),
            jax.ShapeDtypeStruct((left, width), weight.dtype),
        ),
        in_specs=[SMEM, HBM] + [VMEM] * len(parts),
        out_specs=(VMEM, VMEM),
        scratch_shapes=[
            pltpu.VMEM((rows, depth), weight.dtype),
            pltpu.VMEM((width // TILE, depth, TILE), weight.dtype),
            pltpu.SemaphoreType.DMA((width // TILE, len(groups))),
            pltpu.SemaphoreType.DMA((2,)),
        ],
        compiler_params=pltpu.CompilerParams(vmem_limit_bytes=PROJECT_VMEM),
        cost_estimate=pl.CostEstimate(
            flops=2 * rows * depth * width,
            bytes_accessed=2 * (depth + left) * width + 2 * rows * depth + 4 * rows * width,
            transcendentals=0,
        ),
        name="near_project",
    )(starts, in_hbm(weight), *parts)


def last_kernel(across_ref, corner_ref, weight_ref, base_ref, out_ref):
    depth = across_ref.shape[1]
    for column in range(0, out_ref.shape[1], TILE):
        columns = slice(column, column + TILE)
        total = base_ref[:, columns]
        for i, part_ref in enumerate([across_ref, corner_ref]):
            total = total + jnp.dot(
                part_ref[...],
                weight_ref[i * depth : (i + 1) * depth, columns],
                preferred_element_type=jnp.float32,
            )
        out_ref[:, columns] = total.astype(out_ref.dtype)


def last_project(across, corner, weight, base):
    rows, depth = across.shape
    width = weight.shape[1]
    return pl.pallas_call(
        last_kernel,
        out_shape=jax.ShapeDtypeStruct((rows, width), jnp.bfloat16),
        in_specs=[VMEM] * 4,
        out_specs=VMEM,
        compiler_params=pltpu.CompilerParams(vmem_limit_bytes=LAST_VMEM),
        cost_estimate=pl.CostEstimate(
            flops=4 * rows * depth * width,
            bytes_accessed=4 * depth * (rows + width) + 6 * rows * width,
            transcendentals=0,
        ),
        name="last_project",
    )(across, corner, weight, base)


def swap(part, bit):
    size = lax.axis_size("tensor")
    return lax.ppermute(part, "tensor", [(i, i ^ bit) for i in range(size)])


def trade(pieces):
    devices = lax.axis_size("dp")
    rows = [list(range(at, at + ROW)) for at in range(0, devices, ROW)]
    return lax.all_to_all(pieces, "dp", 0, 0, tiled=True, axis_index_groups=rows)


def onward(piece, step):
    devices = lax.axis_size("dp")
    return lax.ppermute(piece, "dp", [(i, (i + step) % devices) for i in range(devices)])


def per_device(queries, key_proj, value_proj, out_weight, parents):
    me = lax.axis_index("tensor")
    first = (lax.axis_index("dp") * 2).astype(jnp.int32).reshape(1)
    pieces = trade(pack(key_proj, value_proj)).reshape(ROW_SEGS, 2 * PIECE, HEAD_DIM)
    to_next, to_second = carry_out(first, parents, pieces)
    inside = pick(first, parents, pieces)
    far = trade(merge(*inside, onward(to_next, ROW), onward(to_second, 2 * ROW)))

    sizes = [1, 2, 2, 3]
    own, across, head = [], [], 0
    for c, size in enumerate(sizes):
        after = [across[c - 2]] if c >= 2 else []
        own.append(
            attend(first, parents, queries, key_proj, value_proj, far, head, size, after)
        )
        across.append(swap(own[c], 2))
        head += size
    beside = [swap(part, 1) for part in own]
    corner = [swap(part, 1) for part in across[:-1]]
    starts = jnp.stack([me, me ^ 1, me ^ 2, me ^ 3]) * queries.shape[1]
    near, weight = near_project([own, beside, across[:-1], corner], starts, out_weight)
    last, near = lax.optimization_barrier((across[-1], near))
    return last_project(last, swap(last, 1), weight, near)


def solution(mesh):
    placed = (P("dp", "tensor"), P("dp", "tensor"), P("dp", "tensor"), P(None, "tensor"), P())
    return jax.shard_map(
        per_device, mesh=mesh, in_specs=placed, out_specs=P("dp", "tensor"), check_vma=False
    )
```

time: 104 us -> 88.1 us (0.85)
  the two profiles are of different devices: /device:TPU:7 before, /device:TPU:1 now
where the time goes in v3:
time: 88.1 us; the launch traced here: 87.9 us
  Pallas kernels  29.7 us (34%)
  starting transfers between devices  26.9 us (31%)
  blocking collectives  15.6 us (18%)
  waiting for transfers between devices  14.8 us (17%)
    all_to_all x1, blocking collectives, trade(): lax.all_to_all(pieces, 'dp', 0, 0, tiled=True, axis_index_groups=rows)  15.6 us
    ppermute x12, starting transfers between devices, swap(): return lax.ppermute(part, 'tensor', [(i, i ^ bit) for i in range(size)])  13.9 us
    pallas_call x4, Pallas kernels, attend(): pl.pallas_call(functools.partial(attend_kernel, first_head, heads), out_s...  12.9 us
    pallas_call x1, Pallas kernels, near_project(): pl.pallas_call(functools.partial(near_kernel, depths, [len(group) for gro...  10.8 us
    all_to_all x1, waiting for transfers between devices, trade(): lax.all_to_all(pieces, 'dp', 0, 0, tiled=True, axis_index_groups=rows)  10.4 us
    all_to_all x1, starting transfers between devices, trade(): lax.all_to_all(pieces, 'dp', 0, 0, tiled=True, axis_index_groups=rows)  9.03 us
    ppermute x2, starting transfers between devices, onward(): lax.ppermute(piece, 'dp', [(i, (i + step) % devices) for i in range(devic...  3.99 us
    ppermute x2, waiting for transfers between devices, onward(): lax.ppermute(piece, 'dp', [(i, (i + step) % devices) for i in range(devic...  2.98 us
  transfers between devices with their start and end apart: 15, of which 3 were waited for; matrix products, arithmetic and copies ran while one was open for 0% of the time, Pallas kernels for 25%

profile of v3, /device:TPU:1, one launch (start us, length us, event | category | flops | bytes accessed | tf_op | source)
XLA Modules:
  0.0 87.9 jit_solution(10885322800451957573)
XLA Ops:
  0.0 1.7 %pack.1 = bf16[8,2,64,128]{3,2,1,0:T(8,128)(2,1)} custom-call(bf16[512,128]{1,0:T(8,128)(2,1)} %key_ref.9, bf16[512,128]{1,0:T(8,128)(2,1)} %value_ref.9), custom_call_target="tpu_custom_call" | custom-call | bytes 524288 | tf_op jit(solution)/shard_map/pack/pallas_call | solution.py:70
  1.8 9.0 %all-to-all-start = ((bf16[8,2,64,128]{3,2,1,0:T(8,128)(2,1)}), bf16[8,2,64,128]{3,2,1,0:T(8,128)(2,1)S(1)}, u32[]{:S(2)}, u32[]{:S(2)}) async-start(bf16[8,2,64,128]{3,2,1,0:T(8,128)(2,1)} %pack.1), calls=%async_computation | async-start | bytes 524288 | tf_op jit(solution)/shard_map/all_to_all | solution.py:375
  10.8 10.4 %all-to-all-done = bf16[8,2,64,128]{3,2,1,0:T(8,128)(2,1)S(1)} async-done(((bf16[8,2,64,128]{3,2,1,0:T(8,128)(2,1)}), bf16[8,2,64,128]{3,2,1,0:T(8,128)(2,1)S(1)}, u32[]{:S(2)}, u32[]{:S(2)}) %all-to-all-start) | async-done | bytes 262176 | tf_op jit(solution)/shard_map/all_to_all | solution.py:375
  21.2 0.7 copy-done.2
  21.8 0.6 carry_out.1
  22.4 1.4 %collective-permute-start = (bf16[4,64,128]{2,1,0:T(8,128)(2,1)S(1)}, bf16[4,64,128]{2,1,0:T(8,128)(2,1)S(1)}, u32[]{:S(2)}, u32[]{:S(2)}) collective-permute-start(bf16[4,64,128]{2,1,0:T(8,128)(2,1)S(1)} %get-tuple-element.17), channel_id=1, source_target_pairs={{0,32},{4,36},{8,40},{12,44},{16,48},{20,52},{24,56},{28,60},{32,6... | collective-permute-start | bytes 196616 | tf_op jit(solution)/shard_map/ppermute | solution.py:380
  23.8 2.6 %collective-permute-start.1 = (bf16[1,64,128]{2,1,0:T(8,128)(2,1)S(1)}, bf16[1,64,128]{2,1,0:T(8,128)(2,1)S(1)}, u32[]{:S(2)}, u32[]{:S(2)}) collective-permute-start(bf16[1,64,128]{2,1,0:T(8,128)(2,1)S(1)} %get-tuple-element.18), channel_id=1, source_target_pairs={{0,64},{4,68},{8,72},{12,76},{16,80},{20,84},{24,88},{28,92},{32,9... | collective-permute-start | bytes 49160 | tf_op jit(solution)/shard_map/ppermute | solution.py:380
  26.4 0.9 %pick.1 = (bf16[8,4,64,128]{3,2,1,0:T(8,128)(2,1)S(1)}, bf16[8,4,16,128]{3,2,1,0:T(8,128)(2,1)S(1)}, bf16[8,16,128]{2,1,0:T(8,128)(2,1)S(1)}) custom-call(s32[1]{0:T(128)} %bitcast.first_ref, s32[128]{0:T(128)S(1)} %copy-done.2, bf16[16,64,128]{2,1,0:T(8,128)(2,1)S(1)} %bitcast.7), custom_call_target="tpu_custom_call" | custom-call | bytes 1048576 | tf_op jit(solution)/shard_map/pick/pallas_call | solution.py:131
  27.3 3.0 %collective-permute-done.1.second_ref = bf16[1,64,128]{2,1,0:T(8,128)(2,1)S(1)} collective-permute-done((bf16[1,64,128]{2,1,0:T(8,128)(2,1)S(1)}, bf16[1,64,128]{2,1,0:T(8,128)(2,1)S(1)}, u32[]{:S(2)}, u32[]{:S(2)}) %collective-permute-start.1) | collective-permute-done | bytes 16416 | tf_op jit(solution)/shard_map/ppermute | solution.py:380
  30.3 0.0 collective-permute-done.next_ref
  30.3 0.1 merge.1
  30.4 15.6 %all_to_all.10.far_ref = bf16[8,4,64,128]{3,2,1,0:T(8,128)(2,1)S(1)} all-to-all(bf16[8,4,64,128]{3,2,1,0:T(8,128)(2,1)S(1)} %merge.1), channel_id=1, replica_groups={{0,4,8,12,16,20,24,28},{32,36,40,44,48,52,56,60},{64,68,72,76,80,84,88,..., dimensions={0} | all-to-all | bytes 1048576 | tf_op jit(solution)/shard_map/all_to_all | solution.py:375
  46.0 2.2 %attend.6.refs_0_ = bf16[512,128]{1,0:T(8,128)(2,1)S(1)} custom-call(s32[1]{0:T(128)} %bitcast.first_ref, s32[128]{0:T(128)S(1)} %copy-done.3, bf16[512,1024]{1,0:T(8,128)(2,1)S(1)} %copy-done.4, bf16[512,128]{1,0:T(8,128)(2,1)S(1)} %copy-done, bf16[512,128]{1,0:T(8,128)(2,1)S(1)} %copy-done.1, bf16[8,4,64,128]{3,2,1,0:T(8,128)(2,1)S(1)} %all_to_all.10.far_ref), custom_call_target="tpu_custom_call" | custom-call | flops 922746880 | bytes 1310720 | tf_op jit(solution)/shard_map/attend/pallas_call | solution.py:243
  48.3 1.3 %collective-permute-start.4 = (bf16[512,128]{1,0:T(8,128)(2,1)S(1)}, bf16[512,128]{1,0:T(8,128)(2,1)S(1)}, u32[]{:S(2)}, u32[]{:S(2)}) collective-permute-start(bf16[512,128]{1,0:T(8,128)(2,1)S(1)} %attend.6.refs_0_), channel_id=1, source_target_pairs={{0,2},{1,3},{2,0},{3,1},{4,6},{5,7},{6,4},{7,5},{8,10},{9,11},{10,... | collective-permute-start | bytes 393224 | tf_op jit(solution)/shard_map/ppermute | solution.py:369
  49.6 3.2 %attend.4.refs_1_ = bf16[512,256]{1,0:T(8,128)(2,1)S(1)} custom-call(s32[1]{0:T(128)} %bitcast.first_ref, s32[128]{0:T(128)S(1)} %copy-done.3, bf16[512,1024]{1,0:T(8,128)(2,1)S(1)} %copy-done.4, bf16[512,128]{1,0:T(8,128)(2,1)S(1)} %copy-done, bf16[512,128]{1,0:T(8,128)(2,1)S(1)} %copy-done.1, bf16[8,4,64,128]{3,2,1,0:T(8,128)(2,1)S(1)} %all_to_all.10.far_ref), custom_call_target="tpu_custom_call" | custom-call | flops 1845493760 | bytes 1572864 | tf_op jit(solution)/shard_map/attend/pallas_call | solution.py:243
  52.8 0.3 collective-permute-start.2
  53.2 6.0 %collective-permute-start.5 = (bf16[512,128]{1,0:T(8,128)(2,1)S(1)}, bf16[512,128]{1,0:T(8,128)(2,1)S(1)}, u32[]{:S(2)}, u32[]{:S(2)}) collective-permute-start(bf16[512,128]{1,0:T(8,128)(2,1)S(1)} %attend.6.refs_0_), channel_id=1, source_target_pairs={{0,1},{1,0},{2,3},{3,2},{4,5},{5,4},{6,7},{7,6},{8,9},{9,8},{10,11... | collective-permute-start | bytes 393224 | tf_op jit(solution)/shard_map/ppermute | solution.py:369
  59.2 3.2 %attend.7.refs_2_ = bf16[512,256]{1,0:T(8,128)(2,1)S(1)} custom-call(s32[1]{0:T(128)} %bitcast.first_ref, s32[128]{0:T(128)S(1)} %copy-done.3, bf16[512,1024]{1,0:T(8,128)(2,1)S(1)} %copy-done.4, bf16[512,128]{1,0:T(8,128)(2,1)S(1)} %copy-done, bf16[512,128]{1,0:T(8,128)(2,1)S(1)} %copy-done.1, bf16[8,4,64,128]{3,2,1,0:T(8,128)(2,1)S(1)} %all_to_all.10.far_ref, ...), custom_call_target="tpu_custom_call" | custom-call | flops 1845493760 | bytes 1572864 | tf_op jit(solution)/shard_map/attend/pallas_call | solution.py:243
  62.4 1.3 %collective-permute-start.9 = (bf16[512,256]{1,0:T(8,128)(2,1)S(1)}, bf16[512,256]{1,0:T(8,128)(2,1)S(1)}, u32[]{:S(2)}, u32[]{:S(2)}) collective-permute-start(bf16[512,256]{1,0:T(8,128)(2,1)S(1)} %attend.7.refs_2_), channel_id=1, source_target_pairs={{0,2},{1,3},{2,0},{3,1},{4,6},{5,7},{6,4},{7,5},{8,10},{9,11},{10,... | collective-permute-start | bytes 786440 | tf_op jit(solution)/shard_map/ppermute | solution.py:369
  63.7 0.3 collective-permute-start.10
  64.1 4.2 %attend.5.refs_3_ = bf16[512,384]{1,0:T(8,128)(2,1)S(1)} custom-call(s32[1]{0:T(128)} %bitcast.first_ref, s32[128]{0:T(128)S(1)} %copy-done.3, bf16[512,1024]{1,0:T(8,128)(2,1)S(1)} %copy-done.4, bf16[512,128]{1,0:T(8,128)(2,1)S(1)} %copy-done, bf16[512,128]{1,0:T(8,128)(2,1)S(1)} %copy-done.1, bf16[8,4,64,128]{3,2,1,0:T(8,128)(2,1)S(1)} %all_to_all.10.far_ref, ...), custom_call_target="tpu_custom_call" | custom-call | flops 2768240640 | bytes 1835008 | tf_op jit(solution)/shard_map/attend/pallas_call | solution.py:243
  68.3 1.0 %collective-permute-start.8 = (bf16[512,384]{1,0:T(8,128)(2,1)S(1)}, bf16[512,384]{1,0:T(8,128)(2,1)S(1)}, u32[]{:S(2)}, u32[]{:S(2)}) collective-permute-start(bf16[512,384]{1,0:T(8,128)(2,1)S(1)} %attend.5.refs_3_), channel_id=1, source_target_pairs={{0,1},{1,0},{2,3},{3,2},{4,5},{5,4},{6,7},{7,6},{8,9},{9,8},{10,11... | collective-permute-start | bytes 1179656 | tf_op jit(solution)/shard_map/ppermute | solution.py:369
  69.3 0.1 collective-permute-start.6
  69.4 0.4 collective-permute-start.7
  69.9 0.1 collective-permute-start.11
  70.0 1.3 %collective-permute-start.12 = (bf16[512,256]{1,0:T(8,128)(2,1)S(1)}, bf16[512,256]{1,0:T(8,128)(2,1)S(1)}, u32[]{:S(2)}, u32[]{:S(2)}) collective-permute-start(bf16[512,256]{1,0:T(8,128)(2,1)S(1)} %collective-permute-done.9.refs_10_), channel_id=1, source_target_pairs={{0,1},{1,0},{2,3},{3,2},{4,5},{5,4},{6,7},{7,6},{8,9},{9,8},{10,11... | collective-permute-start | bytes 786440 | tf_op jit(solution)/shard_map/ppermute | solution.py:369
  71.2 0.1 add_multiply_fusion.starts_ref
  71.3 1.2 %collective-permute-start.3 = (bf16[512,384]{1,0:T(8,128)(2,1)S(1)}, bf16[512,384]{1,0:T(8,128)(2,1)S(1)}, u32[]{:S(2)}, u32[]{:S(2)}) collective-permute-start(bf16[512,384]{1,0:T(8,128)(2,1)S(1)} %attend.5.refs_3_), channel_id=1, source_target_pairs={{0,2},{1,3},{2,0},{3,1},{4,6},{5,7},{6,4},{7,5},{8,10},{9,11},{10,... | collective-permute-start | bytes 1179656 | tf_op jit(solution)/shard_map/ppermute | solution.py:369
  72.6 10.8 %near_project.1 = (f32[512,1280]{1,0:T(8,128)S(1)}, bf16[768,1280]{1,0:T(8,128)(2,1)S(1)}) custom-call(s32[4]{0:T(128)S(1)} %add_multiply_fusion.starts_ref, bf16[4096,1280]{1,0:T(8,128)(2,1)} %weight_ref.1, bf16[512,128]{1,0:T(8,128)(2,1)S(1)} %attend.6.refs_0_, bf16[512,256]{1,0:T(8,128)(2,1)S(1)} %attend.4.refs_1_, bf16[512,256]{1,0:T(8,128)(2,1)S(1)} %attend.7.refs_2_, ...), custom_call_target="tpu_custom_call" | custom-call | flops 4362076160 | bytes 16515072 | tf_op jit(solution)/shard_map/near_project/pallas_call | solution.py:311
  83.5 0.4 collective-permute-start.13
  83.8 1.4 %collective-permute-done.13.corner_ref = bf16[512,384]{1,0:T(8,128)(2,1)S(1)} collective-permute-done((bf16[512,384]{1,0:T(8,128)(2,1)S(1)}, bf16[512,384]{1,0:T(8,128)(2,1)S(1)}, u32[]{:S(2)}, u32[]{:S(2)}) %collective-permute-start.13) | collective-permute-done | bytes 393248 | tf_op jit(solution)/shard_map/ppermute | solution.py:369
  85.3 2.6 %last_project.1 = bf16[512,1280]{1,0:T(8,128)(2,1)} custom-call(bf16[512,384]{1,0:T(8,128)(2,1)S(1)} %collective-permute-done.3.across_ref, bf16[512,384]{1,0:T(8,128)(2,1)S(1)} %collective-permute-done.13.corner_ref, bf16[768,1280]{1,0:T(8,128)(2,1)S(1)} %get-tuple-element.21.weight_ref, f32[512,1280]{1,0:T(8,128)S(1)} %get-tuple-element.22.base_ref), custom_call_target="tpu_custom_call" | custom-call | flops 1006632960 | bytes 6684672 | tf_op jit(solution)/shard_map/last_project/pallas_call | solution.py:352
  (20 shorter events, 0.0 us)
Async XLA Ops:
  0.0 46.0 %copy-start = (bf16[512,128]{1,0:T(8,128)(2,1)S(1)}, bf16[512,128]{1,0:T(8,128)(2,1)}, u32[]{:S(2)}) copy-start(bf16[512,128]{1,0:T(8,128)(2,1)} %key_ref.9) | copy-start | bytes 393220
  0.0 46.0 %copy-start.1 = (bf16[512,128]{1,0:T(8,128)(2,1)S(1)}, bf16[512,128]{1,0:T(8,128)(2,1)}, u32[]{:S(2)}) copy-start(bf16[512,128]{1,0:T(8,128)(2,1)} %value_ref.9) | copy-start | bytes 393220
  0.0 46.0 %copy-start.3 = (s32[128]{0:T(128)S(1)}, s32[128]{0:T(128)}, u32[]{:S(2)}) copy-start(s32[128]{0:T(128)} %parents_ref.11) | copy-start | bytes 1540
  1.8 19.4 %all-to-all-start = ((bf16[8,2,64,128]{3,2,1,0:T(8,128)(2,1)}), bf16[8,2,64,128]{3,2,1,0:T(8,128)(2,1)S(1)}, u32[]{:S(2)}, u32[]{:S(2)}) async-start(bf16[8,2,64,128]{3,2,1,0:T(8,128)(2,1)} %pack.1), calls=%async_computation | async-start | bytes 524288 | tf_op jit(solution)/shard_map/all_to_all | solution.py:375
  21.2 0.7 copy-start.2
  21.8 24.2 %copy-start.4 = (bf16[512,1024]{1,0:T(8,128)(2,1)S(1)}, bf16[512,1024]{1,0:T(8,128)(2,1)}, u32[]{:S(2)}) copy-start(bf16[512,1024]{1,0:T(8,128)(2,1)} %query_ref.7) | copy-start | bytes 3145732
  22.4 7.9 %collective-permute-start = (bf16[4,64,128]{2,1,0:T(8,128)(2,1)S(1)}, bf16[4,64,128]{2,1,0:T(8,128)(2,1)S(1)}, u32[]{:S(2)}, u32[]{:S(2)}) collective-permute-start(bf16[4,64,128]{2,1,0:T(8,128)(2,1)S(1)} %get-tuple-element.17), channel_id=1, source_target_pairs={{0,32},{4,36},{8,40},{12,44},{16,48},{20,52},{24,56},{28,60},{32,6... | collective-permute-start | bytes 196616 | tf_op jit(solution)/shard_map/ppermute | solution.py:380
  23.8 6.5 %collective-permute-start.1 = (bf16[1,64,128]{2,1,0:T(8,128)(2,1)S(1)}, bf16[1,64,128]{2,1,0:T(8,128)(2,1)S(1)}, u32[]{:S(2)}, u32[]{:S(2)}) collective-permute-start(bf16[1,64,128]{2,1,0:T(8,128)(2,1)S(1)} %get-tuple-element.18), channel_id=1, source_target_pairs={{0,64},{4,68},{8,72},{12,76},{16,80},{20,84},{24,88},{28,92},{32,9... | collective-permute-start | bytes 49160 | tf_op jit(solution)/shard_map/ppermute | solution.py:380
  48.3 10.9 %collective-permute-start.4 = (bf16[512,128]{1,0:T(8,128)(2,1)S(1)}, bf16[512,128]{1,0:T(8,128)(2,1)S(1)}, u32[]{:S(2)}, u32[]{:S(2)}) collective-permute-start(bf16[512,128]{1,0:T(8,128)(2,1)S(1)} %attend.6.refs_0_), channel_id=1, source_target_pairs={{0,2},{1,3},{2,0},{3,1},{4,6},{5,7},{6,4},{7,5},{8,10},{9,11},{10,... | collective-permute-start | bytes 393224 | tf_op jit(solution)/shard_map/ppermute | solution.py:369
  52.8 11.3 %collective-permute-start.2 = (bf16[512,256]{1,0:T(8,128)(2,1)S(1)}, bf16[512,256]{1,0:T(8,128)(2,1)S(1)}, u32[]{:S(2)}, u32[]{:S(2)}) collective-permute-start(bf16[512,256]{1,0:T(8,128)(2,1)S(1)} %attend.4.refs_1_), channel_id=1, source_target_pairs={{0,2},{1,3},{2,0},{3,1},{4,6},{5,7},{6,4},{7,5},{8,10},{9,11},{10,... | collective-permute-start | bytes 786440 | tf_op jit(solution)/shard_map/ppermute | solution.py:369
  53.2 16.3 %collective-permute-start.5 = (bf16[512,128]{1,0:T(8,128)(2,1)S(1)}, bf16[512,128]{1,0:T(8,128)(2,1)S(1)}, u32[]{:S(2)}, u32[]{:S(2)}) collective-permute-start(bf16[512,128]{1,0:T(8,128)(2,1)S(1)} %attend.6.refs_0_), channel_id=1, source_target_pairs={{0,1},{1,0},{2,3},{3,2},{4,5},{5,4},{6,7},{7,6},{8,9},{9,8},{10,11... | collective-permute-start | bytes 393224 | tf_op jit(solution)/shard_map/ppermute | solution.py:369
  62.4 7.5 %collective-permute-start.9 = (bf16[512,256]{1,0:T(8,128)(2,1)S(1)}, bf16[512,256]{1,0:T(8,128)(2,1)S(1)}, u32[]{:S(2)}, u32[]{:S(2)}) collective-permute-start(bf16[512,256]{1,0:T(8,128)(2,1)S(1)} %attend.7.refs_2_), channel_id=1, source_target_pairs={{0,2},{1,3},{2,0},{3,1},{4,6},{5,7},{6,4},{7,5},{8,10},{9,11},{10,... | collective-permute-start | bytes 786440 | tf_op jit(solution)/shard_map/ppermute | solution.py:369
  63.7 6.1 %collective-permute-start.10 = (bf16[512,128]{1,0:T(8,128)(2,1)S(1)}, bf16[512,128]{1,0:T(8,128)(2,1)S(1)}, u32[]{:S(2)}, u32[]{:S(2)}) collective-permute-start(bf16[512,128]{1,0:T(8,128)(2,1)S(1)} %collective-permute-done.4.refs_0_.refs_8_), channel_id=1, source_target_pairs={{0,1},{1,0},{2,3},{3,2},{4,5},{5,4},{6,7},{7,6},{8,9},{9,8},{10,11... | collective-permute-start | bytes 393224 | tf_op jit(solution)/shard_map/ppermute | solution.py:369
  68.3 4.3 %collective-permute-start.8 = (bf16[512,384]{1,0:T(8,128)(2,1)S(1)}, bf16[512,384]{1,0:T(8,128)(2,1)S(1)}, u32[]{:S(2)}, u32[]{:S(2)}) collective-permute-start(bf16[512,384]{1,0:T(8,128)(2,1)S(1)} %attend.5.refs_3_), channel_id=1, source_target_pairs={{0,1},{1,0},{2,3},{3,2},{4,5},{5,4},{6,7},{7,6},{8,9},{9,8},{10,11... | collective-permute-start | bytes 1179656 | tf_op jit(solution)/shard_map/ppermute | solution.py:369
  69.3 2.0 %collective-permute-start.6 = (bf16[512,256]{1,0:T(8,128)(2,1)S(1)}, bf16[512,256]{1,0:T(8,128)(2,1)S(1)}, u32[]{:S(2)}, u32[]{:S(2)}) collective-permute-start(bf16[512,256]{1,0:T(8,128)(2,1)S(1)} %attend.4.refs_1_), channel_id=1, source_target_pairs={{0,1},{1,0},{2,3},{3,2},{4,5},{5,4},{6,7},{7,6},{8,9},{9,8},{10,11... | collective-permute-start | bytes 786440 | tf_op jit(solution)/shard_map/ppermute | solution.py:369
  69.4 3.1 %collective-permute-start.7 = (bf16[512,256]{1,0:T(8,128)(2,1)S(1)}, bf16[512,256]{1,0:T(8,128)(2,1)S(1)}, u32[]{:S(2)}, u32[]{:S(2)}) collective-permute-start(bf16[512,256]{1,0:T(8,128)(2,1)S(1)} %attend.7.refs_2_), channel_id=1, source_target_pairs={{0,1},{1,0},{2,3},{3,2},{4,5},{5,4},{6,7},{7,6},{8,9},{9,8},{10,11... | collective-permute-start | bytes 786440 | tf_op jit(solution)/shard_map/ppermute | solution.py:369
  69.9 2.7 %collective-permute-start.11 = (bf16[512,256]{1,0:T(8,128)(2,1)S(1)}, bf16[512,256]{1,0:T(8,128)(2,1)S(1)}, u32[]{:S(2)}, u32[]{:S(2)}) collective-permute-start(bf16[512,256]{1,0:T(8,128)(2,1)S(1)} %collective-permute-done.2.refs_0_.refs_9_), channel_id=1, source_target_pairs={{0,1},{1,0},{2,3},{3,2},{4,5},{5,4},{6,7},{7,6},{8,9},{9,8},{10,11... | collective-permute-start | bytes 786440 | tf_op jit(solution)/shard_map/ppermute | solution.py:369
  70.0 2.6 %collective-permute-start.12 = (bf16[512,256]{1,0:T(8,128)(2,1)S(1)}, bf16[512,256]{1,0:T(8,128)(2,1)S(1)}, u32[]{:S(2)}, u32[]{:S(2)}) collective-permute-start(bf16[512,256]{1,0:T(8,128)(2,1)S(1)} %collective-permute-done.9.refs_10_), channel_id=1, source_target_pairs={{0,1},{1,0},{2,3},{3,2},{4,5},{5,4},{6,7},{7,6},{8,9},{9,8},{10,11... | collective-permute-start | bytes 786440 | tf_op jit(solution)/shard_map/ppermute | solution.py:369
  71.3 12.1 %collective-permute-start.3 = (bf16[512,384]{1,0:T(8,128)(2,1)S(1)}, bf16[512,384]{1,0:T(8,128)(2,1)S(1)}, u32[]{:S(2)}, u32[]{:S(2)}) collective-permute-start(bf16[512,384]{1,0:T(8,128)(2,1)S(1)} %attend.5.refs_3_), channel_id=1, source_target_pairs={{0,2},{1,3},{2,0},{3,1},{4,6},{5,7},{6,4},{7,5},{8,10},{9,11},{10,... | collective-permute-start | bytes 1179656 | tf_op jit(solution)/shard_map/ppermute | solution.py:369
  83.5 1.8 %collective-permute-start.13 = (bf16[512,384]{1,0:T(8,128)(2,1)S(1)}, bf16[512,384]{1,0:T(8,128)(2,1)S(1)}, u32[]{:S(2)}, u32[]{:S(2)}) collective-permute-start(bf16[512,384]{1,0:T(8,128)(2,1)S(1)} %collective-permute-done.3.across_ref), channel_id=1, source_target_pairs={{0,1},{1,0},{2,3},{3,2},{4,5},{5,4},{6,7},{7,6},{8,9},{9,8},{10,11... | collective-permute-start | bytes 1179656 | tf_op jit(solution)/shard_map/ppermute | solution.py:369

commit v4 on v3

--- a/solution.py
+++ b/solution.py
@@ -19,9 +19,10 @@
 MASKED = -1e30
 EXP2_SCALE = math.log2(math.e) * HEAD_DIM ** (-0.5)
 SMALL_VMEM = 6 * 1024 * 1024
-ATTEND_VMEM = 20 * 1024 * 1024
-PROJECT_VMEM = 28 * 1024 * 1024
-LAST_VMEM = 16 * 1024 * 1024
+ATTEND_VMEM = 18 * 1024 * 1024
+PROJECT_VMEM = 14 * 1024 * 1024
+LAST_VMEM = 10 * 1024 * 1024
+HOLD_VMEM = 14 * 1024 * 1024
 TILE = 256
 
 VMEM = pl.BlockSpec(memory_space=pltpu.VMEM)
@@ -33,6 +34,10 @@
 
 def in_hbm(array):
     return pltpu.with_memory_space_constraint(array, pltpu.HBM)
+
+
+def in_vmem(array):
+    return pltpu.with_memory_space_constraint(array, pltpu.VMEM)
 
 
 def path_of(parents_ref, seg):
@@ -83,7 +88,7 @@
     return (first_ref[0] // ROW_SEGS) * ROW_SEGS
 
 
-def carry_kernel(first_ref, parents_ref, pieces_ref, next_ref, second_ref):
+def carry_kernel(first_ref, parents_ref, pieces_ref, _, next_ref, second_ref):
     base = row_start(first_ref)
     last = parents_ref.shape[0] - 1
 
@@ -97,17 +102,17 @@
     second_ref[0] = held(path, depth, 0)
 
 
-def carry_out(first, parents, pieces):
+def carry_out(first, parents, pieces, after):
     shape = lambda n: jax.ShapeDtypeStruct((n,) + pieces.shape[1:], pieces.dtype)
     return pl.pallas_call(
         carry_kernel,
         out_shape=(shape(LEVELS), shape(1)),
-        in_specs=[SMEM, SMEM, VMEM],
+        in_specs=[SMEM, SMEM, VMEM, ANY],
         out_specs=(VMEM, VMEM),
         compiler_params=pltpu.CompilerParams(vmem_limit_bytes=SMALL_VMEM),
         cost_estimate=pl.CostEstimate(flops=0, bytes_accessed=1 << 18, transcendentals=0),
         name="carry_out",
-    )(first, parents, pieces)
+    )(first, parents, pieces, after)
 
 
 def pick_kernel(first_ref, parents_ref, pieces_ref, inside_ref, next_ref, second_ref):
@@ -256,91 +261,86 @@
     )(first, parents, queries, keys, values, far, *after)
 
 
-def near_kernel(
-    depths, counts, starts_ref, weight_ref, *refs
-):
+def hold_kernel(me_ref, weight_ref, held_ref, sem):
+    block = weight_ref.shape[0] // 4
+    copies = []
+    for bit in range(4):
+        rows = pl.ds(pl.multiple_of((me_ref[0] ^ bit) * block, block), block)
+        copies.append(
+            pltpu.make_async_copy(
+                weight_ref.at[rows], held_ref.at[pl.ds(bit * block, block)], sem.at[bit]
+            )
+        )
+    for copy in copies:
+        copy.start()
+    for copy in copies:
+        copy.wait()
+
+
+def hold(me, weight):
+    return pl.pallas_call(
+        hold_kernel,
+        out_shape=pltpu.VMEM(weight.shape, weight.dtype),
+        in_specs=[SMEM, HBM],
+        out_specs=VMEM,
+        scratch_shapes=[pltpu.SemaphoreType.DMA((4,))],
+        compiler_params=pltpu.CompilerParams(vmem_limit_bytes=HOLD_VMEM),
+        cost_estimate=pl.CostEstimate(flops=0, bytes_accessed=4 * weight.size, transcendentals=0),
+        name="hold",
+    )(me, in_hbm(weight))
+
+
+def near_kernel(counts, weight_ref, *refs):
     count = sum(counts)
-    parts = refs[:count]
-    out_ref, last_ref, held_ref, tile_ref, sem, last_sem = refs[count:]
-    width = out_ref.shape[1]
-    tiles = width // TILE
-
-    def fetch(n, g):
-        columns = pl.ds(n * TILE, TILE)
-        rows = pl.ds(pl.multiple_of(starts_ref[g], 2 * HEAD_DIM), depths[g])
-        at = sum(depths[:g])
-        return pltpu.make_async_copy(
-            weight_ref.at[rows, columns], tile_ref.at[n, pl.ds(at, depths[g])], sem.at[n, g]
-        )
-
-    def fetch_last(i):
-        depth = last_ref.shape[0] // 2
-        at = starts_ref[2 + i] + depths[2]
-        rows = pl.ds(pl.multiple_of(at, HEAD_DIM), depth)
-        return pltpu.make_async_copy(
-            weight_ref.at[rows], last_ref.at[pl.ds(i * depth, depth)], last_sem.at[i]
-        )
-
-    groups = range(len(depths))
-    for n in range(tiles):
-        for g in groups:
-            fetch(n, g).start()
-    for i in range(2):
-        fetch_last(i).start()
+    parts, (out_ref, held_ref) = refs[:count], refs[count:]
+    block = weight_ref.shape[0] // 4
     at = 0
     for part in parts:
         held_ref[:, at : at + part.shape[1]] = part[...]
         at += part.shape[1]
-    for n in range(tiles):
-        for g in groups:
-            fetch(n, g).wait()
-        out_ref[:, n * TILE : (n + 1) * TILE] = jnp.dot(
-            held_ref[...], tile_ref[n], preferred_element_type=jnp.float32
+    split = sum(part.shape[1] for part in parts[: -counts[-1]])
+    for column in range(0, out_ref.shape[1], TILE):
+        columns = slice(column, column + TILE)
+        out_ref[:, columns] = jnp.dot(
+            held_ref[:, :split], weight_ref[:split, columns], preferred_element_type=jnp.float32
+        ) + jnp.dot(
+            held_ref[:, split:],
+            weight_ref[3 * block : 3 * block + at - split, columns],
+            preferred_element_type=jnp.float32,
         )
-    for i in range(2):
-        fetch_last(i).wait()
-
-
-def near_project(groups, starts, weight):
+
+
+def near_project(groups, weight):
     parts = [part for group in groups for part in group]
     rows = parts[0].shape[0]
-    depths = [sum(part.shape[1] for part in group) for group in groups]
-    depth = sum(depths)
-    full, width = weight.shape
-    left = 2 * (depths[0] - depths[2])
-    return pl.pallas_call(
-        functools.partial(near_kernel, depths, [len(group) for group in groups]),
-        out_shape=(
-            jax.ShapeDtypeStruct((rows, width), jnp.float32),
-            jax.ShapeDtypeStruct((left, width), weight.dtype),
-        ),
-        in_specs=[SMEM, HBM] + [VMEM] * len(parts),
-        out_specs=(VMEM, VMEM),
-        scratch_shapes=[
-            pltpu.VMEM((rows, depth), weight.dtype),
-            pltpu.VMEM((width // TILE, depth, TILE), weight.dtype),
-            pltpu.SemaphoreType.DMA((width // TILE, len(groups))),
-            pltpu.SemaphoreType.DMA((2,)),
-        ],
+    depth = sum(part.shape[1] for part in parts)
+    width = weight.shape[1]
+    return pl.pallas_call(
+        functools.partial(near_kernel, [len(group) for group in groups]),
+        out_shape=jax.ShapeDtypeStruct((rows, width), jnp.float32),
+        in_specs=[VMEM] * (1 + len(parts)),
+        out_specs=VMEM,
+        scratch_shapes=[pltpu.VMEM((rows, depth), weight.dtype)],
         compiler_params=pltpu.CompilerParams(vmem_limit_bytes=PROJECT_VMEM),
         cost_estimate=pl.CostEstimate(
-            flops=2 * rows * depth * width,
-            bytes_accessed=2 * (depth + left) * width + 2 * rows * depth + 4 * rows * width,
+            flops=rows * depth * width // 4,
+            bytes_accessed=2 * depth * rows,
             transcendentals=0,
         ),
         name="near_project",
-    )(starts, in_hbm(weight), *parts)
+    )(in_vmem(weight), *parts)
 
 
 def last_kernel(across_ref, corner_ref, weight_ref, base_ref, out_ref):
     depth = across_ref.shape[1]
+    block = weight_ref.shape[0] // 4
     for column in range(0, out_ref.shape[1], TILE):
         columns = slice(column, column + TILE)
         total = base_ref[:, columns]
-        for i, part_ref in enumerate([across_ref, corner_ref]):
+        for end, part_ref in [(3 * block, across_ref), (4 * block, corner_ref)]:
             total = total + jnp.dot(
                 part_ref[...],
-                weight_ref[i * depth : (i + 1) * depth, columns],
+                weight_ref[end - depth : end, columns],
                 preferred_element_type=jnp.float32,
             )
         out_ref[:, columns] = total.astype(out_ref.dtype)
@@ -361,7 +361,7 @@
             transcendentals=0,
         ),
         name="last_project",
-    )(across, corner, weight, base)
+    )(across, corner, in_vmem(weight), base)
 
 
 def swap(part, bit):
@@ -384,7 +384,8 @@
     me = lax.axis_index("tensor")
     first = (lax.axis_index("dp") * 2).astype(jnp.int32).reshape(1)
     pieces = trade(pack(key_proj, value_proj)).reshape(ROW_SEGS, 2 * PIECE, HEAD_DIM)
-    to_next, to_second = carry_out(first, parents, pieces)
+    weight = hold(me.astype(jnp.int32).reshape(1), out_weight)
+    to_next, to_second = carry_out(first, parents, pieces, weight)
     inside = pick(first, parents, pieces)
     far = trade(merge(*inside, onward(to_next, ROW), onward(to_second, 2 * ROW)))
 
@@ -399,8 +400,7 @@
         head += size
     beside = [swap(part, 1) for part in own]
     corner = [swap(part, 1) for part in across[:-1]]
-    starts = jnp.stack([me, me ^ 1, me ^ 2, me ^ 3]) * queries.shape[1]
-    near, weight = near_project([own, beside, across[:-1], corner], starts, out_weight)
+    near = near_project([own, beside, across[:-1], corner], weight)
     last, near = lax.optimization_barrier((across[-1], near))
     return last_project(last, swap(last, 1), weight, near)
 

time: 88.1 us -> 90.2 us (1.024)
  local copies, waits for them, and re-layouts: 0.67 us -> 8.01 us
  waiting for transfers between devices: 14.8 us -> 9.96 us
  blocking collectives: 15.6 us -> 18.3 us
  Pallas kernels: 29.7 us -> 27.9 us
  starting transfers between devices: 26.9 us -> 25.6 us
    all_to_all x1, waiting for transfers between devices: 10.4 us -> 2.13 us  [trade(): lax.all_to_all(pieces, 'dp', 0, 0, tiled=True, axis_index_groups=rows)]
    unnamed x10 -> x18, local copies, waits for them, and re-layouts: 0.67 us -> 8.01 us
    ppermute x12, waiting for transfers between devices: 1.47 us -> 4.85 us  [swap(): return lax.ppermute(part, 'tensor', [(i, i ^ bit) for i in range(size)])]
    all_to_all x1, blocking collectives: 15.6 us -> 18.3 us  [trade(): lax.all_to_all(pieces, 'dp', 0, 0, tiled=True, axis_index_groups=rows)]
    pallas_call x1 -> x2, Pallas kernels: 10.8 us -> 9.14 us  [the longest x1 4.95 us: near_project(): pl.pallas_call(functools.partial(near_kernel, [len(group) for group in gr...]
    ppermute x12, starting transfers between devices: 13.9 us -> 12.6 us  [swap(): return lax.ppermute(part, 'tensor', [(i, i ^ bit) for i in range(size)])]
  transfers between devices with their start and end apart: 15 -> 15, of which waited for: 3 -> 7; matrix products, arithmetic and copies ran while one was open for 0% -> 0% of each run, Pallas kernels for 25% -> 23%
where the time goes in v4:
time: 90.2 us; the launch traced here: 89.9 us
  Pallas kernels  27.9 us (31%)
  starting transfers between devices  25.6 us (28%)
  blocking collectives  18.3 us (20%)
  waiting for transfers between devices  9.96 us (11%)
  local copies, waits for them, and re-layouts  8.01 us (9%)
    all_to_all x1, blocking collectives, trade(): lax.all_to_all(pieces, 'dp', 0, 0, tiled=True, axis_index_groups=rows)  18.3 us
    pallas_call x4, Pallas kernels, attend(): pl.pallas_call(functools.partial(attend_kernel, first_head, heads), out_s...  12.9 us
    ppermute x12, starting transfers between devices, swap(): return lax.ppermute(part, 'tensor', [(i, i ^ bit) for i in range(size)])  12.6 us
    all_to_all x1, starting transfers between devices, trade(): lax.all_to_all(pieces, 'dp', 0, 0, tiled=True, axis_index_groups=rows)  9.03 us
    unnamed x18, local copies, waits for them, and re-layouts  8.01 us
    pallas_call x1, Pallas kernels, near_project(): pl.pallas_call(functools.partial(near_kernel, [len(group) for group in gr...  4.95 us
    ppermute x12, waiting for transfers between devices, swap(): return lax.ppermute(part, 'tensor', [(i, i ^ bit) for i in range(size)])  4.85 us
    pallas_call x1, Pallas kernels, hold(): pl.pallas_call(hold_kernel, out_shape=pltpu.VMEM(weight.shape, weight.dty...  4.19 us
  transfers between devices with their start and end apart: 15, of which 7 were waited for; matrix products, arithmetic and copies ran while one was open for 0% of the time, Pallas kernels for 23%

profile of v4, /device:TPU:1, one launch (start us, length us, event | category | flops | bytes accessed | tf_op | source)
XLA Modules:
  0.0 89.9 jit_solution(8748603930889603314)
XLA Ops:
  0.0 1.7 %pack.1 = bf16[8,2,64,128]{3,2,1,0:T(8,128)(2,1)} custom-call(bf16[512,128]{1,0:T(8,128)(2,1)} %key_ref.9, bf16[512,128]{1,0:T(8,128)(2,1)} %value_ref.9), custom_call_target="tpu_custom_call" | custom-call | bytes 524288 | tf_op jit(solution)/shard_map/pack/pallas_call | solution.py:75
  1.7 9.0 %all-to-all-start = ((bf16[8,2,64,128]{3,2,1,0:T(8,128)(2,1)}), bf16[8,2,64,128]{3,2,1,0:T(8,128)(2,1)S(1)}, u32[]{:S(2)}, u32[]{:S(2)}) async-start(bf16[8,2,64,128]{3,2,1,0:T(8,128)(2,1)} %pack.1), calls=%async_computation | async-start | bytes 524288 | tf_op jit(solution)/shard_map/all_to_all | solution.py:375
  10.8 4.2 %hold.1._.weight_ref = bf16[4096,1280]{1,0:T(8,128)(2,1)S(1)} custom-call(s32[1]{0:T(128)} %bitcast.2.me_ref, bf16[4096,1280]{1,0:T(8,128)(2,1)} %weight_ref.1), custom_call_target="tpu_custom_call" | custom-call | bytes 20971520 | tf_op jit(solution)/shard_map/hold/pallas_call | solution.py:281
  15.0 4.0 %copy-done = bf16[4096,1280]{1,0:T(8,128)(2,1)} copy-done((bf16[4096,1280]{1,0:T(8,128)(2,1)}, bf16[4096,1280]{1,0:T(8,128)(2,1)S(1)}, u32[]{:S(2)}) %copy-start) | copy-done | bytes 10485784
  19.0 2.1 %all-to-all-done = bf16[8,2,64,128]{3,2,1,0:T(8,128)(2,1)S(1)} async-done(((bf16[8,2,64,128]{3,2,1,0:T(8,128)(2,1)}), bf16[8,2,64,128]{3,2,1,0:T(8,128)(2,1)S(1)}, u32[]{:S(2)}, u32[]{:S(2)}) %all-to-all-start) | async-done | bytes 262176 | tf_op jit(solution)/shard_map/all_to_all | solution.py:375
  21.1 4.0 %copy-done.1 = bf16[4096,1280]{1,0:T(8,128)(2,1)S(1)} copy-done((bf16[4096,1280]{1,0:T(8,128)(2,1)S(1)}, bf16[4096,1280]{1,0:T(8,128)(2,1)}, u32[]{:S(2)}) %copy-start.1) | copy-done | bytes 10485784
  25.1 0.6 carry_out.1
  25.7 1.4 %collective-permute-start = (bf16[4,64,128]{2,1,0:T(8,128)(2,1)S(1)}, bf16[4,64,128]{2,1,0:T(8,128)(2,1)S(1)}, u32[]{:S(2)}, u32[]{:S(2)}) collective-permute-start(bf16[4,64,128]{2,1,0:T(8,128)(2,1)S(1)} %get-tuple-element.15), channel_id=1, source_target_pairs={{0,32},{4,36},{8,40},{12,44},{16,48},{20,52},{24,56},{28,60},{32,6... | collective-permute-start | bytes 196616 | tf_op jit(solution)/shard_map/ppermute | solution.py:380
  27.1 2.6 %collective-permute-start.1 = (bf16[1,64,128]{2,1,0:T(8,128)(2,1)S(1)}, bf16[1,64,128]{2,1,0:T(8,128)(2,1)S(1)}, u32[]{:S(2)}, u32[]{:S(2)}) collective-permute-start(bf16[1,64,128]{2,1,0:T(8,128)(2,1)S(1)} %get-tuple-element.16), channel_id=1, source_target_pairs={{0,64},{4,68},{8,72},{12,76},{16,80},{20,84},{24,88},{28,92},{32,9... | collective-permute-start | bytes 49160 | tf_op jit(solution)/shard_map/ppermute | solution.py:380
  29.7 0.9 pick.1
  30.6 3.0 %collective-permute-done.1.second_ref = bf16[1,64,128]{2,1,0:T(8,128)(2,1)S(1)} collective-permute-done((bf16[1,64,128]{2,1,0:T(8,128)(2,1)S(1)}, bf16[1,64,128]{2,1,0:T(8,128)(2,1)S(1)}, u32[]{:S(2)}, u32[]{:S(2)}) %collective-permute-start.1) | collective-permute-done | bytes 16416 | tf_op jit(solution)/shard_map/ppermute | solution.py:380
  33.7 18.3 %all_to_all.10.far_ref = bf16[8,4,64,128]{3,2,1,0:T(8,128)(2,1)S(1)} all-to-all(bf16[8,4,64,128]{3,2,1,0:T(8,128)(2,1)S(1)} %merge.1), channel_id=1, replica_groups={{0,4,8,12,16,20,24,28},{32,36,40,44,48,52,56,60},{64,68,72,76,80,84,88,..., dimensions={0} | all-to-all | bytes 1048576 | tf_op jit(solution)/shard_map/all_to_all | solution.py:375
  52.0 2.2 %attend.6.refs_0_ = bf16[512,128]{1,0:T(8,128)(2,1)S(1)} custom-call(s32[1]{0:T(128)} %bitcast.first_ref, s32[128]{0:T(128)S(1)} %copy-done.4, bf16[512,1024]{1,0:T(8,128)(2,1)S(1)} %copy-done.5, bf16[512,128]{1,0:T(8,128)(2,1)S(1)} %copy-done.2, bf16[512,128]{1,0:T(8,128)(2,1)S(1)} %copy-done.3, bf16[8,4,64,128]{3,2,1,0:T(8,128)(2,1)S(1)} %all_to_all.10.far_ref), custom_call_target="tpu_custom_call" | custom-call | flops 922746880 | bytes 1310720 | tf_op jit(solution)/shard_map/attend/pallas_call | solution.py:248
  54.2 1.3 %collective-permute-start.4 = (bf16[512,128]{1,0:T(8,128)(2,1)S(1)}, bf16[512,128]{1,0:T(8,128)(2,1)S(1)}, u32[]{:S(2)}, u32[]{:S(2)}) collective-permute-start(bf16[512,128]{1,0:T(8,128)(2,1)S(1)} %attend.6.refs_0_), channel_id=1, source_target_pairs={{0,2},{1,3},{2,0},{3,1},{4,6},{5,7},{6,4},{7,5},{8,10},{9,11},{10,... | collective-permute-start | bytes 393224 | tf_op jit(solution)/shard_map/ppermute | solution.py:369
  55.5 3.2 %attend.4.refs_1_ = bf16[512,256]{1,0:T(8,128)(2,1)S(1)} custom-call(s32[1]{0:T(128)} %bitcast.first_ref, s32[128]{0:T(128)S(1)} %copy-done.4, bf16[512,1024]{1,0:T(8,128)(2,1)S(1)} %copy-done.5, bf16[512,128]{1,0:T(8,128)(2,1)S(1)} %copy-done.2, bf16[512,128]{1,0:T(8,128)(2,1)S(1)} %copy-done.3, bf16[8,4,64,128]{3,2,1,0:T(8,128)(2,1)S(1)} %all_to_all.10.far_ref), custom_call_target="tpu_custom_call" | custom-call | flops 1845493760 | bytes 1572864 | tf_op jit(solution)/shard_map/attend/pallas_call | solution.py:248
  58.8 0.3 collective-permute-start.2
  59.1 5.1 %collective-permute-start.5 = (bf16[512,128]{1,0:T(8,128)(2,1)S(1)}, bf16[512,128]{1,0:T(8,128)(2,1)S(1)}, u32[]{:S(2)}, u32[]{:S(2)}) collective-permute-start(bf16[512,128]{1,0:T(8,128)(2,1)S(1)} %attend.6.refs_0_), channel_id=1, source_target_pairs={{0,1},{1,0},{2,3},{3,2},{4,5},{5,4},{6,7},{7,6},{8,9},{9,8},{10,11... | collective-permute-start | bytes 393224 | tf_op jit(solution)/shard_map/ppermute | solution.py:369
  64.2 3.2 %attend.7.refs_2_ = bf16[512,256]{1,0:T(8,128)(2,1)S(1)} custom-call(s32[1]{0:T(128)} %bitcast.first_ref, s32[128]{0:T(128)S(1)} %copy-done.4, bf16[512,1024]{1,0:T(8,128)(2,1)S(1)} %copy-done.5, bf16[512,128]{1,0:T(8,128)(2,1)S(1)} %copy-done.2, bf16[512,128]{1,0:T(8,128)(2,1)S(1)} %copy-done.3, bf16[8,4,64,128]{3,2,1,0:T(8,128)(2,1)S(1)} %all_to_all.10.far_ref, ...), custom_call_target="tpu_custom_call" | custom-call | flops 1845493760 | bytes 1572864 | tf_op jit(solution)/shard_map/attend/pallas_call | solution.py:248
  67.5 1.3 %collective-permute-start.9 = (bf16[512,256]{1,0:T(8,128)(2,1)S(1)}, bf16[512,256]{1,0:T(8,128)(2,1)S(1)}, u32[]{:S(2)}, u32[]{:S(2)}) collective-permute-start(bf16[512,256]{1,0:T(8,128)(2,1)S(1)} %attend.7.refs_2_), channel_id=1, source_target_pairs={{0,2},{1,3},{2,0},{3,1},{4,6},{5,7},{6,4},{7,5},{8,10},{9,11},{10,... | collective-permute-start | bytes 786440 | tf_op jit(solution)/shard_map/ppermute | solution.py:369
  68.8 1.3 %collective-permute-start.10 = (bf16[512,128]{1,0:T(8,128)(2,1)S(1)}, bf16[512,128]{1,0:T(8,128)(2,1)S(1)}, u32[]{:S(2)}, u32[]{:S(2)}) collective-permute-start(bf16[512,128]{1,0:T(8,128)(2,1)S(1)} %collective-permute-done.4.refs_0_.refs_8_), channel_id=1, source_target_pairs={{0,1},{1,0},{2,3},{3,2},{4,5},{5,4},{6,7},{7,6},{8,9},{9,8},{10,11... | collective-permute-start | bytes 393224 | tf_op jit(solution)/shard_map/ppermute | solution.py:369
  70.0 4.2 %attend.5.refs_3_ = bf16[512,384]{1,0:T(8,128)(2,1)S(1)} custom-call(s32[1]{0:T(128)} %bitcast.first_ref, s32[128]{0:T(128)S(1)} %copy-done.4, bf16[512,1024]{1,0:T(8,128)(2,1)S(1)} %copy-done.5, bf16[512,128]{1,0:T(8,128)(2,1)S(1)} %copy-done.2, bf16[512,128]{1,0:T(8,128)(2,1)S(1)} %copy-done.3, bf16[8,4,64,128]{3,2,1,0:T(8,128)(2,1)S(1)} %all_to_all.10.far_ref, ...), custom_call_target="tpu_custom_call" | custom-call | flops 2768240640 | bytes 1835008 | tf_op jit(solution)/shard_map/attend/pallas_call | solution.py:248
  74.4 0.3 collective-permute-start.3
  74.7 0.7 collective-permute-start.7
  75.5 0.8 collective-permute-start.12
  76.3 0.2 collective-permute-done.7.refs_6_
  76.5 0.4 collective-permute-done.11.refs_12_
  76.9 0.6 collective-permute-done.12.refs_13_
  77.5 4.9 %near_project.1.base_ref = f32[512,1280]{1,0:T(8,128)S(1)} custom-call(bf16[4096,1280]{1,0:T(8,128)(2,1)S(1)} %bitcast.4, bf16[512,128]{1,0:T(8,128)(2,1)S(1)} %attend.6.refs_0_, bf16[512,256]{1,0:T(8,128)(2,1)S(1)} %attend.4.refs_1_, bf16[512,256]{1,0:T(8,128)(2,1)S(1)} %attend.7.refs_2_, bf16[512,384]{1,0:T(8,128)(2,1)S(1)} %attend.5.refs_3_, ...), custom_call_target="tpu_custom_call" | custom-call | flops 545259520 | bytes 3407872 | tf_op jit(solution)/shard_map/near_project/pallas_call | solution.py:318
  82.4 2.3 %collective-permute-done.3.across_ref = bf16[512,384]{1,0:T(8,128)(2,1)S(1)} collective-permute-done((bf16[512,384]{1,0:T(8,128)(2,1)S(1)}, bf16[512,384]{1,0:T(8,128)(2,1)S(1)}, u32[]{:S(2)}, u32[]{:S(2)}) %collective-permute-start.3) | collective-permute-done | bytes 393248 | tf_op jit(solution)/shard_map/ppermute | solution.py:369
  84.8 1.2 %collective-permute-start.13 = (bf16[512,384]{1,0:T(8,128)(2,1)S(1)}, bf16[512,384]{1,0:T(8,128)(2,1)S(1)}, u32[]{:S(2)}, u32[]{:S(2)}) collective-permute-start(bf16[512,384]{1,0:T(8,128)(2,1)S(1)} %collective-permute-done.3.across_ref), channel_id=1, source_target_pairs={{0,1},{1,0},{2,3},{3,2},{4,5},{5,4},{6,7},{7,6},{8,9},{9,8},{10,11... | collective-permute-start | bytes 1179656 | tf_op jit(solution)/shard_map/ppermute | solution.py:369
  86.0 1.3 %collective-permute-done.13.corner_ref = bf16[512,384]{1,0:T(8,128)(2,1)S(1)} collective-permute-done((bf16[512,384]{1,0:T(8,128)(2,1)S(1)}, bf16[512,384]{1,0:T(8,128)(2,1)S(1)}, u32[]{:S(2)}, u32[]{:S(2)}) %collective-permute-start.13) | collective-permute-done | bytes 393248 | tf_op jit(solution)/shard_map/ppermute | solution.py:369
  87.3 2.6 %last_project.1 = bf16[512,1280]{1,0:T(8,128)(2,1)} custom-call(bf16[512,384]{1,0:T(8,128)(2,1)S(1)} %collective-permute-done.3.across_ref, bf16[512,384]{1,0:T(8,128)(2,1)S(1)} %collective-permute-done.13.corner_ref, bf16[4096,1280]{1,0:T(8,128)(2,1)S(1)} %bitcast.4, f32[512,1280]{1,0:T(8,128)S(1)} %near_project.1.base_ref), custom_call_target="tpu_custom_call" | custom-call | flops 1006632960 | bytes 6684672 | tf_op jit(solution)/shard_map/last_project/pallas_call | solution.py:352
  (29 shorter events, 0.4 us)
Async XLA Ops:
  1.7 19.4 %all-to-all-start = ((bf16[8,2,64,128]{3,2,1,0:T(8,128)(2,1)}), bf16[8,2,64,128]{3,2,1,0:T(8,128)(2,1)S(1)}, u32[]{:S(2)}, u32[]{:S(2)}) async-start(bf16[8,2,64,128]{3,2,1,0:T(8,128)(2,1)} %pack.1), calls=%async_computation | async-start | bytes 524288 | tf_op jit(solution)/shard_map/all_to_all | solution.py:375
  10.7 10.4 %copy-start.4 = (s32[128]{0:T(128)S(1)}, s32[128]{0:T(128)}, u32[]{:S(2)}) copy-start(s32[128]{0:T(128)} %parents_ref.11) | copy-start | bytes 1540
  10.7 41.2 %copy-start.2 = (bf16[512,128]{1,0:T(8,128)(2,1)S(1)}, bf16[512,128]{1,0:T(8,128)(2,1)}, u32[]{:S(2)}) copy-start(bf16[512,128]{1,0:T(8,128)(2,1)} %key_ref.9) | copy-start | bytes 393220
  10.7 41.2 %copy-start.3 = (bf16[512,128]{1,0:T(8,128)(2,1)S(1)}, bf16[512,128]{1,0:T(8,128)(2,1)}, u32[]{:S(2)}) copy-start(bf16[512,128]{1,0:T(8,128)(2,1)} %value_ref.9) | copy-start | bytes 393220
  10.8 41.2 %copy-start.5 = (bf16[512,1024]{1,0:T(8,128)(2,1)S(1)}, bf16[512,1024]{1,0:T(8,128)(2,1)}, u32[]{:S(2)}) copy-start(bf16[512,1024]{1,0:T(8,128)(2,1)} %query_ref.7) | copy-start | bytes 3145732
  15.0 4.0 %copy-start = (bf16[4096,1280]{1,0:T(8,128)(2,1)}, bf16[4096,1280]{1,0:T(8,128)(2,1)S(1)}, u32[]{:S(2)}) copy-start(bf16[4096,1280]{1,0:T(8,128)(2,1)S(1)} %hold.1._.weight_ref) | copy-start | bytes 31457284
  21.1 4.0 %copy-start.1 = (bf16[4096,1280]{1,0:T(8,128)(2,1)S(1)}, bf16[4096,1280]{1,0:T(8,128)(2,1)}, u32[]{:S(2)}) copy-start(bf16[4096,1280]{1,0:T(8,128)(2,1)} %copy-done) | copy-start | bytes 31457284
  25.7 7.9 %collective-permute-start = (bf16[4,64,128]{2,1,0:T(8,128)(2,1)S(1)}, bf16[4,64,128]{2,1,0:T(8,128)(2,1)S(1)}, u32[]{:S(2)}, u32[]{:S(2)}) collective-permute-start(bf16[4,64,128]{2,1,0:T(8,128)(2,1)S(1)} %get-tuple-element.15), channel_id=1, source_target_pairs={{0,32},{4,36},{8,40},{12,44},{16,48},{20,52},{24,56},{28,60},{32,6... | collective-permute-start | bytes 196616 | tf_op jit(solution)/shard_map/ppermute | solution.py:380
  27.1 6.5 %collective-permute-start.1 = (bf16[1,64,128]{2,1,0:T(8,128)(2,1)S(1)}, bf16[1,64,128]{2,1,0:T(8,128)(2,1)S(1)}, u32[]{:S(2)}, u32[]{:S(2)}) collective-permute-start(bf16[1,64,128]{2,1,0:T(8,128)(2,1)S(1)} %get-tuple-element.16), channel_id=1, source_target_pairs={{0,64},{4,68},{8,72},{12,76},{16,80},{20,84},{24,88},{28,92},{32,9... | collective-permute-start | bytes 49160 | tf_op jit(solution)/shard_map/ppermute | solution.py:380
  54.2 23.2 %slice-start = ((s8[10485760]{0:T(1024)(128)(4,1)}), s8[4194304]{0:T(1024)(128)(4,1)S(1)}, s32[]{:S(2)}) async-start(s8[10485760]{0:T(1024)(128)(4,1)} %bitcast.3), calls=%async_computation.2 | async-start | bytes 8388608
  54.2 10.0 %collective-permute-start.4 = (bf16[512,128]{1,0:T(8,128)(2,1)S(1)}, bf16[512,128]{1,0:T(8,128)(2,1)S(1)}, u32[]{:S(2)}, u32[]{:S(2)}) collective-permute-start(bf16[512,128]{1,0:T(8,128)(2,1)S(1)} %attend.6.refs_0_), channel_id=1, source_target_pairs={{0,2},{1,3},{2,0},{3,1},{4,6},{5,7},{6,4},{7,5},{8,10},{9,11},{10,... | collective-permute-start | bytes 393224 | tf_op jit(solution)/shard_map/ppermute | solution.py:369
  58.8 18.7 %slice-start.1 = ((s8[10485760]{0:T(1024)(128)(4,1)}), s8[4194304]{0:T(1024)(128)(4,1)S(1)}, s32[]{:S(2)}) async-start(s8[10485760]{0:T(1024)(128)(4,1)} %bitcast.3), calls=%async_computation.3 | async-start | bytes 8388608
  58.8 11.3 %collective-permute-start.2 = (bf16[512,256]{1,0:T(8,128)(2,1)S(1)}, bf16[512,256]{1,0:T(8,128)(2,1)S(1)}, u32[]{:S(2)}, u32[]{:S(2)}) collective-permute-start(bf16[512,256]{1,0:T(8,128)(2,1)S(1)} %attend.4.refs_1_), channel_id=1, source_target_pairs={{0,2},{1,3},{2,0},{3,1},{4,6},{5,7},{6,4},{7,5},{8,10},{9,11},{10,... | collective-permute-start | bytes 786440 | tf_op jit(solution)/shard_map/ppermute | solution.py:369
  59.1 15.3 %collective-permute-start.5 = (bf16[512,128]{1,0:T(8,128)(2,1)S(1)}, bf16[512,128]{1,0:T(8,128)(2,1)S(1)}, u32[]{:S(2)}, u32[]{:S(2)}) collective-permute-start(bf16[512,128]{1,0:T(8,128)(2,1)S(1)} %attend.6.refs_0_), channel_id=1, source_target_pairs={{0,1},{1,0},{2,3},{3,2},{4,5},{5,4},{6,7},{7,6},{8,9},{9,8},{10,11... | collective-permute-start | bytes 393224 | tf_op jit(solution)/shard_map/ppermute | solution.py:369
  64.2 11.1 %collective-permute-start.6 = (bf16[512,256]{1,0:T(8,128)(2,1)S(1)}, bf16[512,256]{1,0:T(8,128)(2,1)S(1)}, u32[]{:S(2)}, u32[]{:S(2)}) collective-permute-start(bf16[512,256]{1,0:T(8,128)(2,1)S(1)} %attend.4.refs_1_), channel_id=1, source_target_pairs={{0,1},{1,0},{2,3},{3,2},{4,5},{5,4},{6,7},{7,6},{8,9},{9,8},{10,11... | collective-permute-start | bytes 786440 | tf_op jit(solution)/shard_map/ppermute | solution.py:369
  67.5 10.0 %slice-start.2 = ((s8[10485760]{0:T(1024)(128)(4,1)}), s8[2097152]{0:T(1024)(128)(4,1)S(1)}, s32[]{:S(2)}) async-start(s8[10485760]{0:T(1024)(128)(4,1)} %bitcast.3), calls=%async_computation.4 | async-start | bytes 4194304
  67.5 8.0 %collective-permute-start.9 = (bf16[512,256]{1,0:T(8,128)(2,1)S(1)}, bf16[512,256]{1,0:T(8,128)(2,1)S(1)}, u32[]{:S(2)}, u32[]{:S(2)}) collective-permute-start(bf16[512,256]{1,0:T(8,128)(2,1)S(1)} %attend.7.refs_2_), channel_id=1, source_target_pairs={{0,2},{1,3},{2,0},{3,1},{4,6},{5,7},{6,4},{7,5},{8,10},{9,11},{10,... | collective-permute-start | bytes 786440 | tf_op jit(solution)/shard_map/ppermute | solution.py:369
  68.8 5.9 %collective-permute-start.10 = (bf16[512,128]{1,0:T(8,128)(2,1)S(1)}, bf16[512,128]{1,0:T(8,128)(2,1)S(1)}, u32[]{:S(2)}, u32[]{:S(2)}) collective-permute-start(bf16[512,128]{1,0:T(8,128)(2,1)S(1)} %collective-permute-done.4.refs_0_.refs_8_), channel_id=1, source_target_pairs={{0,1},{1,0},{2,3},{3,2},{4,5},{5,4},{6,7},{7,6},{8,9},{9,8},{10,11... | collective-permute-start | bytes 393224 | tf_op jit(solution)/shard_map/ppermute | solution.py:369
  74.3 3.2 %collective-permute-start.8 = (bf16[512,384]{1,0:T(8,128)(2,1)S(1)}, bf16[512,384]{1,0:T(8,128)(2,1)S(1)}, u32[]{:S(2)}, u32[]{:S(2)}) collective-permute-start(bf16[512,384]{1,0:T(8,128)(2,1)S(1)} %attend.5.refs_3_), channel_id=1, source_target_pairs={{0,1},{1,0},{2,3},{3,2},{4,5},{5,4},{6,7},{7,6},{8,9},{9,8},{10,11... | collective-permute-start | bytes 1179656 | tf_op jit(solution)/shard_map/ppermute | solution.py:369
  74.4 10.4 %collective-permute-start.3 = (bf16[512,384]{1,0:T(8,128)(2,1)S(1)}, bf16[512,384]{1,0:T(8,128)(2,1)S(1)}, u32[]{:S(2)}, u32[]{:S(2)}) collective-permute-start(bf16[512,384]{1,0:T(8,128)(2,1)S(1)} %attend.5.refs_3_), channel_id=1, source_target_pairs={{0,2},{1,3},{2,0},{3,1},{4,6},{5,7},{6,4},{7,5},{8,10},{9,11},{10,... | collective-permute-start | bytes 1179656 | tf_op jit(solution)/shard_map/ppermute | solution.py:369
  74.7 1.8 %collective-permute-start.7 = (bf16[512,256]{1,0:T(8,128)(2,1)S(1)}, bf16[512,256]{1,0:T(8,128)(2,1)S(1)}, u32[]{:S(2)}, u32[]{:S(2)}) collective-permute-start(bf16[512,256]{1,0:T(8,128)(2,1)S(1)} %attend.7.refs_2_), channel_id=1, source_target_pairs={{0,1},{1,0},{2,3},{3,2},{4,5},{5,4},{6,7},{7,6},{8,9},{9,8},{10,11... | collective-permute-start | bytes 786440 | tf_op jit(solution)/shard_map/ppermute | solution.py:369
  75.4 1.5 %collective-permute-start.11 = (bf16[512,256]{1,0:T(8,128)(2,1)S(1)}, bf16[512,256]{1,0:T(8,128)(2,1)S(1)}, u32[]{:S(2)}, u32[]{:S(2)}) collective-permute-start(bf16[512,256]{1,0:T(8,128)(2,1)S(1)} %collective-permute-done.2.refs_0_.refs_9_), channel_id=1, source_target_pairs={{0,1},{1,0},{2,3},{3,2},{4,5},{5,4},{6,7},{7,6},{8,9},{9,8},{10,11... | collective-permute-start | bytes 786440 | tf_op jit(solution)/shard_map/ppermute | solution.py:369
  75.5 2.0 %collective-permute-start.12 = (bf16[512,256]{1,0:T(8,128)(2,1)S(1)}, bf16[512,256]{1,0:T(8,128)(2,1)S(1)}, u32[]{:S(2)}, u32[]{:S(2)}) collective-permute-start(bf16[512,256]{1,0:T(8,128)(2,1)S(1)} %collective-permute-done.9.refs_10_), channel_id=1, source_target_pairs={{0,1},{1,0},{2,3},{3,2},{4,5},{5,4},{6,7},{7,6},{8,9},{9,8},{10,11... | collective-permute-start | bytes 786440 | tf_op jit(solution)/shard_map/ppermute | solution.py:369
  84.8 2.6 %collective-permute-start.13 = (bf16[512,384]{1,0:T(8,128)(2,1)S(1)}, bf16[512,384]{1,0:T(8,128)(2,1)S(1)}, u32[]{:S(2)}, u32[]{:S(2)}) collective-permute-start(bf16[512,384]{1,0:T(8,128)(2,1)S(1)} %collective-permute-done.3.across_ref), channel_id=1, source_target_pairs={{0,1},{1,0},{2,3},{3,2},{4,5},{5,4},{6,7},{7,6},{8,9},{9,8},{10,11... | collective-permute-start | bytes 1179656 | tf_op jit(solution)/shard_map/ppermute | solution.py:369

commit v5 on v4

--- a/solution.py
+++ b/solution.py
@@ -21,13 +21,11 @@
 SMALL_VMEM = 6 * 1024 * 1024
 ATTEND_VMEM = 18 * 1024 * 1024
 PROJECT_VMEM = 14 * 1024 * 1024
-LAST_VMEM = 10 * 1024 * 1024
-HOLD_VMEM = 14 * 1024 * 1024
 TILE = 256
+TOGETHER = 2
 
 VMEM = pl.BlockSpec(memory_space=pltpu.VMEM)
 SMEM = pl.BlockSpec(memory_space=pltpu.SMEM)
-ANY = pl.BlockSpec(memory_space=pl.ANY)
 HBM = pl.BlockSpec(memory_space=pltpu.HBM)
 FLAG_ROWS = 16
 
@@ -74,10 +72,13 @@
 def pack(keys, values):
     return pl.pallas_call(
         pack_kernel,
-        out_shape=jax.ShapeDtypeStruct((ROW, 2, 2 * PIECE, HEAD_DIM), keys.dtype),
+        out_shape=(
+            jax.ShapeDtypeStruct((ROW, 2, 2 * PIECE, HEAD_DIM), keys.dtype),
+            jax.ShapeDtypeStruct((2,) + keys.shape, keys.dtype),
+        ),
         in_specs=[HBM, HBM],
-        out_specs=VMEM,
-        scratch_shapes=[pltpu.VMEM((2,) + keys.shape, keys.dtype), pltpu.SemaphoreType.DMA((2,))],
+        out_specs=(VMEM, VMEM),
+        scratch_shapes=[pltpu.SemaphoreType.DMA((2,))],
         compiler_params=pltpu.CompilerParams(vmem_limit_bytes=SMALL_VMEM),
         cost_estimate=pl.CostEstimate(flops=0, bytes_accessed=1 << 19, transcendentals=0),
         name="pack",
@@ -88,7 +89,7 @@
     return (first_ref[0] // ROW_SEGS) * ROW_SEGS
 
 
-def carry_kernel(first_ref, parents_ref, pieces_ref, _, next_ref, second_ref):
+def carry_kernel(first_ref, parents_ref, pieces_ref, next_ref, second_ref):
     base = row_start(first_ref)
     last = parents_ref.shape[0] - 1
 
@@ -102,17 +103,17 @@
     second_ref[0] = held(path, depth, 0)
 
 
-def carry_out(first, parents, pieces, after):
+def carry_out(first, parents, pieces):
     shape = lambda n: jax.ShapeDtypeStruct((n,) + pieces.shape[1:], pieces.dtype)
     return pl.pallas_call(
         carry_kernel,
         out_shape=(shape(LEVELS), shape(1)),
-        in_specs=[SMEM, SMEM, VMEM, ANY],
+        in_specs=[SMEM, SMEM, VMEM],
         out_specs=(VMEM, VMEM),
         compiler_params=pltpu.CompilerParams(vmem_limit_bytes=SMALL_VMEM),
         cost_estimate=pl.CostEstimate(flops=0, bytes_accessed=1 << 18, transcendentals=0),
         name="carry_out",
-    )(first, parents, pieces, after)
+    )(first, parents, pieces)
 
 
 def pick_kernel(first_ref, parents_ref, pieces_ref, inside_ref, next_ref, second_ref):
@@ -173,10 +174,18 @@
     )(inside, on_next, on_second, carried, second)
 
 
-def attend_kernel(
-    first_head, heads, first_ref, parents_ref, query_ref, key_ref, value_ref, far_ref, *refs
-):
-    out_ref, path_key_ref, path_value_ref = refs[-3:]
+def attend_kernel(first_ref, parents_ref, query_ref, pair_ref, far_ref, *refs):
+    key_ref, value_ref = pair_ref.at[0], pair_ref.at[1]
+    bring = len(refs) > 3
+    if bring:
+        me_ref, weight_ref, out_ref, held_ref, path_key_ref, path_value_ref, near_ref, sem = refs
+        ready = pltpu.make_async_copy(query_ref, near_ref, sem.at[4])
+        copies = weight_copies(me_ref, weight_ref, held_ref, sem)
+        for copy in [ready] + copies:
+            copy.start()
+        query_ref = near_ref
+    else:
+        out_ref, path_key_ref, path_value_ref = refs
     first = first_ref[0]
     _, depth0 = path_of(parents_ref, first)
     _, depth1 = path_of(parents_ref, first + 1)
@@ -201,7 +210,6 @@
     level = lax.rem(row // PIECE, LEVELS)
     limit = jnp.where(lane == 0, depth0, jnp.where(lane == 1, jnp.minimum(depth0, depth1), LEVELS))
     path_key_ref[:, HEAD_DIM:] = jnp.where(level < limit, 0.0, MASKED).astype(jnp.bfloat16)
-    path_keys, path_values = path_key_ref[...], path_value_ref[...]
 
     rows = lax.broadcasted_iota(jnp.int32, (2 * SEG_LEN, HEAD_DIM), 0)
     lanes = lax.broadcasted_iota(jnp.int32, (2 * SEG_LEN, HEAD_DIM), 1)
@@ -210,11 +218,10 @@
         jnp.int32, (SEG_LEN, SEG_LEN), 0
     )
     halves = [slice(0, SEG_LEN), slice(SEG_LEN, 2 * SEG_LEN)]
-    own_values = [with_ones(value_ref[half]) for half in halves]
-    for head in range(heads):
-        at = (first_head + head) * HEAD_DIM
-        query = query_ref[:, at : at + HEAD_DIM]
-        path_scores = scores_of(jnp.concatenate([query, marks], axis=1), path_keys)
+
+    def attend_head(query):
+        path_scores = scores_of(jnp.concatenate([query, marks], axis=1), path_key_ref[...])
+        own_values = [with_ones(value_ref[half]) for half in halves]
         own = [
             [(jnp.where(causal, scores_of(query[half], key_ref[half]), MASKED), values)]
             for half, values in zip(halves, own_values)
@@ -236,32 +243,27 @@
                 )
             )
         total = jnp.dot(
-            jnp.concatenate(path_weights, axis=0), path_values, preferred_element_type=jnp.float32
+            jnp.concatenate(path_weights, axis=0),
+            path_value_ref[...],
+            preferred_element_type=jnp.float32,
         ) + jnp.concatenate(own_parts, axis=0)
-        mixture = total[:, :HEAD_DIM] / total[:, HEAD_DIM:]
-        out_ref[:, head * HEAD_DIM : (head + 1) * HEAD_DIM] = mixture.astype(out_ref.dtype)
-
-
-def attend(first, parents, queries, keys, values, far, first_head, heads, after):
-    rows = queries.shape[0]
-    key_count = PATH + SEG_LEN + SEG_LEN // 2
-    return pl.pallas_call(
-        functools.partial(attend_kernel, first_head, heads),
-        out_shape=jax.ShapeDtypeStruct((rows, heads * HEAD_DIM), jnp.bfloat16),
-        in_specs=[SMEM, SMEM] + [VMEM] * 4 + [ANY] * len(after),
-        out_specs=VMEM,
-        scratch_shapes=[pltpu.VMEM((PATH, 2 * HEAD_DIM), jnp.bfloat16)] * 2,
-        compiler_params=pltpu.CompilerParams(vmem_limit_bytes=ATTEND_VMEM),
-        cost_estimate=pl.CostEstimate(
-            flops=heads * rows * key_count * HEAD_DIM * 10,
-            bytes_accessed=heads * rows * HEAD_DIM * 4 + 8 * PATH * HEAD_DIM,
-            transcendentals=heads * rows * key_count,
-        ),
-        name="attend",
-    )(first, parents, queries, keys, values, far, *after)
-
-
-def hold_kernel(me_ref, weight_ref, held_ref, sem):
+        return (total[:, :HEAD_DIM] / total[:, HEAD_DIM:]).astype(out_ref.dtype)
+
+    if bring:
+        ready.wait()
+
+    @pl.loop(0, query_ref.shape[1] // (TOGETHER * HEAD_DIM))
+    def _(turn):
+        for head in range(TOGETHER):
+            at = pl.multiple_of((turn * TOGETHER + head) * HEAD_DIM, HEAD_DIM)
+            out_ref[:, pl.ds(at, HEAD_DIM)] = attend_head(query_ref[:, pl.ds(at, HEAD_DIM)])
+
+    if bring:
+        for copy in copies:
+            copy.wait()
+
+
+def weight_copies(me_ref, weight_ref, held_ref, sem):
     block = weight_ref.shape[0] // 4
     copies = []
     for bit in range(4):
@@ -271,97 +273,72 @@
                 weight_ref.at[rows], held_ref.at[pl.ds(bit * block, block)], sem.at[bit]
             )
         )
-    for copy in copies:
-        copy.start()
-    for copy in copies:
-        copy.wait()
-
-
-def hold(me, weight):
-    return pl.pallas_call(
-        hold_kernel,
-        out_shape=pltpu.VMEM(weight.shape, weight.dtype),
-        in_specs=[SMEM, HBM],
-        out_specs=VMEM,
-        scratch_shapes=[pltpu.SemaphoreType.DMA((4,))],
-        compiler_params=pltpu.CompilerParams(vmem_limit_bytes=HOLD_VMEM),
-        cost_estimate=pl.CostEstimate(flops=0, bytes_accessed=4 * weight.size, transcendentals=0),
-        name="hold",
-    )(me, in_hbm(weight))
-
-
-def near_kernel(counts, weight_ref, *refs):
-    count = sum(counts)
-    parts, (out_ref, held_ref) = refs[:count], refs[count:]
-    block = weight_ref.shape[0] // 4
-    at = 0
-    for part in parts:
-        held_ref[:, at : at + part.shape[1]] = part[...]
-        at += part.shape[1]
-    split = sum(part.shape[1] for part in parts[: -counts[-1]])
+    return copies
+
+
+def attend(first, parents, queries, pair, far, bring):
+    rows, width = queries.shape
+    out_shape = [jax.ShapeDtypeStruct((rows, width), jnp.bfloat16)]
+    in_specs = [SMEM, SMEM, HBM if bring else VMEM, VMEM, VMEM]
+    scratch = [pltpu.VMEM((PATH, 2 * HEAD_DIM), jnp.bfloat16)] * 2
+    if bring:
+        weight = bring[1]
+        bring = [bring[0], in_hbm(weight)]
+        queries = in_hbm(queries)
+        in_specs += [SMEM, HBM]
+        out_shape.append(pltpu.VMEM(weight.shape, weight.dtype))
+        scratch.append(pltpu.VMEM(queries.shape, queries.dtype))
+        scratch.append(pltpu.SemaphoreType.DMA((5,)))
+    pairs = rows * (PATH + SEG_LEN + SEG_LEN // 2) * width // HEAD_DIM
+    return pl.pallas_call(
+        attend_kernel,
+        out_shape=out_shape,
+        in_specs=in_specs,
+        out_specs=[VMEM] * len(out_shape),
+        scratch_shapes=scratch,
+        compiler_params=pltpu.CompilerParams(vmem_limit_bytes=ATTEND_VMEM),
+        cost_estimate=pl.CostEstimate(
+            flops=pairs * HEAD_DIM * 10,
+            bytes_accessed=rows * width * 4 + 8 * PATH * HEAD_DIM,
+            transcendentals=pairs,
+        ),
+        name="attend",
+    )(first, parents, queries, pair, far, *bring)
+
+
+def project_kernel(spans, has_base, weight_ref, *refs):
+    parts, out_ref = refs[: len(spans)], refs[-1]
     for column in range(0, out_ref.shape[1], TILE):
         columns = slice(column, column + TILE)
-        out_ref[:, columns] = jnp.dot(
-            held_ref[:, :split], weight_ref[:split, columns], preferred_element_type=jnp.float32
-        ) + jnp.dot(
-            held_ref[:, split:],
-            weight_ref[3 * block : 3 * block + at - split, columns],
-            preferred_element_type=jnp.float32,
-        )
-
-
-def near_project(groups, weight):
-    parts = [part for group in groups for part in group]
+        total = refs[len(spans)][:, columns] if has_base else None
+        for start, part_ref in zip(spans, parts):
+            product = jnp.dot(
+                part_ref[...],
+                weight_ref[start : start + part_ref.shape[1], columns],
+                preferred_element_type=jnp.float32,
+            )
+            total = product if total is None else total + product
+        out_ref[:, columns] = total.astype(out_ref.dtype)
+
+
+def project(parts, spans, weight, base, dtype):
     rows = parts[0].shape[0]
     depth = sum(part.shape[1] for part in parts)
     width = weight.shape[1]
-    return pl.pallas_call(
-        functools.partial(near_kernel, [len(group) for group in groups]),
-        out_shape=jax.ShapeDtypeStruct((rows, width), jnp.float32),
-        in_specs=[VMEM] * (1 + len(parts)),
+    bases = [] if base is None else [base]
+    return pl.pallas_call(
+        functools.partial(project_kernel, spans, base is not None),
+        out_shape=jax.ShapeDtypeStruct((rows, width), dtype),
+        in_specs=[VMEM] * (1 + len(parts) + len(bases)),
         out_specs=VMEM,
-        scratch_shapes=[pltpu.VMEM((rows, depth), weight.dtype)],
         compiler_params=pltpu.CompilerParams(vmem_limit_bytes=PROJECT_VMEM),
         cost_estimate=pl.CostEstimate(
-            flops=rows * depth * width // 4,
+            flops=2 * rows * depth * width,
             bytes_accessed=2 * depth * rows,
             transcendentals=0,
         ),
-        name="near_project",
-    )(in_vmem(weight), *parts)
-
-
-def last_kernel(across_ref, corner_ref, weight_ref, base_ref, out_ref):
-    depth = across_ref.shape[1]
-    block = weight_ref.shape[0] // 4
-    for column in range(0, out_ref.shape[1], TILE):
-        columns = slice(column, column + TILE)
-        total = base_ref[:, columns]
-        for end, part_ref in [(3 * block, across_ref), (4 * block, corner_ref)]:
-            total = total + jnp.dot(
-                part_ref[...],
-                weight_ref[end - depth : end, columns],
-                preferred_element_type=jnp.float32,
-            )
-        out_ref[:, columns] = total.astype(out_ref.dtype)
-
-
-def last_project(across, corner, weight, base):
-    rows, depth = across.shape
-    width = weight.shape[1]
-    return pl.pallas_call(
-        last_kernel,
-        out_shape=jax.ShapeDtypeStruct((rows, width), jnp.bfloat16),
-        in_specs=[VMEM] * 4,
-        out_specs=VMEM,
-        compiler_params=pltpu.CompilerParams(vmem_limit_bytes=LAST_VMEM),
-        cost_estimate=pl.CostEstimate(
-            flops=4 * rows * depth * width,
-            bytes_accessed=4 * depth * (rows + width) + 6 * rows * width,
-            transcendentals=0,
-        ),
-        name="last_project",
-    )(across, corner, in_vmem(weight), base)
+        name="project",
+    )(in_vmem(weight), *parts, *bases)
 
 
 def swap(part, bit):
@@ -381,28 +358,28 @@
 
 
 def per_device(queries, key_proj, value_proj, out_weight, parents):
-    me = lax.axis_index("tensor")
+    me = lax.axis_index("tensor").astype(jnp.int32).reshape(1)
     first = (lax.axis_index("dp") * 2).astype(jnp.int32).reshape(1)
-    pieces = trade(pack(key_proj, value_proj)).reshape(ROW_SEGS, 2 * PIECE, HEAD_DIM)
-    weight = hold(me.astype(jnp.int32).reshape(1), out_weight)
-    to_next, to_second = carry_out(first, parents, pieces, weight)
+    packed, pair = pack(key_proj, value_proj)
+    other_pair = swap(pair, 2)
+    pieces = trade(packed).reshape(ROW_SEGS, 2 * PIECE, HEAD_DIM)
+    pieces, other_pair = lax.optimization_barrier((pieces, other_pair))
+    to_next, to_second = carry_out(first, parents, pieces)
+    other_queries = swap(queries, 2)
     inside = pick(first, parents, pieces)
     far = trade(merge(*inside, onward(to_next, ROW), onward(to_second, 2 * ROW)))
-
-    sizes = [1, 2, 2, 3]
-    own, across, head = [], [], 0
-    for c, size in enumerate(sizes):
-        after = [across[c - 2]] if c >= 2 else []
-        own.append(
-            attend(first, parents, queries, key_proj, value_proj, far, head, size, after)
-        )
-        across.append(swap(own[c], 2))
-        head += size
-    beside = [swap(part, 1) for part in own]
-    corner = [swap(part, 1) for part in across[:-1]]
-    near = near_project([own, beside, across[:-1], corner], weight)
-    last, near = lax.optimization_barrier((across[-1], near))
-    return last_project(last, swap(last, 1), weight, near)
+    far, other_queries = lax.optimization_barrier((far, other_queries))
+
+    other_far = swap(far, 2)
+    own, weight = attend(first, parents, queries, pair, far, [me, out_weight])
+    beside = swap(own, 1)
+    width = queries.shape[1]
+    total = project([own], [0], weight, None, jnp.float32)
+    other_far, total = lax.optimization_barrier((other_far, total))
+    [across] = attend(first, parents, other_queries, other_pair, other_far, [])
+    corner = swap(across, 1)
+    total = project([beside, across], [width, 2 * width], weight, total, jnp.float32)
+    return project([corner], [3 * width], weight, total, jnp.bfloat16)
 
 
 def solution(mesh):

time: 90.2 us -> 103 us (1.14)
  waiting for transfers between devices: 9.96 us -> 41.9 us
  blocking collectives: 18.3 us -> 0 us
  local copies, waits for them, and re-layouts: 8.01 us -> 0.66 us
  Pallas kernels: 27.9 us -> 34.2 us
    all_to_all x1 -> x0, blocking collectives: 18.3 us -> none  [trade(): lax.all_to_all(pieces, 'dp', 0, 0, tiled=True, axis_index_groups=rows)]
    all_to_all x1 -> x2, waiting for transfers between devices: 2.13 us -> 18 us  [trade(): lax.all_to_all(pieces, 'dp', 0, 0, tiled=True, axis_index_groups=rows)]
    ppermute x2, waiting for transfers between devices: 2.98 us -> 18.6 us  [onward(): lax.ppermute(piece, 'dp', [(i, (i + step) % devices) for i in range(devic...]
    unnamed x18 -> x4, local copies, waits for them, and re-layouts: 8.01 us -> 0.66 us
    ppermute x12 -> x5, starting transfers between devices: 12.6 us -> 6.02 us  [swap(): return lax.ppermute(part, 'tensor', [(i, i ^ bit) for i in range(size)])]
    all_to_all x1 -> x2, starting transfers between devices: 9.03 us -> 15.4 us  [trade(): lax.all_to_all(pieces, 'dp', 0, 0, tiled=True, axis_index_groups=rows)]
    pallas_call x8 -> x6, Pallas kernels: 26.3 us -> 31.8 us  [the longest x2 23 us: attend(): pl.pallas_call(attend_kernel, out_shape=out_shape, in_specs=in_specs, out...]
    ppermute x12 -> x5, waiting for transfers between devices: 4.85 us -> 5.4 us  [swap(): return lax.ppermute(part, 'tensor', [(i, i ^ bit) for i in range(size)])]
  transfers between devices with their start and end apart: 15 -> 9, of which waited for: 7 -> 5; matrix products, arithmetic and copies ran while one was open for 0% -> 0% of each run, Pallas kernels for 23% -> 29%
where the time goes in v5:
time: 103 us; the launch traced here: 102 us
  waiting for transfers between devices  41.9 us (41%)
  Pallas kernels  34.2 us (33%)
  starting transfers between devices  25.4 us (25%)
    pallas_call x2, Pallas kernels, attend(): pl.pallas_call(attend_kernel, out_shape=out_shape, in_specs=in_specs, out...  23 us
    ppermute x2, waiting for transfers between devices, onward(): lax.ppermute(piece, 'dp', [(i, (i + step) % devices) for i in range(devic...  18.6 us
    all_to_all x2, waiting for transfers between devices, trade(): lax.all_to_all(pieces, 'dp', 0, 0, tiled=True, axis_index_groups=rows)  18 us
    all_to_all x2, starting transfers between devices, trade(): lax.all_to_all(pieces, 'dp', 0, 0, tiled=True, axis_index_groups=rows)  15.4 us
    pallas_call x3, Pallas kernels, project(): pl.pallas_call(functools.partial(project_kernel, spans, base is not None)...  7.07 us
    ppermute x5, starting transfers between devices, swap(): return lax.ppermute(part, 'tensor', [(i, i ^ bit) for i in range(size)])  6.02 us
    ppermute x5, waiting for transfers between devices, swap(): return lax.ppermute(part, 'tensor', [(i, i ^ bit) for i in range(size)])  5.4 us
    ppermute x2, starting transfers between devices, onward(): lax.ppermute(piece, 'dp', [(i, (i + step) % devices) for i in range(devic...  3.99 us
  transfers between devices with their start and end apart: 9, of which 5 were waited for; matrix products, arithmetic and copies ran while one was open for 0% of the time, Pallas kernels for 29%

profile of v5, /device:TPU:1, one launch (start us, length us, event | category | flops | bytes accessed | tf_op | source)
XLA Modules:
  0.0 102.3 jit_solution(11618855871837208022)
XLA Ops:
  0.0 0.0 copy-start.1
  0.0 1.7 %pack.1 = (bf16[8,2,64,128]{3,2,1,0:T(8,128)(2,1)}, bf16[2,512,128]{2,1,0:T(8,128)(2,1)S(1)}) custom-call(bf16[512,128]{1,0:T(8,128)(2,1)} %key_ref.1, bf16[512,128]{1,0:T(8,128)(2,1)} %value_ref.1), custom_call_target="tpu_custom_call" | custom-call | bytes 524288 | tf_op jit(solution)/shard_map/pack/pallas_call | solution.py:73
  1.7 9.0 %all-to-all-start = ((bf16[8,2,64,128]{3,2,1,0:T(8,128)(2,1)}), bf16[8,2,64,128]{3,2,1,0:T(8,128)(2,1)S(1)}, u32[]{:S(2)}, u32[]{:S(2)}) async-start(bf16[8,2,64,128]{3,2,1,0:T(8,128)(2,1)} %get-tuple-element.21), calls=%async_computation | async-start | bytes 524288 | tf_op jit(solution)/shard_map/all_to_all | solution.py:352
  10.7 1.2 %collective-permute-start = (bf16[2,512,128]{2,1,0:T(8,128)(2,1)S(1)}, bf16[2,512,128]{2,1,0:T(8,128)(2,1)S(1)}, u32[]{:S(2)}, u32[]{:S(2)}) collective-permute-start(bf16[2,512,128]{2,1,0:T(8,128)(2,1)S(1)} %get-tuple-element.20.pair_ref), channel_id=1, source_target_pairs={{0,2},{1,3},{2,0},{3,1},{4,6},{5,7},{6,4},{7,5},{8,10},{9,11},{10,... | collective-permute-start | bytes 786440 | tf_op jit(solution)/shard_map/ppermute | solution.py:346
  12.0 0.3 collective-permute-start.3
  12.2 5.4 %collective-permute-done.pair_ref = bf16[2,512,128]{2,1,0:T(8,128)(2,1)S(1)} collective-permute-done((bf16[2,512,128]{2,1,0:T(8,128)(2,1)S(1)}, bf16[2,512,128]{2,1,0:T(8,128)(2,1)S(1)}, u32[]{:S(2)}, u32[]{:S(2)}) %collective-permute-start) | collective-permute-done | bytes 262176 | tf_op jit(solution)/shard_map/ppermute | solution.py:346
  17.6 3.5 %all-to-all-done = bf16[8,2,64,128]{3,2,1,0:T(8,128)(2,1)S(1)} async-done(((bf16[8,2,64,128]{3,2,1,0:T(8,128)(2,1)}), bf16[8,2,64,128]{3,2,1,0:T(8,128)(2,1)S(1)}, u32[]{:S(2)}, u32[]{:S(2)}) %all-to-all-start) | async-done | bytes 262176 | tf_op jit(solution)/shard_map/all_to_all | solution.py:352
  21.1 0.0 copy-start
  21.1 0.7 copy-done
  21.8 0.6 carry_out.1
  22.4 1.4 %collective-permute-start.1 = (bf16[4,64,128]{2,1,0:T(8,128)(2,1)S(1)}, bf16[4,64,128]{2,1,0:T(8,128)(2,1)S(1)}, u32[]{:S(2)}, u32[]{:S(2)}) collective-permute-start(bf16[4,64,128]{2,1,0:T(8,128)(2,1)S(1)} %get-tuple-element.26), channel_id=1, source_target_pairs={{0,32},{4,36},{8,40},{12,44},{16,48},{20,52},{24,56},{28,60},{32,6... | collective-permute-start | bytes 196616 | tf_op jit(solution)/shard_map/ppermute | solution.py:357
  23.8 2.6 %collective-permute-start.2 = (bf16[1,64,128]{2,1,0:T(8,128)(2,1)S(1)}, bf16[1,64,128]{2,1,0:T(8,128)(2,1)S(1)}, u32[]{:S(2)}, u32[]{:S(2)}) collective-permute-start(bf16[1,64,128]{2,1,0:T(8,128)(2,1)S(1)} %get-tuple-element.27), channel_id=1, source_target_pairs={{0,64},{4,68},{8,72},{12,76},{16,80},{20,84},{24,88},{28,92},{32,9... | collective-permute-start | bytes 49160 | tf_op jit(solution)/shard_map/ppermute | solution.py:357
  26.4 0.9 pick.1
  27.3 17.7 %collective-permute-done.2.second_ref = bf16[1,64,128]{2,1,0:T(8,128)(2,1)S(1)} collective-permute-done((bf16[1,64,128]{2,1,0:T(8,128)(2,1)S(1)}, bf16[1,64,128]{2,1,0:T(8,128)(2,1)S(1)}, u32[]{:S(2)}, u32[]{:S(2)}) %collective-permute-start.2) | collective-permute-done | bytes 16416 | tf_op jit(solution)/shard_map/ppermute | solution.py:357
  45.0 0.9 collective-permute-done.1.next_ref
  45.8 0.9 merge.1
  46.7 6.4 %all-to-all-start.1 = ((bf16[8,4,64,128]{3,2,1,0:T(8,128)(2,1)}), bf16[8,4,64,128]{3,2,1,0:T(8,128)(2,1)S(1)}, u32[]{:S(2)}, u32[]{:S(2)}) async-start(bf16[8,4,64,128]{3,2,1,0:T(8,128)(2,1)} %merge.1), calls=%async_computation.1 | async-start | bytes 1048576 | tf_op jit(solution)/shard_map/all_to_all | solution.py:352
  53.1 0.0 collective-permute-done.3.query_ref
  53.1 14.5 %all-to-all-done.1.far_ref = bf16[8,4,64,128]{3,2,1,0:T(8,128)(2,1)S(1)} async-done(((bf16[8,4,64,128]{3,2,1,0:T(8,128)(2,1)}), bf16[8,4,64,128]{3,2,1,0:T(8,128)(2,1)S(1)}, u32[]{:S(2)}, u32[]{:S(2)}) %all-to-all-start.1) | async-done | bytes 524320 | tf_op jit(solution)/shard_map/all_to_all | solution.py:352
  67.6 0.0 collective-permute-start.4
  67.6 0.0 copy-done.1
  67.6 12.0 %attend.2 = (bf16[512,1024]{1,0:T(8,128)(2,1)S(1)}, bf16[4096,1280]{1,0:T(8,128)(2,1)S(1)}) custom-call(s32[1]{0:T(128)} %bitcast.first_ref, s32[128]{0:T(128)S(1)} %copy-done.1, bf16[512,1024]{1,0:T(8,128)(2,1)} %query_ref.1, bf16[2,512,128]{2,1,0:T(8,128)(2,1)S(1)} %get-tuple-element.20.pair_ref, bf16[8,4,64,128]{3,2,1,0:T(8,128)(2,1)S(1)} %all-to-all-done.1.far_ref, ...), custom_call_target="tpu_custom_call" | custom-call | flops 7381975040 | bytes 3145728 | tf_op jit(solution)/shard_map/attend/pallas_call | solution.py:293
  79.6 4.3 %collective-permute-start.6 = (bf16[512,1024]{1,0:T(8,128)(2,1)S(1)}, bf16[512,1024]{1,0:T(8,128)(2,1)S(1)}, u32[]{:S(2)}, u32[]{:S(2)}) collective-permute-start(bf16[512,1024]{1,0:T(8,128)(2,1)S(1)} %get-tuple-element.32.refs_0_), channel_id=1, source_target_pairs={{0,1},{1,0},{2,3},{3,2},{4,5},{5,4},{6,7},{7,6},{8,9},{9,8},{10,11... | collective-permute-start | bytes 3145736 | tf_op jit(solution)/shard_map/ppermute | solution.py:346
  83.9 1.5 %project.3.refs_2_ = f32[512,1280]{1,0:T(8,128)S(1)} custom-call(bf16[4096,1280]{1,0:T(8,128)(2,1)S(1)} %get-tuple-element.29.weight_ref, bf16[512,1024]{1,0:T(8,128)(2,1)S(1)} %get-tuple-element.32.refs_0_), custom_call_target="tpu_custom_call" | custom-call | flops 1342177280 | bytes 1048576 | tf_op jit(solution)/shard_map/project/pallas_call | solution.py:329
  85.4 0.0 collective-permute-done.4.far_ref
  85.4 11.0 %attend.3.refs_1_ = bf16[512,1024]{1,0:T(8,128)(2,1)S(1)} custom-call(s32[1]{0:T(128)} %bitcast.first_ref, s32[128]{0:T(128)S(1)} %copy-done.1, bf16[512,1024]{1,0:T(8,128)(2,1)S(1)} %collective-permute-done.3.query_ref, bf16[2,512,128]{2,1,0:T(8,128)(2,1)S(1)} %collective-permute-done.pair_ref, bf16[8,4,64,128]{3,2,1,0:T(8,128)(2,1)S(1)} %collective-permute-done.4.far_ref), custom_call_target="tpu_custom_call" | custom-call | flops 7381975040 | bytes 3145728 | tf_op jit(solution)/shard_map/attend/pallas_call | solution.py:293
  96.4 0.3 collective-permute-start.5
  96.7 0.0 collective-permute-done.6.refs_0_
  96.7 2.9 %project.4.refs_1_ = f32[512,1280]{1,0:T(8,128)S(1)} custom-call(bf16[4096,1280]{1,0:T(8,128)(2,1)S(1)} %get-tuple-element.29.weight_ref, bf16[512,1024]{1,0:T(8,128)(2,1)S(1)} %collective-permute-done.6.refs_0_, bf16[512,1024]{1,0:T(8,128)(2,1)S(1)} %attend.3.refs_1_, f32[512,1280]{1,0:T(8,128)S(1)} %project.3.refs_2_), custom_call_target="tpu_custom_call" | custom-call | flops 2684354560 | bytes 2097152 | tf_op jit(solution)/shard_map/project/pallas_call | solution.py:329
  99.6 0.0 collective-permute-done.5.refs_0_
  99.6 2.6 %project.5 = bf16[512,1280]{1,0:T(8,128)(2,1)} custom-call(bf16[4096,1280]{1,0:T(8,128)(2,1)S(1)} %get-tuple-element.29.weight_ref, bf16[512,1024]{1,0:T(8,128)(2,1)S(1)} %collective-permute-done.5.refs_0_, f32[512,1280]{1,0:T(8,128)S(1)} %project.4.refs_1_), custom_call_target="tpu_custom_call" | custom-call | flops 1342177280 | bytes 1048576 | tf_op jit(solution)/shard_map/project/pallas_call | solution.py:329
Async XLA Ops:
  0.0 67.6 %copy-start.1 = (s32[128]{0:T(128)S(1)}, s32[128]{0:T(128)}, u32[]{:S(2)}) copy-start(s32[128]{0:T(128)} %parents_ref.7) | copy-start | bytes 1540
  1.7 19.4 %all-to-all-start = ((bf16[8,2,64,128]{3,2,1,0:T(8,128)(2,1)}), bf16[8,2,64,128]{3,2,1,0:T(8,128)(2,1)S(1)}, u32[]{:S(2)}, u32[]{:S(2)}) async-start(bf16[8,2,64,128]{3,2,1,0:T(8,128)(2,1)} %get-tuple-element.21), calls=%async_computation | async-start | bytes 524288 | tf_op jit(solution)/shard_map/all_to_all | solution.py:352
  10.7 6.9 %collective-permute-start = (bf16[2,512,128]{2,1,0:T(8,128)(2,1)S(1)}, bf16[2,512,128]{2,1,0:T(8,128)(2,1)S(1)}, u32[]{:S(2)}, u32[]{:S(2)}) collective-permute-start(bf16[2,512,128]{2,1,0:T(8,128)(2,1)S(1)} %get-tuple-element.20.pair_ref), channel_id=1, source_target_pairs={{0,2},{1,3},{2,0},{3,1},{4,6},{5,7},{6,4},{7,5},{8,10},{9,11},{10,... | collective-permute-start | bytes 786440 | tf_op jit(solution)/shard_map/ppermute | solution.py:346
  12.0 41.1 %collective-permute-start.3 = (bf16[512,1024]{1,0:T(8,128)(2,1)}, bf16[512,1024]{1,0:T(8,128)(2,1)S(1)}, u32[]{:S(2)}, u32[]{:S(2)}) collective-permute-start(bf16[512,1024]{1,0:T(8,128)(2,1)} %query_ref.1), channel_id=1, source_target_pairs={{0,2},{1,3},{2,0},{3,1},{4,6},{5,7},{6,4},{7,5},{8,10},{9,11},{10,... | collective-permute-start | bytes 3145736 | tf_op jit(solution)/shard_map/ppermute | solution.py:346
  21.1 0.7 copy-start
  22.4 23.4 %collective-permute-start.1 = (bf16[4,64,128]{2,1,0:T(8,128)(2,1)S(1)}, bf16[4,64,128]{2,1,0:T(8,128)(2,1)S(1)}, u32[]{:S(2)}, u32[]{:S(2)}) collective-permute-start(bf16[4,64,128]{2,1,0:T(8,128)(2,1)S(1)} %get-tuple-element.26), channel_id=1, source_target_pairs={{0,32},{4,36},{8,40},{12,44},{16,48},{20,52},{24,56},{28,60},{32,6... | collective-permute-start | bytes 196616 | tf_op jit(solution)/shard_map/ppermute | solution.py:357
  23.8 21.2 %collective-permute-start.2 = (bf16[1,64,128]{2,1,0:T(8,128)(2,1)S(1)}, bf16[1,64,128]{2,1,0:T(8,128)(2,1)S(1)}, u32[]{:S(2)}, u32[]{:S(2)}) collective-permute-start(bf16[1,64,128]{2,1,0:T(8,128)(2,1)S(1)} %get-tuple-element.27), channel_id=1, source_target_pairs={{0,64},{4,68},{8,72},{12,76},{16,80},{20,84},{24,88},{28,92},{32,9... | collective-permute-start | bytes 49160 | tf_op jit(solution)/shard_map/ppermute | solution.py:357
  46.7 20.8 %all-to-all-start.1 = ((bf16[8,4,64,128]{3,2,1,0:T(8,128)(2,1)}), bf16[8,4,64,128]{3,2,1,0:T(8,128)(2,1)S(1)}, u32[]{:S(2)}, u32[]{:S(2)}) async-start(bf16[8,4,64,128]{3,2,1,0:T(8,128)(2,1)} %merge.1), calls=%async_computation.1 | async-start | bytes 1048576 | tf_op jit(solution)/shard_map/all_to_all | solution.py:352
  67.6 17.8 %collective-permute-start.4 = (bf16[8,4,64,128]{3,2,1,0:T(8,128)(2,1)S(1)}, bf16[8,4,64,128]{3,2,1,0:T(8,128)(2,1)S(1)}, u32[]{:S(2)}, u32[]{:S(2)}) collective-permute-start(bf16[8,4,64,128]{3,2,1,0:T(8,128)(2,1)S(1)} %all-to-all-done.1.far_ref), channel_id=1, source_target_pairs={{0,2},{1,3},{2,0},{3,1},{4,6},{5,7},{6,4},{7,5},{8,10},{9,11},{10,... | collective-permute-start | bytes 1572872 | tf_op jit(solution)/shard_map/ppermute | solution.py:346
  79.6 17.1 %collective-permute-start.6 = (bf16[512,1024]{1,0:T(8,128)(2,1)S(1)}, bf16[512,1024]{1,0:T(8,128)(2,1)S(1)}, u32[]{:S(2)}, u32[]{:S(2)}) collective-permute-start(bf16[512,1024]{1,0:T(8,128)(2,1)S(1)} %get-tuple-element.32.refs_0_), channel_id=1, source_target_pairs={{0,1},{1,0},{2,3},{3,2},{4,5},{5,4},{6,7},{7,6},{8,9},{9,8},{10,11... | collective-permute-start | bytes 3145736 | tf_op jit(solution)/shard_map/ppermute | solution.py:346
  96.4 3.2 %collective-permute-start.5 = (bf16[512,1024]{1,0:T(8,128)(2,1)S(1)}, bf16[512,1024]{1,0:T(8,128)(2,1)S(1)}, u32[]{:S(2)}, u32[]{:S(2)}) collective-permute-start(bf16[512,1024]{1,0:T(8,128)(2,1)S(1)} %attend.3.refs_1_), channel_id=1, source_target_pairs={{0,1},{1,0},{2,3},{3,2},{4,5},{5,4},{6,7},{7,6},{8,9},{9,8},{10,11... | collective-permute-start | bytes 3145736 | tf_op jit(solution)/shard_map/ppermute | solution.py:346

commit v6 on v5

--- a/solution.py
+++ b/solution.py
@@ -22,10 +22,10 @@
 ATTEND_VMEM = 18 * 1024 * 1024
 PROJECT_VMEM = 14 * 1024 * 1024
 TILE = 256
-TOGETHER = 2
 
 VMEM = pl.BlockSpec(memory_space=pltpu.VMEM)
 SMEM = pl.BlockSpec(memory_space=pltpu.SMEM)
+ANY = pl.BlockSpec(memory_space=pl.ANY)
 HBM = pl.BlockSpec(memory_space=pltpu.HBM)
 FLAG_ROWS = 16
 
@@ -72,13 +72,10 @@
 def pack(keys, values):
     return pl.pallas_call(
         pack_kernel,
-        out_shape=(
-            jax.ShapeDtypeStruct((ROW, 2, 2 * PIECE, HEAD_DIM), keys.dtype),
-            jax.ShapeDtypeStruct((2,) + keys.shape, keys.dtype),
-        ),
+        out_shape=jax.ShapeDtypeStruct((ROW, 2, 2 * PIECE, HEAD_DIM), keys.dtype),
         in_specs=[HBM, HBM],
-        out_specs=(VMEM, VMEM),
-        scratch_shapes=[pltpu.SemaphoreType.DMA((2,))],
+        out_specs=VMEM,
+        scratch_shapes=[pltpu.VMEM((2,) + keys.shape, keys.dtype), pltpu.SemaphoreType.DMA((2,))],
         compiler_params=pltpu.CompilerParams(vmem_limit_bytes=SMALL_VMEM),
         cost_estimate=pl.CostEstimate(flops=0, bytes_accessed=1 << 19, transcendentals=0),
         name="pack",
@@ -89,12 +86,23 @@
     return (first_ref[0] // ROW_SEGS) * ROW_SEGS
 
 
-def carry_kernel(first_ref, parents_ref, pieces_ref, next_ref, second_ref):
+def slot_of(seg):
+    return seg ^ (ROW_SEGS - 2)
+
+
+def bring_parents(source_ref, parents_ref, sem):
+    copy = pltpu.make_async_copy(source_ref, parents_ref, sem)
+    copy.start()
+    copy.wait()
+
+
+def carry_kernel(first_ref, source_ref, pieces_ref, next_ref, second_ref, parents_ref, sem):
+    bring_parents(source_ref, parents_ref, sem)
     base = row_start(first_ref)
     last = parents_ref.shape[0] - 1
 
     def held(path, depth, level):
-        return pieces_ref[jnp.clip(level_of(path, depth, level) - base, 0, ROW_SEGS - 1)]
+        return pieces_ref[slot_of(jnp.clip(level_of(path, depth, level) - base, 0, ROW_SEGS - 1))]
 
     path, depth = path_of(parents_ref, jnp.minimum(base + ROW_SEGS, last))
     for level in range(LEVELS):
@@ -108,23 +116,27 @@
     return pl.pallas_call(
         carry_kernel,
         out_shape=(shape(LEVELS), shape(1)),
-        in_specs=[SMEM, SMEM, VMEM],
+        in_specs=[SMEM, HBM, VMEM],
         out_specs=(VMEM, VMEM),
+        scratch_shapes=[pltpu.SMEM(parents.shape, parents.dtype), pltpu.SemaphoreType.DMA],
         compiler_params=pltpu.CompilerParams(vmem_limit_bytes=SMALL_VMEM),
         cost_estimate=pl.CostEstimate(flops=0, bytes_accessed=1 << 18, transcendentals=0),
         name="carry_out",
-    )(first, parents, pieces)
-
-
-def pick_kernel(first_ref, parents_ref, pieces_ref, inside_ref, next_ref, second_ref):
+    )(first, in_hbm(parents), pieces)
+
+
+def pick_kernel(
+    first_ref, source_ref, pieces_ref, inside_ref, next_ref, second_ref, parents_ref, sem
+):
+    bring_parents(source_ref, parents_ref, sem)
     base = row_start(first_ref)
     ones = lambda on: jnp.full((FLAG_ROWS, HEAD_DIM), on, jnp.float32).astype(jnp.bfloat16)
     for target in range(ROW):
-        path, depth = path_of(parents_ref, base + 2 * target)
+        path, depth = path_of(parents_ref, base + 2 * (ROW - 1 - target))
         for level in range(LEVELS):
             seg = level_of(path, depth, level)
             within = seg >= base
-            piece = pieces_ref[jnp.maximum(seg - base, 0)]
+            piece = pieces_ref[slot_of(jnp.maximum(seg - base, 0))]
             inside_ref[target, level] = jnp.where(within, piece, jnp.zeros_like(piece))
             before = jnp.logical_and(seg < base, seg >= base - ROW_SEGS)
             next_ref[target, level] = ones(jnp.where(before, 1.0, 0.0))
@@ -141,12 +153,13 @@
             shape(ROW, LEVELS, FLAG_ROWS, HEAD_DIM),
             shape(ROW, FLAG_ROWS, HEAD_DIM),
         ),
-        in_specs=[SMEM, SMEM, VMEM],
+        in_specs=[SMEM, HBM, VMEM],
         out_specs=(VMEM, VMEM, VMEM),
+        scratch_shapes=[pltpu.SMEM(parents.shape, parents.dtype), pltpu.SemaphoreType.DMA],
         compiler_params=pltpu.CompilerParams(vmem_limit_bytes=SMALL_VMEM),
         cost_estimate=pl.CostEstimate(flops=0, bytes_accessed=1 << 20, transcendentals=0),
         name="pick",
-    )(first, parents, pieces)
+    )(first, in_hbm(parents), pieces)
 
 
 def merge_kernel(inside_ref, on_next_ref, on_second_ref, next_ref, second_ref, picked_ref):
@@ -174,22 +187,23 @@
     )(inside, on_next, on_second, carried, second)
 
 
-def attend_kernel(first_ref, parents_ref, query_ref, pair_ref, far_ref, *refs):
-    key_ref, value_ref = pair_ref.at[0], pair_ref.at[1]
-    bring = len(refs) > 3
+def attend_kernel(first_head, bring, first_ref, *refs):
+    sources, (far_ref, *refs) = refs[:4], refs[4:]
     if bring:
-        me_ref, weight_ref, out_ref, held_ref, path_key_ref, path_value_ref, near_ref, sem = refs
-        ready = pltpu.make_async_copy(query_ref, near_ref, sem.at[4])
-        copies = weight_copies(me_ref, weight_ref, held_ref, sem)
-        for copy in [ready] + copies:
-            copy.start()
-        query_ref = near_ref
-    else:
-        out_ref, path_key_ref, path_value_ref = refs
-    first = first_ref[0]
-    _, depth0 = path_of(parents_ref, first)
-    _, depth1 = path_of(parents_ref, first + 1)
-    follows = jnp.where(parents_ref[first + 1] == first, 0.0, MASKED)
+        me_ref, weight_ref = refs[:2]
+        weight_sem = refs.pop()
+        held_ref = refs.pop(-8)
+    out_ref, path_key_ref, path_value_ref, parents_ref, query_ref, key_ref, value_ref, sem = refs[-8:]
+    heads = query_ref.shape[1] // HEAD_DIM
+    columns = pl.ds(first_head * HEAD_DIM, query_ref.shape[1])
+    views = [sources[0], sources[1].at[:, columns], sources[2], sources[3]]
+    fetches = [
+        pltpu.make_async_copy(view, target, sem.at[i])
+        for i, (view, target) in enumerate(zip(views, [parents_ref, query_ref, key_ref, value_ref]))
+    ]
+    copies = weight_copies(me_ref, weight_ref, held_ref, weight_sem) if bring else []
+    for copy in fetches + copies:
+        copy.start()
 
     def scores_of(query, keys):
         return lax.dot_general(
@@ -205,11 +219,18 @@
             path_key_ref[rows, :HEAD_DIM] = far_ref[piece, level, :PIECE]
             path_value_ref[rows, :HEAD_DIM] = far_ref[piece, level, PIECE:]
     path_value_ref[:, HEAD_DIM:] = jnp.ones((PATH, HEAD_DIM), jnp.bfloat16)
+    for copy in fetches:
+        copy.wait()
+    first = first_ref[0]
+    _, depth0 = path_of(parents_ref, first)
+    _, depth1 = path_of(parents_ref, first + 1)
+    follows = jnp.where(parents_ref[first + 1] == first, 0.0, MASKED)
     row = lax.broadcasted_iota(jnp.int32, (PATH, HEAD_DIM), 0)
     lane = lax.broadcasted_iota(jnp.int32, (PATH, HEAD_DIM), 1)
     level = lax.rem(row // PIECE, LEVELS)
     limit = jnp.where(lane == 0, depth0, jnp.where(lane == 1, jnp.minimum(depth0, depth1), LEVELS))
     path_key_ref[:, HEAD_DIM:] = jnp.where(level < limit, 0.0, MASKED).astype(jnp.bfloat16)
+    path_keys, path_values = path_key_ref[...], path_value_ref[...]
 
     rows = lax.broadcasted_iota(jnp.int32, (2 * SEG_LEN, HEAD_DIM), 0)
     lanes = lax.broadcasted_iota(jnp.int32, (2 * SEG_LEN, HEAD_DIM), 1)
@@ -218,10 +239,10 @@
         jnp.int32, (SEG_LEN, SEG_LEN), 0
     )
     halves = [slice(0, SEG_LEN), slice(SEG_LEN, 2 * SEG_LEN)]
-
-    def attend_head(query):
-        path_scores = scores_of(jnp.concatenate([query, marks], axis=1), path_key_ref[...])
-        own_values = [with_ones(value_ref[half]) for half in halves]
+    own_values = [with_ones(value_ref[half]) for half in halves]
+    for head in range(heads):
+        query = query_ref[:, head * HEAD_DIM : (head + 1) * HEAD_DIM]
+        path_scores = scores_of(jnp.concatenate([query, marks], axis=1), path_keys)
         own = [
             [(jnp.where(causal, scores_of(query[half], key_ref[half]), MASKED), values)]
             for half, values in zip(halves, own_values)
@@ -243,24 +264,12 @@
                 )
             )
         total = jnp.dot(
-            jnp.concatenate(path_weights, axis=0),
-            path_value_ref[...],
-            preferred_element_type=jnp.float32,
+            jnp.concatenate(path_weights, axis=0), path_values, preferred_element_type=jnp.float32
         ) + jnp.concatenate(own_parts, axis=0)
-        return (total[:, :HEAD_DIM] / total[:, HEAD_DIM:]).astype(out_ref.dtype)
-
-    if bring:
-        ready.wait()
-
-    @pl.loop(0, query_ref.shape[1] // (TOGETHER * HEAD_DIM))
-    def _(turn):
-        for head in range(TOGETHER):
-            at = pl.multiple_of((turn * TOGETHER + head) * HEAD_DIM, HEAD_DIM)
-            out_ref[:, pl.ds(at, HEAD_DIM)] = attend_head(query_ref[:, pl.ds(at, HEAD_DIM)])
-
-    if bring:
-        for copy in copies:
-            copy.wait()
+        mixture = total[:, :HEAD_DIM] / total[:, HEAD_DIM:]
+        out_ref[:, head * HEAD_DIM : (head + 1) * HEAD_DIM] = mixture.astype(out_ref.dtype)
+    for copy in copies:
+        copy.wait()
 
 
 def weight_copies(me_ref, weight_ref, held_ref, sem):
@@ -276,65 +285,88 @@
     return copies
 
 
-def attend(first, parents, queries, pair, far, bring):
-    rows, width = queries.shape
-    out_shape = [jax.ShapeDtypeStruct((rows, width), jnp.bfloat16)]
-    in_specs = [SMEM, SMEM, HBM if bring else VMEM, VMEM, VMEM]
-    scratch = [pltpu.VMEM((PATH, 2 * HEAD_DIM), jnp.bfloat16)] * 2
+def attend(first, parents, queries, keys, values, far, first_head, heads, bring, after):
+    rows = queries.shape[0]
+    pairs = heads * rows * (PATH + SEG_LEN + SEG_LEN // 2)
+    out_shape = [jax.ShapeDtypeStruct((rows, heads * HEAD_DIM), jnp.bfloat16)]
+    in_specs = [SMEM] + [HBM] * 4 + [VMEM]
+    scratch = [pltpu.VMEM((PATH, 2 * HEAD_DIM), jnp.bfloat16)] * 2 + [
+        pltpu.SMEM(parents.shape, parents.dtype),
+        pltpu.VMEM((rows, heads * HEAD_DIM), queries.dtype),
+        pltpu.VMEM(keys.shape, keys.dtype),
+        pltpu.VMEM(values.shape, values.dtype),
+        pltpu.SemaphoreType.DMA((4,)),
+    ]
     if bring:
         weight = bring[1]
         bring = [bring[0], in_hbm(weight)]
-        queries = in_hbm(queries)
         in_specs += [SMEM, HBM]
         out_shape.append(pltpu.VMEM(weight.shape, weight.dtype))
-        scratch.append(pltpu.VMEM(queries.shape, queries.dtype))
-        scratch.append(pltpu.SemaphoreType.DMA((5,)))
-    pairs = rows * (PATH + SEG_LEN + SEG_LEN // 2) * width // HEAD_DIM
-    return pl.pallas_call(
-        attend_kernel,
+        scratch.append(pltpu.SemaphoreType.DMA((4,)))
+    return pl.pallas_call(
+        functools.partial(attend_kernel, first_head, bool(bring)),
         out_shape=out_shape,
-        in_specs=in_specs,
+        in_specs=in_specs + [ANY] * len(after),
         out_specs=[VMEM] * len(out_shape),
         scratch_shapes=scratch,
         compiler_params=pltpu.CompilerParams(vmem_limit_bytes=ATTEND_VMEM),
         cost_estimate=pl.CostEstimate(
             flops=pairs * HEAD_DIM * 10,
-            bytes_accessed=rows * width * 4 + 8 * PATH * HEAD_DIM,
+            bytes_accessed=heads * rows * HEAD_DIM * 4 + 8 * PATH * HEAD_DIM,
             transcendentals=pairs,
         ),
         name="attend",
-    )(first, parents, queries, pair, far, *bring)
-
-
-def project_kernel(spans, has_base, weight_ref, *refs):
-    parts, out_ref = refs[: len(spans)], refs[-1]
+    )(
+        first,
+        in_hbm(parents),
+        in_hbm(queries),
+        in_hbm(keys),
+        in_hbm(values),
+        far,
+        *bring,
+        *after,
+    )
+
+
+def project_kernel(counts, spans, has_base, weight_ref, *refs):
+    parts = refs[: sum(counts)]
+    out_ref, held_ref = refs[-2:]
+    at, ends = 0, [0]
+    for count in counts:
+        for part in parts[:count]:
+            held_ref[:, at : at + part.shape[1]] = part[...]
+            at += part.shape[1]
+        parts = parts[count:]
+        ends.append(at)
     for column in range(0, out_ref.shape[1], TILE):
         columns = slice(column, column + TILE)
-        total = refs[len(spans)][:, columns] if has_base else None
-        for start, part_ref in zip(spans, parts):
+        total = refs[sum(counts)][:, columns] if has_base else None
+        for start, begin, end in zip(spans, ends, ends[1:]):
             product = jnp.dot(
-                part_ref[...],
-                weight_ref[start : start + part_ref.shape[1], columns],
+                held_ref[:, begin:end],
+                weight_ref[start : start + end - begin, columns],
                 preferred_element_type=jnp.float32,
             )
             total = product if total is None else total + product
         out_ref[:, columns] = total.astype(out_ref.dtype)
 
 
-def project(parts, spans, weight, base, dtype):
+def project(groups, spans, weight, base, dtype):
+    parts = [part for group in groups for part in group]
     rows = parts[0].shape[0]
     depth = sum(part.shape[1] for part in parts)
     width = weight.shape[1]
     bases = [] if base is None else [base]
     return pl.pallas_call(
-        functools.partial(project_kernel, spans, base is not None),
+        functools.partial(project_kernel, [len(g) for g in groups], spans, base is not None),
         out_shape=jax.ShapeDtypeStruct((rows, width), dtype),
         in_specs=[VMEM] * (1 + len(parts) + len(bases)),
         out_specs=VMEM,
+        scratch_shapes=[pltpu.VMEM((rows, depth), weight.dtype)],
         compiler_params=pltpu.CompilerParams(vmem_limit_bytes=PROJECT_VMEM),
         cost_estimate=pl.CostEstimate(
-            flops=2 * rows * depth * width,
-            bytes_accessed=2 * depth * rows,
+            flops=rows * width,
+            bytes_accessed=rows * width,
             transcendentals=0,
         ),
         name="project",
@@ -348,7 +380,7 @@
 
 def trade(pieces):
     devices = lax.axis_size("dp")
-    rows = [list(range(at, at + ROW)) for at in range(0, devices, ROW)]
+    rows = [list(range(at, at + ROW))[::-1] for at in range(0, devices, ROW)]
     return lax.all_to_all(pieces, "dp", 0, 0, tiled=True, axis_index_groups=rows)
 
 
@@ -358,28 +390,42 @@
 
 
 def per_device(queries, key_proj, value_proj, out_weight, parents):
-    me = lax.axis_index("tensor").astype(jnp.int32).reshape(1)
+    me = lax.axis_index("tensor")
     first = (lax.axis_index("dp") * 2).astype(jnp.int32).reshape(1)
-    packed, pair = pack(key_proj, value_proj)
-    other_pair = swap(pair, 2)
-    pieces = trade(packed).reshape(ROW_SEGS, 2 * PIECE, HEAD_DIM)
-    pieces, other_pair = lax.optimization_barrier((pieces, other_pair))
+    pieces = trade(pack(key_proj, value_proj)).reshape(ROW_SEGS, 2 * PIECE, HEAD_DIM)
     to_next, to_second = carry_out(first, parents, pieces)
-    other_queries = swap(queries, 2)
     inside = pick(first, parents, pieces)
     far = trade(merge(*inside, onward(to_next, ROW), onward(to_second, 2 * ROW)))
-    far, other_queries = lax.optimization_barrier((far, other_queries))
-
-    other_far = swap(far, 2)
-    own, weight = attend(first, parents, queries, pair, far, [me, out_weight])
-    beside = swap(own, 1)
+
     width = queries.shape[1]
-    total = project([own], [0], weight, None, jnp.float32)
-    other_far, total = lax.optimization_barrier((other_far, total))
-    [across] = attend(first, parents, other_queries, other_pair, other_far, [])
-    corner = swap(across, 1)
-    total = project([beside, across], [width, 2 * width], weight, total, jnp.float32)
-    return project([corner], [3 * width], weight, total, jnp.bfloat16)
+    size = 2
+    chunks = width // (size * HEAD_DIM)
+    own, across, weight = [], [], None
+    for c in range(chunks):
+        after = [across[c - 2]] if c >= 2 else []
+        bring = [me.astype(jnp.int32).reshape(1), out_weight] if c == 2 else []
+        part, *brought = attend(
+            first, parents, queries, key_proj, value_proj, far, c * size, size, bring, after
+        )
+        weight = brought[0] if brought else weight
+        own.append(part)
+        across.append(swap(part, 2))
+    beside = [swap(part, 1) for part in own]
+    early = chunks - 1
+    corner = [swap(part, 1) for part in across[:-1]]
+    near = project(
+        [own + beside + across[:early], corner[:early]], [0, 3 * width], weight, None, jnp.float32
+    )
+    across[-1], near = lax.optimization_barrier((across[-1], near))
+    corner.append(swap(across[-1], 1))
+    done = early * size * HEAD_DIM
+    return project(
+        [across[early:], corner[early:]],
+        [2 * width + done, 3 * width + done],
+        weight,
+        near,
+        jnp.bfloat16,
+    )
 
 
 def solution(mesh):

time: 103 us -> 85 us (0.83)
  waiting for transfers between devices: 41.9 us -> 11.6 us
  blocking collectives: 0 us -> 16.2 us
  Pallas kernels: 34.2 us -> 27.4 us
  starting transfers between devices: 25.4 us -> 29.4 us
    all_to_all x0 -> x1, blocking collectives: none -> 16.2 us  [trade(): lax.all_to_all(pieces, 'dp', 0, 0, tiled=True, axis_index_groups=rows)]
    ppermute x2, waiting for transfers between devices: 18.6 us -> 2.84 us  [onward(): lax.ppermute(piece, 'dp', [(i, (i + step) % devices) for i in range(devic...]
    all_to_all x2 -> x1, waiting for transfers between devices: 18 us -> 5.77 us  [trade(): lax.all_to_all(pieces, 'dp', 0, 0, tiled=True, axis_index_groups=rows)]
    ppermute x5 -> x12, starting transfers between devices: 6.02 us -> 15.6 us  [swap(): return lax.ppermute(part, 'tensor', [(i, i ^ bit) for i in range(size)])]
    pallas_call x6 -> x7, Pallas kernels: 31.8 us -> 25.6 us  [the longest x4 17.1 us: attend(): pl.pallas_call(functools.partial(attend_kernel, first_head, bool(bring)),...]
    all_to_all x2 -> x1, starting transfers between devices: 15.4 us -> 9.77 us  [trade(): lax.all_to_all(pieces, 'dp', 0, 0, tiled=True, axis_index_groups=rows)]
    ppermute x5 -> x12, waiting for transfers between devices: 5.4 us -> 2.98 us  [swap(): return lax.ppermute(part, 'tensor', [(i, i ^ bit) for i in range(size)])]
  transfers between devices with their start and end apart: 9 -> 15, of which waited for: 5 -> 4; matrix products, arithmetic and copies ran while one was open for 0% -> 0% of each run, Pallas kernels for 29% -> 23%
where the time goes in v6:
time: 85 us; the launch traced here: 84.7 us
  starting transfers between devices  29.4 us (35%)
  Pallas kernels  27.4 us (32%)
  blocking collectives  16.2 us (19%)
  waiting for transfers between devices  11.6 us (14%)
    pallas_call x4, Pallas kernels, attend(): pl.pallas_call(functools.partial(attend_kernel, first_head, bool(bring)),...  17.1 us
    all_to_all x1, blocking collectives, trade(): lax.all_to_all(pieces, 'dp', 0, 0, tiled=True, axis_index_groups=rows)  16.2 us
    ppermute x12, starting transfers between devices, swap(): return lax.ppermute(part, 'tensor', [(i, i ^ bit) for i in range(size)])  15.6 us
    all_to_all x1, starting transfers between devices, trade(): lax.all_to_all(pieces, 'dp', 0, 0, tiled=True, axis_index_groups=rows)  9.77 us
    pallas_call x2, Pallas kernels, project(): pl.pallas_call(functools.partial(project_kernel, [len(g) for g in groups]...  6.81 us
    all_to_all x1, waiting for transfers between devices, trade(): lax.all_to_all(pieces, 'dp', 0, 0, tiled=True, axis_index_groups=rows)  5.77 us
    ppermute x2, starting transfers between devices, onward(): lax.ppermute(piece, 'dp', [(i, (i + step) % devices) for i in range(devic...  3.99 us
    ppermute x12, waiting for transfers between devices, swap(): return lax.ppermute(part, 'tensor', [(i, i ^ bit) for i in range(size)])  2.98 us
  transfers between devices with their start and end apart: 15, of which 4 were waited for; matrix products, arithmetic and copies ran while one was open for 0% of the time, Pallas kernels for 23%

profile of v6, /device:TPU:1, one launch (start us, length us, event | category | flops | bytes accessed | tf_op | source)
XLA Modules:
  0.0 84.7 jit_solution(11182225088614848159)
XLA Ops:
  0.0 1.7 %pack.1 = bf16[8,2,64,128]{3,2,1,0:T(8,128)(2,1)} custom-call(bf16[512,128]{1,0:T(8,128)(2,1)} %refs_2_.7, bf16[512,128]{1,0:T(8,128)(2,1)} %refs_3_.7), custom_call_target="tpu_custom_call" | custom-call | bytes 524288 | tf_op jit(solution)/shard_map/pack/pallas_call | solution.py:73
  1.7 9.8 %all-to-all-start = ((bf16[8,2,64,128]{3,2,1,0:T(8,128)(2,1)}), bf16[8,2,64,128]{3,2,1,0:T(8,128)(2,1)S(1)}, u32[]{:S(2)}, u32[]{:S(2)}) async-start(bf16[8,2,64,128]{3,2,1,0:T(8,128)(2,1)} %pack.1), calls=%async_computation | async-start | bytes 524288 | tf_op jit(solution)/shard_map/all_to_all | solution.py:384
  11.5 5.8 %all-to-all-done = bf16[8,2,64,128]{3,2,1,0:T(8,128)(2,1)S(1)} async-done(((bf16[8,2,64,128]{3,2,1,0:T(8,128)(2,1)}), bf16[8,2,64,128]{3,2,1,0:T(8,128)(2,1)S(1)}, u32[]{:S(2)}, u32[]{:S(2)}) %all-to-all-start) | async-done | bytes 262176 | tf_op jit(solution)/shard_map/all_to_all | solution.py:384
  17.3 0.7 carry_out.1
  18.0 1.4 %collective-permute-start = (bf16[4,64,128]{2,1,0:T(8,128)(2,1)S(1)}, bf16[4,64,128]{2,1,0:T(8,128)(2,1)S(1)}, u32[]{:S(2)}, u32[]{:S(2)}) collective-permute-start(bf16[4,64,128]{2,1,0:T(8,128)(2,1)S(1)} %get-tuple-element.17), channel_id=1, source_target_pairs={{0,32},{4,36},{8,40},{12,44},{16,48},{20,52},{24,56},{28,60},{32,6... | collective-permute-start | bytes 196616 | tf_op jit(solution)/shard_map/ppermute | solution.py:389
  19.4 2.6 %collective-permute-start.1 = (bf16[1,64,128]{2,1,0:T(8,128)(2,1)S(1)}, bf16[1,64,128]{2,1,0:T(8,128)(2,1)S(1)}, u32[]{:S(2)}, u32[]{:S(2)}) collective-permute-start(bf16[1,64,128]{2,1,0:T(8,128)(2,1)S(1)} %get-tuple-element.18), channel_id=1, source_target_pairs={{0,64},{4,68},{8,72},{12,76},{16,80},{20,84},{24,88},{28,92},{32,9... | collective-permute-start | bytes 49160 | tf_op jit(solution)/shard_map/ppermute | solution.py:389
  22.0 1.0 %pick.1 = (bf16[8,4,64,128]{3,2,1,0:T(8,128)(2,1)S(1)}, bf16[8,4,16,128]{3,2,1,0:T(8,128)(2,1)S(1)}, bf16[8,16,128]{2,1,0:T(8,128)(2,1)S(1)}) custom-call(s32[1]{0:T(128)} %bitcast.first_ref, s32[128]{0:T(128)} %refs_0_.7, bf16[16,64,128]{2,1,0:T(8,128)(2,1)S(1)} %bitcast.4), custom_call_target="tpu_custom_call" | custom-call | bytes 1048576 | tf_op jit(solution)/shard_map/pick/pallas_call | solution.py:149
  23.0 2.8 %collective-permute-done.1.second_ref = bf16[1,64,128]{2,1,0:T(8,128)(2,1)S(1)} collective-permute-done((bf16[1,64,128]{2,1,0:T(8,128)(2,1)S(1)}, bf16[1,64,128]{2,1,0:T(8,128)(2,1)S(1)}, u32[]{:S(2)}, u32[]{:S(2)}) %collective-permute-start.1) | collective-permute-done | bytes 16416 | tf_op jit(solution)/shard_map/ppermute | solution.py:389
  25.9 0.0 collective-permute-done.next_ref
  25.9 0.1 merge.1
  26.0 16.2 %all_to_all.10.refs_4_ = bf16[8,4,64,128]{3,2,1,0:T(8,128)(2,1)S(1)} all-to-all(bf16[8,4,64,128]{3,2,1,0:T(8,128)(2,1)S(1)} %merge.1), channel_id=1, replica_groups={{28,24,20,16,12,8,4,0},{60,56,52,48,44,40,36,32},{92,88,84,80,76,72,68,..., dimensions={0} | all-to-all | bytes 1048576 | tf_op jit(solution)/shard_map/all_to_all | solution.py:384
  42.1 3.7 %attend.4.refs_0_ = bf16[512,256]{1,0:T(8,128)(2,1)S(1)} custom-call(s32[1]{0:T(128)} %bitcast.first_ref, s32[128]{0:T(128)} %refs_0_.7, bf16[512,1024]{1,0:T(8,128)(2,1)} %refs_1_.7, bf16[512,128]{1,0:T(8,128)(2,1)} %refs_2_.7, bf16[512,128]{1,0:T(8,128)(2,1)} %refs_3_.7, bf16[8,4,64,128]{3,2,1,0:T(8,128)(2,1)S(1)} %all_to_all.10.refs_4_), custom_call_target="tpu_custom_call" | custom-call | flops 1845493760 | bytes 1572864 | tf_op jit(solution)/shard_map/attend/pallas_call | solution.py:306
  45.8 1.3 %collective-permute-start.2 = (bf16[512,256]{1,0:T(8,128)(2,1)S(1)}, bf16[512,256]{1,0:T(8,128)(2,1)S(1)}, u32[]{:S(2)}, u32[]{:S(2)}) collective-permute-start(bf16[512,256]{1,0:T(8,128)(2,1)S(1)} %attend.4.refs_0_), channel_id=1, source_target_pairs={{0,2},{1,3},{2,0},{3,1},{4,6},{5,7},{6,4},{7,5},{8,10},{9,11},{10,... | collective-permute-start | bytes 786440 | tf_op jit(solution)/shard_map/ppermute | solution.py:378
  47.1 3.7 %attend.6.refs_1_ = bf16[512,256]{1,0:T(8,128)(2,1)S(1)} custom-call(s32[1]{0:T(128)} %bitcast.first_ref, s32[128]{0:T(128)} %refs_0_.7, bf16[512,1024]{1,0:T(8,128)(2,1)} %refs_1_.7, bf16[512,128]{1,0:T(8,128)(2,1)} %refs_2_.7, bf16[512,128]{1,0:T(8,128)(2,1)} %refs_3_.7, bf16[8,4,64,128]{3,2,1,0:T(8,128)(2,1)S(1)} %all_to_all.10.refs_4_), custom_call_target="tpu_custom_call" | custom-call | flops 1845493760 | bytes 1572864 | tf_op jit(solution)/shard_map/attend/pallas_call | solution.py:306
  50.8 0.3 collective-permute-start.3
  51.2 6.9 %collective-permute-start.6 = (bf16[512,256]{1,0:T(8,128)(2,1)S(1)}, bf16[512,256]{1,0:T(8,128)(2,1)S(1)}, u32[]{:S(2)}, u32[]{:S(2)}) collective-permute-start(bf16[512,256]{1,0:T(8,128)(2,1)S(1)} %attend.6.refs_1_), channel_id=1, source_target_pairs={{0,1},{1,0},{2,3},{3,2},{4,5},{5,4},{6,7},{7,6},{8,9},{9,8},{10,11... | collective-permute-start | bytes 786440 | tf_op jit(solution)/shard_map/ppermute | solution.py:378
  58.1 0.0 collective-permute-start.5
  58.1 6.0 %attend.5 = (bf16[512,256]{1,0:T(8,128)(2,1)S(1)}, bf16[4096,1280]{1,0:T(8,128)(2,1)S(1)}) custom-call(s32[1]{0:T(128)} %bitcast.first_ref, s32[128]{0:T(128)} %refs_0_.7, bf16[512,1024]{1,0:T(8,128)(2,1)} %refs_1_.7, bf16[512,128]{1,0:T(8,128)(2,1)} %refs_2_.7, bf16[512,128]{1,0:T(8,128)(2,1)} %refs_3_.7, bf16[8,4,64,128]{3,2,1,0:T(8,128)(2,1)S(1)} %all_to_all.10.refs_4_, ...), custom_call_target="tpu_custom_call" | custom-call | flops 1845493760 | bytes 1572864 | tf_op jit(solution)/shard_map/attend/pallas_call | solution.py:306
  64.1 1.3 %collective-permute-start.9 = (bf16[512,256]{1,0:T(8,128)(2,1)S(1)}, bf16[512,256]{1,0:T(8,128)(2,1)S(1)}, u32[]{:S(2)}, u32[]{:S(2)}) collective-permute-start(bf16[512,256]{1,0:T(8,128)(2,1)S(1)} %get-tuple-element.20.refs_2_), channel_id=1, source_target_pairs={{0,2},{1,3},{2,0},{3,1},{4,6},{5,7},{6,4},{7,5},{8,10},{9,11},{10,... | collective-permute-start | bytes 786440 | tf_op jit(solution)/shard_map/ppermute | solution.py:378
  65.4 0.9 %collective-permute-start.7 = (bf16[512,256]{1,0:T(8,128)(2,1)S(1)}, bf16[512,256]{1,0:T(8,128)(2,1)S(1)}, u32[]{:S(2)}, u32[]{:S(2)}) collective-permute-start(bf16[512,256]{1,0:T(8,128)(2,1)S(1)} %get-tuple-element.20.refs_2_), channel_id=1, source_target_pairs={{0,1},{1,0},{2,3},{3,2},{4,5},{5,4},{6,7},{7,6},{8,9},{9,8},{10,11... | collective-permute-start | bytes 786440 | tf_op jit(solution)/shard_map/ppermute | solution.py:378
  66.3 0.0 collective-permute-done.3.refs_5_.refs_9_
  66.3 3.7 %attend.7.refs_3_ = bf16[512,256]{1,0:T(8,128)(2,1)S(1)} custom-call(s32[1]{0:T(128)} %bitcast.first_ref, s32[128]{0:T(128)} %refs_0_.7, bf16[512,1024]{1,0:T(8,128)(2,1)} %refs_1_.7, bf16[512,128]{1,0:T(8,128)(2,1)} %refs_2_.7, bf16[512,128]{1,0:T(8,128)(2,1)} %refs_3_.7, bf16[8,4,64,128]{3,2,1,0:T(8,128)(2,1)S(1)} %all_to_all.10.refs_4_, ...), custom_call_target="tpu_custom_call" | custom-call | flops 1845493760 | bytes 1572864 | tf_op jit(solution)/shard_map/attend/pallas_call | solution.py:306
  70.0 0.1 collective-permute-start.8
  70.1 0.5 collective-permute-start.11
  70.6 0.1 collective-permute-start.10
  70.7 2.2 %collective-permute-start.12 = (bf16[512,256]{1,0:T(8,128)(2,1)S(1)}, bf16[512,256]{1,0:T(8,128)(2,1)S(1)}, u32[]{:S(2)}, u32[]{:S(2)}) collective-permute-start(bf16[512,256]{1,0:T(8,128)(2,1)S(1)} %collective-permute-done.9.refs_10_), channel_id=1, source_target_pairs={{0,1},{1,0},{2,3},{3,2},{4,5},{5,4},{6,7},{7,6},{8,9},{9,8},{10,11... | collective-permute-start | bytes 786440 | tf_op jit(solution)/shard_map/ppermute | solution.py:378
  72.9 1.2 %collective-permute-start.4 = (bf16[512,256]{1,0:T(8,128)(2,1)S(1)}, bf16[512,256]{1,0:T(8,128)(2,1)S(1)}, u32[]{:S(2)}, u32[]{:S(2)}) collective-permute-start(bf16[512,256]{1,0:T(8,128)(2,1)S(1)} %attend.7.refs_3_), channel_id=1, source_target_pairs={{0,2},{1,3},{2,0},{3,1},{4,6},{5,7},{6,4},{7,5},{8,10},{9,11},{10,... | collective-permute-start | bytes 786440 | tf_op jit(solution)/shard_map/ppermute | solution.py:378
  74.2 4.9 %project.2.refs_2_ = f32[512,1280]{1,0:T(8,128)S(1)} custom-call(bf16[4096,1280]{1,0:T(8,128)(2,1)S(1)} %get-tuple-element.19.weight_ref, bf16[512,256]{1,0:T(8,128)(2,1)S(1)} %attend.4.refs_0_, bf16[512,256]{1,0:T(8,128)(2,1)S(1)} %attend.6.refs_1_, bf16[512,256]{1,0:T(8,128)(2,1)S(1)} %get-tuple-element.20.refs_2_, bf16[512,256]{1,0:T(8,128)(2,1)S(1)} %attend.7.refs_3_, ...), custom_call_target="tpu_custom_call" | custom-call | flops 655360 | bytes 655360 | tf_op jit(solution)/shard_map/project/pallas_call | solution.py:360
  79.1 1.8 %collective-permute-done.4.refs_0_ = bf16[512,256]{1,0:T(8,128)(2,1)S(1)} collective-permute-done((bf16[512,256]{1,0:T(8,128)(2,1)S(1)}, bf16[512,256]{1,0:T(8,128)(2,1)S(1)}, u32[]{:S(2)}, u32[]{:S(2)}) %collective-permute-start.4) | collective-permute-done | bytes 262176 | tf_op jit(solution)/shard_map/ppermute | solution.py:378
  80.9 0.8 collective-permute-start.13
  81.6 1.2 %collective-permute-done.13.refs_1_ = bf16[512,256]{1,0:T(8,128)(2,1)S(1)} collective-permute-done((bf16[512,256]{1,0:T(8,128)(2,1)S(1)}, bf16[512,256]{1,0:T(8,128)(2,1)S(1)}, u32[]{:S(2)}, u32[]{:S(2)}) %collective-permute-start.13) | collective-permute-done | bytes 262176 | tf_op jit(solution)/shard_map/ppermute | solution.py:378
  82.8 1.9 %project.3 = bf16[512,1280]{1,0:T(8,128)(2,1)} custom-call(bf16[4096,1280]{1,0:T(8,128)(2,1)S(1)} %get-tuple-element.19.weight_ref, bf16[512,256]{1,0:T(8,128)(2,1)S(1)} %collective-permute-done.4.refs_0_, bf16[512,256]{1,0:T(8,128)(2,1)S(1)} %collective-permute-done.13.refs_1_, f32[512,1280]{1,0:T(8,128)S(1)} %project.2.refs_2_), custom_call_target="tpu_custom_call" | custom-call | flops 655360 | bytes 655360 | tf_op jit(solution)/shard_map/project/pallas_call | solution.py:360
  (9 shorter events, 0.0 us)
Async XLA Ops:
  1.7 15.5 %all-to-all-start = ((bf16[8,2,64,128]{3,2,1,0:T(8,128)(2,1)}), bf16[8,2,64,128]{3,2,1,0:T(8,128)(2,1)S(1)}, u32[]{:S(2)}, u32[]{:S(2)}) async-start(bf16[8,2,64,128]{3,2,1,0:T(8,128)(2,1)} %pack.1), calls=%async_computation | async-start | bytes 524288 | tf_op jit(solution)/shard_map/all_to_all | solution.py:384
  18.0 7.9 %collective-permute-start = (bf16[4,64,128]{2,1,0:T(8,128)(2,1)S(1)}, bf16[4,64,128]{2,1,0:T(8,128)(2,1)S(1)}, u32[]{:S(2)}, u32[]{:S(2)}) collective-permute-start(bf16[4,64,128]{2,1,0:T(8,128)(2,1)S(1)} %get-tuple-element.17), channel_id=1, source_target_pairs={{0,32},{4,36},{8,40},{12,44},{16,48},{20,52},{24,56},{28,60},{32,6... | collective-permute-start | bytes 196616 | tf_op jit(solution)/shard_map/ppermute | solution.py:389
  19.4 6.5 %collective-permute-start.1 = (bf16[1,64,128]{2,1,0:T(8,128)(2,1)S(1)}, bf16[1,64,128]{2,1,0:T(8,128)(2,1)S(1)}, u32[]{:S(2)}, u32[]{:S(2)}) collective-permute-start(bf16[1,64,128]{2,1,0:T(8,128)(2,1)S(1)} %get-tuple-element.18), channel_id=1, source_target_pairs={{0,64},{4,68},{8,72},{12,76},{16,80},{20,84},{24,88},{28,92},{32,9... | collective-permute-start | bytes 49160 | tf_op jit(solution)/shard_map/ppermute | solution.py:389
  45.8 12.3 %collective-permute-start.2 = (bf16[512,256]{1,0:T(8,128)(2,1)S(1)}, bf16[512,256]{1,0:T(8,128)(2,1)S(1)}, u32[]{:S(2)}, u32[]{:S(2)}) collective-permute-start(bf16[512,256]{1,0:T(8,128)(2,1)S(1)} %attend.4.refs_0_), channel_id=1, source_target_pairs={{0,2},{1,3},{2,0},{3,1},{4,6},{5,7},{6,4},{7,5},{8,10},{9,11},{10,... | collective-permute-start | bytes 786440 | tf_op jit(solution)/shard_map/ppermute | solution.py:378
  50.8 15.4 %collective-permute-start.3 = (bf16[512,256]{1,0:T(8,128)(2,1)S(1)}, bf16[512,256]{1,0:T(8,128)(2,1)S(1)}, u32[]{:S(2)}, u32[]{:S(2)}) collective-permute-start(bf16[512,256]{1,0:T(8,128)(2,1)S(1)} %attend.6.refs_1_), channel_id=1, source_target_pairs={{0,2},{1,3},{2,0},{3,1},{4,6},{5,7},{6,4},{7,5},{8,10},{9,11},{10,... | collective-permute-start | bytes 786440 | tf_op jit(solution)/shard_map/ppermute | solution.py:378
  51.2 18.9 %collective-permute-start.6 = (bf16[512,256]{1,0:T(8,128)(2,1)S(1)}, bf16[512,256]{1,0:T(8,128)(2,1)S(1)}, u32[]{:S(2)}, u32[]{:S(2)}) collective-permute-start(bf16[512,256]{1,0:T(8,128)(2,1)S(1)} %attend.6.refs_1_), channel_id=1, source_target_pairs={{0,1},{1,0},{2,3},{3,2},{4,5},{5,4},{6,7},{7,6},{8,9},{9,8},{10,11... | collective-permute-start | bytes 786440 | tf_op jit(solution)/shard_map/ppermute | solution.py:378
  58.1 12.5 %collective-permute-start.5 = (bf16[512,256]{1,0:T(8,128)(2,1)S(1)}, bf16[512,256]{1,0:T(8,128)(2,1)S(1)}, u32[]{:S(2)}, u32[]{:S(2)}) collective-permute-start(bf16[512,256]{1,0:T(8,128)(2,1)S(1)} %attend.4.refs_0_), channel_id=1, source_target_pairs={{0,1},{1,0},{2,3},{3,2},{4,5},{5,4},{6,7},{7,6},{8,9},{9,8},{10,11... | collective-permute-start | bytes 786440 | tf_op jit(solution)/shard_map/ppermute | solution.py:378
  64.1 6.6 %collective-permute-start.9 = (bf16[512,256]{1,0:T(8,128)(2,1)S(1)}, bf16[512,256]{1,0:T(8,128)(2,1)S(1)}, u32[]{:S(2)}, u32[]{:S(2)}) collective-permute-start(bf16[512,256]{1,0:T(8,128)(2,1)S(1)} %get-tuple-element.20.refs_2_), channel_id=1, source_target_pairs={{0,2},{1,3},{2,0},{3,1},{4,6},{5,7},{6,4},{7,5},{8,10},{9,11},{10,... | collective-permute-start | bytes 786440 | tf_op jit(solution)/shard_map/ppermute | solution.py:378
  65.4 7.5 %collective-permute-start.7 = (bf16[512,256]{1,0:T(8,128)(2,1)S(1)}, bf16[512,256]{1,0:T(8,128)(2,1)S(1)}, u32[]{:S(2)}, u32[]{:S(2)}) collective-permute-start(bf16[512,256]{1,0:T(8,128)(2,1)S(1)} %get-tuple-element.20.refs_2_), channel_id=1, source_target_pairs={{0,1},{1,0},{2,3},{3,2},{4,5},{5,4},{6,7},{7,6},{8,9},{9,8},{10,11... | collective-permute-start | bytes 786440 | tf_op jit(solution)/shard_map/ppermute | solution.py:378
  70.0 4.2 %collective-permute-start.8 = (bf16[512,256]{1,0:T(8,128)(2,1)S(1)}, bf16[512,256]{1,0:T(8,128)(2,1)S(1)}, u32[]{:S(2)}, u32[]{:S(2)}) collective-permute-start(bf16[512,256]{1,0:T(8,128)(2,1)S(1)} %attend.7.refs_3_), channel_id=1, source_target_pairs={{0,1},{1,0},{2,3},{3,2},{4,5},{5,4},{6,7},{7,6},{8,9},{9,8},{10,11... | collective-permute-start | bytes 786440 | tf_op jit(solution)/shard_map/ppermute | solution.py:378
  70.1 4.1 %collective-permute-start.11 = (bf16[512,256]{1,0:T(8,128)(2,1)S(1)}, bf16[512,256]{1,0:T(8,128)(2,1)S(1)}, u32[]{:S(2)}, u32[]{:S(2)}) collective-permute-start(bf16[512,256]{1,0:T(8,128)(2,1)S(1)} %collective-permute-done.3.refs_5_.refs_9_), channel_id=1, source_target_pairs={{0,1},{1,0},{2,3},{3,2},{4,5},{5,4},{6,7},{7,6},{8,9},{9,8},{10,11... | collective-permute-start | bytes 786440 | tf_op jit(solution)/shard_map/ppermute | solution.py:378
  70.6 3.6 %collective-permute-start.10 = (bf16[512,256]{1,0:T(8,128)(2,1)S(1)}, bf16[512,256]{1,0:T(8,128)(2,1)S(1)}, u32[]{:S(2)}, u32[]{:S(2)}) collective-permute-start(bf16[512,256]{1,0:T(8,128)(2,1)S(1)} %collective-permute-done.2.refs_7_.refs_8_), channel_id=1, source_target_pairs={{0,1},{1,0},{2,3},{3,2},{4,5},{5,4},{6,7},{7,6},{8,9},{9,8},{10,11... | collective-permute-start | bytes 786440 | tf_op jit(solution)/shard_map/ppermute | solution.py:378
  70.7 3.5 %collective-permute-start.12 = (bf16[512,256]{1,0:T(8,128)(2,1)S(1)}, bf16[512,256]{1,0:T(8,128)(2,1)S(1)}, u32[]{:S(2)}, u32[]{:S(2)}) collective-permute-start(bf16[512,256]{1,0:T(8,128)(2,1)S(1)} %collective-permute-done.9.refs_10_), channel_id=1, source_target_pairs={{0,1},{1,0},{2,3},{3,2},{4,5},{5,4},{6,7},{7,6},{8,9},{9,8},{10,11... | collective-permute-start | bytes 786440 | tf_op jit(solution)/shard_map/ppermute | solution.py:378
  72.9 7.9 %collective-permute-start.4 = (bf16[512,256]{1,0:T(8,128)(2,1)S(1)}, bf16[512,256]{1,0:T(8,128)(2,1)S(1)}, u32[]{:S(2)}, u32[]{:S(2)}) collective-permute-start(bf16[512,256]{1,0:T(8,128)(2,1)S(1)} %attend.7.refs_3_), channel_id=1, source_target_pairs={{0,2},{1,3},{2,0},{3,1},{4,6},{5,7},{6,4},{7,5},{8,10},{9,11},{10,... | collective-permute-start | bytes 786440 | tf_op jit(solution)/shard_map/ppermute | solution.py:378
  80.9 1.9 %collective-permute-start.13 = (bf16[512,256]{1,0:T(8,128)(2,1)S(1)}, bf16[512,256]{1,0:T(8,128)(2,1)S(1)}, u32[]{:S(2)}, u32[]{:S(2)}) collective-permute-start(bf16[512,256]{1,0:T(8,128)(2,1)S(1)} %collective-permute-done.4.refs_0_), channel_id=1, source_target_pairs={{0,1},{1,0},{2,3},{3,2},{4,5},{5,4},{6,7},{7,6},{8,9},{9,8},{10,11... | collective-permute-start | bytes 786440 | tf_op jit(solution)/shard_map/ppermute | solution.py:378

commit v7 on v6

--- a/solution.py
+++ b/solution.py
@@ -13,6 +13,7 @@
 LEVELS = 4
 ROW = 8
 ROW_SEGS = 2 * ROW
+LISTED = (7, 3, 6, 2, 5, 1, 4, 0)
 PIECE = SEG_LEN // ROW
 PATH = LEVELS * SEG_LEN
 STACK = LEVELS * PIECE
@@ -87,7 +88,9 @@
 
 
 def slot_of(seg):
-    return seg ^ (ROW_SEGS - 2)
+    place = seg // 2
+    member = 2 * (ROW // 2 - 1 - place % (ROW // 2)) + 1 - place // (ROW // 2)
+    return 2 * member + seg % 2
 
 
 def bring_parents(source_ref, parents_ref, sem):
@@ -131,8 +134,8 @@
     bring_parents(source_ref, parents_ref, sem)
     base = row_start(first_ref)
     ones = lambda on: jnp.full((FLAG_ROWS, HEAD_DIM), on, jnp.float32).astype(jnp.bfloat16)
-    for target in range(ROW):
-        path, depth = path_of(parents_ref, base + 2 * (ROW - 1 - target))
+    for target, place in enumerate(LISTED):
+        path, depth = path_of(parents_ref, base + 2 * place)
         for level in range(LEVELS):
             seg = level_of(path, depth, level)
             within = seg >= base
@@ -187,9 +190,9 @@
     )(inside, on_next, on_second, carried, second)
 
 
-def attend_kernel(first_head, bring, first_ref, *refs):
+def attend_kernel(first_head, blocks, first_ref, *refs):
     sources, (far_ref, *refs) = refs[:4], refs[4:]
-    if bring:
+    if blocks:
         me_ref, weight_ref = refs[:2]
         weight_sem = refs.pop()
         held_ref = refs.pop(-8)
@@ -201,7 +204,7 @@
         pltpu.make_async_copy(view, target, sem.at[i])
         for i, (view, target) in enumerate(zip(views, [parents_ref, query_ref, key_ref, value_ref]))
     ]
-    copies = weight_copies(me_ref, weight_ref, held_ref, weight_sem) if bring else []
+    copies = weight_copies(blocks, me_ref, weight_ref, held_ref, weight_sem) if blocks else []
     for copy in fetches + copies:
         copy.start()
 
@@ -272,20 +275,20 @@
         copy.wait()
 
 
-def weight_copies(me_ref, weight_ref, held_ref, sem):
+def weight_copies(blocks, me_ref, weight_ref, held_ref, sem):
     block = weight_ref.shape[0] // 4
     copies = []
-    for bit in range(4):
+    for i, bit in enumerate(blocks):
         rows = pl.ds(pl.multiple_of((me_ref[0] ^ bit) * block, block), block)
         copies.append(
             pltpu.make_async_copy(
-                weight_ref.at[rows], held_ref.at[pl.ds(bit * block, block)], sem.at[bit]
+                weight_ref.at[rows], held_ref.at[pl.ds(i * block, block)], sem.at[i]
             )
         )
     return copies
 
 
-def attend(first, parents, queries, keys, values, far, first_head, heads, bring, after):
+def attend(first, parents, queries, keys, values, far, first_head, heads, blocks, bring, after):
     rows = queries.shape[0]
     pairs = heads * rows * (PATH + SEG_LEN + SEG_LEN // 2)
     out_shape = [jax.ShapeDtypeStruct((rows, heads * HEAD_DIM), jnp.bfloat16)]
@@ -297,14 +300,17 @@
         pltpu.VMEM(values.shape, values.dtype),
         pltpu.SemaphoreType.DMA((4,)),
     ]
-    if bring:
-        weight = bring[1]
-        bring = [bring[0], in_hbm(weight)]
+    if blocks:
+        me, weight = bring
+        bring = [me, in_hbm(weight)]
         in_specs += [SMEM, HBM]
-        out_shape.append(pltpu.VMEM(weight.shape, weight.dtype))
-        scratch.append(pltpu.SemaphoreType.DMA((4,)))
-    return pl.pallas_call(
-        functools.partial(attend_kernel, first_head, bool(bring)),
+        shape = (len(blocks) * weight.shape[0] // 4, weight.shape[1])
+        out_shape.append(pltpu.VMEM(shape, weight.dtype))
+        scratch.append(pltpu.SemaphoreType.DMA((len(blocks),)))
+    else:
+        bring = []
+    return pl.pallas_call(
+        functools.partial(attend_kernel, first_head, blocks),
         out_shape=out_shape,
         in_specs=in_specs + [ANY] * len(after),
         out_specs=[VMEM] * len(out_shape),
@@ -328,7 +334,7 @@
     )
 
 
-def project_kernel(counts, spans, has_base, weight_ref, *refs):
+def project_kernel(counts, spans, has_base, near_ref, far_ref, *refs):
     parts = refs[: sum(counts)]
     out_ref, held_ref = refs[-2:]
     at, ends = 0, [0]
@@ -341,28 +347,28 @@
     for column in range(0, out_ref.shape[1], TILE):
         columns = slice(column, column + TILE)
         total = refs[sum(counts)][:, columns] if has_base else None
-        for start, begin, end in zip(spans, ends, ends[1:]):
+        for (half, start), begin, end in zip(spans, ends, ends[1:]):
             product = jnp.dot(
                 held_ref[:, begin:end],
-                weight_ref[start : start + end - begin, columns],
+                (near_ref, far_ref)[half][start : start + end - begin, columns],
                 preferred_element_type=jnp.float32,
             )
             total = product if total is None else total + product
         out_ref[:, columns] = total.astype(out_ref.dtype)
 
 
-def project(groups, spans, weight, base, dtype):
+def project(groups, spans, weights, base, dtype):
     parts = [part for group in groups for part in group]
     rows = parts[0].shape[0]
     depth = sum(part.shape[1] for part in parts)
-    width = weight.shape[1]
+    width = weights[0].shape[1]
     bases = [] if base is None else [base]
     return pl.pallas_call(
         functools.partial(project_kernel, [len(g) for g in groups], spans, base is not None),
         out_shape=jax.ShapeDtypeStruct((rows, width), dtype),
-        in_specs=[VMEM] * (1 + len(parts) + len(bases)),
+        in_specs=[VMEM] * (2 + len(parts) + len(bases)),
         out_specs=VMEM,
-        scratch_shapes=[pltpu.VMEM((rows, depth), weight.dtype)],
+        scratch_shapes=[pltpu.VMEM((rows, depth), parts[0].dtype)],
         compiler_params=pltpu.CompilerParams(vmem_limit_bytes=PROJECT_VMEM),
         cost_estimate=pl.CostEstimate(
             flops=rows * width,
@@ -370,7 +376,7 @@
             transcendentals=0,
         ),
         name="project",
-    )(in_vmem(weight), *parts, *bases)
+    )(*[in_vmem(weight) for weight in weights], *parts, *bases)
 
 
 def swap(part, bit):
@@ -380,7 +386,7 @@
 
 def trade(pieces):
     devices = lax.axis_size("dp")
-    rows = [list(range(at, at + ROW))[::-1] for at in range(0, devices, ROW)]
+    rows = [[at + place for place in LISTED] for at in range(0, devices, ROW)]
     return lax.all_to_all(pieces, "dp", 0, 0, tiled=True, axis_index_groups=rows)
 
 
@@ -398,33 +404,28 @@
     far = trade(merge(*inside, onward(to_next, ROW), onward(to_second, 2 * ROW)))
 
     width = queries.shape[1]
-    size = 2
-    chunks = width // (size * HEAD_DIM)
-    own, across, weight = [], [], None
-    for c in range(chunks):
+    bring = (me.astype(jnp.int32).reshape(1), out_weight)
+    own, across, weights, head = [], [], [], 0
+    for c, (size, blocks) in enumerate([(2, ()), (3, (0, 1)), (3, (2, 3))]):
         after = [across[c - 2]] if c >= 2 else []
-        bring = [me.astype(jnp.int32).reshape(1), out_weight] if c == 2 else []
         part, *brought = attend(
-            first, parents, queries, key_proj, value_proj, far, c * size, size, bring, after
+            first, parents, queries, key_proj, value_proj, far, head, size, blocks, bring, after
         )
-        weight = brought[0] if brought else weight
+        weights += brought
         own.append(part)
         across.append(swap(part, 2))
+        head += size
     beside = [swap(part, 1) for part in own]
-    early = chunks - 1
     corner = [swap(part, 1) for part in across[:-1]]
     near = project(
-        [own + beside + across[:early], corner[:early]], [0, 3 * width], weight, None, jnp.float32
+        [own + beside, across[:-1], corner[:-1]], [(0, 0), (1, 0), (1, width)], weights, None, jnp.float32
     )
-    across[-1], near = lax.optimization_barrier((across[-1], near))
-    corner.append(swap(across[-1], 1))
-    done = early * size * HEAD_DIM
+    last, near = lax.optimization_barrier((across[-1], near))
+    corner.append(swap(last, 1))
+    done = width - last.shape[1]
+    turned = sum(part.shape[1] for part in corner[:-2])
     return project(
-        [across[early:], corner[early:]],
-        [2 * width + done, 3 * width + done],
-        weight,
-        near,
-        jnp.bfloat16,
+        [[last], corner[-2:]], [(1, done), (1, width + turned)], weights, near, jnp.bfloat16
     )
 
 

time: 85 us -> 82 us (0.965)
  starting transfers between devices: 29.4 us -> 24.1 us
  waiting for transfers between devices: 11.6 us -> 14.2 us
  Pallas kernels: 27.4 us -> 25.8 us
  blocking collectives: 16.2 us -> 17.6 us
    ppermute x12 -> x9, starting transfers between devices: 15.6 us -> 10.4 us  [swap(): return lax.ppermute(part, 'tensor', [(i, i ^ bit) for i in range(size)])]
    ppermute x12 -> x9, waiting for transfers between devices: 2.98 us -> 5.9 us  [swap(): return lax.ppermute(part, 'tensor', [(i, i ^ bit) for i in range(size)])]
    pallas_call x4 -> x3, Pallas kernels: 17.1 us -> 14.7 us  [attend(): pl.pallas_call(functools.partial(attend_kernel, first_head, blocks), out_...]
    all_to_all x1, blocking collectives: 16.2 us -> 17.6 us  [trade(): lax.all_to_all(pieces, 'dp', 0, 0, tiled=True, axis_index_groups=rows)]
  transfers between devices with their start and end apart: 15 -> 12, of which waited for: 4 -> 5; matrix products, arithmetic and copies ran while one was open for 0% -> 0% of each run, Pallas kernels for 23% -> 20%
where the time goes in v7:
time: 82 us; the launch traced here: 81.7 us
  Pallas kernels  25.8 us (31%)
  starting transfers between devices  24.1 us (29%)
  blocking collectives  17.6 us (21%)
  waiting for transfers between devices  14.2 us (17%)
    all_to_all x1, blocking collectives, trade(): lax.all_to_all(pieces, 'dp', 0, 0, tiled=True, axis_index_groups=rows)  17.6 us
    pallas_call x3, Pallas kernels, attend(): pl.pallas_call(functools.partial(attend_kernel, first_head, blocks), out_...  14.7 us
    ppermute x9, starting transfers between devices, swap(): return lax.ppermute(part, 'tensor', [(i, i ^ bit) for i in range(size)])  10.4 us
    all_to_all x1, starting transfers between devices, trade(): lax.all_to_all(pieces, 'dp', 0, 0, tiled=True, axis_index_groups=rows)  9.77 us
    pallas_call x2, Pallas kernels, project(): pl.pallas_call(functools.partial(project_kernel, [len(g) for g in groups]...  7.16 us
    ppermute x9, waiting for transfers between devices, swap(): return lax.ppermute(part, 'tensor', [(i, i ^ bit) for i in range(size)])  5.9 us
    all_to_all x1, waiting for transfers between devices, trade(): lax.all_to_all(pieces, 'dp', 0, 0, tiled=True, axis_index_groups=rows)  5.73 us
    ppermute x2, starting transfers between devices, onward(): lax.ppermute(piece, 'dp', [(i, (i + step) % devices) for i in range(devic...  3.99 us
  transfers between devices with their start and end apart: 12, of which 5 were waited for; matrix products, arithmetic and copies ran while one was open for 0% of the time, Pallas kernels for 20%

profile of v7, /device:TPU:1, one launch (start us, length us, event | category | flops | bytes accessed | tf_op | source)
XLA Modules:
  0.0 81.7 jit_solution(6821018946942695117)
XLA Ops:
  0.0 1.7 %pack.1 = bf16[8,2,64,128]{3,2,1,0:T(8,128)(2,1)} custom-call(bf16[512,128]{1,0:T(8,128)(2,1)} %refs_2_.5, bf16[512,128]{1,0:T(8,128)(2,1)} %refs_3_.5), custom_call_target="tpu_custom_call" | custom-call | bytes 524288 | tf_op jit(solution)/shard_map/pack/pallas_call | solution.py:74
  1.7 9.8 %all-to-all-start = ((bf16[8,2,64,128]{3,2,1,0:T(8,128)(2,1)}), bf16[8,2,64,128]{3,2,1,0:T(8,128)(2,1)S(1)}, u32[]{:S(2)}, u32[]{:S(2)}) async-start(bf16[8,2,64,128]{3,2,1,0:T(8,128)(2,1)} %pack.1), calls=%async_computation | async-start | bytes 524288 | tf_op jit(solution)/shard_map/all_to_all | solution.py:390
  11.5 5.7 %all-to-all-done = bf16[8,2,64,128]{3,2,1,0:T(8,128)(2,1)S(1)} async-done(((bf16[8,2,64,128]{3,2,1,0:T(8,128)(2,1)}), bf16[8,2,64,128]{3,2,1,0:T(8,128)(2,1)S(1)}, u32[]{:S(2)}, u32[]{:S(2)}) %all-to-all-start) | async-done | bytes 262176 | tf_op jit(solution)/shard_map/all_to_all | solution.py:390
  17.2 0.8 carry_out.1
  18.0 1.4 %collective-permute-start = (bf16[4,64,128]{2,1,0:T(8,128)(2,1)S(1)}, bf16[4,64,128]{2,1,0:T(8,128)(2,1)S(1)}, u32[]{:S(2)}, u32[]{:S(2)}) collective-permute-start(bf16[4,64,128]{2,1,0:T(8,128)(2,1)S(1)} %get-tuple-element.19), channel_id=1, source_target_pairs={{0,32},{4,36},{8,40},{12,44},{16,48},{20,52},{24,56},{28,60},{32,6... | collective-permute-start | bytes 196616 | tf_op jit(solution)/shard_map/ppermute | solution.py:395
  19.4 2.6 %collective-permute-start.1 = (bf16[1,64,128]{2,1,0:T(8,128)(2,1)S(1)}, bf16[1,64,128]{2,1,0:T(8,128)(2,1)S(1)}, u32[]{:S(2)}, u32[]{:S(2)}) collective-permute-start(bf16[1,64,128]{2,1,0:T(8,128)(2,1)S(1)} %get-tuple-element.20), channel_id=1, source_target_pairs={{0,64},{4,68},{8,72},{12,76},{16,80},{20,84},{24,88},{28,92},{32,9... | collective-permute-start | bytes 49160 | tf_op jit(solution)/shard_map/ppermute | solution.py:395
  22.0 1.3 %pick.1 = (bf16[8,4,64,128]{3,2,1,0:T(8,128)(2,1)S(1)}, bf16[8,4,16,128]{3,2,1,0:T(8,128)(2,1)S(1)}, bf16[8,16,128]{2,1,0:T(8,128)(2,1)S(1)}) custom-call(s32[1]{0:T(128)} %bitcast.first_ref, s32[128]{0:T(128)} %refs_0_.5, bf16[16,64,128]{2,1,0:T(8,128)(2,1)S(1)} %bitcast.4), custom_call_target="tpu_custom_call" | custom-call | bytes 1048576 | tf_op jit(solution)/shard_map/pick/pallas_call | solution.py:152
  23.3 2.5 %collective-permute-done.1.second_ref = bf16[1,64,128]{2,1,0:T(8,128)(2,1)S(1)} collective-permute-done((bf16[1,64,128]{2,1,0:T(8,128)(2,1)S(1)}, bf16[1,64,128]{2,1,0:T(8,128)(2,1)S(1)}, u32[]{:S(2)}, u32[]{:S(2)}) %collective-permute-start.1) | collective-permute-done | bytes 16416 | tf_op jit(solution)/shard_map/ppermute | solution.py:395
  25.9 0.0 collective-permute-done.next_ref
  25.9 0.1 merge.1
  26.0 17.6 %all_to_all.10.refs_4_ = bf16[8,4,64,128]{3,2,1,0:T(8,128)(2,1)S(1)} all-to-all(bf16[8,4,64,128]{3,2,1,0:T(8,128)(2,1)S(1)} %merge.1), channel_id=1, replica_groups={{28,12,24,8,20,4,16,0},{60,44,56,40,52,36,48,32},{92,76,88,72,84,68,80,..., dimensions={0} | all-to-all | bytes 1048576 | tf_op jit(solution)/shard_map/all_to_all | solution.py:390
  43.5 3.7 %attend.4.refs_0_ = bf16[512,256]{1,0:T(8,128)(2,1)S(1)} custom-call(s32[1]{0:T(128)} %bitcast.first_ref, s32[128]{0:T(128)} %refs_0_.5, bf16[512,1024]{1,0:T(8,128)(2,1)} %refs_1_.5, bf16[512,128]{1,0:T(8,128)(2,1)} %refs_2_.5, bf16[512,128]{1,0:T(8,128)(2,1)} %refs_3_.5, bf16[8,4,64,128]{3,2,1,0:T(8,128)(2,1)S(1)} %all_to_all.10.refs_4_), custom_call_target="tpu_custom_call" | custom-call | flops 1845493760 | bytes 1572864 | tf_op jit(solution)/shard_map/attend/pallas_call | solution.py:312
  47.2 1.3 %collective-permute-start.2 = (bf16[512,256]{1,0:T(8,128)(2,1)S(1)}, bf16[512,256]{1,0:T(8,128)(2,1)S(1)}, u32[]{:S(2)}, u32[]{:S(2)}) collective-permute-start(bf16[512,256]{1,0:T(8,128)(2,1)S(1)} %attend.4.refs_0_), channel_id=1, source_target_pairs={{0,2},{1,3},{2,0},{3,1},{4,6},{5,7},{6,4},{7,5},{8,10},{9,11},{10,... | collective-permute-start | bytes 786440 | tf_op jit(solution)/shard_map/ppermute | solution.py:384
  48.5 5.5 %attend.3 = (bf16[512,384]{1,0:T(8,128)(2,1)S(1)}, bf16[2048,1280]{1,0:T(8,128)(2,1)S(1)}) custom-call(s32[1]{0:T(128)} %bitcast.first_ref, s32[128]{0:T(128)} %refs_0_.5, bf16[512,1024]{1,0:T(8,128)(2,1)} %refs_1_.5, bf16[512,128]{1,0:T(8,128)(2,1)} %refs_2_.5, bf16[512,128]{1,0:T(8,128)(2,1)} %refs_3_.5, bf16[8,4,64,128]{3,2,1,0:T(8,128)(2,1)S(1)} %all_to_all.10.refs_4_, ...), custom_call_target="tpu_custom_call" | custom-call | flops 2768240640 | bytes 1835008 | tf_op jit(solution)/shard_map/attend/pallas_call | solution.py:312
  54.0 0.3 collective-permute-start.7
  54.4 5.2 %collective-permute-start.5 = (bf16[512,384]{1,0:T(8,128)(2,1)S(1)}, bf16[512,384]{1,0:T(8,128)(2,1)S(1)}, u32[]{:S(2)}, u32[]{:S(2)}) collective-permute-start(bf16[512,384]{1,0:T(8,128)(2,1)S(1)} %get-tuple-element.24.refs_1_), channel_id=1, source_target_pairs={{0,1},{1,0},{2,3},{3,2},{4,5},{5,4},{6,7},{7,6},{8,9},{9,8},{10,11... | collective-permute-start | bytes 1179656 | tf_op jit(solution)/shard_map/ppermute | solution.py:384
  59.6 0.0 collective-permute-start.4
  59.6 5.5 %attend.5 = (bf16[512,384]{1,0:T(8,128)(2,1)S(1)}, bf16[2048,1280]{1,0:T(8,128)(2,1)S(1)}) custom-call(s32[1]{0:T(128)} %bitcast.first_ref, s32[128]{0:T(128)} %refs_0_.5, bf16[512,1024]{1,0:T(8,128)(2,1)} %refs_1_.5, bf16[512,128]{1,0:T(8,128)(2,1)} %refs_2_.5, bf16[512,128]{1,0:T(8,128)(2,1)} %refs_3_.5, bf16[8,4,64,128]{3,2,1,0:T(8,128)(2,1)S(1)} %all_to_all.10.refs_4_, ...), custom_call_target="tpu_custom_call" | custom-call | flops 2768240640 | bytes 1835008 | tf_op jit(solution)/shard_map/attend/pallas_call | solution.py:312
  65.2 0.6 collective-permute-start.6
  65.8 1.6 %collective-permute-start.3 = (bf16[512,384]{1,0:T(8,128)(2,1)S(1)}, bf16[512,384]{1,0:T(8,128)(2,1)S(1)}, u32[]{:S(2)}, u32[]{:S(2)}) collective-permute-start(bf16[512,384]{1,0:T(8,128)(2,1)S(1)} %get-tuple-element.23.refs_2_), channel_id=1, source_target_pairs={{0,2},{1,3},{2,0},{3,1},{4,6},{5,7},{6,4},{7,5},{8,10},{9,11},{10,... | collective-permute-start | bytes 1179656 | tf_op jit(solution)/shard_map/ppermute | solution.py:384
  67.4 0.0 collective-permute-done.4.refs_3_
  67.4 0.4 collective-permute-start.8
  67.7 0.0 collective-permute-done.7.refs_7_
  67.7 0.1 collective-permute-start.9
  67.9 0.0 collective-permute-done.5.refs_4_
  67.9 1.0 %collective-permute-done.8.refs_8_ = bf16[512,256]{1,0:T(8,128)(2,1)S(1)} collective-permute-done((bf16[512,256]{1,0:T(8,128)(2,1)S(1)}, bf16[512,256]{1,0:T(8,128)(2,1)S(1)}, u32[]{:S(2)}, u32[]{:S(2)}) %collective-permute-start.8) | collective-permute-done | bytes 262176 | tf_op jit(solution)/shard_map/ppermute | solution.py:384
  68.9 0.0 collective-permute-done.6.refs_5_
  68.9 4.2 %project.2.refs_3_ = f32[512,1280]{1,0:T(8,128)S(1)} custom-call(bf16[2048,1280]{1,0:T(8,128)(2,1)S(1)} %get-tuple-element.21.near_ref, bf16[2048,1280]{1,0:T(8,128)(2,1)S(1)} %get-tuple-element.22.far_ref, bf16[512,256]{1,0:T(8,128)(2,1)S(1)} %attend.4.refs_0_, bf16[512,384]{1,0:T(8,128)(2,1)S(1)} %get-tuple-element.24.refs_1_, ...), custom_call_target="tpu_custom_call" | custom-call | flops 655360 | bytes 655360 | tf_op jit(solution)/shard_map/project/pallas_call | solution.py:366
  73.2 3.5 %collective-permute-done.3.refs_0_ = bf16[512,384]{1,0:T(8,128)(2,1)S(1)} collective-permute-done((bf16[512,384]{1,0:T(8,128)(2,1)S(1)}, bf16[512,384]{1,0:T(8,128)(2,1)S(1)}, u32[]{:S(2)}, u32[]{:S(2)}) %collective-permute-start.3) | collective-permute-done | bytes 393248 | tf_op jit(solution)/shard_map/ppermute | solution.py:384
  76.7 0.7 collective-permute-start.10
  77.4 1.3 %collective-permute-done.10.refs_2_ = bf16[512,384]{1,0:T(8,128)(2,1)S(1)} collective-permute-done((bf16[512,384]{1,0:T(8,128)(2,1)S(1)}, bf16[512,384]{1,0:T(8,128)(2,1)S(1)}, u32[]{:S(2)}, u32[]{:S(2)}) %collective-permute-start.10) | collective-permute-done | bytes 393248 | tf_op jit(solution)/shard_map/ppermute | solution.py:384
  78.8 2.9 %project.3 = bf16[512,1280]{1,0:T(8,128)(2,1)} custom-call(bf16[2048,1280]{1,0:T(8,128)(2,1)S(1)} %get-tuple-element.21.near_ref, bf16[2048,1280]{1,0:T(8,128)(2,1)S(1)} %get-tuple-element.22.far_ref, bf16[512,384]{1,0:T(8,128)(2,1)S(1)} %collective-permute-done.3.refs_0_, bf16[512,384]{1,0:T(8,128)(2,1)S(1)} %collective-permute-done.9.refs_1_, ...), custom_call_target="tpu_custom_call" | custom-call | flops 655360 | bytes 655360 | tf_op jit(solution)/shard_map/project/pallas_call | solution.py:366
  (2 shorter events, 0.0 us)
Async XLA Ops:
  1.7 15.5 %all-to-all-start = ((bf16[8,2,64,128]{3,2,1,0:T(8,128)(2,1)}), bf16[8,2,64,128]{3,2,1,0:T(8,128)(2,1)S(1)}, u32[]{:S(2)}, u32[]{:S(2)}) async-start(bf16[8,2,64,128]{3,2,1,0:T(8,128)(2,1)} %pack.1), calls=%async_computation | async-start | bytes 524288 | tf_op jit(solution)/shard_map/all_to_all | solution.py:390
  18.0 7.9 %collective-permute-start = (bf16[4,64,128]{2,1,0:T(8,128)(2,1)S(1)}, bf16[4,64,128]{2,1,0:T(8,128)(2,1)S(1)}, u32[]{:S(2)}, u32[]{:S(2)}) collective-permute-start(bf16[4,64,128]{2,1,0:T(8,128)(2,1)S(1)} %get-tuple-element.19), channel_id=1, source_target_pairs={{0,32},{4,36},{8,40},{12,44},{16,48},{20,52},{24,56},{28,60},{32,6... | collective-permute-start | bytes 196616 | tf_op jit(solution)/shard_map/ppermute | solution.py:395
  19.4 6.5 %collective-permute-start.1 = (bf16[1,64,128]{2,1,0:T(8,128)(2,1)S(1)}, bf16[1,64,128]{2,1,0:T(8,128)(2,1)S(1)}, u32[]{:S(2)}, u32[]{:S(2)}) collective-permute-start(bf16[1,64,128]{2,1,0:T(8,128)(2,1)S(1)} %get-tuple-element.20), channel_id=1, source_target_pairs={{0,64},{4,68},{8,72},{12,76},{16,80},{20,84},{24,88},{28,92},{32,9... | collective-permute-start | bytes 49160 | tf_op jit(solution)/shard_map/ppermute | solution.py:395
  47.2 12.4 %collective-permute-start.2 = (bf16[512,256]{1,0:T(8,128)(2,1)S(1)}, bf16[512,256]{1,0:T(8,128)(2,1)S(1)}, u32[]{:S(2)}, u32[]{:S(2)}) collective-permute-start(bf16[512,256]{1,0:T(8,128)(2,1)S(1)} %attend.4.refs_0_), channel_id=1, source_target_pairs={{0,2},{1,3},{2,0},{3,1},{4,6},{5,7},{6,4},{7,5},{8,10},{9,11},{10,... | collective-permute-start | bytes 786440 | tf_op jit(solution)/shard_map/ppermute | solution.py:384
  54.0 13.7 %collective-permute-start.7 = (bf16[512,384]{1,0:T(8,128)(2,1)S(1)}, bf16[512,384]{1,0:T(8,128)(2,1)S(1)}, u32[]{:S(2)}, u32[]{:S(2)}) collective-permute-start(bf16[512,384]{1,0:T(8,128)(2,1)S(1)} %get-tuple-element.24.refs_1_), channel_id=1, source_target_pairs={{0,2},{1,3},{2,0},{3,1},{4,6},{5,7},{6,4},{7,5},{8,10},{9,11},{10,... | collective-permute-start | bytes 1179656 | tf_op jit(solution)/shard_map/ppermute | solution.py:384
  54.4 13.5 %collective-permute-start.5 = (bf16[512,384]{1,0:T(8,128)(2,1)S(1)}, bf16[512,384]{1,0:T(8,128)(2,1)S(1)}, u32[]{:S(2)}, u32[]{:S(2)}) collective-permute-start(bf16[512,384]{1,0:T(8,128)(2,1)S(1)} %get-tuple-element.24.refs_1_), channel_id=1, source_target_pairs={{0,1},{1,0},{2,3},{3,2},{4,5},{5,4},{6,7},{7,6},{8,9},{9,8},{10,11... | collective-permute-start | bytes 1179656 | tf_op jit(solution)/shard_map/ppermute | solution.py:384
  59.6 7.7 %collective-permute-start.4 = (bf16[512,256]{1,0:T(8,128)(2,1)S(1)}, bf16[512,256]{1,0:T(8,128)(2,1)S(1)}, u32[]{:S(2)}, u32[]{:S(2)}) collective-permute-start(bf16[512,256]{1,0:T(8,128)(2,1)S(1)} %attend.4.refs_0_), channel_id=1, source_target_pairs={{0,1},{1,0},{2,3},{3,2},{4,5},{5,4},{6,7},{7,6},{8,9},{9,8},{10,11... | collective-permute-start | bytes 786440 | tf_op jit(solution)/shard_map/ppermute | solution.py:384
  65.2 3.8 %collective-permute-start.6 = (bf16[512,384]{1,0:T(8,128)(2,1)S(1)}, bf16[512,384]{1,0:T(8,128)(2,1)S(1)}, u32[]{:S(2)}, u32[]{:S(2)}) collective-permute-start(bf16[512,384]{1,0:T(8,128)(2,1)S(1)} %get-tuple-element.23.refs_2_), channel_id=1, source_target_pairs={{0,1},{1,0},{2,3},{3,2},{4,5},{5,4},{6,7},{7,6},{8,9},{9,8},{10,11... | collective-permute-start | bytes 1179656 | tf_op jit(solution)/shard_map/ppermute | solution.py:384
  65.8 10.9 %collective-permute-start.3 = (bf16[512,384]{1,0:T(8,128)(2,1)S(1)}, bf16[512,384]{1,0:T(8,128)(2,1)S(1)}, u32[]{:S(2)}, u32[]{:S(2)}) collective-permute-start(bf16[512,384]{1,0:T(8,128)(2,1)S(1)} %get-tuple-element.23.refs_2_), channel_id=1, source_target_pairs={{0,2},{1,3},{2,0},{3,1},{4,6},{5,7},{6,4},{7,5},{8,10},{9,11},{10,... | collective-permute-start | bytes 1179656 | tf_op jit(solution)/shard_map/ppermute | solution.py:384
  67.4 1.5 %collective-permute-start.8 = (bf16[512,256]{1,0:T(8,128)(2,1)S(1)}, bf16[512,256]{1,0:T(8,128)(2,1)S(1)}, u32[]{:S(2)}, u32[]{:S(2)}) collective-permute-start(bf16[512,256]{1,0:T(8,128)(2,1)S(1)} %collective-permute-done.2.refs_7_.refs_6_), channel_id=1, source_target_pairs={{0,1},{1,0},{2,3},{3,2},{4,5},{5,4},{6,7},{7,6},{8,9},{9,8},{10,11... | collective-permute-start | bytes 786440 | tf_op jit(solution)/shard_map/ppermute | solution.py:384
  67.7 9.7 %collective-permute-start.9 = (bf16[512,384]{1,0:T(8,128)(2,1)S(1)}, bf16[512,384]{1,0:T(8,128)(2,1)S(1)}, u32[]{:S(2)}, u32[]{:S(2)}) collective-permute-start(bf16[512,384]{1,0:T(8,128)(2,1)S(1)} %collective-permute-done.7.refs_7_), channel_id=1, source_target_pairs={{0,1},{1,0},{2,3},{3,2},{4,5},{5,4},{6,7},{7,6},{8,9},{9,8},{10,11... | collective-permute-start | bytes 1179656 | tf_op jit(solution)/shard_map/ppermute | solution.py:384
  76.7 2.1 %collective-permute-start.10 = (bf16[512,384]{1,0:T(8,128)(2,1)S(1)}, bf16[512,384]{1,0:T(8,128)(2,1)S(1)}, u32[]{:S(2)}, u32[]{:S(2)}) collective-permute-start(bf16[512,384]{1,0:T(8,128)(2,1)S(1)} %collective-permute-done.3.refs_0_), channel_id=1, source_target_pairs={{0,1},{1,0},{2,3},{3,2},{4,5},{5,4},{6,7},{7,6},{8,9},{9,8},{10,11... | collective-permute-start | bytes 1179656 | tf_op jit(solution)/shard_map/ppermute | solution.py:384

commit v8 on v7

--- a/solution.py
+++ b/solution.py
@@ -16,7 +16,8 @@
 LISTED = (7, 3, 6, 2, 5, 1, 4, 0)
 PIECE = SEG_LEN // ROW
 PATH = LEVELS * SEG_LEN
-STACK = LEVELS * PIECE
+FAR = LEVELS - 1
+STACK = FAR * PIECE
 MASKED = -1e30
 EXP2_SCALE = math.log2(math.e) * HEAD_DIM ** (-0.5)
 SMALL_VMEM = 6 * 1024 * 1024
@@ -108,7 +109,7 @@
         return pieces_ref[slot_of(jnp.clip(level_of(path, depth, level) - base, 0, ROW_SEGS - 1))]
 
     path, depth = path_of(parents_ref, jnp.minimum(base + ROW_SEGS, last))
-    for level in range(LEVELS):
+    for level in range(FAR):
         next_ref[level] = held(path, depth, level)
     path, depth = path_of(parents_ref, jnp.minimum(base + 2 * ROW_SEGS, last))
     second_ref[0] = held(path, depth, 0)
@@ -118,7 +119,7 @@
     shape = lambda n: jax.ShapeDtypeStruct((n,) + pieces.shape[1:], pieces.dtype)
     return pl.pallas_call(
         carry_kernel,
-        out_shape=(shape(LEVELS), shape(1)),
+        out_shape=(shape(FAR), shape(1)),
         in_specs=[SMEM, HBM, VMEM],
         out_specs=(VMEM, VMEM),
         scratch_shapes=[pltpu.SMEM(parents.shape, parents.dtype), pltpu.SemaphoreType.DMA],
@@ -129,14 +130,32 @@
 
 
 def pick_kernel(
-    first_ref, source_ref, pieces_ref, inside_ref, next_ref, second_ref, parents_ref, sem
+    first_ref,
+    source_ref,
+    key_ref,
+    value_ref,
+    pieces_ref,
+    inside_ref,
+    next_ref,
+    second_ref,
+    deep_ref,
+    parents_ref,
+    pair_ref,
+    sem,
+    pair_sem,
 ):
+    copies = [
+        pltpu.make_async_copy(source, pair_ref.at[i], pair_sem.at[i])
+        for i, source in enumerate([key_ref, value_ref])
+    ]
+    for copy in copies:
+        copy.start()
     bring_parents(source_ref, parents_ref, sem)
     base = row_start(first_ref)
     ones = lambda on: jnp.full((FLAG_ROWS, HEAD_DIM), on, jnp.float32).astype(jnp.bfloat16)
     for target, place in enumerate(LISTED):
         path, depth = path_of(parents_ref, base + 2 * place)
-        for level in range(LEVELS):
+        for level in range(FAR):
             seg = level_of(path, depth, level)
             within = seg >= base
             piece = pieces_ref[slot_of(jnp.maximum(seg - base, 0))]
@@ -145,28 +164,40 @@
             next_ref[target, level] = ones(jnp.where(before, 1.0, 0.0))
             if level == 0:
                 second_ref[target] = ones(jnp.where(seg < base - ROW_SEGS, 1.0, 0.0))
-
-
-def pick(first, parents, pieces):
+    _, depth = path_of(parents_ref, first_ref[0] + 1)
+    start = jnp.where(depth == FAR, SEG_LEN, 0)
+    rows = pl.ds(pl.multiple_of(start, SEG_LEN), SEG_LEN)
+    for i, copy in enumerate(copies):
+        copy.wait()
+        deep_ref[i] = pair_ref[i, rows]
+
+
+def pick(first, parents, keys, values, pieces):
     shape = lambda *dims: jax.ShapeDtypeStruct(dims, pieces.dtype)
     return pl.pallas_call(
         pick_kernel,
         out_shape=(
-            shape(ROW, LEVELS, *pieces.shape[1:]),
-            shape(ROW, LEVELS, FLAG_ROWS, HEAD_DIM),
+            shape(ROW, FAR, *pieces.shape[1:]),
+            shape(ROW, FAR, FLAG_ROWS, HEAD_DIM),
             shape(ROW, FLAG_ROWS, HEAD_DIM),
+            shape(2, SEG_LEN, HEAD_DIM),
         ),
-        in_specs=[SMEM, HBM, VMEM],
-        out_specs=(VMEM, VMEM, VMEM),
-        scratch_shapes=[pltpu.SMEM(parents.shape, parents.dtype), pltpu.SemaphoreType.DMA],
+        in_specs=[SMEM, HBM, HBM, HBM, VMEM],
+        out_specs=(VMEM,) * 4,
+        scratch_shapes=[
+            pltpu.SMEM(parents.shape, parents.dtype),
+            pltpu.VMEM((2,) + keys.shape, keys.dtype),
+            pltpu.SemaphoreType.DMA,
+            pltpu.SemaphoreType.DMA((2,)),
+        ],
         compiler_params=pltpu.CompilerParams(vmem_limit_bytes=SMALL_VMEM),
         cost_estimate=pl.CostEstimate(flops=0, bytes_accessed=1 << 20, transcendentals=0),
         name="pick",
-    )(first, in_hbm(parents), pieces)
+    )(first, in_hbm(parents), in_hbm(keys), in_hbm(values), pieces)
 
 
 def merge_kernel(inside_ref, on_next_ref, on_second_ref, next_ref, second_ref, picked_ref):
-    for level in range(LEVELS):
+    for level in range(FAR):
         for at in range(0, 2 * PIECE, FLAG_ROWS):
             rows = pl.ds(at, FLAG_ROWS)
             carried = next_ref[level, rows]
@@ -191,7 +222,7 @@
 
 
 def attend_kernel(first_head, blocks, first_ref, *refs):
-    sources, (far_ref, *refs) = refs[:4], refs[4:]
+    sources, (far_ref, deep_ref, *refs) = refs[:4], refs[4:]
     if blocks:
         me_ref, weight_ref = refs[:2]
         weight_sem = refs.pop()
@@ -217,10 +248,12 @@
         return jnp.concatenate([values, jnp.ones_like(values)], axis=1)
 
     for piece in range(ROW):
-        for level in range(LEVELS):
+        for level in range(FAR):
             rows = pl.ds(piece * STACK + level * PIECE, PIECE)
             path_key_ref[rows, :HEAD_DIM] = far_ref[piece, level, :PIECE]
             path_value_ref[rows, :HEAD_DIM] = far_ref[piece, level, PIECE:]
+    path_key_ref[FAR * SEG_LEN :, :HEAD_DIM] = deep_ref[0]
+    path_value_ref[FAR * SEG_LEN :, :HEAD_DIM] = deep_ref[1]
     path_value_ref[:, HEAD_DIM:] = jnp.ones((PATH, HEAD_DIM), jnp.bfloat16)
     for copy in fetches:
         copy.wait()
@@ -230,7 +263,7 @@
     follows = jnp.where(parents_ref[first + 1] == first, 0.0, MASKED)
     row = lax.broadcasted_iota(jnp.int32, (PATH, HEAD_DIM), 0)
     lane = lax.broadcasted_iota(jnp.int32, (PATH, HEAD_DIM), 1)
-    level = lax.rem(row // PIECE, LEVELS)
+    level = jnp.where(row < FAR * SEG_LEN, lax.rem(row // PIECE, FAR), FAR)
     limit = jnp.where(lane == 0, depth0, jnp.where(lane == 1, jnp.minimum(depth0, depth1), LEVELS))
     path_key_ref[:, HEAD_DIM:] = jnp.where(level < limit, 0.0, MASKED).astype(jnp.bfloat16)
     path_keys, path_values = path_key_ref[...], path_value_ref[...]
@@ -288,11 +321,11 @@
     return copies
 
 
-def attend(first, parents, queries, keys, values, far, first_head, heads, blocks, bring, after):
+def attend(first, parents, queries, keys, values, far, deep, first_head, heads, blocks, bring, after):
     rows = queries.shape[0]
     pairs = heads * rows * (PATH + SEG_LEN + SEG_LEN // 2)
     out_shape = [jax.ShapeDtypeStruct((rows, heads * HEAD_DIM), jnp.bfloat16)]
-    in_specs = [SMEM] + [HBM] * 4 + [VMEM]
+    in_specs = [SMEM] + [HBM] * 4 + [VMEM, VMEM]
     scratch = [pltpu.VMEM((PATH, 2 * HEAD_DIM), jnp.bfloat16)] * 2 + [
         pltpu.SMEM(parents.shape, parents.dtype),
         pltpu.VMEM((rows, heads * HEAD_DIM), queries.dtype),
@@ -329,6 +362,7 @@
         in_hbm(keys),
         in_hbm(values),
         far,
+        deep,
         *bring,
         *after,
     )
@@ -400,7 +434,8 @@
     first = (lax.axis_index("dp") * 2).astype(jnp.int32).reshape(1)
     pieces = trade(pack(key_proj, value_proj)).reshape(ROW_SEGS, 2 * PIECE, HEAD_DIM)
     to_next, to_second = carry_out(first, parents, pieces)
-    inside = pick(first, parents, pieces)
+    *inside, deep = pick(first, parents, key_proj, value_proj, pieces)
+    deep = onward(deep, 1)
     far = trade(merge(*inside, onward(to_next, ROW), onward(to_second, 2 * ROW)))
 
     width = queries.shape[1]
@@ -409,7 +444,7 @@
     for c, (size, blocks) in enumerate([(2, ()), (3, (0, 1)), (3, (2, 3))]):
         after = [across[c - 2]] if c >= 2 else []
         part, *brought = attend(
-            first, parents, queries, key_proj, value_proj, far, head, size, blocks, bring, after
+            first, parents, queries, key_proj, value_proj, far, deep, head, size, blocks, bring, after
         )
         weights += brought
         own.append(part)

time: 82 us -> 82.8 us (level)
  blocking collectives: 17.6 us -> 0 us
  waiting for transfers between devices: 14.2 us -> 24.3 us
  starting transfers between devices: 24.1 us -> 31.6 us
    all_to_all x1 -> x0, blocking collectives: 17.6 us -> none  [trade(): lax.all_to_all(pieces, 'dp', 0, 0, tiled=True, axis_index_groups=rows)]
    ppermute x2 -> x3, waiting for transfers between devices: 2.53 us -> 12.5 us  [onward(): lax.ppermute(piece, 'dp', [(i, (i + step) % devices) for i in range(devic...]
    all_to_all x1 -> x2, starting transfers between devices: 9.77 us -> 17.7 us  [trade(): lax.all_to_all(pieces, 'dp', 0, 0, tiled=True, axis_index_groups=rows)]
    ppermute x9, starting transfers between devices: 10.4 us -> 8.73 us  [swap(): return lax.ppermute(part, 'tensor', [(i, i ^ bit) for i in range(size)])]
    ppermute x2 -> x3, starting transfers between devices: 3.99 us -> 5.18 us  [onward(): lax.ppermute(piece, 'dp', [(i, (i + step) % devices) for i in range(devic...]
    all_to_all x1 -> x2, waiting for transfers between devices: 5.73 us -> 5.73 us  [trade(): lax.all_to_all(pieces, 'dp', 0, 0, tiled=True, axis_index_groups=rows)]
  transfers between devices with their start and end apart: 12 -> 14, of which waited for: 5 -> 6; matrix products, arithmetic and copies ran while one was open for 0% -> 0% of each run, Pallas kernels for 20% -> 20%
where the time goes in v8:
time: 82.8 us; the launch traced here: 82.5 us
  starting transfers between devices  31.6 us (38%)
  Pallas kernels  26.5 us (32%)
  waiting for transfers between devices  24.3 us (29%)
    all_to_all x2, starting transfers between devices, trade(): lax.all_to_all(pieces, 'dp', 0, 0, tiled=True, axis_index_groups=rows)  17.7 us
    pallas_call x3, Pallas kernels, attend(): pl.pallas_call(functools.partial(attend_kernel, first_head, blocks), out_...  14.7 us
    ppermute x3, waiting for transfers between devices, onward(): lax.ppermute(piece, 'dp', [(i, (i + step) % devices) for i in range(devic...  12.5 us
    ppermute x9, starting transfers between devices, swap(): return lax.ppermute(part, 'tensor', [(i, i ^ bit) for i in range(size)])  8.73 us
    pallas_call x2, Pallas kernels, project(): pl.pallas_call(functools.partial(project_kernel, [len(g) for g in groups]...  7.16 us
    ppermute x9, waiting for transfers between devices, swap(): return lax.ppermute(part, 'tensor', [(i, i ^ bit) for i in range(size)])  6.14 us
    all_to_all x2, waiting for transfers between devices, trade(): lax.all_to_all(pieces, 'dp', 0, 0, tiled=True, axis_index_groups=rows)  5.73 us
    ppermute x3, starting transfers between devices, onward(): lax.ppermute(piece, 'dp', [(i, (i + step) % devices) for i in range(devic...  5.18 us
  transfers between devices with their start and end apart: 14, of which 6 were waited for; matrix products, arithmetic and copies ran while one was open for 0% of the time, Pallas kernels for 20%

profile of v8, /device:TPU:1, one launch (start us, length us, event | category | flops | bytes accessed | tf_op | source)
XLA Modules:
  0.0 82.5 jit_solution(14992467154249694135)
XLA Ops:
  0.0 1.7 %pack.1 = bf16[8,2,64,128]{3,2,1,0:T(8,128)(2,1)} custom-call(bf16[512,128]{1,0:T(8,128)(2,1)} %refs_2_.5, bf16[512,128]{1,0:T(8,128)(2,1)} %refs_3_.5), custom_call_target="tpu_custom_call" | custom-call | bytes 524288 | tf_op jit(solution)/shard_map/pack/pallas_call | solution.py:75
  1.7 9.8 %all-to-all-start = ((bf16[8,2,64,128]{3,2,1,0:T(8,128)(2,1)}), bf16[8,2,64,128]{3,2,1,0:T(8,128)(2,1)S(1)}, u32[]{:S(2)}, u32[]{:S(2)}) async-start(bf16[8,2,64,128]{3,2,1,0:T(8,128)(2,1)} %pack.1), calls=%async_computation | async-start | bytes 524288 | tf_op jit(solution)/shard_map/all_to_all | solution.py:424
  11.5 5.7 %all-to-all-done = bf16[8,2,64,128]{3,2,1,0:T(8,128)(2,1)S(1)} async-done(((bf16[8,2,64,128]{3,2,1,0:T(8,128)(2,1)}), bf16[8,2,64,128]{3,2,1,0:T(8,128)(2,1)S(1)}, u32[]{:S(2)}, u32[]{:S(2)}) %all-to-all-start) | async-done | bytes 262176 | tf_op jit(solution)/shard_map/all_to_all | solution.py:424
  17.2 0.8 carry_out.1
  18.0 1.4 %collective-permute-start = (bf16[3,64,128]{2,1,0:T(8,128)(2,1)S(1)}, bf16[3,64,128]{2,1,0:T(8,128)(2,1)S(1)}, u32[]{:S(2)}, u32[]{:S(2)}) collective-permute-start(bf16[3,64,128]{2,1,0:T(8,128)(2,1)S(1)} %get-tuple-element.20), channel_id=1, source_target_pairs={{0,32},{4,36},{8,40},{12,44},{16,48},{20,52},{24,56},{28,60},{32,6... | collective-permute-start | bytes 147464 | tf_op jit(solution)/shard_map/ppermute | solution.py:429
  19.4 2.6 %collective-permute-start.1 = (bf16[1,64,128]{2,1,0:T(8,128)(2,1)S(1)}, bf16[1,64,128]{2,1,0:T(8,128)(2,1)S(1)}, u32[]{:S(2)}, u32[]{:S(2)}) collective-permute-start(bf16[1,64,128]{2,1,0:T(8,128)(2,1)S(1)} %get-tuple-element.21), channel_id=1, source_target_pairs={{0,64},{4,68},{8,72},{12,76},{16,80},{20,84},{24,88},{28,92},{32,9... | collective-permute-start | bytes 49160 | tf_op jit(solution)/shard_map/ppermute | solution.py:429
  22.0 1.4 %pick.1 = (bf16[8,3,64,128]{3,2,1,0:T(8,128)(2,1)S(1)}, bf16[8,3,16,128]{3,2,1,0:T(8,128)(2,1)S(1)}, bf16[8,16,128]{2,1,0:T(8,128)(2,1)S(1)}, bf16[2,256,128]{2,1,0:T(8,128)(2,1)S(1)}) custom-call(s32[1]{0:T(128)} %bitcast.first_ref, s32[128]{0:T(128)} %refs_0_.5, bf16[512,128]{1,0:T(8,128)(2,1)} %refs_2_.5, bf16[512,128]{1,0:T(8,128)(2,1)} %refs_3_.5, ...), custom_call_target="tpu_custom_call" | custom-call | bytes 1048576 | tf_op jit(solution)/shard_map/pick/pallas_call | solution.py:177
  23.4 2.5 %collective-permute-done.1.second_ref = bf16[1,64,128]{2,1,0:T(8,128)(2,1)S(1)} collective-permute-done((bf16[1,64,128]{2,1,0:T(8,128)(2,1)S(1)}, bf16[1,64,128]{2,1,0:T(8,128)(2,1)S(1)}, u32[]{:S(2)}, u32[]{:S(2)}) %collective-permute-start.1) | collective-permute-done | bytes 16416 | tf_op jit(solution)/shard_map/ppermute | solution.py:429
  25.9 0.0 collective-permute-done.next_ref
  25.9 0.8 %merge.1 = bf16[8,3,64,128]{3,2,1,0:T(8,128)(2,1)} custom-call(bf16[8,3,64,128]{3,2,1,0:T(8,128)(2,1)S(1)} %get-tuple-element.17.inside_ref, bf16[8,3,16,128]{3,2,1,0:T(8,128)(2,1)S(1)} %get-tuple-element.18.on_next_ref, bf16[8,16,128]{2,1,0:T(8,128)(2,1)S(1)} %get-tuple-element.19.on_second_ref, bf16[3,64,128]{2,1,0:T(8,128)(2,1)S(1)} %collective-permute-done.next_ref, ...), custom_call_target="tpu_custom_call" | custom-call | bytes 1048576 | tf_op jit(solution)/shard_map/merge/pallas_call | solution.py:213
  26.7 7.9 %all-to-all-start.1 = ((bf16[8,3,64,128]{3,2,1,0:T(8,128)(2,1)}), bf16[8,3,64,128]{3,2,1,0:T(8,128)(2,1)S(1)}, u32[]{:S(2)}, u32[]{:S(2)}) async-start(bf16[8,3,64,128]{3,2,1,0:T(8,128)(2,1)} %merge.1), calls=%async_computation.1 | async-start | bytes 786432 | tf_op jit(solution)/shard_map/all_to_all | solution.py:424
  34.6 1.2 %collective-permute-start.2 = (bf16[2,256,128]{2,1,0:T(8,128)(2,1)S(1)}, bf16[2,256,128]{2,1,0:T(8,128)(2,1)S(1)}, u32[]{:S(2)}, u32[]{:S(2)}) collective-permute-start(bf16[2,256,128]{2,1,0:T(8,128)(2,1)S(1)} %get-tuple-element.22), channel_id=1, source_target_pairs={{0,4},{4,8},{8,12},{12,16},{16,20},{20,24},{24,28},{28,32},{32,36}... | collective-permute-start | bytes 393224 | tf_op jit(solution)/shard_map/ppermute | solution.py:429
  35.8 10.0 %collective-permute-done.2.refs_5_ = bf16[2,256,128]{2,1,0:T(8,128)(2,1)S(1)} collective-permute-done((bf16[2,256,128]{2,1,0:T(8,128)(2,1)S(1)}, bf16[2,256,128]{2,1,0:T(8,128)(2,1)S(1)}, u32[]{:S(2)}, u32[]{:S(2)}) %collective-permute-start.2) | collective-permute-done | bytes 131104 | tf_op jit(solution)/shard_map/ppermute | solution.py:429
  45.8 0.0 all-to-all-done.1.refs_4_
  45.8 3.7 %attend.4.refs_0_ = bf16[512,256]{1,0:T(8,128)(2,1)S(1)} custom-call(s32[1]{0:T(128)} %bitcast.first_ref, s32[128]{0:T(128)} %refs_0_.5, bf16[512,1024]{1,0:T(8,128)(2,1)} %refs_1_.5, bf16[512,128]{1,0:T(8,128)(2,1)} %refs_2_.5, bf16[512,128]{1,0:T(8,128)(2,1)} %refs_3_.5, bf16[8,3,64,128]{3,2,1,0:T(8,128)(2,1)S(1)} %all-to-all-done.1.refs_4_, ...), custom_call_target="tpu_custom_call" | custom-call | flops 1845493760 | bytes 1572864 | tf_op jit(solution)/shard_map/attend/pallas_call | solution.py:345
  49.4 1.1 %collective-permute-start.3 = (bf16[512,256]{1,0:T(8,128)(2,1)S(1)}, bf16[512,256]{1,0:T(8,128)(2,1)S(1)}, u32[]{:S(2)}, u32[]{:S(2)}) collective-permute-start(bf16[512,256]{1,0:T(8,128)(2,1)S(1)} %attend.4.refs_0_), channel_id=1, source_target_pairs={{0,2},{1,3},{2,0},{3,1},{4,6},{5,7},{6,4},{7,5},{8,10},{9,11},{10,... | collective-permute-start | bytes 786440 | tf_op jit(solution)/shard_map/ppermute | solution.py:418
  50.5 5.5 %attend.3 = (bf16[512,384]{1,0:T(8,128)(2,1)S(1)}, bf16[2048,1280]{1,0:T(8,128)(2,1)S(1)}) custom-call(s32[1]{0:T(128)} %bitcast.first_ref, s32[128]{0:T(128)} %refs_0_.5, bf16[512,1024]{1,0:T(8,128)(2,1)} %refs_1_.5, bf16[512,128]{1,0:T(8,128)(2,1)} %refs_2_.5, bf16[512,128]{1,0:T(8,128)(2,1)} %refs_3_.5, ...), custom_call_target="tpu_custom_call" | custom-call | flops 2768240640 | bytes 1835008 | tf_op jit(solution)/shard_map/attend/pallas_call | solution.py:345
  56.0 0.6 collective-permute-start.8
  56.6 4.0 %collective-permute-start.6 = (bf16[512,384]{1,0:T(8,128)(2,1)S(1)}, bf16[512,384]{1,0:T(8,128)(2,1)S(1)}, u32[]{:S(2)}, u32[]{:S(2)}) collective-permute-start(bf16[512,384]{1,0:T(8,128)(2,1)S(1)} %get-tuple-element.26.refs_1_), channel_id=1, source_target_pairs={{0,1},{1,0},{2,3},{3,2},{4,5},{5,4},{6,7},{7,6},{8,9},{9,8},{10,11... | collective-permute-start | bytes 1179656 | tf_op jit(solution)/shard_map/ppermute | solution.py:418
  60.6 0.0 collective-permute-start.5
  60.6 0.0 collective-permute-done.3.refs_8_.refs_6_
  60.6 5.5 %attend.5 = (bf16[512,384]{1,0:T(8,128)(2,1)S(1)}, bf16[2048,1280]{1,0:T(8,128)(2,1)S(1)}) custom-call(s32[1]{0:T(128)} %bitcast.first_ref, s32[128]{0:T(128)} %refs_0_.5, bf16[512,1024]{1,0:T(8,128)(2,1)} %refs_1_.5, bf16[512,128]{1,0:T(8,128)(2,1)} %refs_2_.5, bf16[512,128]{1,0:T(8,128)(2,1)} %refs_3_.5, ...), custom_call_target="tpu_custom_call" | custom-call | flops 2768240640 | bytes 1835008 | tf_op jit(solution)/shard_map/attend/pallas_call | solution.py:345
  66.1 0.6 collective-permute-start.7
  66.7 1.1 %collective-permute-start.4 = (bf16[512,384]{1,0:T(8,128)(2,1)S(1)}, bf16[512,384]{1,0:T(8,128)(2,1)S(1)}, u32[]{:S(2)}, u32[]{:S(2)}) collective-permute-start(bf16[512,384]{1,0:T(8,128)(2,1)S(1)} %get-tuple-element.25.refs_2_), channel_id=1, source_target_pairs={{0,2},{1,3},{2,0},{3,1},{4,6},{5,7},{6,4},{7,5},{8,10},{9,11},{10,... | collective-permute-start | bytes 1179656 | tf_op jit(solution)/shard_map/ppermute | solution.py:418
  67.8 0.4 collective-permute-start.9
  68.2 0.1 collective-permute-start.10
  68.3 1.0 %collective-permute-done.9.refs_8_ = bf16[512,256]{1,0:T(8,128)(2,1)S(1)} collective-permute-done((bf16[512,256]{1,0:T(8,128)(2,1)S(1)}, bf16[512,256]{1,0:T(8,128)(2,1)S(1)}, u32[]{:S(2)}, u32[]{:S(2)}) %collective-permute-start.9) | collective-permute-done | bytes 262176 | tf_op jit(solution)/shard_map/ppermute | solution.py:418
  69.3 4.2 %project.2.refs_3_ = f32[512,1280]{1,0:T(8,128)S(1)} custom-call(bf16[2048,1280]{1,0:T(8,128)(2,1)S(1)} %get-tuple-element.23.near_ref, bf16[2048,1280]{1,0:T(8,128)(2,1)S(1)} %get-tuple-element.24.far_ref, bf16[512,256]{1,0:T(8,128)(2,1)S(1)} %attend.4.refs_0_, bf16[512,384]{1,0:T(8,128)(2,1)S(1)} %get-tuple-element.26.refs_1_, ...), custom_call_target="tpu_custom_call" | custom-call | flops 655360 | bytes 655360 | tf_op jit(solution)/shard_map/project/pallas_call | solution.py:400
  73.6 3.8 %collective-permute-done.4.refs_0_ = bf16[512,384]{1,0:T(8,128)(2,1)S(1)} collective-permute-done((bf16[512,384]{1,0:T(8,128)(2,1)S(1)}, bf16[512,384]{1,0:T(8,128)(2,1)S(1)}, u32[]{:S(2)}, u32[]{:S(2)}) %collective-permute-start.4) | collective-permute-done | bytes 393248 | tf_op jit(solution)/shard_map/ppermute | solution.py:418
  77.4 0.9 %collective-permute-start.11 = (bf16[512,384]{1,0:T(8,128)(2,1)S(1)}, bf16[512,384]{1,0:T(8,128)(2,1)S(1)}, u32[]{:S(2)}, u32[]{:S(2)}) collective-permute-start(bf16[512,384]{1,0:T(8,128)(2,1)S(1)} %collective-permute-done.4.refs_0_), channel_id=1, source_target_pairs={{0,1},{1,0},{2,3},{3,2},{4,5},{5,4},{6,7},{7,6},{8,9},{9,8},{10,11... | collective-permute-start | bytes 1179656 | tf_op jit(solution)/shard_map/ppermute | solution.py:418
  78.2 1.3 %collective-permute-done.11.refs_2_ = bf16[512,384]{1,0:T(8,128)(2,1)S(1)} collective-permute-done((bf16[512,384]{1,0:T(8,128)(2,1)S(1)}, bf16[512,384]{1,0:T(8,128)(2,1)S(1)}, u32[]{:S(2)}, u32[]{:S(2)}) %collective-permute-start.11) | collective-permute-done | bytes 393248 | tf_op jit(solution)/shard_map/ppermute | solution.py:418
  79.6 2.9 %project.3 = bf16[512,1280]{1,0:T(8,128)(2,1)} custom-call(bf16[2048,1280]{1,0:T(8,128)(2,1)S(1)} %get-tuple-element.23.near_ref, bf16[2048,1280]{1,0:T(8,128)(2,1)S(1)} %get-tuple-element.24.far_ref, bf16[512,384]{1,0:T(8,128)(2,1)S(1)} %collective-permute-done.4.refs_0_, bf16[512,384]{1,0:T(8,128)(2,1)S(1)} %collective-permute-done.10.refs_1_, ...), custom_call_target="tpu_custom_call" | custom-call | flops 655360 | bytes 655360 | tf_op jit(solution)/shard_map/project/pallas_call | solution.py:400
  (5 shorter events, 0.0 us)
Async XLA Ops:
  1.7 15.5 %all-to-all-start = ((bf16[8,2,64,128]{3,2,1,0:T(8,128)(2,1)}), bf16[8,2,64,128]{3,2,1,0:T(8,128)(2,1)S(1)}, u32[]{:S(2)}, u32[]{:S(2)}) async-start(bf16[8,2,64,128]{3,2,1,0:T(8,128)(2,1)} %pack.1), calls=%async_computation | async-start | bytes 524288 | tf_op jit(solution)/shard_map/all_to_all | solution.py:424
  18.0 7.9 %collective-permute-start = (bf16[3,64,128]{2,1,0:T(8,128)(2,1)S(1)}, bf16[3,64,128]{2,1,0:T(8,128)(2,1)S(1)}, u32[]{:S(2)}, u32[]{:S(2)}) collective-permute-start(bf16[3,64,128]{2,1,0:T(8,128)(2,1)S(1)} %get-tuple-element.20), channel_id=1, source_target_pairs={{0,32},{4,36},{8,40},{12,44},{16,48},{20,52},{24,56},{28,60},{32,6... | collective-permute-start | bytes 147464 | tf_op jit(solution)/shard_map/ppermute | solution.py:429
  19.4 6.5 %collective-permute-start.1 = (bf16[1,64,128]{2,1,0:T(8,128)(2,1)S(1)}, bf16[1,64,128]{2,1,0:T(8,128)(2,1)S(1)}, u32[]{:S(2)}, u32[]{:S(2)}) collective-permute-start(bf16[1,64,128]{2,1,0:T(8,128)(2,1)S(1)} %get-tuple-element.21), channel_id=1, source_target_pairs={{0,64},{4,68},{8,72},{12,76},{16,80},{20,84},{24,88},{28,92},{32,9... | collective-permute-start | bytes 49160 | tf_op jit(solution)/shard_map/ppermute | solution.py:429
  26.7 19.1 %all-to-all-start.1 = ((bf16[8,3,64,128]{3,2,1,0:T(8,128)(2,1)}), bf16[8,3,64,128]{3,2,1,0:T(8,128)(2,1)S(1)}, u32[]{:S(2)}, u32[]{:S(2)}) async-start(bf16[8,3,64,128]{3,2,1,0:T(8,128)(2,1)} %merge.1), calls=%async_computation.1 | async-start | bytes 786432 | tf_op jit(solution)/shard_map/all_to_all | solution.py:424
  34.6 11.2 %collective-permute-start.2 = (bf16[2,256,128]{2,1,0:T(8,128)(2,1)S(1)}, bf16[2,256,128]{2,1,0:T(8,128)(2,1)S(1)}, u32[]{:S(2)}, u32[]{:S(2)}) collective-permute-start(bf16[2,256,128]{2,1,0:T(8,128)(2,1)S(1)} %get-tuple-element.22), channel_id=1, source_target_pairs={{0,4},{4,8},{8,12},{12,16},{16,20},{20,24},{24,28},{28,32},{32,36}... | collective-permute-start | bytes 393224 | tf_op jit(solution)/shard_map/ppermute | solution.py:429
  49.4 11.1 %collective-permute-start.3 = (bf16[512,256]{1,0:T(8,128)(2,1)S(1)}, bf16[512,256]{1,0:T(8,128)(2,1)S(1)}, u32[]{:S(2)}, u32[]{:S(2)}) collective-permute-start(bf16[512,256]{1,0:T(8,128)(2,1)S(1)} %attend.4.refs_0_), channel_id=1, source_target_pairs={{0,2},{1,3},{2,0},{3,1},{4,6},{5,7},{6,4},{7,5},{8,10},{9,11},{10,... | collective-permute-start | bytes 786440 | tf_op jit(solution)/shard_map/ppermute | solution.py:418
  56.0 12.1 %collective-permute-start.8 = (bf16[512,384]{1,0:T(8,128)(2,1)S(1)}, bf16[512,384]{1,0:T(8,128)(2,1)S(1)}, u32[]{:S(2)}, u32[]{:S(2)}) collective-permute-start(bf16[512,384]{1,0:T(8,128)(2,1)S(1)} %get-tuple-element.26.refs_1_), channel_id=1, source_target_pairs={{0,2},{1,3},{2,0},{3,1},{4,6},{5,7},{6,4},{7,5},{8,10},{9,11},{10,... | collective-permute-start | bytes 1179656 | tf_op jit(solution)/shard_map/ppermute | solution.py:418
  56.6 11.7 %collective-permute-start.6 = (bf16[512,384]{1,0:T(8,128)(2,1)S(1)}, bf16[512,384]{1,0:T(8,128)(2,1)S(1)}, u32[]{:S(2)}, u32[]{:S(2)}) collective-permute-start(bf16[512,384]{1,0:T(8,128)(2,1)S(1)} %get-tuple-element.26.refs_1_), channel_id=1, source_target_pairs={{0,1},{1,0},{2,3},{3,2},{4,5},{5,4},{6,7},{7,6},{8,9},{9,8},{10,11... | collective-permute-start | bytes 1179656 | tf_op jit(solution)/shard_map/ppermute | solution.py:418
  60.6 7.2 %collective-permute-start.5 = (bf16[512,256]{1,0:T(8,128)(2,1)S(1)}, bf16[512,256]{1,0:T(8,128)(2,1)S(1)}, u32[]{:S(2)}, u32[]{:S(2)}) collective-permute-start(bf16[512,256]{1,0:T(8,128)(2,1)S(1)} %attend.4.refs_0_), channel_id=1, source_target_pairs={{0,1},{1,0},{2,3},{3,2},{4,5},{5,4},{6,7},{7,6},{8,9},{9,8},{10,11... | collective-permute-start | bytes 786440 | tf_op jit(solution)/shard_map/ppermute | solution.py:418
  66.1 3.3 %collective-permute-start.7 = (bf16[512,384]{1,0:T(8,128)(2,1)S(1)}, bf16[512,384]{1,0:T(8,128)(2,1)S(1)}, u32[]{:S(2)}, u32[]{:S(2)}) collective-permute-start(bf16[512,384]{1,0:T(8,128)(2,1)S(1)} %get-tuple-element.25.refs_2_), channel_id=1, source_target_pairs={{0,1},{1,0},{2,3},{3,2},{4,5},{5,4},{6,7},{7,6},{8,9},{9,8},{10,11... | collective-permute-start | bytes 1179656 | tf_op jit(solution)/shard_map/ppermute | solution.py:418
  66.7 10.7 %collective-permute-start.4 = (bf16[512,384]{1,0:T(8,128)(2,1)S(1)}, bf16[512,384]{1,0:T(8,128)(2,1)S(1)}, u32[]{:S(2)}, u32[]{:S(2)}) collective-permute-start(bf16[512,384]{1,0:T(8,128)(2,1)S(1)} %get-tuple-element.25.refs_2_), channel_id=1, source_target_pairs={{0,2},{1,3},{2,0},{3,1},{4,6},{5,7},{6,4},{7,5},{8,10},{9,11},{10,... | collective-permute-start | bytes 1179656 | tf_op jit(solution)/shard_map/ppermute | solution.py:418
  67.8 1.5 %collective-permute-start.9 = (bf16[512,256]{1,0:T(8,128)(2,1)S(1)}, bf16[512,256]{1,0:T(8,128)(2,1)S(1)}, u32[]{:S(2)}, u32[]{:S(2)}) collective-permute-start(bf16[512,256]{1,0:T(8,128)(2,1)S(1)} %collective-permute-done.3.refs_8_.refs_6_), channel_id=1, source_target_pairs={{0,1},{1,0},{2,3},{3,2},{4,5},{5,4},{6,7},{7,6},{8,9},{9,8},{10,11... | collective-permute-start | bytes 786440 | tf_op jit(solution)/shard_map/ppermute | solution.py:418
  68.2 10.1 %collective-permute-start.10 = (bf16[512,384]{1,0:T(8,128)(2,1)S(1)}, bf16[512,384]{1,0:T(8,128)(2,1)S(1)}, u32[]{:S(2)}, u32[]{:S(2)}) collective-permute-start(bf16[512,384]{1,0:T(8,128)(2,1)S(1)} %collective-permute-done.8.refs_7_), channel_id=1, source_target_pairs={{0,1},{1,0},{2,3},{3,2},{4,5},{5,4},{6,7},{7,6},{8,9},{9,8},{10,11... | collective-permute-start | bytes 1179656 | tf_op jit(solution)/shard_map/ppermute | solution.py:418
  77.4 2.2 %collective-permute-start.11 = (bf16[512,384]{1,0:T(8,128)(2,1)S(1)}, bf16[512,384]{1,0:T(8,128)(2,1)S(1)}, u32[]{:S(2)}, u32[]{:S(2)}) collective-permute-start(bf16[512,384]{1,0:T(8,128)(2,1)S(1)} %collective-permute-done.4.refs_0_), channel_id=1, source_target_pairs={{0,1},{1,0},{2,3},{3,2},{4,5},{5,4},{6,7},{7,6},{8,9},{9,8},{10,11... | collective-permute-start | bytes 1179656 | tf_op jit(solution)/shard_map/ppermute | solution.py:418

commit v9 on v7

--- a/solution.py
+++ b/solution.py
@@ -23,6 +23,7 @@
 ATTEND_VMEM = 18 * 1024 * 1024
 PROJECT_VMEM = 14 * 1024 * 1024
 TILE = 256
+SHARED = (3, 3, 2)
 
 VMEM = pl.BlockSpec(memory_space=pltpu.VMEM)
 SMEM = pl.BlockSpec(memory_space=pltpu.SMEM)
@@ -190,12 +191,14 @@
     )(inside, on_next, on_second, carried, second)
 
 
-def attend_kernel(first_head, blocks, first_ref, *refs):
+def attend_kernel(first_head, blocks, earlier, first_ref, *refs):
     sources, (far_ref, *refs) = refs[:4], refs[4:]
     if blocks:
         me_ref, weight_ref = refs[:2]
         weight_sem = refs.pop()
         held_ref = refs.pop(-8)
+    earlier = refs[2 : 2 + earlier]
+    shared = [refs.pop(-7 - n) for n in range(len(SHARED), 0, -1)] if earlier else []
     out_ref, path_key_ref, path_value_ref, parents_ref, query_ref, key_ref, value_ref, sem = refs[-8:]
     heads = query_ref.shape[1] // HEAD_DIM
     columns = pl.ds(first_head * HEAD_DIM, query_ref.shape[1])
@@ -243,6 +246,18 @@
     )
     halves = [slice(0, SEG_LEN), slice(SEG_LEN, 2 * SEG_LEN)]
     own_values = [with_ones(value_ref[half]) for half in halves]
+
+    def share(head, mixture):
+        for size, ref in zip(SHARED, shared):
+            if 0 <= head < size:
+                ref[:, head * HEAD_DIM : (head + 1) * HEAD_DIM] = mixture
+            head -= size
+
+    head = 0
+    for part in earlier:
+        for at in range(0, part.shape[1], HEAD_DIM):
+            share(head, part[:, at : at + HEAD_DIM])
+            head += 1
     for head in range(heads):
         query = query_ref[:, head * HEAD_DIM : (head + 1) * HEAD_DIM]
         path_scores = scores_of(jnp.concatenate([query, marks], axis=1), path_keys)
@@ -270,7 +285,9 @@
             jnp.concatenate(path_weights, axis=0), path_values, preferred_element_type=jnp.float32
         ) + jnp.concatenate(own_parts, axis=0)
         mixture = total[:, :HEAD_DIM] / total[:, HEAD_DIM:]
-        out_ref[:, head * HEAD_DIM : (head + 1) * HEAD_DIM] = mixture.astype(out_ref.dtype)
+        mixture = mixture.astype(out_ref.dtype)
+        out_ref[:, head * HEAD_DIM : (head + 1) * HEAD_DIM] = mixture
+        share(first_head + head, mixture)
     for copy in copies:
         copy.wait()
 
@@ -288,11 +305,13 @@
     return copies
 
 
-def attend(first, parents, queries, keys, values, far, first_head, heads, blocks, bring, after):
+def attend(first, parents, queries, keys, values, far, first_head, heads, blocks, bring, after, earlier):
     rows = queries.shape[0]
     pairs = heads * rows * (PATH + SEG_LEN + SEG_LEN // 2)
     out_shape = [jax.ShapeDtypeStruct((rows, heads * HEAD_DIM), jnp.bfloat16)]
     in_specs = [SMEM] + [HBM] * 4 + [VMEM]
+    if earlier:
+        out_shape += [jax.ShapeDtypeStruct((rows, n * HEAD_DIM), jnp.bfloat16) for n in SHARED]
     scratch = [pltpu.VMEM((PATH, 2 * HEAD_DIM), jnp.bfloat16)] * 2 + [
         pltpu.SMEM(parents.shape, parents.dtype),
         pltpu.VMEM((rows, heads * HEAD_DIM), queries.dtype),
@@ -310,9 +329,9 @@
     else:
         bring = []
     return pl.pallas_call(
-        functools.partial(attend_kernel, first_head, blocks),
+        functools.partial(attend_kernel, first_head, blocks, len(earlier)),
         out_shape=out_shape,
-        in_specs=in_specs + [ANY] * len(after),
+        in_specs=in_specs + [VMEM] * len(earlier) + [ANY] * len(after),
         out_specs=[VMEM] * len(out_shape),
         scratch_shapes=scratch,
         compiler_params=pltpu.CompilerParams(vmem_limit_bytes=ATTEND_VMEM),
@@ -330,6 +349,7 @@
         in_hbm(values),
         far,
         *bring,
+        *earlier,
         *after,
     )
 
@@ -406,26 +426,29 @@
     width = queries.shape[1]
     bring = (me.astype(jnp.int32).reshape(1), out_weight)
     own, across, weights, head = [], [], [], 0
-    for c, (size, blocks) in enumerate([(2, ()), (3, (0, 1)), (3, (2, 3))]):
+    for c, (size, blocks) in enumerate([(2, ()), (2, (0, 1)), (4, (2, 3))]):
         after = [across[c - 2]] if c >= 2 else []
-        part, *brought = attend(
-            first, parents, queries, key_proj, value_proj, far, head, size, blocks, bring, after
+        earlier = own if c == 2 else []
+        part, *rest = attend(
+            first, parents, queries, key_proj, value_proj, far, head, size, blocks, bring, after, earlier
         )
-        weights += brought
-        own.append(part)
+        weights += rest[len(rest) - len(blocks) // 2 :]
+        own = rest[: len(SHARED)] if earlier else own + [part]
         across.append(swap(part, 2))
         head += size
+    *own, across[0], across[1] = lax.optimization_barrier(own + across[:2])
     beside = [swap(part, 1) for part in own]
     corner = [swap(part, 1) for part in across[:-1]]
-    near = project(
-        [own + beside, across[:-1], corner[:-1]], [(0, 0), (1, 0), (1, width)], weights, None, jnp.float32
+    total = project([own, across[:-1]], [(0, 0), (1, 0)], weights, None, jnp.float32)
+    total = project(
+        [beside, corner[:-1]], [(0, width), (1, width)], weights, total, jnp.float32
     )
-    last, near = lax.optimization_barrier((across[-1], near))
+    last, total, corner[-1] = lax.optimization_barrier((across[-1], total, corner[-1]))
     corner.append(swap(last, 1))
     done = width - last.shape[1]
     turned = sum(part.shape[1] for part in corner[:-2])
     return project(
-        [[last], corner[-2:]], [(1, done), (1, width + turned)], weights, near, jnp.bfloat16
+        [[last], corner[-2:]], [(1, done), (1, width + turned)], weights, total, jnp.bfloat16
     )
 
 

time: 82 us -> 86.5 us (1.055)
  waiting for transfers between devices: 14.2 us -> 17.2 us
  starting transfers between devices: 24.1 us -> 25.7 us
    ppermute x9, waiting for transfers between devices: 5.9 us -> 8.94 us  [swap(): return lax.ppermute(part, 'tensor', [(i, i ^ bit) for i in range(size)])]
    ppermute x9, starting transfers between devices: 10.4 us -> 11.9 us  [swap(): return lax.ppermute(part, 'tensor', [(i, i ^ bit) for i in range(size)])]
    pallas_call x2 -> x3, Pallas kernels: 7.16 us -> 7.03 us  [project(): pl.pallas_call(functools.partial(project_kernel, [len(g) for g in groups]...]
  transfers between devices with their start and end apart: 12 -> 12, of which waited for: 5 -> 5; matrix products, arithmetic and copies ran while one was open for 0% -> 0% of each run, Pallas kernels for 20% -> 19%
where the time goes in v9:
time: 86.5 us; the launch traced here: 86.2 us
  Pallas kernels  25.7 us (30%)
  starting transfers between devices  25.7 us (30%)
  blocking collectives  17.6 us (20%)
  waiting for transfers between devices  17.2 us (20%)
    all_to_all x1, blocking collectives, trade(): lax.all_to_all(pieces, 'dp', 0, 0, tiled=True, axis_index_groups=rows)  17.6 us
    pallas_call x3, Pallas kernels, attend(): pl.pallas_call(functools.partial(attend_kernel, first_head, blocks, len(e...  14.7 us
    ppermute x9, starting transfers between devices, swap(): return lax.ppermute(part, 'tensor', [(i, i ^ bit) for i in range(size)])  11.9 us
    all_to_all x1, starting transfers between devices, trade(): lax.all_to_all(pieces, 'dp', 0, 0, tiled=True, axis_index_groups=rows)  9.77 us
    ppermute x9, waiting for transfers between devices, swap(): return lax.ppermute(part, 'tensor', [(i, i ^ bit) for i in range(size)])  8.94 us
    pallas_call x3, Pallas kernels, project(): pl.pallas_call(functools.partial(project_kernel, [len(g) for g in groups]...  7.03 us
    all_to_all x1, waiting for transfers between devices, trade(): lax.all_to_all(pieces, 'dp', 0, 0, tiled=True, axis_index_groups=rows)  5.73 us
    ppermute x2, starting transfers between devices, onward(): lax.ppermute(piece, 'dp', [(i, (i + step) % devices) for i in range(devic...  3.99 us
  transfers between devices with their start and end apart: 12, of which 5 were waited for; matrix products, arithmetic and copies ran while one was open for 0% of the time, Pallas kernels for 19%

profile of v9, /device:TPU:1, one launch (start us, length us, event | category | flops | bytes accessed | tf_op | source)
XLA Modules:
  0.0 86.2 jit_solution(10570922182858343008)
XLA Ops:
  0.0 1.7 %pack.1 = bf16[8,2,64,128]{3,2,1,0:T(8,128)(2,1)} custom-call(bf16[512,128]{1,0:T(8,128)(2,1)} %refs_2_.5, bf16[512,128]{1,0:T(8,128)(2,1)} %refs_3_.5), custom_call_target="tpu_custom_call" | custom-call | bytes 524288 | tf_op jit(solution)/shard_map/pack/pallas_call | solution.py:75
  1.7 9.8 %all-to-all-start = ((bf16[8,2,64,128]{3,2,1,0:T(8,128)(2,1)}), bf16[8,2,64,128]{3,2,1,0:T(8,128)(2,1)S(1)}, u32[]{:S(2)}, u32[]{:S(2)}) async-start(bf16[8,2,64,128]{3,2,1,0:T(8,128)(2,1)} %pack.1), calls=%async_computation | async-start | bytes 524288 | tf_op jit(solution)/shard_map/all_to_all | solution.py:410
  11.5 5.7 %all-to-all-done = bf16[8,2,64,128]{3,2,1,0:T(8,128)(2,1)S(1)} async-done(((bf16[8,2,64,128]{3,2,1,0:T(8,128)(2,1)}), bf16[8,2,64,128]{3,2,1,0:T(8,128)(2,1)S(1)}, u32[]{:S(2)}, u32[]{:S(2)}) %all-to-all-start) | async-done | bytes 262176 | tf_op jit(solution)/shard_map/all_to_all | solution.py:410
  17.2 0.8 carry_out.1
  18.0 1.4 %collective-permute-start = (bf16[4,64,128]{2,1,0:T(8,128)(2,1)S(1)}, bf16[4,64,128]{2,1,0:T(8,128)(2,1)S(1)}, u32[]{:S(2)}, u32[]{:S(2)}) collective-permute-start(bf16[4,64,128]{2,1,0:T(8,128)(2,1)S(1)} %get-tuple-element.28), channel_id=1, source_target_pairs={{0,32},{4,36},{8,40},{12,44},{16,48},{20,52},{24,56},{28,60},{32,6... | collective-permute-start | bytes 196616 | tf_op jit(solution)/shard_map/ppermute | solution.py:415
  19.4 2.6 %collective-permute-start.1 = (bf16[1,64,128]{2,1,0:T(8,128)(2,1)S(1)}, bf16[1,64,128]{2,1,0:T(8,128)(2,1)S(1)}, u32[]{:S(2)}, u32[]{:S(2)}) collective-permute-start(bf16[1,64,128]{2,1,0:T(8,128)(2,1)S(1)} %get-tuple-element.29), channel_id=1, source_target_pairs={{0,64},{4,68},{8,72},{12,76},{16,80},{20,84},{24,88},{28,92},{32,9... | collective-permute-start | bytes 49160 | tf_op jit(solution)/shard_map/ppermute | solution.py:415
  22.0 1.3 %pick.1 = (bf16[8,4,64,128]{3,2,1,0:T(8,128)(2,1)S(1)}, bf16[8,4,16,128]{3,2,1,0:T(8,128)(2,1)S(1)}, bf16[8,16,128]{2,1,0:T(8,128)(2,1)S(1)}) custom-call(s32[1]{0:T(128)} %bitcast.first_ref, s32[128]{0:T(128)} %refs_0_.5, bf16[16,64,128]{2,1,0:T(8,128)(2,1)S(1)} %bitcast.4), custom_call_target="tpu_custom_call" | custom-call | bytes 1048576 | tf_op jit(solution)/shard_map/pick/pallas_call | solution.py:153
  23.3 2.5 %collective-permute-done.1.second_ref = bf16[1,64,128]{2,1,0:T(8,128)(2,1)S(1)} collective-permute-done((bf16[1,64,128]{2,1,0:T(8,128)(2,1)S(1)}, bf16[1,64,128]{2,1,0:T(8,128)(2,1)S(1)}, u32[]{:S(2)}, u32[]{:S(2)}) %collective-permute-start.1) | collective-permute-done | bytes 16416 | tf_op jit(solution)/shard_map/ppermute | solution.py:415
  25.9 0.1 merge.1
  26.0 17.6 %all_to_all.10.refs_4_ = bf16[8,4,64,128]{3,2,1,0:T(8,128)(2,1)S(1)} all-to-all(bf16[8,4,64,128]{3,2,1,0:T(8,128)(2,1)S(1)} %merge.1), channel_id=1, replica_groups={{28,12,24,8,20,4,16,0},{60,44,56,40,52,36,48,32},{92,76,88,72,84,68,80,..., dimensions={0} | all-to-all | bytes 1048576 | tf_op jit(solution)/shard_map/all_to_all | solution.py:410
  43.5 3.7 %attend.4.refs_7_ = bf16[512,256]{1,0:T(8,128)(2,1)S(1)} custom-call(s32[1]{0:T(128)} %bitcast.first_ref, s32[128]{0:T(128)} %refs_0_.5, bf16[512,1024]{1,0:T(8,128)(2,1)} %refs_1_.5, bf16[512,128]{1,0:T(8,128)(2,1)} %refs_2_.5, bf16[512,128]{1,0:T(8,128)(2,1)} %refs_3_.5, bf16[8,4,64,128]{3,2,1,0:T(8,128)(2,1)S(1)} %all_to_all.10.refs_4_), custom_call_target="tpu_custom_call" | custom-call | flops 1845493760 | bytes 1572864 | tf_op jit(solution)/shard_map/attend/pallas_call | solution.py:331
  47.2 1.3 %collective-permute-start.2 = (bf16[512,256]{1,0:T(8,128)(2,1)S(1)}, bf16[512,256]{1,0:T(8,128)(2,1)S(1)}, u32[]{:S(2)}, u32[]{:S(2)}) collective-permute-start(bf16[512,256]{1,0:T(8,128)(2,1)S(1)} %attend.4.refs_7_), channel_id=1, source_target_pairs={{0,2},{1,3},{2,0},{3,1},{4,6},{5,7},{6,4},{7,5},{8,10},{9,11},{10,... | collective-permute-start | bytes 786440 | tf_op jit(solution)/shard_map/ppermute | solution.py:404
  48.5 4.5 %attend.3 = (bf16[512,256]{1,0:T(8,128)(2,1)S(1)}, bf16[2048,1280]{1,0:T(8,128)(2,1)S(1)}) custom-call(s32[1]{0:T(128)} %bitcast.first_ref, s32[128]{0:T(128)} %refs_0_.5, bf16[512,1024]{1,0:T(8,128)(2,1)} %refs_1_.5, bf16[512,128]{1,0:T(8,128)(2,1)} %refs_2_.5, bf16[512,128]{1,0:T(8,128)(2,1)} %refs_3_.5, bf16[8,4,64,128]{3,2,1,0:T(8,128)(2,1)S(1)} %all_to_all.10.refs_4_, ...), custom_call_target="tpu_custom_call" | custom-call | flops 1845493760 | bytes 1572864 | tf_op jit(solution)/shard_map/attend/pallas_call | solution.py:331
  53.0 0.5 collective-permute-start.4
  53.6 0.0 collective-permute-done.2.refs_9_.refs_3_
  53.6 6.5 %attend.5 = (bf16[512,512]{1,0:T(8,128)(2,1)S(1)}, bf16[512,384]{1,0:T(8,128)(2,1)S(1)}, bf16[512,384]{1,0:T(8,128)(2,1)S(1)}, bf16[512,256]{1,0:T(8,128)(2,1)S(1)}, bf16[2048,1280]{1,0:T(8,128)(2,1)S(1)}) custom-call(s32[1]{0:T(128)} %bitcast.first_ref, s32[128]{0:T(128)} %refs_0_.5, bf16[512,1024]{1,0:T(8,128)(2,1)} %refs_1_.5, bf16[512,128]{1,0:T(8,128)(2,1)} %refs_2_.5, ...), custom_call_target="tpu_custom_call" | custom-call | flops 3690987520 | bytes 2097152 | tf_op jit(solution)/shard_map/attend/pallas_call | solution.py:331
  60.1 0.4 collective-permute-done.4.refs_4_
  60.5 6.5 %collective-permute-start.7 = (bf16[512,256]{1,0:T(8,128)(2,1)S(1)}, bf16[512,256]{1,0:T(8,128)(2,1)S(1)}, u32[]{:S(2)}, u32[]{:S(2)}) collective-permute-start(bf16[512,256]{1,0:T(8,128)(2,1)S(1)} %get-tuple-element.39.refs_2_), channel_id=1, source_target_pairs={{0,1},{1,0},{2,3},{3,2},{4,5},{5,4},{6,7},{7,6},{8,9},{9,8},{10,11... | collective-permute-start | bytes 786440 | tf_op jit(solution)/shard_map/ppermute | solution.py:404
  67.0 1.9 %collective-permute-start.3 = (bf16[512,512]{1,0:T(8,128)(2,1)S(1)}, bf16[512,512]{1,0:T(8,128)(2,1)S(1)}, u32[]{:S(2)}, u32[]{:S(2)}) collective-permute-start(bf16[512,512]{1,0:T(8,128)(2,1)S(1)} %get-tuple-element.33), channel_id=1, source_target_pairs={{0,2},{1,3},{2,0},{3,1},{4,6},{5,7},{6,4},{7,5},{8,10},{9,11},{10,... | collective-permute-start | bytes 1572872 | tf_op jit(solution)/shard_map/ppermute | solution.py:404
  68.9 0.4 collective-permute-start.5
  69.3 0.1 collective-permute-start.6
  69.4 0.4 collective-permute-start.8
  69.8 0.0 collective-permute-done.7.refs_2_
  69.8 0.1 collective-permute-start.9
  70.0 2.2 %project.3.refs_4_ = f32[512,1280]{1,0:T(8,128)S(1)} custom-call(bf16[2048,1280]{1,0:T(8,128)(2,1)S(1)} %get-tuple-element.30.near_ref, bf16[2048,1280]{1,0:T(8,128)(2,1)S(1)} %get-tuple-element.32.far_ref, bf16[512,384]{1,0:T(8,128)(2,1)S(1)} %get-tuple-element.37.refs_0_, bf16[512,384]{1,0:T(8,128)(2,1)S(1)} %get-tuple-element.38.refs_1_, ...), custom_call_target="tpu_custom_call" | custom-call | flops 655360 | bytes 655360 | tf_op jit(solution)/shard_map/project/pallas_call | solution.py:386
  72.2 0.0 collective-permute-done.8.refs_3_
  72.2 0.0 collective-permute-done.6.refs_1_
  72.2 1.9 %project.4.refs_3_ = f32[512,1280]{1,0:T(8,128)S(1)} custom-call(bf16[2048,1280]{1,0:T(8,128)(2,1)S(1)} %get-tuple-element.30.near_ref, bf16[2048,1280]{1,0:T(8,128)(2,1)S(1)} %get-tuple-element.32.far_ref, bf16[512,384]{1,0:T(8,128)(2,1)S(1)} %collective-permute-done.5.refs_0_, bf16[512,384]{1,0:T(8,128)(2,1)S(1)} %collective-permute-done.6.refs_1_, ...), custom_call_target="tpu_custom_call" | custom-call | flops 655360 | bytes 655360 | tf_op jit(solution)/shard_map/project/pallas_call | solution.py:386
  74.1 7.0 %collective-permute-done.3.refs_0_ = bf16[512,512]{1,0:T(8,128)(2,1)S(1)} collective-permute-done((bf16[512,512]{1,0:T(8,128)(2,1)S(1)}, bf16[512,512]{1,0:T(8,128)(2,1)S(1)}, u32[]{:S(2)}, u32[]{:S(2)}) %collective-permute-start.3) | collective-permute-done | bytes 524320 | tf_op jit(solution)/shard_map/ppermute | solution.py:404
  81.1 0.7 collective-permute-start.10
  81.8 1.5 %collective-permute-done.10.refs_2_ = bf16[512,512]{1,0:T(8,128)(2,1)S(1)} collective-permute-done((bf16[512,512]{1,0:T(8,128)(2,1)S(1)}, bf16[512,512]{1,0:T(8,128)(2,1)S(1)}, u32[]{:S(2)}, u32[]{:S(2)}) %collective-permute-start.10) | collective-permute-done | bytes 524320 | tf_op jit(solution)/shard_map/ppermute | solution.py:404
  83.3 2.9 %project.5 = bf16[512,1280]{1,0:T(8,128)(2,1)} custom-call(bf16[2048,1280]{1,0:T(8,128)(2,1)S(1)} %get-tuple-element.30.near_ref, bf16[2048,1280]{1,0:T(8,128)(2,1)S(1)} %get-tuple-element.32.far_ref, bf16[512,512]{1,0:T(8,128)(2,1)S(1)} %collective-permute-done.3.refs_0_, bf16[512,256]{1,0:T(8,128)(2,1)S(1)} %collective-permute-done.9.refs_1_, ...), custom_call_target="tpu_custom_call" | custom-call | flops 655360 | bytes 655360 | tf_op jit(solution)/shard_map/project/pallas_call | solution.py:386
  (3 shorter events, 0.0 us)
Async XLA Ops:
  1.7 15.5 %all-to-all-start = ((bf16[8,2,64,128]{3,2,1,0:T(8,128)(2,1)}), bf16[8,2,64,128]{3,2,1,0:T(8,128)(2,1)S(1)}, u32[]{:S(2)}, u32[]{:S(2)}) async-start(bf16[8,2,64,128]{3,2,1,0:T(8,128)(2,1)} %pack.1), calls=%async_computation | async-start | bytes 524288 | tf_op jit(solution)/shard_map/all_to_all | solution.py:410
  18.0 7.9 %collective-permute-start = (bf16[4,64,128]{2,1,0:T(8,128)(2,1)S(1)}, bf16[4,64,128]{2,1,0:T(8,128)(2,1)S(1)}, u32[]{:S(2)}, u32[]{:S(2)}) collective-permute-start(bf16[4,64,128]{2,1,0:T(8,128)(2,1)S(1)} %get-tuple-element.28), channel_id=1, source_target_pairs={{0,32},{4,36},{8,40},{12,44},{16,48},{20,52},{24,56},{28,60},{32,6... | collective-permute-start | bytes 196616 | tf_op jit(solution)/shard_map/ppermute | solution.py:415
  19.4 6.5 %collective-permute-start.1 = (bf16[1,64,128]{2,1,0:T(8,128)(2,1)S(1)}, bf16[1,64,128]{2,1,0:T(8,128)(2,1)S(1)}, u32[]{:S(2)}, u32[]{:S(2)}) collective-permute-start(bf16[1,64,128]{2,1,0:T(8,128)(2,1)S(1)} %get-tuple-element.29), channel_id=1, source_target_pairs={{0,64},{4,68},{8,72},{12,76},{16,80},{20,84},{24,88},{28,92},{32,9... | collective-permute-start | bytes 49160 | tf_op jit(solution)/shard_map/ppermute | solution.py:415
  47.2 6.3 %collective-permute-start.2 = (bf16[512,256]{1,0:T(8,128)(2,1)S(1)}, bf16[512,256]{1,0:T(8,128)(2,1)S(1)}, u32[]{:S(2)}, u32[]{:S(2)}) collective-permute-start(bf16[512,256]{1,0:T(8,128)(2,1)S(1)} %attend.4.refs_7_), channel_id=1, source_target_pairs={{0,2},{1,3},{2,0},{3,1},{4,6},{5,7},{6,4},{7,5},{8,10},{9,11},{10,... | collective-permute-start | bytes 786440 | tf_op jit(solution)/shard_map/ppermute | solution.py:404
  53.0 7.5 %collective-permute-start.4 = (bf16[512,256]{1,0:T(8,128)(2,1)S(1)}, bf16[512,256]{1,0:T(8,128)(2,1)S(1)}, u32[]{:S(2)}, u32[]{:S(2)}) collective-permute-start(bf16[512,256]{1,0:T(8,128)(2,1)S(1)} %get-tuple-element.31.refs_8_), channel_id=1, source_target_pairs={{0,2},{1,3},{2,0},{3,1},{4,6},{5,7},{6,4},{7,5},{8,10},{9,11},{10,... | collective-permute-start | bytes 786440 | tf_op jit(solution)/shard_map/ppermute | solution.py:404
  60.5 9.3 %collective-permute-start.7 = (bf16[512,256]{1,0:T(8,128)(2,1)S(1)}, bf16[512,256]{1,0:T(8,128)(2,1)S(1)}, u32[]{:S(2)}, u32[]{:S(2)}) collective-permute-start(bf16[512,256]{1,0:T(8,128)(2,1)S(1)} %get-tuple-element.39.refs_2_), channel_id=1, source_target_pairs={{0,1},{1,0},{2,3},{3,2},{4,5},{5,4},{6,7},{7,6},{8,9},{9,8},{10,11... | collective-permute-start | bytes 786440 | tf_op jit(solution)/shard_map/ppermute | solution.py:404
  67.0 14.1 %collective-permute-start.3 = (bf16[512,512]{1,0:T(8,128)(2,1)S(1)}, bf16[512,512]{1,0:T(8,128)(2,1)S(1)}, u32[]{:S(2)}, u32[]{:S(2)}) collective-permute-start(bf16[512,512]{1,0:T(8,128)(2,1)S(1)} %get-tuple-element.33), channel_id=1, source_target_pairs={{0,2},{1,3},{2,0},{3,1},{4,6},{5,7},{6,4},{7,5},{8,10},{9,11},{10,... | collective-permute-start | bytes 1572872 | tf_op jit(solution)/shard_map/ppermute | solution.py:404
  68.9 3.3 %collective-permute-start.5 = (bf16[512,384]{1,0:T(8,128)(2,1)S(1)}, bf16[512,384]{1,0:T(8,128)(2,1)S(1)}, u32[]{:S(2)}, u32[]{:S(2)}) collective-permute-start(bf16[512,384]{1,0:T(8,128)(2,1)S(1)} %get-tuple-element.37.refs_0_), channel_id=1, source_target_pairs={{0,1},{1,0},{2,3},{3,2},{4,5},{5,4},{6,7},{7,6},{8,9},{9,8},{10,11... | collective-permute-start | bytes 1179656 | tf_op jit(solution)/shard_map/ppermute | solution.py:404
  69.3 2.9 %collective-permute-start.6 = (bf16[512,384]{1,0:T(8,128)(2,1)S(1)}, bf16[512,384]{1,0:T(8,128)(2,1)S(1)}, u32[]{:S(2)}, u32[]{:S(2)}) collective-permute-start(bf16[512,384]{1,0:T(8,128)(2,1)S(1)} %get-tuple-element.38.refs_1_), channel_id=1, source_target_pairs={{0,1},{1,0},{2,3},{3,2},{4,5},{5,4},{6,7},{7,6},{8,9},{9,8},{10,11... | collective-permute-start | bytes 1179656 | tf_op jit(solution)/shard_map/ppermute | solution.py:404
  69.4 2.7 %collective-permute-start.8 = (bf16[512,256]{1,0:T(8,128)(2,1)S(1)}, bf16[512,256]{1,0:T(8,128)(2,1)S(1)}, u32[]{:S(2)}, u32[]{:S(2)}) collective-permute-start(bf16[512,256]{1,0:T(8,128)(2,1)S(1)} %collective-permute-done.2.refs_9_.refs_3_), channel_id=1, source_target_pairs={{0,1},{1,0},{2,3},{3,2},{4,5},{5,4},{6,7},{7,6},{8,9},{9,8},{10,11... | collective-permute-start | bytes 786440 | tf_op jit(solution)/shard_map/ppermute | solution.py:404
  69.8 4.3 %collective-permute-start.9 = (bf16[512,256]{1,0:T(8,128)(2,1)S(1)}, bf16[512,256]{1,0:T(8,128)(2,1)S(1)}, u32[]{:S(2)}, u32[]{:S(2)}) collective-permute-start(bf16[512,256]{1,0:T(8,128)(2,1)S(1)} %collective-permute-done.4.refs_4_), channel_id=1, source_target_pairs={{0,1},{1,0},{2,3},{3,2},{4,5},{5,4},{6,7},{7,6},{8,9},{9,8},{10,11... | collective-permute-start | bytes 786440 | tf_op jit(solution)/shard_map/ppermute | solution.py:404
  81.1 2.2 %collective-permute-start.10 = (bf16[512,512]{1,0:T(8,128)(2,1)S(1)}, bf16[512,512]{1,0:T(8,128)(2,1)S(1)}, u32[]{:S(2)}, u32[]{:S(2)}) collective-permute-start(bf16[512,512]{1,0:T(8,128)(2,1)S(1)} %collective-permute-done.3.refs_0_), channel_id=1, source_target_pairs={{0,1},{1,0},{2,3},{3,2},{4,5},{5,4},{6,7},{7,6},{8,9},{9,8},{10,11... | collective-permute-start | bytes 1572872 | tf_op jit(solution)/shard_map/ppermute | solution.py:404

commit v10 on v9

--- a/solution.py
+++ b/solution.py
@@ -27,7 +27,6 @@
 
 VMEM = pl.BlockSpec(memory_space=pltpu.VMEM)
 SMEM = pl.BlockSpec(memory_space=pltpu.SMEM)
-ANY = pl.BlockSpec(memory_space=pl.ANY)
 HBM = pl.BlockSpec(memory_space=pltpu.HBM)
 FLAG_ROWS = 16
 
@@ -305,7 +304,7 @@
     return copies
 
 
-def attend(first, parents, queries, keys, values, far, first_head, heads, blocks, bring, after, earlier):
+def attend(first, parents, queries, keys, values, far, first_head, heads, blocks, bring, earlier):
     rows = queries.shape[0]
     pairs = heads * rows * (PATH + SEG_LEN + SEG_LEN // 2)
     out_shape = [jax.ShapeDtypeStruct((rows, heads * HEAD_DIM), jnp.bfloat16)]
@@ -331,7 +330,7 @@
     return pl.pallas_call(
         functools.partial(attend_kernel, first_head, blocks, len(earlier)),
         out_shape=out_shape,
-        in_specs=in_specs + [VMEM] * len(earlier) + [ANY] * len(after),
+        in_specs=in_specs + [VMEM] * len(earlier),
         out_specs=[VMEM] * len(out_shape),
         scratch_shapes=scratch,
         compiler_params=pltpu.CompilerParams(vmem_limit_bytes=ATTEND_VMEM),
@@ -350,7 +349,6 @@
         far,
         *bring,
         *earlier,
-        *after,
     )
 
 
@@ -427,10 +425,9 @@
     bring = (me.astype(jnp.int32).reshape(1), out_weight)
     own, across, weights, head = [], [], [], 0
     for c, (size, blocks) in enumerate([(2, ()), (2, (0, 1)), (4, (2, 3))]):
-        after = [across[c - 2]] if c >= 2 else []
         earlier = own if c == 2 else []
         part, *rest = attend(
-            first, parents, queries, key_proj, value_proj, far, head, size, blocks, bring, after, earlier
+            first, parents, queries, key_proj, value_proj, far, head, size, blocks, bring, earlier
         )
         weights += rest[len(rest) - len(blocks) // 2 :]
         own = rest[: len(SHARED)] if earlier else own + [part]
@@ -443,7 +440,7 @@
     total = project(
         [beside, corner[:-1]], [(0, width), (1, width)], weights, total, jnp.float32
     )
-    last, total, corner[-1] = lax.optimization_barrier((across[-1], total, corner[-1]))
+    last, total = lax.optimization_barrier((across[-1], total))
     corner.append(swap(last, 1))
     done = width - last.shape[1]
     turned = sum(part.shape[1] for part in corner[:-2])

time: 86.5 us -> 82 us (0.948)
  blocking collectives: 17.6 us -> 0 us
  starting transfers between devices: 25.7 us -> 33.9 us
  waiting for transfers between devices: 17.2 us -> 20.9 us
    all_to_all x1 -> x0, blocking collectives: 17.6 us -> none  [trade(): lax.all_to_all(pieces, 'dp', 0, 0, tiled=True, axis_index_groups=rows)]
    all_to_all x1 -> x2, waiting for transfers between devices: 5.73 us -> 16.4 us  [trade(): lax.all_to_all(pieces, 'dp', 0, 0, tiled=True, axis_index_groups=rows)]
    all_to_all x1 -> x2, starting transfers between devices: 9.77 us -> 17.8 us  [trade(): lax.all_to_all(pieces, 'dp', 0, 0, tiled=True, axis_index_groups=rows)]
    ppermute x9, waiting for transfers between devices: 8.94 us -> 1.93 us  [swap(): return lax.ppermute(part, 'tensor', [(i, i ^ bit) for i in range(size)])]
  transfers between devices with their start and end apart: 12 -> 13, of which waited for: 5 -> 4; matrix products, arithmetic and copies ran while one was open for 0% -> 0% of each run, Pallas kernels for 19% -> 20%
where the time goes in v10:
time: 82 us; the launch traced here: 81.4 us
  starting transfers between devices  33.9 us (41%)
  Pallas kernels  26.5 us (32%)
  waiting for transfers between devices  20.9 us (25%)
    all_to_all x2, starting transfers between devices, trade(): lax.all_to_all(pieces, 'dp', 0, 0, tiled=True, axis_index_groups=rows)  17.8 us
    all_to_all x2, waiting for transfers between devices, trade(): lax.all_to_all(pieces, 'dp', 0, 0, tiled=True, axis_index_groups=rows)  16.4 us
    pallas_call x3, Pallas kernels, attend(): pl.pallas_call(functools.partial(attend_kernel, first_head, blocks, len(e...  14.7 us
    ppermute x9, starting transfers between devices, swap(): return lax.ppermute(part, 'tensor', [(i, i ^ bit) for i in range(size)])  12.2 us
    pallas_call x3, Pallas kernels, project(): pl.pallas_call(functools.partial(project_kernel, [len(g) for g in groups]...  7.03 us
    ppermute x2, starting transfers between devices, onward(): lax.ppermute(piece, 'dp', [(i, (i + step) % devices) for i in range(devic...  3.99 us
    ppermute x2, waiting for transfers between devices, onward(): lax.ppermute(piece, 'dp', [(i, (i + step) % devices) for i in range(devic...  2.53 us
    ppermute x9, waiting for transfers between devices, swap(): return lax.ppermute(part, 'tensor', [(i, i ^ bit) for i in range(size)])  1.93 us
  transfers between devices with their start and end apart: 13, of which 4 were waited for; matrix products, arithmetic and copies ran while one was open for 0% of the time, Pallas kernels for 20%

profile of v10, /device:TPU:1, one launch (start us, length us, event | category | flops | bytes accessed | tf_op | source)
XLA Modules:
  0.0 81.4 jit_solution(7827037214385904727)
XLA Ops:
  0.0 1.7 %pack.1 = bf16[8,2,64,128]{3,2,1,0:T(8,128)(2,1)} custom-call(bf16[512,128]{1,0:T(8,128)(2,1)} %refs_2_.5, bf16[512,128]{1,0:T(8,128)(2,1)} %refs_3_.5), custom_call_target="tpu_custom_call" | custom-call | bytes 524288 | tf_op jit(solution)/shard_map/pack/pallas_call | solution.py:74
  1.7 9.8 %all-to-all-start = ((bf16[8,2,64,128]{3,2,1,0:T(8,128)(2,1)}), bf16[8,2,64,128]{3,2,1,0:T(8,128)(2,1)S(1)}, u32[]{:S(2)}, u32[]{:S(2)}) async-start(bf16[8,2,64,128]{3,2,1,0:T(8,128)(2,1)} %pack.1), calls=%async_computation | async-start | bytes 524288 | tf_op jit(solution)/shard_map/all_to_all | solution.py:408
  11.5 5.7 %all-to-all-done = bf16[8,2,64,128]{3,2,1,0:T(8,128)(2,1)S(1)} async-done(((bf16[8,2,64,128]{3,2,1,0:T(8,128)(2,1)}), bf16[8,2,64,128]{3,2,1,0:T(8,128)(2,1)S(1)}, u32[]{:S(2)}, u32[]{:S(2)}) %all-to-all-start) | async-done | bytes 262176 | tf_op jit(solution)/shard_map/all_to_all | solution.py:408
  17.2 0.8 carry_out.1
  18.0 1.4 %collective-permute-start = (bf16[4,64,128]{2,1,0:T(8,128)(2,1)S(1)}, bf16[4,64,128]{2,1,0:T(8,128)(2,1)S(1)}, u32[]{:S(2)}, u32[]{:S(2)}) collective-permute-start(bf16[4,64,128]{2,1,0:T(8,128)(2,1)S(1)} %get-tuple-element.27), channel_id=1, source_target_pairs={{0,32},{4,36},{8,40},{12,44},{16,48},{20,52},{24,56},{28,60},{32,6... | collective-permute-start | bytes 196616 | tf_op jit(solution)/shard_map/ppermute | solution.py:413
  19.4 2.6 %collective-permute-start.1 = (bf16[1,64,128]{2,1,0:T(8,128)(2,1)S(1)}, bf16[1,64,128]{2,1,0:T(8,128)(2,1)S(1)}, u32[]{:S(2)}, u32[]{:S(2)}) collective-permute-start(bf16[1,64,128]{2,1,0:T(8,128)(2,1)S(1)} %get-tuple-element.28), channel_id=1, source_target_pairs={{0,64},{4,68},{8,72},{12,76},{16,80},{20,84},{24,88},{28,92},{32,9... | collective-permute-start | bytes 49160 | tf_op jit(solution)/shard_map/ppermute | solution.py:413
  22.0 1.3 %pick.1 = (bf16[8,4,64,128]{3,2,1,0:T(8,128)(2,1)S(1)}, bf16[8,4,16,128]{3,2,1,0:T(8,128)(2,1)S(1)}, bf16[8,16,128]{2,1,0:T(8,128)(2,1)S(1)}) custom-call(s32[1]{0:T(128)} %bitcast.first_ref, s32[128]{0:T(128)} %refs_0_.5, bf16[16,64,128]{2,1,0:T(8,128)(2,1)S(1)} %bitcast.4), custom_call_target="tpu_custom_call" | custom-call | bytes 1048576 | tf_op jit(solution)/shard_map/pick/pallas_call | solution.py:152
  23.3 2.5 %collective-permute-done.1.second_ref = bf16[1,64,128]{2,1,0:T(8,128)(2,1)S(1)} collective-permute-done((bf16[1,64,128]{2,1,0:T(8,128)(2,1)S(1)}, bf16[1,64,128]{2,1,0:T(8,128)(2,1)S(1)}, u32[]{:S(2)}, u32[]{:S(2)}) %collective-permute-start.1) | collective-permute-done | bytes 16416 | tf_op jit(solution)/shard_map/ppermute | solution.py:413
  25.9 0.0 collective-permute-done.next_ref
  25.9 0.9 %merge.1 = bf16[8,4,64,128]{3,2,1,0:T(8,128)(2,1)} custom-call(bf16[8,4,64,128]{3,2,1,0:T(8,128)(2,1)S(1)} %get-tuple-element.24.inside_ref, bf16[8,4,16,128]{3,2,1,0:T(8,128)(2,1)S(1)} %get-tuple-element.25.on_next_ref, bf16[8,16,128]{2,1,0:T(8,128)(2,1)S(1)} %get-tuple-element.26.on_second_ref, bf16[4,64,128]{2,1,0:T(8,128)(2,1)S(1)} %collective-permute-done.next_ref, ...), custom_call_target="tpu_custom_call" | custom-call | bytes 1048576 | tf_op jit(solution)/shard_map/merge/pallas_call | solution.py:182
  26.8 8.0 %all-to-all-start.1 = ((bf16[8,4,64,128]{3,2,1,0:T(8,128)(2,1)}), bf16[8,4,64,128]{3,2,1,0:T(8,128)(2,1)S(1)}, u32[]{:S(2)}, u32[]{:S(2)}) async-start(bf16[8,4,64,128]{3,2,1,0:T(8,128)(2,1)} %merge.1), calls=%async_computation.1 | async-start | bytes 1048576 | tf_op jit(solution)/shard_map/all_to_all | solution.py:408
  34.8 10.7 %all-to-all-done.1.refs_4_ = bf16[8,4,64,128]{3,2,1,0:T(8,128)(2,1)S(1)} async-done(((bf16[8,4,64,128]{3,2,1,0:T(8,128)(2,1)}), bf16[8,4,64,128]{3,2,1,0:T(8,128)(2,1)S(1)}, u32[]{:S(2)}, u32[]{:S(2)}) %all-to-all-start.1) | async-done | bytes 524320 | tf_op jit(solution)/shard_map/all_to_all | solution.py:408
  45.5 3.7 %attend.4.refs_7_ = bf16[512,256]{1,0:T(8,128)(2,1)S(1)} custom-call(s32[1]{0:T(128)} %bitcast.first_ref, s32[128]{0:T(128)} %refs_0_.5, bf16[512,1024]{1,0:T(8,128)(2,1)} %refs_1_.5, bf16[512,128]{1,0:T(8,128)(2,1)} %refs_2_.5, bf16[512,128]{1,0:T(8,128)(2,1)} %refs_3_.5, bf16[8,4,64,128]{3,2,1,0:T(8,128)(2,1)S(1)} %all-to-all-done.1.refs_4_), custom_call_target="tpu_custom_call" | custom-call | flops 1845493760 | bytes 1572864 | tf_op jit(solution)/shard_map/attend/pallas_call | solution.py:330
  49.2 1.3 %collective-permute-start.3 = (bf16[512,256]{1,0:T(8,128)(2,1)S(1)}, bf16[512,256]{1,0:T(8,128)(2,1)S(1)}, u32[]{:S(2)}, u32[]{:S(2)}) collective-permute-start(bf16[512,256]{1,0:T(8,128)(2,1)S(1)} %attend.4.refs_7_), channel_id=1, source_target_pairs={{0,2},{1,3},{2,0},{3,1},{4,6},{5,7},{6,4},{7,5},{8,10},{9,11},{10,... | collective-permute-start | bytes 786440 | tf_op jit(solution)/shard_map/ppermute | solution.py:402
  50.5 4.5 %attend.3 = (bf16[512,256]{1,0:T(8,128)(2,1)S(1)}, bf16[2048,1280]{1,0:T(8,128)(2,1)S(1)}) custom-call(s32[1]{0:T(128)} %bitcast.first_ref, s32[128]{0:T(128)} %refs_0_.5, bf16[512,1024]{1,0:T(8,128)(2,1)} %refs_1_.5, bf16[512,128]{1,0:T(8,128)(2,1)} %refs_2_.5, bf16[512,128]{1,0:T(8,128)(2,1)} %refs_3_.5, ...), custom_call_target="tpu_custom_call" | custom-call | flops 1845493760 | bytes 1572864 | tf_op jit(solution)/shard_map/attend/pallas_call | solution.py:330
  55.0 0.5 collective-permute-start.4
  55.5 6.5 %attend.5 = (bf16[512,512]{1,0:T(8,128)(2,1)S(1)}, bf16[512,384]{1,0:T(8,128)(2,1)S(1)}, bf16[512,384]{1,0:T(8,128)(2,1)S(1)}, bf16[512,256]{1,0:T(8,128)(2,1)S(1)}, bf16[2048,1280]{1,0:T(8,128)(2,1)S(1)}) custom-call(s32[1]{0:T(128)} %bitcast.first_ref, s32[128]{0:T(128)} %refs_0_.5, bf16[512,1024]{1,0:T(8,128)(2,1)} %refs_1_.5, bf16[512,128]{1,0:T(8,128)(2,1)} %refs_2_.5, ...), custom_call_target="tpu_custom_call" | custom-call | flops 3690987520 | bytes 2097152 | tf_op jit(solution)/shard_map/attend/pallas_call | solution.py:330
  62.0 1.3 %collective-permute-start.2 = (bf16[512,512]{1,0:T(8,128)(2,1)S(1)}, bf16[512,512]{1,0:T(8,128)(2,1)S(1)}, u32[]{:S(2)}, u32[]{:S(2)}) collective-permute-start(bf16[512,512]{1,0:T(8,128)(2,1)S(1)} %get-tuple-element.32), channel_id=1, source_target_pairs={{0,2},{1,3},{2,0},{3,1},{4,6},{5,7},{6,4},{7,5},{8,10},{9,11},{10,... | collective-permute-start | bytes 1572872 | tf_op jit(solution)/shard_map/ppermute | solution.py:402
  63.3 0.0 collective-permute-done.3.refs_3_
  63.3 0.0 collective-permute-done.4.refs_4_
  63.3 4.3 %collective-permute-start.5 = (bf16[512,384]{1,0:T(8,128)(2,1)S(1)}, bf16[512,384]{1,0:T(8,128)(2,1)S(1)}, u32[]{:S(2)}, u32[]{:S(2)}) collective-permute-start(bf16[512,384]{1,0:T(8,128)(2,1)S(1)} %get-tuple-element.36.refs_0_), channel_id=1, source_target_pairs={{0,1},{1,0},{2,3},{3,2},{4,5},{5,4},{6,7},{7,6},{8,9},{9,8},{10,11... | collective-permute-start | bytes 1179656 | tf_op jit(solution)/shard_map/ppermute | solution.py:402
  67.6 0.1 collective-permute-start.6
  67.7 0.4 collective-permute-start.7
  68.1 0.1 collective-permute-start.8
  68.2 2.2 %project.3.refs_4_ = f32[512,1280]{1,0:T(8,128)S(1)} custom-call(bf16[2048,1280]{1,0:T(8,128)(2,1)S(1)} %get-tuple-element.29.near_ref, bf16[2048,1280]{1,0:T(8,128)(2,1)S(1)} %get-tuple-element.31.far_ref, bf16[512,384]{1,0:T(8,128)(2,1)S(1)} %get-tuple-element.36.refs_0_, bf16[512,384]{1,0:T(8,128)(2,1)S(1)} %get-tuple-element.37.refs_1_, ...), custom_call_target="tpu_custom_call" | custom-call | flops 655360 | bytes 655360 | tf_op jit(solution)/shard_map/project/pallas_call | solution.py:384
  70.4 0.0 collective-permute-done.8.refs_3_
  70.4 0.0 collective-permute-done.5.refs_0_
  70.5 1.9 %project.4.refs_3_ = f32[512,1280]{1,0:T(8,128)S(1)} custom-call(bf16[2048,1280]{1,0:T(8,128)(2,1)S(1)} %get-tuple-element.29.near_ref, bf16[2048,1280]{1,0:T(8,128)(2,1)S(1)} %get-tuple-element.31.far_ref, bf16[512,384]{1,0:T(8,128)(2,1)S(1)} %collective-permute-done.5.refs_0_, bf16[512,384]{1,0:T(8,128)(2,1)S(1)} %collective-permute-done.6.refs_1_, ...), custom_call_target="tpu_custom_call" | custom-call | flops 655360 | bytes 655360 | tf_op jit(solution)/shard_map/project/pallas_call | solution.py:384
  72.4 4.2 %collective-permute-start.10 = (bf16[512,512]{1,0:T(8,128)(2,1)S(1)}, bf16[512,512]{1,0:T(8,128)(2,1)S(1)}, u32[]{:S(2)}, u32[]{:S(2)}) collective-permute-start(bf16[512,512]{1,0:T(8,128)(2,1)S(1)} %collective-permute-done.2.refs_0_), channel_id=1, source_target_pairs={{0,1},{1,0},{2,3},{3,2},{4,5},{5,4},{6,7},{7,6},{8,9},{9,8},{10,11... | collective-permute-start | bytes 1572872 | tf_op jit(solution)/shard_map/ppermute | solution.py:402
  76.5 0.0 collective-permute-start.9
  76.5 1.9 %collective-permute-done.9.refs_1_ = bf16[512,256]{1,0:T(8,128)(2,1)S(1)} collective-permute-done((bf16[512,256]{1,0:T(8,128)(2,1)S(1)}, bf16[512,256]{1,0:T(8,128)(2,1)S(1)}, u32[]{:S(2)}, u32[]{:S(2)}) %collective-permute-start.9) | collective-permute-done | bytes 262176 | tf_op jit(solution)/shard_map/ppermute | solution.py:402
  78.5 2.9 %project.5 = bf16[512,1280]{1,0:T(8,128)(2,1)} custom-call(bf16[2048,1280]{1,0:T(8,128)(2,1)S(1)} %get-tuple-element.29.near_ref, bf16[2048,1280]{1,0:T(8,128)(2,1)S(1)} %get-tuple-element.31.far_ref, bf16[512,512]{1,0:T(8,128)(2,1)S(1)} %collective-permute-done.2.refs_0_, bf16[512,256]{1,0:T(8,128)(2,1)S(1)} %collective-permute-done.9.refs_1_, ...), custom_call_target="tpu_custom_call" | custom-call | flops 655360 | bytes 655360 | tf_op jit(solution)/shard_map/project/pallas_call | solution.py:384
  (4 shorter events, 0.0 us)
Async XLA Ops:
  1.7 15.5 %all-to-all-start = ((bf16[8,2,64,128]{3,2,1,0:T(8,128)(2,1)}), bf16[8,2,64,128]{3,2,1,0:T(8,128)(2,1)S(1)}, u32[]{:S(2)}, u32[]{:S(2)}) async-start(bf16[8,2,64,128]{3,2,1,0:T(8,128)(2,1)} %pack.1), calls=%async_computation | async-start | bytes 524288 | tf_op jit(solution)/shard_map/all_to_all | solution.py:408
  18.0 7.9 %collective-permute-start = (bf16[4,64,128]{2,1,0:T(8,128)(2,1)S(1)}, bf16[4,64,128]{2,1,0:T(8,128)(2,1)S(1)}, u32[]{:S(2)}, u32[]{:S(2)}) collective-permute-start(bf16[4,64,128]{2,1,0:T(8,128)(2,1)S(1)} %get-tuple-element.27), channel_id=1, source_target_pairs={{0,32},{4,36},{8,40},{12,44},{16,48},{20,52},{24,56},{28,60},{32,6... | collective-permute-start | bytes 196616 | tf_op jit(solution)/shard_map/ppermute | solution.py:413
  19.4 6.5 %collective-permute-start.1 = (bf16[1,64,128]{2,1,0:T(8,128)(2,1)S(1)}, bf16[1,64,128]{2,1,0:T(8,128)(2,1)S(1)}, u32[]{:S(2)}, u32[]{:S(2)}) collective-permute-start(bf16[1,64,128]{2,1,0:T(8,128)(2,1)S(1)} %get-tuple-element.28), channel_id=1, source_target_pairs={{0,64},{4,68},{8,72},{12,76},{16,80},{20,84},{24,88},{28,92},{32,9... | collective-permute-start | bytes 49160 | tf_op jit(solution)/shard_map/ppermute | solution.py:413
  26.8 18.7 %all-to-all-start.1 = ((bf16[8,4,64,128]{3,2,1,0:T(8,128)(2,1)}), bf16[8,4,64,128]{3,2,1,0:T(8,128)(2,1)S(1)}, u32[]{:S(2)}, u32[]{:S(2)}) async-start(bf16[8,4,64,128]{3,2,1,0:T(8,128)(2,1)} %merge.1), calls=%async_computation.1 | async-start | bytes 1048576 | tf_op jit(solution)/shard_map/all_to_all | solution.py:408
  49.2 14.2 %collective-permute-start.3 = (bf16[512,256]{1,0:T(8,128)(2,1)S(1)}, bf16[512,256]{1,0:T(8,128)(2,1)S(1)}, u32[]{:S(2)}, u32[]{:S(2)}) collective-permute-start(bf16[512,256]{1,0:T(8,128)(2,1)S(1)} %attend.4.refs_7_), channel_id=1, source_target_pairs={{0,2},{1,3},{2,0},{3,1},{4,6},{5,7},{6,4},{7,5},{8,10},{9,11},{10,... | collective-permute-start | bytes 786440 | tf_op jit(solution)/shard_map/ppermute | solution.py:402
  55.0 8.4 %collective-permute-start.4 = (bf16[512,256]{1,0:T(8,128)(2,1)S(1)}, bf16[512,256]{1,0:T(8,128)(2,1)S(1)}, u32[]{:S(2)}, u32[]{:S(2)}) collective-permute-start(bf16[512,256]{1,0:T(8,128)(2,1)S(1)} %get-tuple-element.30.refs_8_), channel_id=1, source_target_pairs={{0,2},{1,3},{2,0},{3,1},{4,6},{5,7},{6,4},{7,5},{8,10},{9,11},{10,... | collective-permute-start | bytes 786440 | tf_op jit(solution)/shard_map/ppermute | solution.py:402
  62.0 10.3 %collective-permute-start.2 = (bf16[512,512]{1,0:T(8,128)(2,1)S(1)}, bf16[512,512]{1,0:T(8,128)(2,1)S(1)}, u32[]{:S(2)}, u32[]{:S(2)}) collective-permute-start(bf16[512,512]{1,0:T(8,128)(2,1)S(1)} %get-tuple-element.32), channel_id=1, source_target_pairs={{0,2},{1,3},{2,0},{3,1},{4,6},{5,7},{6,4},{7,5},{8,10},{9,11},{10,... | collective-permute-start | bytes 1572872 | tf_op jit(solution)/shard_map/ppermute | solution.py:402
  63.3 7.1 %collective-permute-start.5 = (bf16[512,384]{1,0:T(8,128)(2,1)S(1)}, bf16[512,384]{1,0:T(8,128)(2,1)S(1)}, u32[]{:S(2)}, u32[]{:S(2)}) collective-permute-start(bf16[512,384]{1,0:T(8,128)(2,1)S(1)} %get-tuple-element.36.refs_0_), channel_id=1, source_target_pairs={{0,1},{1,0},{2,3},{3,2},{4,5},{5,4},{6,7},{7,6},{8,9},{9,8},{10,11... | collective-permute-start | bytes 1179656 | tf_op jit(solution)/shard_map/ppermute | solution.py:402
  67.6 2.9 %collective-permute-start.6 = (bf16[512,384]{1,0:T(8,128)(2,1)S(1)}, bf16[512,384]{1,0:T(8,128)(2,1)S(1)}, u32[]{:S(2)}, u32[]{:S(2)}) collective-permute-start(bf16[512,384]{1,0:T(8,128)(2,1)S(1)} %get-tuple-element.37.refs_1_), channel_id=1, source_target_pairs={{0,1},{1,0},{2,3},{3,2},{4,5},{5,4},{6,7},{7,6},{8,9},{9,8},{10,11... | collective-permute-start | bytes 1179656 | tf_op jit(solution)/shard_map/ppermute | solution.py:402
  67.7 2.7 %collective-permute-start.7 = (bf16[512,256]{1,0:T(8,128)(2,1)S(1)}, bf16[512,256]{1,0:T(8,128)(2,1)S(1)}, u32[]{:S(2)}, u32[]{:S(2)}) collective-permute-start(bf16[512,256]{1,0:T(8,128)(2,1)S(1)} %get-tuple-element.38.refs_2_), channel_id=1, source_target_pairs={{0,1},{1,0},{2,3},{3,2},{4,5},{5,4},{6,7},{7,6},{8,9},{9,8},{10,11... | collective-permute-start | bytes 786440 | tf_op jit(solution)/shard_map/ppermute | solution.py:402
  68.1 2.3 %collective-permute-start.8 = (bf16[512,256]{1,0:T(8,128)(2,1)S(1)}, bf16[512,256]{1,0:T(8,128)(2,1)S(1)}, u32[]{:S(2)}, u32[]{:S(2)}) collective-permute-start(bf16[512,256]{1,0:T(8,128)(2,1)S(1)} %collective-permute-done.3.refs_3_), channel_id=1, source_target_pairs={{0,1},{1,0},{2,3},{3,2},{4,5},{5,4},{6,7},{7,6},{8,9},{9,8},{10,11... | collective-permute-start | bytes 786440 | tf_op jit(solution)/shard_map/ppermute | solution.py:402
  72.4 6.1 %collective-permute-start.10 = (bf16[512,512]{1,0:T(8,128)(2,1)S(1)}, bf16[512,512]{1,0:T(8,128)(2,1)S(1)}, u32[]{:S(2)}, u32[]{:S(2)}) collective-permute-start(bf16[512,512]{1,0:T(8,128)(2,1)S(1)} %collective-permute-done.2.refs_0_), channel_id=1, source_target_pairs={{0,1},{1,0},{2,3},{3,2},{4,5},{5,4},{6,7},{7,6},{8,9},{9,8},{10,11... | collective-permute-start | bytes 1572872 | tf_op jit(solution)/shard_map/ppermute | solution.py:402
  76.5 1.9 %collective-permute-start.9 = (bf16[512,256]{1,0:T(8,128)(2,1)S(1)}, bf16[512,256]{1,0:T(8,128)(2,1)S(1)}, u32[]{:S(2)}, u32[]{:S(2)}) collective-permute-start(bf16[512,256]{1,0:T(8,128)(2,1)S(1)} %collective-permute-done.4.refs_4_), channel_id=1, source_target_pairs={{0,1},{1,0},{2,3},{3,2},{4,5},{5,4},{6,7},{7,6},{8,9},{9,8},{10,11... | collective-permute-start | bytes 786440 | tf_op jit(solution)/shard_map/ppermute | solution.py:402

commit v11 on v9

--- a/solution.py
+++ b/solution.py
@@ -56,19 +56,23 @@
     return found
 
 
-def pack_kernel(key_ref, value_ref, piece_ref, held_ref, sem):
-    copies = [
-        pltpu.make_async_copy(source, held_ref.at[i], sem.at[i])
-        for i, source in enumerate([key_ref, value_ref])
-    ]
+def pack_kernel(key_ref, value_ref, piece_ref, sem):
+    copies = []
+    for piece in range(ROW):
+        for seg in range(2):
+            rows = pl.ds(seg * SEG_LEN + piece * PIECE, PIECE)
+            for i, source in enumerate([key_ref, value_ref]):
+                copies.append(
+                    pltpu.make_async_copy(
+                        source.at[rows],
+                        piece_ref.at[piece, seg, pl.ds(i * PIECE, PIECE)],
+                        sem.at[len(copies)],
+                    )
+                )
     for copy in copies:
         copy.start()
-    for i, copy in enumerate(copies):
+    for copy in copies:
         copy.wait()
-        for piece in range(ROW):
-            for seg in range(2):
-                rows = pl.ds(seg * SEG_LEN + piece * PIECE, PIECE)
-                piece_ref[piece, seg, i * PIECE : (i + 1) * PIECE] = held_ref[i, rows]
 
 
 def pack(keys, values):
@@ -77,7 +81,7 @@
         out_shape=jax.ShapeDtypeStruct((ROW, 2, 2 * PIECE, HEAD_DIM), keys.dtype),
         in_specs=[HBM, HBM],
         out_specs=VMEM,
-        scratch_shapes=[pltpu.VMEM((2,) + keys.shape, keys.dtype), pltpu.SemaphoreType.DMA((2,))],
+        scratch_shapes=[pltpu.SemaphoreType.DMA((4 * ROW,))],
         compiler_params=pltpu.CompilerParams(vmem_limit_bytes=SMALL_VMEM),
         cost_estimate=pl.CostEstimate(flops=0, bytes_accessed=1 << 19, transcendentals=0),
         name="pack",
@@ -191,13 +195,9 @@
     )(inside, on_next, on_second, carried, second)
 
 
-def attend_kernel(first_head, blocks, earlier, first_ref, *refs):
+def attend_kernel(first_head, earlier, first_ref, *refs):
     sources, (far_ref, *refs) = refs[:4], refs[4:]
-    if blocks:
-        me_ref, weight_ref = refs[:2]
-        weight_sem = refs.pop()
-        held_ref = refs.pop(-8)
-    earlier = refs[2 : 2 + earlier]
+    earlier = refs[:earlier]
     shared = [refs.pop(-7 - n) for n in range(len(SHARED), 0, -1)] if earlier else []
     out_ref, path_key_ref, path_value_ref, parents_ref, query_ref, key_ref, value_ref, sem = refs[-8:]
     heads = query_ref.shape[1] // HEAD_DIM
@@ -207,8 +207,7 @@
         pltpu.make_async_copy(view, target, sem.at[i])
         for i, (view, target) in enumerate(zip(views, [parents_ref, query_ref, key_ref, value_ref]))
     ]
-    copies = weight_copies(blocks, me_ref, weight_ref, held_ref, weight_sem) if blocks else []
-    for copy in fetches + copies:
+    for copy in fetches:
         copy.start()
 
     def scores_of(query, keys):
@@ -288,24 +287,9 @@
         mixture = mixture.astype(out_ref.dtype)
         out_ref[:, head * HEAD_DIM : (head + 1) * HEAD_DIM] = mixture
         share(first_head + head, mixture)
-    for copy in copies:
-        copy.wait()
-
-
-def weight_copies(blocks, me_ref, weight_ref, held_ref, sem):
-    block = weight_ref.shape[0] // 4
-    copies = []
-    for i, bit in enumerate(blocks):
-        rows = pl.ds(pl.multiple_of((me_ref[0] ^ bit) * block, block), block)
-        copies.append(
-            pltpu.make_async_copy(
-                weight_ref.at[rows], held_ref.at[pl.ds(i * block, block)], sem.at[i]
-            )
-        )
-    return copies
-
-
-def attend(first, parents, queries, keys, values, far, first_head, heads, blocks, bring, after, earlier):
+
+
+def attend(first, parents, queries, keys, values, far, first_head, heads, earlier, after):
     rows = queries.shape[0]
     pairs = heads * rows * (PATH + SEG_LEN + SEG_LEN // 2)
     out_shape = [jax.ShapeDtypeStruct((rows, heads * HEAD_DIM), jnp.bfloat16)]
@@ -319,17 +303,8 @@
         pltpu.VMEM(values.shape, values.dtype),
         pltpu.SemaphoreType.DMA((4,)),
     ]
-    if blocks:
-        me, weight = bring
-        bring = [me, in_hbm(weight)]
-        in_specs += [SMEM, HBM]
-        shape = (len(blocks) * weight.shape[0] // 4, weight.shape[1])
-        out_shape.append(pltpu.VMEM(shape, weight.dtype))
-        scratch.append(pltpu.SemaphoreType.DMA((len(blocks),)))
-    else:
-        bring = []
-    return pl.pallas_call(
-        functools.partial(attend_kernel, first_head, blocks, len(earlier)),
+    return pl.pallas_call(
+        functools.partial(attend_kernel, first_head, len(earlier)),
         out_shape=out_shape,
         in_specs=in_specs + [VMEM] * len(earlier) + [ANY] * len(after),
         out_specs=[VMEM] * len(out_shape),
@@ -348,55 +323,111 @@
         in_hbm(keys),
         in_hbm(values),
         far,
-        *bring,
         *earlier,
         *after,
     )
 
 
-def project_kernel(counts, spans, has_base, near_ref, far_ref, *refs):
+def gather_parts(parts, held_ref):
+    at = 0
+    for part in parts:
+        held_ref[:, at : at + part.shape[1]] = part[...]
+        at += part.shape[1]
+
+
+def first_kernel(counts, me_ref, weight_ref, *refs):
     parts = refs[: sum(counts)]
-    out_ref, held_ref = refs[-2:]
-    at, ends = 0, [0]
+    out_ref, kept_ref, own_ref, held_ref, sem = refs[sum(counts) :]
+    block = own_ref.shape[0]
+    copies = []
+    for bit in range(4):
+        rows = pl.ds(pl.multiple_of((me_ref[0] ^ bit) * block, block), block)
+        target = kept_ref.at[pl.ds((bit - 1) * block, block)] if bit else own_ref
+        copies.append(pltpu.make_async_copy(weight_ref.at[rows], target, sem.at[bit]))
+    for bit in (0, 2, 1, 3):
+        copies[bit].start()
+    gather_parts(parts, held_ref)
+    tiles = [slice(at, at + TILE) for at in range(0, out_ref.shape[1], TILE)]
+    copies[0].wait()
+    for columns in tiles:
+        out_ref[:, columns] = jnp.dot(
+            held_ref[:, :block], own_ref[:, columns], preferred_element_type=jnp.float32
+        )
+    copies[2].wait()
+    depth = held_ref.shape[1] - block
+    for columns in tiles:
+        out_ref[:, columns] += jnp.dot(
+            held_ref[:, block:],
+            kept_ref[block : block + depth, columns],
+            preferred_element_type=jnp.float32,
+        )
+    copies[1].wait()
+    copies[3].wait()
+
+
+def first_project(me, weight, own, across):
+    parts = own + across
+    rows = parts[0].shape[0]
+    depth = sum(part.shape[1] for part in parts)
+    full, width = weight.shape
+    return pl.pallas_call(
+        functools.partial(first_kernel, [len(own), len(across)]),
+        out_shape=(
+            jax.ShapeDtypeStruct((rows, width), jnp.float32),
+            pltpu.VMEM((3 * full // 4, width), weight.dtype),
+        ),
+        in_specs=[SMEM, HBM] + [VMEM] * len(parts),
+        out_specs=(VMEM, VMEM),
+        scratch_shapes=[
+            pltpu.VMEM((full // 4, width), weight.dtype),
+            pltpu.VMEM((rows, depth), parts[0].dtype),
+            pltpu.SemaphoreType.DMA((4,)),
+        ],
+        compiler_params=pltpu.CompilerParams(vmem_limit_bytes=PROJECT_VMEM),
+        cost_estimate=pl.CostEstimate(
+            flops=rows * width, bytes_accessed=rows * width, transcendentals=0
+        ),
+        name="first_project",
+    )(me, in_hbm(weight), *parts)
+
+
+def project_kernel(counts, spans, weight_ref, *refs):
+    parts = refs[: sum(counts)]
+    base_ref, out_ref, held_ref = refs[-3:]
+    gather_parts(parts, held_ref)
+    ends = [0]
     for count in counts:
-        for part in parts[:count]:
-            held_ref[:, at : at + part.shape[1]] = part[...]
-            at += part.shape[1]
+        ends.append(ends[-1] + sum(part.shape[1] for part in parts[:count]))
         parts = parts[count:]
-        ends.append(at)
     for column in range(0, out_ref.shape[1], TILE):
         columns = slice(column, column + TILE)
-        total = refs[sum(counts)][:, columns] if has_base else None
-        for (half, start), begin, end in zip(spans, ends, ends[1:]):
-            product = jnp.dot(
+        total = base_ref[:, columns]
+        for start, begin, end in zip(spans, ends, ends[1:]):
+            total = total + jnp.dot(
                 held_ref[:, begin:end],
-                (near_ref, far_ref)[half][start : start + end - begin, columns],
+                weight_ref[start : start + end - begin, columns],
                 preferred_element_type=jnp.float32,
             )
-            total = product if total is None else total + product
         out_ref[:, columns] = total.astype(out_ref.dtype)
 
 
-def project(groups, spans, weights, base, dtype):
+def project(groups, spans, weight, base, dtype):
     parts = [part for group in groups for part in group]
     rows = parts[0].shape[0]
     depth = sum(part.shape[1] for part in parts)
-    width = weights[0].shape[1]
-    bases = [] if base is None else [base]
-    return pl.pallas_call(
-        functools.partial(project_kernel, [len(g) for g in groups], spans, base is not None),
+    width = weight.shape[1]
+    return pl.pallas_call(
+        functools.partial(project_kernel, [len(g) for g in groups], spans),
         out_shape=jax.ShapeDtypeStruct((rows, width), dtype),
-        in_specs=[VMEM] * (2 + len(parts) + len(bases)),
+        in_specs=[VMEM] * (2 + len(parts)),
         out_specs=VMEM,
         scratch_shapes=[pltpu.VMEM((rows, depth), parts[0].dtype)],
         compiler_params=pltpu.CompilerParams(vmem_limit_bytes=PROJECT_VMEM),
         cost_estimate=pl.CostEstimate(
-            flops=rows * width,
-            bytes_accessed=rows * width,
-            transcendentals=0,
+            flops=rows * width, bytes_accessed=rows * width, transcendentals=0
         ),
         name="project",
-    )(*[in_vmem(weight) for weight in weights], *parts, *bases)
+    )(in_vmem(weight), *parts, base)
 
 
 def swap(part, bit):
@@ -424,31 +455,26 @@
     far = trade(merge(*inside, onward(to_next, ROW), onward(to_second, 2 * ROW)))
 
     width = queries.shape[1]
-    bring = (me.astype(jnp.int32).reshape(1), out_weight)
-    own, across, weights, head = [], [], [], 0
-    for c, (size, blocks) in enumerate([(2, ()), (2, (0, 1)), (4, (2, 3))]):
-        after = [across[c - 2]] if c >= 2 else []
+    own, across, head = [], [], 0
+    for c, size in enumerate((2, 2, 4)):
         earlier = own if c == 2 else []
         part, *rest = attend(
-            first, parents, queries, key_proj, value_proj, far, head, size, blocks, bring, after, earlier
+            first, parents, queries, key_proj, value_proj, far, head, size, earlier, across[: c - 1]
         )
-        weights += rest[len(rest) - len(blocks) // 2 :]
-        own = rest[: len(SHARED)] if earlier else own + [part]
+        own = rest if earlier else own + [part]
         across.append(swap(part, 2))
         head += size
     *own, across[0], across[1] = lax.optimization_barrier(own + across[:2])
     beside = [swap(part, 1) for part in own]
     corner = [swap(part, 1) for part in across[:-1]]
-    total = project([own, across[:-1]], [(0, 0), (1, 0)], weights, None, jnp.float32)
-    total = project(
-        [beside, corner[:-1]], [(0, width), (1, width)], weights, total, jnp.float32
-    )
-    last, total, corner[-1] = lax.optimization_barrier((across[-1], total, corner[-1]))
+    total, weight = first_project(me.astype(jnp.int32).reshape(1), out_weight, own, across[:-1])
+    total = project([beside, corner[:-1]], [0, 2 * width], weight, total, jnp.float32)
+    last, total = lax.optimization_barrier((across[-1], total))
     corner.append(swap(last, 1))
     done = width - last.shape[1]
     turned = sum(part.shape[1] for part in corner[:-2])
     return project(
-        [[last], corner[-2:]], [(1, done), (1, width + turned)], weights, total, jnp.bfloat16
+        [[last], corner[-2:]], [width + done, 2 * width + turned], weight, total, jnp.bfloat16
     )
 
 

time: 86.5 us -> 82.6 us (0.955)
  waiting for transfers between devices: 17.2 us -> 10.4 us
  Pallas kernels: 25.7 us -> 27.2 us
  starting transfers between devices: 25.7 us -> 27 us
    ppermute x9, waiting for transfers between devices: 8.94 us -> 2.17 us  [swap(): return lax.ppermute(part, 'tensor', [(i, i ^ bit) for i in range(size)])]
    pallas_call x3 -> x4, Pallas kernels: 14.7 us -> 18.2 us  [the longest x3 13.9 us: attend(): pl.pallas_call(functools.partial(attend_kernel, first_head, len(earlier))...]
    pallas_call x3 -> x2, Pallas kernels: 7.03 us -> 4.81 us  [project(): pl.pallas_call(functools.partial(project_kernel, [len(g) for g in groups]...]
    ppermute x9, starting transfers between devices: 11.9 us -> 13.2 us  [swap(): return lax.ppermute(part, 'tensor', [(i, i ^ bit) for i in range(size)])]
  transfers between devices with their start and end apart: 12 -> 12, of which waited for: 5 -> 4; matrix products, arithmetic and copies ran while one was open for 0% -> 0% of each run, Pallas kernels for 19% -> 22%
where the time goes in v11:
time: 82.6 us; the launch traced here: 82.2 us
  Pallas kernels  27.2 us (33%)
  starting transfers between devices  27 us (33%)
  blocking collectives  17.6 us (21%)
  waiting for transfers between devices  10.4 us (13%)
    all_to_all x1, blocking collectives, trade(): lax.all_to_all(pieces, 'dp', 0, 0, tiled=True, axis_index_groups=rows)  17.6 us
    pallas_call x3, Pallas kernels, attend(): pl.pallas_call(functools.partial(attend_kernel, first_head, len(earlier))...  13.9 us
    ppermute x9, starting transfers between devices, swap(): return lax.ppermute(part, 'tensor', [(i, i ^ bit) for i in range(size)])  13.2 us
    all_to_all x1, starting transfers between devices, trade(): lax.all_to_all(pieces, 'dp', 0, 0, tiled=True, axis_index_groups=rows)  9.77 us
    all_to_all x1, waiting for transfers between devices, trade(): lax.all_to_all(pieces, 'dp', 0, 0, tiled=True, axis_index_groups=rows)  5.73 us
    pallas_call x2, Pallas kernels, project(): pl.pallas_call(functools.partial(project_kernel, [len(g) for g in groups]...  4.81 us
    pallas_call x1, Pallas kernels, first_project(): pl.pallas_call(functools.partial(first_kernel, [len(own), len(across)]),...  4.32 us
    ppermute x2, starting transfers between devices, onward(): lax.ppermute(piece, 'dp', [(i, (i + step) % devices) for i in range(devic...  3.99 us
  transfers between devices with their start and end apart: 12, of which 4 were waited for; matrix products, arithmetic and copies ran while one was open for 0% of the time, Pallas kernels for 22%

profile of v11, /device:TPU:1, one launch (start us, length us, event | category | flops | bytes accessed | tf_op | source)
XLA Modules:
  0.0 82.2 jit_solution(3106921294653062076)
XLA Ops:
  0.0 1.9 %pack.1 = bf16[8,2,64,128]{3,2,1,0:T(8,128)(2,1)} custom-call(bf16[512,128]{1,0:T(8,128)(2,1)} %refs_2_.5, bf16[512,128]{1,0:T(8,128)(2,1)} %refs_3_.5), custom_call_target="tpu_custom_call" | custom-call | bytes 524288 | tf_op jit(solution)/shard_map/pack/pallas_call | solution.py:79
  1.9 9.8 %all-to-all-start = ((bf16[8,2,64,128]{3,2,1,0:T(8,128)(2,1)}), bf16[8,2,64,128]{3,2,1,0:T(8,128)(2,1)S(1)}, u32[]{:S(2)}, u32[]{:S(2)}) async-start(bf16[8,2,64,128]{3,2,1,0:T(8,128)(2,1)} %pack.1), calls=%async_computation | async-start | bytes 524288 | tf_op jit(solution)/shard_map/all_to_all | solution.py:441
  11.7 5.7 %all-to-all-done = bf16[8,2,64,128]{3,2,1,0:T(8,128)(2,1)S(1)} async-done(((bf16[8,2,64,128]{3,2,1,0:T(8,128)(2,1)}), bf16[8,2,64,128]{3,2,1,0:T(8,128)(2,1)S(1)}, u32[]{:S(2)}, u32[]{:S(2)}) %all-to-all-start) | async-done | bytes 262176 | tf_op jit(solution)/shard_map/all_to_all | solution.py:441
  17.4 0.8 carry_out.1
  18.2 1.4 %collective-permute-start = (bf16[4,64,128]{2,1,0:T(8,128)(2,1)S(1)}, bf16[4,64,128]{2,1,0:T(8,128)(2,1)S(1)}, u32[]{:S(2)}, u32[]{:S(2)}) collective-permute-start(bf16[4,64,128]{2,1,0:T(8,128)(2,1)S(1)} %get-tuple-element.26), channel_id=1, source_target_pairs={{0,32},{4,36},{8,40},{12,44},{16,48},{20,52},{24,56},{28,60},{32,6... | collective-permute-start | bytes 196616 | tf_op jit(solution)/shard_map/ppermute | solution.py:446
  19.6 2.6 %collective-permute-start.1 = (bf16[1,64,128]{2,1,0:T(8,128)(2,1)S(1)}, bf16[1,64,128]{2,1,0:T(8,128)(2,1)S(1)}, u32[]{:S(2)}, u32[]{:S(2)}) collective-permute-start(bf16[1,64,128]{2,1,0:T(8,128)(2,1)S(1)} %get-tuple-element.27), channel_id=1, source_target_pairs={{0,64},{4,68},{8,72},{12,76},{16,80},{20,84},{24,88},{28,92},{32,9... | collective-permute-start | bytes 49160 | tf_op jit(solution)/shard_map/ppermute | solution.py:446
  22.2 1.3 %pick.1 = (bf16[8,4,64,128]{3,2,1,0:T(8,128)(2,1)S(1)}, bf16[8,4,16,128]{3,2,1,0:T(8,128)(2,1)S(1)}, bf16[8,16,128]{2,1,0:T(8,128)(2,1)S(1)}) custom-call(s32[1]{0:T(128)} %bitcast.1.first_ref, s32[128]{0:T(128)} %refs_0_.5, bf16[16,64,128]{2,1,0:T(8,128)(2,1)S(1)} %bitcast.4), custom_call_target="tpu_custom_call" | custom-call | bytes 1048576 | tf_op jit(solution)/shard_map/pick/pallas_call | solution.py:157
  23.6 2.5 %collective-permute-done.1.second_ref = bf16[1,64,128]{2,1,0:T(8,128)(2,1)S(1)} collective-permute-done((bf16[1,64,128]{2,1,0:T(8,128)(2,1)S(1)}, bf16[1,64,128]{2,1,0:T(8,128)(2,1)S(1)}, u32[]{:S(2)}, u32[]{:S(2)}) %collective-permute-start.1) | collective-permute-done | bytes 16416 | tf_op jit(solution)/shard_map/ppermute | solution.py:446
  26.1 0.0 collective-permute-done.next_ref
  26.1 0.1 merge.1
  26.2 17.6 %all_to_all.10.refs_4_ = bf16[8,4,64,128]{3,2,1,0:T(8,128)(2,1)S(1)} all-to-all(bf16[8,4,64,128]{3,2,1,0:T(8,128)(2,1)S(1)} %merge.1), channel_id=1, replica_groups={{28,12,24,8,20,4,16,0},{60,44,56,40,52,36,48,32},{92,76,88,72,84,68,80,..., dimensions={0} | all-to-all | bytes 1048576 | tf_op jit(solution)/shard_map/all_to_all | solution.py:441
  43.8 3.7 %attend.3.refs_5_ = bf16[512,256]{1,0:T(8,128)(2,1)S(1)} custom-call(s32[1]{0:T(128)} %bitcast.1.first_ref, s32[128]{0:T(128)} %refs_0_.5, bf16[512,1024]{1,0:T(8,128)(2,1)} %refs_1_.5, bf16[512,128]{1,0:T(8,128)(2,1)} %refs_2_.5, bf16[512,128]{1,0:T(8,128)(2,1)} %refs_3_.5, bf16[8,4,64,128]{3,2,1,0:T(8,128)(2,1)S(1)} %all_to_all.10.refs_4_), custom_call_target="tpu_custom_call" | custom-call | flops 1845493760 | bytes 1572864 | tf_op jit(solution)/shard_map/attend/pallas_call | solution.py:306
  47.5 1.3 %collective-permute-start.2 = (bf16[512,256]{1,0:T(8,128)(2,1)S(1)}, bf16[512,256]{1,0:T(8,128)(2,1)S(1)}, u32[]{:S(2)}, u32[]{:S(2)}) collective-permute-start(bf16[512,256]{1,0:T(8,128)(2,1)S(1)} %attend.3.refs_5_), channel_id=1, source_target_pairs={{0,2},{1,3},{2,0},{3,1},{4,6},{5,7},{6,4},{7,5},{8,10},{9,11},{10,... | collective-permute-start | bytes 786440 | tf_op jit(solution)/shard_map/ppermute | solution.py:435
  48.8 3.7 %attend.4.refs_6_ = bf16[512,256]{1,0:T(8,128)(2,1)S(1)} custom-call(s32[1]{0:T(128)} %bitcast.1.first_ref, s32[128]{0:T(128)} %refs_0_.5, bf16[512,1024]{1,0:T(8,128)(2,1)} %refs_1_.5, bf16[512,128]{1,0:T(8,128)(2,1)} %refs_2_.5, bf16[512,128]{1,0:T(8,128)(2,1)} %refs_3_.5, bf16[8,4,64,128]{3,2,1,0:T(8,128)(2,1)S(1)} %all_to_all.10.refs_4_), custom_call_target="tpu_custom_call" | custom-call | flops 1845493760 | bytes 1572864 | tf_op jit(solution)/shard_map/attend/pallas_call | solution.py:306
  52.4 0.5 collective-permute-start.3
  53.0 0.0 collective-permute-done.2.refs_7_.refs_3_
  53.0 6.5 %attend.5 = (bf16[512,512]{1,0:T(8,128)(2,1)}, bf16[512,384]{1,0:T(8,128)(2,1)S(1)}, bf16[512,384]{1,0:T(8,128)(2,1)S(1)}, bf16[512,256]{1,0:T(8,128)(2,1)S(1)}) custom-call(s32[1]{0:T(128)} %bitcast.1.first_ref, s32[128]{0:T(128)} %refs_0_.5, bf16[512,1024]{1,0:T(8,128)(2,1)} %refs_1_.5, bf16[512,128]{1,0:T(8,128)(2,1)} %refs_2_.5, ...), custom_call_target="tpu_custom_call" | custom-call | flops 3690987520 | bytes 2097152 | tf_op jit(solution)/shard_map/attend/pallas_call | solution.py:306
  59.5 1.3 %collective-permute-start.4 = (bf16[512,512]{1,0:T(8,128)(2,1)}, bf16[512,512]{1,0:T(8,128)(2,1)S(1)}, u32[]{:S(2)}, u32[]{:S(2)}) collective-permute-start(bf16[512,512]{1,0:T(8,128)(2,1)} %get-tuple-element.37), channel_id=1, source_target_pairs={{0,2},{1,3},{2,0},{3,1},{4,6},{5,7},{6,4},{7,5},{8,10},{9,11},{10,... | collective-permute-start | bytes 1572872 | tf_op jit(solution)/shard_map/ppermute | solution.py:435
  60.8 0.2 collective-permute-done.3.refs_4_
  61.0 7.5 %collective-permute-start.5 = (bf16[512,384]{1,0:T(8,128)(2,1)S(1)}, bf16[512,384]{1,0:T(8,128)(2,1)S(1)}, u32[]{:S(2)}, u32[]{:S(2)}) collective-permute-start(bf16[512,384]{1,0:T(8,128)(2,1)S(1)} %get-tuple-element.31.refs_0_), channel_id=1, source_target_pairs={{0,1},{1,0},{2,3},{3,2},{4,5},{5,4},{6,7},{7,6},{8,9},{9,8},{10,11... | collective-permute-start | bytes 1179656 | tf_op jit(solution)/shard_map/ppermute | solution.py:435
  68.6 0.0 collective-permute-start.6
  68.6 0.5 collective-permute-start.7
  69.1 0.0 collective-permute-start.8
  69.1 4.3 %first_project.1 = (f32[512,1280]{1,0:T(8,128)S(1)}, bf16[3072,1280]{1,0:T(8,128)(2,1)S(1)}) custom-call(s32[1]{0:T(128)} %bitcast.me_ref, bf16[4096,1280]{1,0:T(8,128)(2,1)} %weight_ref.1, bf16[512,384]{1,0:T(8,128)(2,1)S(1)} %get-tuple-element.31.refs_0_, bf16[512,384]{1,0:T(8,128)(2,1)S(1)} %get-tuple-element.32.refs_1_, ...), custom_call_target="tpu_custom_call" | custom-call | flops 655360 | bytes 655360 | tf_op jit(solution)/shard_map/first_project/pallas_call | solution.py:373
  73.4 0.0 collective-permute-done.8.refs_3_
  73.4 0.0 collective-permute-done.5.refs_0_
  73.5 1.9 %project.2.refs_3_ = f32[512,1280]{1,0:T(8,128)S(1)} custom-call(bf16[3072,1280]{1,0:T(8,128)(2,1)S(1)} %get-tuple-element.36.weight_ref, bf16[512,384]{1,0:T(8,128)(2,1)S(1)} %collective-permute-done.5.refs_0_, bf16[512,384]{1,0:T(8,128)(2,1)S(1)} %collective-permute-done.6.refs_1_, bf16[512,256]{1,0:T(8,128)(2,1)S(1)} %collective-permute-done.7.refs_2_, ...), custom_call_target="tpu_custom_call" | custom-call | flops 655360 | bytes 655360 | tf_op jit(solution)/shard_map/project/pallas_call | solution.py:419
  75.4 2.0 %collective-permute-start.10 = (bf16[512,512]{1,0:T(8,128)(2,1)S(1)}, bf16[512,512]{1,0:T(8,128)(2,1)S(1)}, u32[]{:S(2)}, u32[]{:S(2)}) collective-permute-start(bf16[512,512]{1,0:T(8,128)(2,1)S(1)} %collective-permute-done.4.refs_0_), channel_id=1, source_target_pairs={{0,1},{1,0},{2,3},{3,2},{4,5},{5,4},{6,7},{7,6},{8,9},{9,8},{10,11... | collective-permute-start | bytes 1572872 | tf_op jit(solution)/shard_map/ppermute | solution.py:435
  77.4 0.0 collective-permute-start.9
  77.4 1.9 %collective-permute-done.9.refs_1_ = bf16[512,256]{1,0:T(8,128)(2,1)S(1)} collective-permute-done((bf16[512,256]{1,0:T(8,128)(2,1)S(1)}, bf16[512,256]{1,0:T(8,128)(2,1)S(1)}, u32[]{:S(2)}, u32[]{:S(2)}) %collective-permute-start.9) | collective-permute-done | bytes 262176 | tf_op jit(solution)/shard_map/ppermute | solution.py:435
  79.3 0.0 collective-permute-done.10.refs_2_
  79.3 2.9 %project.3 = bf16[512,1280]{1,0:T(8,128)(2,1)} custom-call(bf16[3072,1280]{1,0:T(8,128)(2,1)S(1)} %get-tuple-element.36.weight_ref, bf16[512,512]{1,0:T(8,128)(2,1)S(1)} %collective-permute-done.4.refs_0_, bf16[512,256]{1,0:T(8,128)(2,1)S(1)} %collective-permute-done.9.refs_1_, bf16[512,512]{1,0:T(8,128)(2,1)S(1)} %collective-permute-done.10.refs_2_, ...), custom_call_target="tpu_custom_call" | custom-call | flops 655360 | bytes 655360 | tf_op jit(solution)/shard_map/project/pallas_call | solution.py:419
  (3 shorter events, 0.0 us)
Async XLA Ops:
  1.9 15.5 %all-to-all-start = ((bf16[8,2,64,128]{3,2,1,0:T(8,128)(2,1)}), bf16[8,2,64,128]{3,2,1,0:T(8,128)(2,1)S(1)}, u32[]{:S(2)}, u32[]{:S(2)}) async-start(bf16[8,2,64,128]{3,2,1,0:T(8,128)(2,1)} %pack.1), calls=%async_computation | async-start | bytes 524288 | tf_op jit(solution)/shard_map/all_to_all | solution.py:441
  18.2 7.9 %collective-permute-start = (bf16[4,64,128]{2,1,0:T(8,128)(2,1)S(1)}, bf16[4,64,128]{2,1,0:T(8,128)(2,1)S(1)}, u32[]{:S(2)}, u32[]{:S(2)}) collective-permute-start(bf16[4,64,128]{2,1,0:T(8,128)(2,1)S(1)} %get-tuple-element.26), channel_id=1, source_target_pairs={{0,32},{4,36},{8,40},{12,44},{16,48},{20,52},{24,56},{28,60},{32,6... | collective-permute-start | bytes 196616 | tf_op jit(solution)/shard_map/ppermute | solution.py:446
  19.6 6.5 %collective-permute-start.1 = (bf16[1,64,128]{2,1,0:T(8,128)(2,1)S(1)}, bf16[1,64,128]{2,1,0:T(8,128)(2,1)S(1)}, u32[]{:S(2)}, u32[]{:S(2)}) collective-permute-start(bf16[1,64,128]{2,1,0:T(8,128)(2,1)S(1)} %get-tuple-element.27), channel_id=1, source_target_pairs={{0,64},{4,68},{8,72},{12,76},{16,80},{20,84},{24,88},{28,92},{32,9... | collective-permute-start | bytes 49160 | tf_op jit(solution)/shard_map/ppermute | solution.py:446
  47.5 5.5 %collective-permute-start.2 = (bf16[512,256]{1,0:T(8,128)(2,1)S(1)}, bf16[512,256]{1,0:T(8,128)(2,1)S(1)}, u32[]{:S(2)}, u32[]{:S(2)}) collective-permute-start(bf16[512,256]{1,0:T(8,128)(2,1)S(1)} %attend.3.refs_5_), channel_id=1, source_target_pairs={{0,2},{1,3},{2,0},{3,1},{4,6},{5,7},{6,4},{7,5},{8,10},{9,11},{10,... | collective-permute-start | bytes 786440 | tf_op jit(solution)/shard_map/ppermute | solution.py:435
  52.4 8.6 %collective-permute-start.3 = (bf16[512,256]{1,0:T(8,128)(2,1)S(1)}, bf16[512,256]{1,0:T(8,128)(2,1)S(1)}, u32[]{:S(2)}, u32[]{:S(2)}) collective-permute-start(bf16[512,256]{1,0:T(8,128)(2,1)S(1)} %attend.4.refs_6_), channel_id=1, source_target_pairs={{0,2},{1,3},{2,0},{3,1},{4,6},{5,7},{6,4},{7,5},{8,10},{9,11},{10,... | collective-permute-start | bytes 786440 | tf_op jit(solution)/shard_map/ppermute | solution.py:435
  59.5 15.9 %collective-permute-start.4 = (bf16[512,512]{1,0:T(8,128)(2,1)}, bf16[512,512]{1,0:T(8,128)(2,1)S(1)}, u32[]{:S(2)}, u32[]{:S(2)}) collective-permute-start(bf16[512,512]{1,0:T(8,128)(2,1)} %get-tuple-element.37), channel_id=1, source_target_pairs={{0,2},{1,3},{2,0},{3,1},{4,6},{5,7},{6,4},{7,5},{8,10},{9,11},{10,... | collective-permute-start | bytes 1572872 | tf_op jit(solution)/shard_map/ppermute | solution.py:435
  61.0 12.4 %collective-permute-start.5 = (bf16[512,384]{1,0:T(8,128)(2,1)S(1)}, bf16[512,384]{1,0:T(8,128)(2,1)S(1)}, u32[]{:S(2)}, u32[]{:S(2)}) collective-permute-start(bf16[512,384]{1,0:T(8,128)(2,1)S(1)} %get-tuple-element.31.refs_0_), channel_id=1, source_target_pairs={{0,1},{1,0},{2,3},{3,2},{4,5},{5,4},{6,7},{7,6},{8,9},{9,8},{10,11... | collective-permute-start | bytes 1179656 | tf_op jit(solution)/shard_map/ppermute | solution.py:435
  68.6 4.9 %collective-permute-start.6 = (bf16[512,384]{1,0:T(8,128)(2,1)S(1)}, bf16[512,384]{1,0:T(8,128)(2,1)S(1)}, u32[]{:S(2)}, u32[]{:S(2)}) collective-permute-start(bf16[512,384]{1,0:T(8,128)(2,1)S(1)} %get-tuple-element.32.refs_1_), channel_id=1, source_target_pairs={{0,1},{1,0},{2,3},{3,2},{4,5},{5,4},{6,7},{7,6},{8,9},{9,8},{10,11... | collective-permute-start | bytes 1179656 | tf_op jit(solution)/shard_map/ppermute | solution.py:435
  68.6 4.8 %collective-permute-start.7 = (bf16[512,256]{1,0:T(8,128)(2,1)S(1)}, bf16[512,256]{1,0:T(8,128)(2,1)S(1)}, u32[]{:S(2)}, u32[]{:S(2)}) collective-permute-start(bf16[512,256]{1,0:T(8,128)(2,1)S(1)} %get-tuple-element.33.refs_2_), channel_id=1, source_target_pairs={{0,1},{1,0},{2,3},{3,2},{4,5},{5,4},{6,7},{7,6},{8,9},{9,8},{10,11... | collective-permute-start | bytes 786440 | tf_op jit(solution)/shard_map/ppermute | solution.py:435
  69.1 4.3 %collective-permute-start.8 = (bf16[512,256]{1,0:T(8,128)(2,1)S(1)}, bf16[512,256]{1,0:T(8,128)(2,1)S(1)}, u32[]{:S(2)}, u32[]{:S(2)}) collective-permute-start(bf16[512,256]{1,0:T(8,128)(2,1)S(1)} %collective-permute-done.2.refs_7_.refs_3_), channel_id=1, source_target_pairs={{0,1},{1,0},{2,3},{3,2},{4,5},{5,4},{6,7},{7,6},{8,9},{9,8},{10,11... | collective-permute-start | bytes 786440 | tf_op jit(solution)/shard_map/ppermute | solution.py:435
  75.4 3.9 %collective-permute-start.10 = (bf16[512,512]{1,0:T(8,128)(2,1)S(1)}, bf16[512,512]{1,0:T(8,128)(2,1)S(1)}, u32[]{:S(2)}, u32[]{:S(2)}) collective-permute-start(bf16[512,512]{1,0:T(8,128)(2,1)S(1)} %collective-permute-done.4.refs_0_), channel_id=1, source_target_pairs={{0,1},{1,0},{2,3},{3,2},{4,5},{5,4},{6,7},{7,6},{8,9},{9,8},{10,11... | collective-permute-start | bytes 1572872 | tf_op jit(solution)/shard_map/ppermute | solution.py:435
  77.4 1.9 %collective-permute-start.9 = (bf16[512,256]{1,0:T(8,128)(2,1)S(1)}, bf16[512,256]{1,0:T(8,128)(2,1)S(1)}, u32[]{:S(2)}, u32[]{:S(2)}) collective-permute-start(bf16[512,256]{1,0:T(8,128)(2,1)S(1)} %collective-permute-done.3.refs_4_), channel_id=1, source_target_pairs={{0,1},{1,0},{2,3},{3,2},{4,5},{5,4},{6,7},{7,6},{8,9},{9,8},{10,11... | collective-permute-start | bytes 786440 | tf_op jit(solution)/shard_map/ppermute | solution.py:435

commit v12 on v7

--- a/solution.py
+++ b/solution.py
@@ -406,7 +406,7 @@
     width = queries.shape[1]
     bring = (me.astype(jnp.int32).reshape(1), out_weight)
     own, across, weights, head = [], [], [], 0
-    for c, (size, blocks) in enumerate([(2, ()), (3, (0, 1)), (3, (2, 3))]):
+    for c, (size, blocks) in enumerate([(3, ()), (3, (0, 1)), (2, (2, 3))]):
         after = [across[c - 2]] if c >= 2 else []
         part, *brought = attend(
             first, parents, queries, key_proj, value_proj, far, head, size, blocks, bring, after

time: 82 us -> 82.2 us (level)
  blocking collectives: 17.6 us -> 0 us
  starting transfers between devices: 24.1 us -> 34.4 us
  waiting for transfers between devices: 14.2 us -> 20.2 us
    all_to_all x1 -> x0, blocking collectives: 17.6 us -> none  [trade(): lax.all_to_all(pieces, 'dp', 0, 0, tiled=True, axis_index_groups=rows)]
    all_to_all x1 -> x2, waiting for transfers between devices: 5.73 us -> 16.4 us  [trade(): lax.all_to_all(pieces, 'dp', 0, 0, tiled=True, axis_index_groups=rows)]
    all_to_all x1 -> x2, starting transfers between devices: 9.77 us -> 17.8 us  [trade(): lax.all_to_all(pieces, 'dp', 0, 0, tiled=True, axis_index_groups=rows)]
    ppermute x9, waiting for transfers between devices: 5.9 us -> 1.18 us  [swap(): return lax.ppermute(part, 'tensor', [(i, i ^ bit) for i in range(size)])]
    ppermute x9, starting transfers between devices: 10.4 us -> 12.6 us  [swap(): return lax.ppermute(part, 'tensor', [(i, i ^ bit) for i in range(size)])]
  transfers between devices with their start and end apart: 12 -> 13, of which waited for: 5 -> 4; matrix products, arithmetic and copies ran while one was open for 0% -> 0% of each run, Pallas kernels for 20% -> 20%
where the time goes in v12:
time: 82.2 us; the launch traced here: 81.2 us
  starting transfers between devices  34.4 us (42%)
  Pallas kernels  26.6 us (32%)
  waiting for transfers between devices  20.2 us (25%)
    all_to_all x2, starting transfers between devices, trade(): lax.all_to_all(pieces, 'dp', 0, 0, tiled=True, axis_index_groups=rows)  17.8 us
    all_to_all x2, waiting for transfers between devices, trade(): lax.all_to_all(pieces, 'dp', 0, 0, tiled=True, axis_index_groups=rows)  16.4 us
    pallas_call x3, Pallas kernels, attend(): pl.pallas_call(functools.partial(attend_kernel, first_head, blocks), out_...  14.7 us
    ppermute x9, starting transfers between devices, swap(): return lax.ppermute(part, 'tensor', [(i, i ^ bit) for i in range(size)])  12.6 us
    pallas_call x2, Pallas kernels, project(): pl.pallas_call(functools.partial(project_kernel, [len(g) for g in groups]...  7.2 us
    ppermute x2, starting transfers between devices, onward(): lax.ppermute(piece, 'dp', [(i, (i + step) % devices) for i in range(devic...  3.99 us
    ppermute x2, waiting for transfers between devices, onward(): lax.ppermute(piece, 'dp', [(i, (i + step) % devices) for i in range(devic...  2.53 us
    pallas_call x1, Pallas kernels, pack(): pl.pallas_call(pack_kernel, out_shape=jax.ShapeDtypeStruct((ROW, 2, 2 * P...  1.69 us
  transfers between devices with their start and end apart: 13, of which 4 were waited for; matrix products, arithmetic and copies ran while one was open for 0% of the time, Pallas kernels for 20%

profile of v12, /device:TPU:1, one launch (start us, length us, event | category | flops | bytes accessed | tf_op | source)
XLA Modules:
  0.0 81.2 jit_solution(2093346194489183337)
XLA Ops:
  0.0 1.7 %pack.1 = bf16[8,2,64,128]{3,2,1,0:T(8,128)(2,1)} custom-call(bf16[512,128]{1,0:T(8,128)(2,1)} %refs_2_.5, bf16[512,128]{1,0:T(8,128)(2,1)} %refs_3_.5), custom_call_target="tpu_custom_call" | custom-call | bytes 524288 | tf_op jit(solution)/shard_map/pack/pallas_call | solution.py:74
  1.7 9.8 %all-to-all-start = ((bf16[8,2,64,128]{3,2,1,0:T(8,128)(2,1)}), bf16[8,2,64,128]{3,2,1,0:T(8,128)(2,1)S(1)}, u32[]{:S(2)}, u32[]{:S(2)}) async-start(bf16[8,2,64,128]{3,2,1,0:T(8,128)(2,1)} %pack.1), calls=%async_computation | async-start | bytes 524288 | tf_op jit(solution)/shard_map/all_to_all | solution.py:390
  11.5 5.7 %all-to-all-done = bf16[8,2,64,128]{3,2,1,0:T(8,128)(2,1)S(1)} async-done(((bf16[8,2,64,128]{3,2,1,0:T(8,128)(2,1)}), bf16[8,2,64,128]{3,2,1,0:T(8,128)(2,1)S(1)}, u32[]{:S(2)}, u32[]{:S(2)}) %all-to-all-start) | async-done | bytes 262176 | tf_op jit(solution)/shard_map/all_to_all | solution.py:390
  17.2 0.8 carry_out.1
  18.0 1.4 %collective-permute-start = (bf16[4,64,128]{2,1,0:T(8,128)(2,1)S(1)}, bf16[4,64,128]{2,1,0:T(8,128)(2,1)S(1)}, u32[]{:S(2)}, u32[]{:S(2)}) collective-permute-start(bf16[4,64,128]{2,1,0:T(8,128)(2,1)S(1)} %get-tuple-element.19), channel_id=1, source_target_pairs={{0,32},{4,36},{8,40},{12,44},{16,48},{20,52},{24,56},{28,60},{32,6... | collective-permute-start | bytes 196616 | tf_op jit(solution)/shard_map/ppermute | solution.py:395
  19.4 2.6 %collective-permute-start.1 = (bf16[1,64,128]{2,1,0:T(8,128)(2,1)S(1)}, bf16[1,64,128]{2,1,0:T(8,128)(2,1)S(1)}, u32[]{:S(2)}, u32[]{:S(2)}) collective-permute-start(bf16[1,64,128]{2,1,0:T(8,128)(2,1)S(1)} %get-tuple-element.20), channel_id=1, source_target_pairs={{0,64},{4,68},{8,72},{12,76},{16,80},{20,84},{24,88},{28,92},{32,9... | collective-permute-start | bytes 49160 | tf_op jit(solution)/shard_map/ppermute | solution.py:395
  22.0 1.3 %pick.1 = (bf16[8,4,64,128]{3,2,1,0:T(8,128)(2,1)S(1)}, bf16[8,4,16,128]{3,2,1,0:T(8,128)(2,1)S(1)}, bf16[8,16,128]{2,1,0:T(8,128)(2,1)S(1)}) custom-call(s32[1]{0:T(128)} %bitcast.first_ref, s32[128]{0:T(128)} %refs_0_.5, bf16[16,64,128]{2,1,0:T(8,128)(2,1)S(1)} %bitcast.4), custom_call_target="tpu_custom_call" | custom-call | bytes 1048576 | tf_op jit(solution)/shard_map/pick/pallas_call | solution.py:152
  23.3 2.5 %collective-permute-done.1.second_ref = bf16[1,64,128]{2,1,0:T(8,128)(2,1)S(1)} collective-permute-done((bf16[1,64,128]{2,1,0:T(8,128)(2,1)S(1)}, bf16[1,64,128]{2,1,0:T(8,128)(2,1)S(1)}, u32[]{:S(2)}, u32[]{:S(2)}) %collective-permute-start.1) | collective-permute-done | bytes 16416 | tf_op jit(solution)/shard_map/ppermute | solution.py:395
  25.9 0.0 collective-permute-done.next_ref
  25.9 0.9 %merge.1 = bf16[8,4,64,128]{3,2,1,0:T(8,128)(2,1)} custom-call(bf16[8,4,64,128]{3,2,1,0:T(8,128)(2,1)S(1)} %get-tuple-element.16.inside_ref, bf16[8,4,16,128]{3,2,1,0:T(8,128)(2,1)S(1)} %get-tuple-element.17.on_next_ref, bf16[8,16,128]{2,1,0:T(8,128)(2,1)S(1)} %get-tuple-element.18.on_second_ref, bf16[4,64,128]{2,1,0:T(8,128)(2,1)S(1)} %collective-permute-done.next_ref, ...), custom_call_target="tpu_custom_call" | custom-call | bytes 1048576 | tf_op jit(solution)/shard_map/merge/pallas_call | solution.py:182
  26.8 8.0 %all-to-all-start.1 = ((bf16[8,4,64,128]{3,2,1,0:T(8,128)(2,1)}), bf16[8,4,64,128]{3,2,1,0:T(8,128)(2,1)S(1)}, u32[]{:S(2)}, u32[]{:S(2)}) async-start(bf16[8,4,64,128]{3,2,1,0:T(8,128)(2,1)} %merge.1), calls=%async_computation.1 | async-start | bytes 1048576 | tf_op jit(solution)/shard_map/all_to_all | solution.py:390
  34.8 10.7 %all-to-all-done.1.refs_4_ = bf16[8,4,64,128]{3,2,1,0:T(8,128)(2,1)S(1)} async-done(((bf16[8,4,64,128]{3,2,1,0:T(8,128)(2,1)}), bf16[8,4,64,128]{3,2,1,0:T(8,128)(2,1)S(1)}, u32[]{:S(2)}, u32[]{:S(2)}) %all-to-all-start.1) | async-done | bytes 524320 | tf_op jit(solution)/shard_map/all_to_all | solution.py:390
  45.5 4.7 %attend.4.refs_0_ = bf16[512,384]{1,0:T(8,128)(2,1)S(1)} custom-call(s32[1]{0:T(128)} %bitcast.first_ref, s32[128]{0:T(128)} %refs_0_.5, bf16[512,1024]{1,0:T(8,128)(2,1)} %refs_1_.5, bf16[512,128]{1,0:T(8,128)(2,1)} %refs_2_.5, bf16[512,128]{1,0:T(8,128)(2,1)} %refs_3_.5, bf16[8,4,64,128]{3,2,1,0:T(8,128)(2,1)S(1)} %all-to-all-done.1.refs_4_), custom_call_target="tpu_custom_call" | custom-call | flops 2768240640 | bytes 1835008 | tf_op jit(solution)/shard_map/attend/pallas_call | solution.py:312
  50.2 1.3 %collective-permute-start.2 = (bf16[512,384]{1,0:T(8,128)(2,1)S(1)}, bf16[512,384]{1,0:T(8,128)(2,1)S(1)}, u32[]{:S(2)}, u32[]{:S(2)}) collective-permute-start(bf16[512,384]{1,0:T(8,128)(2,1)S(1)} %attend.4.refs_0_), channel_id=1, source_target_pairs={{0,2},{1,3},{2,0},{3,1},{4,6},{5,7},{6,4},{7,5},{8,10},{9,11},{10,... | collective-permute-start | bytes 1179656 | tf_op jit(solution)/shard_map/ppermute | solution.py:384
  51.5 5.5 %attend.3 = (bf16[512,384]{1,0:T(8,128)(2,1)S(1)}, bf16[2048,1280]{1,0:T(8,128)(2,1)S(1)}) custom-call(s32[1]{0:T(128)} %bitcast.first_ref, s32[128]{0:T(128)} %refs_0_.5, bf16[512,1024]{1,0:T(8,128)(2,1)} %refs_1_.5, bf16[512,128]{1,0:T(8,128)(2,1)} %refs_2_.5, bf16[512,128]{1,0:T(8,128)(2,1)} %refs_3_.5, ...), custom_call_target="tpu_custom_call" | custom-call | flops 2768240640 | bytes 1835008 | tf_op jit(solution)/shard_map/attend/pallas_call | solution.py:312
  57.0 0.3 collective-permute-start.7
  57.3 4.0 %collective-permute-start.5 = (bf16[512,384]{1,0:T(8,128)(2,1)S(1)}, bf16[512,384]{1,0:T(8,128)(2,1)S(1)}, u32[]{:S(2)}, u32[]{:S(2)}) collective-permute-start(bf16[512,384]{1,0:T(8,128)(2,1)S(1)} %get-tuple-element.24.refs_1_), channel_id=1, source_target_pairs={{0,1},{1,0},{2,3},{3,2},{4,5},{5,4},{6,7},{7,6},{8,9},{9,8},{10,11... | collective-permute-start | bytes 1179656 | tf_op jit(solution)/shard_map/ppermute | solution.py:384
  61.3 0.0 collective-permute-start.4
  61.3 0.0 collective-permute-done.2.refs_7_.refs_6_
  61.3 2.0 %collective-permute-start.8 = (bf16[512,384]{1,0:T(8,128)(2,1)S(1)}, bf16[512,384]{1,0:T(8,128)(2,1)S(1)}, u32[]{:S(2)}, u32[]{:S(2)}) collective-permute-start(bf16[512,384]{1,0:T(8,128)(2,1)S(1)} %collective-permute-done.2.refs_7_.refs_6_), channel_id=1, source_target_pairs={{0,1},{1,0},{2,3},{3,2},{4,5},{5,4},{6,7},{7,6},{8,9},{9,8},{10,11... | collective-permute-start | bytes 1179656 | tf_op jit(solution)/shard_map/ppermute | solution.py:384
  63.3 4.5 %attend.5 = (bf16[512,256]{1,0:T(8,128)(2,1)S(1)}, bf16[2048,1280]{1,0:T(8,128)(2,1)S(1)}) custom-call(s32[1]{0:T(128)} %bitcast.first_ref, s32[128]{0:T(128)} %refs_0_.5, bf16[512,1024]{1,0:T(8,128)(2,1)} %refs_1_.5, bf16[512,128]{1,0:T(8,128)(2,1)} %refs_2_.5, bf16[512,128]{1,0:T(8,128)(2,1)} %refs_3_.5, ...), custom_call_target="tpu_custom_call" | custom-call | flops 1845493760 | bytes 1572864 | tf_op jit(solution)/shard_map/attend/pallas_call | solution.py:312
  67.8 0.1 collective-permute-start.6
  67.9 0.0 collective-permute-done.7.refs_7_
  68.0 2.3 %collective-permute-start.3 = (bf16[512,256]{1,0:T(8,128)(2,1)S(1)}, bf16[512,256]{1,0:T(8,128)(2,1)S(1)}, u32[]{:S(2)}, u32[]{:S(2)}) collective-permute-start(bf16[512,256]{1,0:T(8,128)(2,1)S(1)} %get-tuple-element.23.refs_2_), channel_id=1, source_target_pairs={{0,2},{1,3},{2,0},{3,1},{4,6},{5,7},{6,4},{7,5},{8,10},{9,11},{10,... | collective-permute-start | bytes 786440 | tf_op jit(solution)/shard_map/ppermute | solution.py:384
  70.2 0.0 collective-permute-done.5.refs_4_
  70.2 1.5 %collective-permute-start.9 = (bf16[512,384]{1,0:T(8,128)(2,1)S(1)}, bf16[512,384]{1,0:T(8,128)(2,1)S(1)}, u32[]{:S(2)}, u32[]{:S(2)}) collective-permute-start(bf16[512,384]{1,0:T(8,128)(2,1)S(1)} %collective-permute-done.7.refs_7_), channel_id=1, source_target_pairs={{0,1},{1,0},{2,3},{3,2},{4,5},{5,4},{6,7},{7,6},{8,9},{9,8},{10,11... | collective-permute-start | bytes 1179656 | tf_op jit(solution)/shard_map/ppermute | solution.py:384
  71.7 0.0 collective-permute-done.4.refs_3_
  71.7 0.0 collective-permute-done.6.refs_5_
  71.7 4.6 %project.2.refs_3_ = f32[512,1280]{1,0:T(8,128)S(1)} custom-call(bf16[2048,1280]{1,0:T(8,128)(2,1)S(1)} %get-tuple-element.21.near_ref, bf16[2048,1280]{1,0:T(8,128)(2,1)S(1)} %get-tuple-element.22.far_ref, bf16[512,384]{1,0:T(8,128)(2,1)S(1)} %attend.4.refs_0_, bf16[512,384]{1,0:T(8,128)(2,1)S(1)} %get-tuple-element.24.refs_1_, ...), custom_call_target="tpu_custom_call" | custom-call | flops 655360 | bytes 655360 | tf_op jit(solution)/shard_map/project/pallas_call | solution.py:366
  76.4 1.1 %collective-permute-start.10 = (bf16[512,256]{1,0:T(8,128)(2,1)S(1)}, bf16[512,256]{1,0:T(8,128)(2,1)S(1)}, u32[]{:S(2)}, u32[]{:S(2)}) collective-permute-start(bf16[512,256]{1,0:T(8,128)(2,1)S(1)} %collective-permute-done.3.refs_0_), channel_id=1, source_target_pairs={{0,1},{1,0},{2,3},{3,2},{4,5},{5,4},{6,7},{7,6},{8,9},{9,8},{10,11... | collective-permute-start | bytes 786440 | tf_op jit(solution)/shard_map/ppermute | solution.py:384
  77.5 1.2 %collective-permute-done.10.refs_2_ = bf16[512,256]{1,0:T(8,128)(2,1)S(1)} collective-permute-done((bf16[512,256]{1,0:T(8,128)(2,1)S(1)}, bf16[512,256]{1,0:T(8,128)(2,1)S(1)}, u32[]{:S(2)}, u32[]{:S(2)}) %collective-permute-start.10) | collective-permute-done | bytes 262176 | tf_op jit(solution)/shard_map/ppermute | solution.py:384
  78.6 2.6 %project.3 = bf16[512,1280]{1,0:T(8,128)(2,1)} custom-call(bf16[2048,1280]{1,0:T(8,128)(2,1)S(1)} %get-tuple-element.21.near_ref, bf16[2048,1280]{1,0:T(8,128)(2,1)S(1)} %get-tuple-element.22.far_ref, bf16[512,256]{1,0:T(8,128)(2,1)S(1)} %collective-permute-done.3.refs_0_, bf16[512,384]{1,0:T(8,128)(2,1)S(1)} %collective-permute-done.9.refs_1_, ...), custom_call_target="tpu_custom_call" | custom-call | flops 655360 | bytes 655360 | tf_op jit(solution)/shard_map/project/pallas_call | solution.py:366
  (3 shorter events, 0.0 us)
Async XLA Ops:
  1.7 15.5 %all-to-all-start = ((bf16[8,2,64,128]{3,2,1,0:T(8,128)(2,1)}), bf16[8,2,64,128]{3,2,1,0:T(8,128)(2,1)S(1)}, u32[]{:S(2)}, u32[]{:S(2)}) async-start(bf16[8,2,64,128]{3,2,1,0:T(8,128)(2,1)} %pack.1), calls=%async_computation | async-start | bytes 524288 | tf_op jit(solution)/shard_map/all_to_all | solution.py:390
  18.0 7.9 %collective-permute-start = (bf16[4,64,128]{2,1,0:T(8,128)(2,1)S(1)}, bf16[4,64,128]{2,1,0:T(8,128)(2,1)S(1)}, u32[]{:S(2)}, u32[]{:S(2)}) collective-permute-start(bf16[4,64,128]{2,1,0:T(8,128)(2,1)S(1)} %get-tuple-element.19), channel_id=1, source_target_pairs={{0,32},{4,36},{8,40},{12,44},{16,48},{20,52},{24,56},{28,60},{32,6... | collective-permute-start | bytes 196616 | tf_op jit(solution)/shard_map/ppermute | solution.py:395
  19.4 6.5 %collective-permute-start.1 = (bf16[1,64,128]{2,1,0:T(8,128)(2,1)S(1)}, bf16[1,64,128]{2,1,0:T(8,128)(2,1)S(1)}, u32[]{:S(2)}, u32[]{:S(2)}) collective-permute-start(bf16[1,64,128]{2,1,0:T(8,128)(2,1)S(1)} %get-tuple-element.20), channel_id=1, source_target_pairs={{0,64},{4,68},{8,72},{12,76},{16,80},{20,84},{24,88},{28,92},{32,9... | collective-permute-start | bytes 49160 | tf_op jit(solution)/shard_map/ppermute | solution.py:395
  26.8 18.7 %all-to-all-start.1 = ((bf16[8,4,64,128]{3,2,1,0:T(8,128)(2,1)}), bf16[8,4,64,128]{3,2,1,0:T(8,128)(2,1)S(1)}, u32[]{:S(2)}, u32[]{:S(2)}) async-start(bf16[8,4,64,128]{3,2,1,0:T(8,128)(2,1)} %merge.1), calls=%async_computation.1 | async-start | bytes 1048576 | tf_op jit(solution)/shard_map/all_to_all | solution.py:390
  50.2 11.1 %collective-permute-start.2 = (bf16[512,384]{1,0:T(8,128)(2,1)S(1)}, bf16[512,384]{1,0:T(8,128)(2,1)S(1)}, u32[]{:S(2)}, u32[]{:S(2)}) collective-permute-start(bf16[512,384]{1,0:T(8,128)(2,1)S(1)} %attend.4.refs_0_), channel_id=1, source_target_pairs={{0,2},{1,3},{2,0},{3,1},{4,6},{5,7},{6,4},{7,5},{8,10},{9,11},{10,... | collective-permute-start | bytes 1179656 | tf_op jit(solution)/shard_map/ppermute | solution.py:384
  57.0 11.0 %collective-permute-start.7 = (bf16[512,384]{1,0:T(8,128)(2,1)S(1)}, bf16[512,384]{1,0:T(8,128)(2,1)S(1)}, u32[]{:S(2)}, u32[]{:S(2)}) collective-permute-start(bf16[512,384]{1,0:T(8,128)(2,1)S(1)} %get-tuple-element.24.refs_1_), channel_id=1, source_target_pairs={{0,2},{1,3},{2,0},{3,1},{4,6},{5,7},{6,4},{7,5},{8,10},{9,11},{10,... | collective-permute-start | bytes 1179656 | tf_op jit(solution)/shard_map/ppermute | solution.py:384
  57.3 12.9 %collective-permute-start.5 = (bf16[512,384]{1,0:T(8,128)(2,1)S(1)}, bf16[512,384]{1,0:T(8,128)(2,1)S(1)}, u32[]{:S(2)}, u32[]{:S(2)}) collective-permute-start(bf16[512,384]{1,0:T(8,128)(2,1)S(1)} %get-tuple-element.24.refs_1_), channel_id=1, source_target_pairs={{0,1},{1,0},{2,3},{3,2},{4,5},{5,4},{6,7},{7,6},{8,9},{9,8},{10,11... | collective-permute-start | bytes 1179656 | tf_op jit(solution)/shard_map/ppermute | solution.py:384
  61.3 10.4 %collective-permute-start.4 = (bf16[512,384]{1,0:T(8,128)(2,1)S(1)}, bf16[512,384]{1,0:T(8,128)(2,1)S(1)}, u32[]{:S(2)}, u32[]{:S(2)}) collective-permute-start(bf16[512,384]{1,0:T(8,128)(2,1)S(1)} %attend.4.refs_0_), channel_id=1, source_target_pairs={{0,1},{1,0},{2,3},{3,2},{4,5},{5,4},{6,7},{7,6},{8,9},{9,8},{10,11... | collective-permute-start | bytes 1179656 | tf_op jit(solution)/shard_map/ppermute | solution.py:384
  61.3 10.4 %collective-permute-start.8 = (bf16[512,384]{1,0:T(8,128)(2,1)S(1)}, bf16[512,384]{1,0:T(8,128)(2,1)S(1)}, u32[]{:S(2)}, u32[]{:S(2)}) collective-permute-start(bf16[512,384]{1,0:T(8,128)(2,1)S(1)} %collective-permute-done.2.refs_7_.refs_6_), channel_id=1, source_target_pairs={{0,1},{1,0},{2,3},{3,2},{4,5},{5,4},{6,7},{7,6},{8,9},{9,8},{10,11... | collective-permute-start | bytes 1179656 | tf_op jit(solution)/shard_map/ppermute | solution.py:384
  67.8 3.9 %collective-permute-start.6 = (bf16[512,256]{1,0:T(8,128)(2,1)S(1)}, bf16[512,256]{1,0:T(8,128)(2,1)S(1)}, u32[]{:S(2)}, u32[]{:S(2)}) collective-permute-start(bf16[512,256]{1,0:T(8,128)(2,1)S(1)} %get-tuple-element.23.refs_2_), channel_id=1, source_target_pairs={{0,1},{1,0},{2,3},{3,2},{4,5},{5,4},{6,7},{7,6},{8,9},{9,8},{10,11... | collective-permute-start | bytes 786440 | tf_op jit(solution)/shard_map/ppermute | solution.py:384
  68.0 8.4 %collective-permute-start.3 = (bf16[512,256]{1,0:T(8,128)(2,1)S(1)}, bf16[512,256]{1,0:T(8,128)(2,1)S(1)}, u32[]{:S(2)}, u32[]{:S(2)}) collective-permute-start(bf16[512,256]{1,0:T(8,128)(2,1)S(1)} %get-tuple-element.23.refs_2_), channel_id=1, source_target_pairs={{0,2},{1,3},{2,0},{3,1},{4,6},{5,7},{6,4},{7,5},{8,10},{9,11},{10,... | collective-permute-start | bytes 786440 | tf_op jit(solution)/shard_map/ppermute | solution.py:384
  70.2 7.3 %collective-permute-start.9 = (bf16[512,384]{1,0:T(8,128)(2,1)S(1)}, bf16[512,384]{1,0:T(8,128)(2,1)S(1)}, u32[]{:S(2)}, u32[]{:S(2)}) collective-permute-start(bf16[512,384]{1,0:T(8,128)(2,1)S(1)} %collective-permute-done.7.refs_7_), channel_id=1, source_target_pairs={{0,1},{1,0},{2,3},{3,2},{4,5},{5,4},{6,7},{7,6},{8,9},{9,8},{10,11... | collective-permute-start | bytes 1179656 | tf_op jit(solution)/shard_map/ppermute | solution.py:384
  76.4 2.3 %collective-permute-start.10 = (bf16[512,256]{1,0:T(8,128)(2,1)S(1)}, bf16[512,256]{1,0:T(8,128)(2,1)S(1)}, u32[]{:S(2)}, u32[]{:S(2)}) collective-permute-start(bf16[512,256]{1,0:T(8,128)(2,1)S(1)} %collective-permute-done.3.refs_0_), channel_id=1, source_target_pairs={{0,1},{1,0},{2,3},{3,2},{4,5},{5,4},{6,7},{7,6},{8,9},{9,8},{10,11... | collective-permute-start | bytes 786440 | tf_op jit(solution)/shard_map/ppermute | solution.py:384

commit v13 on v12

--- a/solution.py
+++ b/solution.py
@@ -416,16 +416,17 @@
         across.append(swap(part, 2))
         head += size
     beside = [swap(part, 1) for part in own]
-    corner = [swap(part, 1) for part in across[:-1]]
+    corner = [swap(across[0], 1)]
     near = project(
-        [own + beside, across[:-1], corner[:-1]], [(0, 0), (1, 0), (1, width)], weights, None, jnp.float32
+        [own + beside, across[:1], corner], [(0, 0), (1, 0), (1, width)], weights, None, jnp.float32
     )
-    last, near = lax.optimization_barrier((across[-1], near))
-    corner.append(swap(last, 1))
-    done = width - last.shape[1]
-    turned = sum(part.shape[1] for part in corner[:-2])
+    across[1], near = lax.optimization_barrier((across[1], near))
+    corner.append(swap(across[1], 1))
+    across[2], near = lax.optimization_barrier((across[2], near))
+    corner.append(swap(across[2], 1))
+    done = across[0].shape[1]
     return project(
-        [[last], corner[-2:]], [(1, done), (1, width + turned)], weights, near, jnp.bfloat16
+        [across[1:], corner[1:]], [(1, done), (1, width + done)], weights, near, jnp.bfloat16
     )
 
 

time: 82.2 us -> 82.1 us (level)
  blocking collectives: 0 us -> 17.6 us
  starting transfers between devices: 34.4 us -> 24.8 us
  waiting for transfers between devices: 20.2 us -> 13.2 us
    all_to_all x0 -> x1, blocking collectives: none -> 17.6 us  [trade(): lax.all_to_all(pieces, 'dp', 0, 0, tiled=True, axis_index_groups=rows)]
    all_to_all x2 -> x1, waiting for transfers between devices: 16.4 us -> 5.73 us  [trade(): lax.all_to_all(pieces, 'dp', 0, 0, tiled=True, axis_index_groups=rows)]
    all_to_all x2 -> x1, starting transfers between devices: 17.8 us -> 9.77 us  [trade(): lax.all_to_all(pieces, 'dp', 0, 0, tiled=True, axis_index_groups=rows)]
    ppermute x9, waiting for transfers between devices: 1.18 us -> 4.92 us  [swap(): return lax.ppermute(part, 'tensor', [(i, i ^ bit) for i in range(size)])]
    ppermute x9, starting transfers between devices: 12.6 us -> 11.1 us  [swap(): return lax.ppermute(part, 'tensor', [(i, i ^ bit) for i in range(size)])]
  transfers between devices with their start and end apart: 13 -> 12, of which waited for: 4 -> 5; matrix products, arithmetic and copies ran while one was open for 0% -> 0% of each run, Pallas kernels for 20% -> 19%
where the time goes in v13:
time: 82.1 us; the launch traced here: 81.8 us
  Pallas kernels  26.1 us (32%)
  starting transfers between devices  24.8 us (30%)
  blocking collectives  17.6 us (21%)
  waiting for transfers between devices  13.2 us (16%)
    all_to_all x1, blocking collectives, trade(): lax.all_to_all(pieces, 'dp', 0, 0, tiled=True, axis_index_groups=rows)  17.6 us
    pallas_call x3, Pallas kernels, attend(): pl.pallas_call(functools.partial(attend_kernel, first_head, blocks), out_...  14.7 us
    ppermute x9, starting transfers between devices, swap(): return lax.ppermute(part, 'tensor', [(i, i ^ bit) for i in range(size)])  11.1 us
    all_to_all x1, starting transfers between devices, trade(): lax.all_to_all(pieces, 'dp', 0, 0, tiled=True, axis_index_groups=rows)  9.77 us
    pallas_call x2, Pallas kernels, project(): pl.pallas_call(functools.partial(project_kernel, [len(g) for g in groups]...  7.53 us
    all_to_all x1, waiting for transfers between devices, trade(): lax.all_to_all(pieces, 'dp', 0, 0, tiled=True, axis_index_groups=rows)  5.73 us
    ppermute x9, waiting for transfers between devices, swap(): return lax.ppermute(part, 'tensor', [(i, i ^ bit) for i in range(size)])  4.92 us
    ppermute x2, starting transfers between devices, onward(): lax.ppermute(piece, 'dp', [(i, (i + step) % devices) for i in range(devic...  3.99 us
  transfers between devices with their start and end apart: 12, of which 5 were waited for; matrix products, arithmetic and copies ran while one was open for 0% of the time, Pallas kernels for 19%

profile of v13, /device:TPU:1, one launch (start us, length us, event | category | flops | bytes accessed | tf_op | source)
XLA Modules:
  0.0 81.8 jit_solution(18119253463192807795)
XLA Ops:
  0.0 1.7 %pack.1 = bf16[8,2,64,128]{3,2,1,0:T(8,128)(2,1)} custom-call(bf16[512,128]{1,0:T(8,128)(2,1)} %refs_2_.5, bf16[512,128]{1,0:T(8,128)(2,1)} %refs_3_.5), custom_call_target="tpu_custom_call" | custom-call | bytes 524288 | tf_op jit(solution)/shard_map/pack/pallas_call | solution.py:74
  1.7 9.8 %all-to-all-start = ((bf16[8,2,64,128]{3,2,1,0:T(8,128)(2,1)}), bf16[8,2,64,128]{3,2,1,0:T(8,128)(2,1)S(1)}, u32[]{:S(2)}, u32[]{:S(2)}) async-start(bf16[8,2,64,128]{3,2,1,0:T(8,128)(2,1)} %pack.1), calls=%async_computation | async-start | bytes 524288 | tf_op jit(solution)/shard_map/all_to_all | solution.py:390
  11.5 5.7 %all-to-all-done = bf16[8,2,64,128]{3,2,1,0:T(8,128)(2,1)S(1)} async-done(((bf16[8,2,64,128]{3,2,1,0:T(8,128)(2,1)}), bf16[8,2,64,128]{3,2,1,0:T(8,128)(2,1)S(1)}, u32[]{:S(2)}, u32[]{:S(2)}) %all-to-all-start) | async-done | bytes 262176 | tf_op jit(solution)/shard_map/all_to_all | solution.py:390
  17.2 0.8 carry_out.1
  18.0 1.4 %collective-permute-start = (bf16[4,64,128]{2,1,0:T(8,128)(2,1)S(1)}, bf16[4,64,128]{2,1,0:T(8,128)(2,1)S(1)}, u32[]{:S(2)}, u32[]{:S(2)}) collective-permute-start(bf16[4,64,128]{2,1,0:T(8,128)(2,1)S(1)} %get-tuple-element.21), channel_id=1, source_target_pairs={{0,32},{4,36},{8,40},{12,44},{16,48},{20,52},{24,56},{28,60},{32,6... | collective-permute-start | bytes 196616 | tf_op jit(solution)/shard_map/ppermute | solution.py:395
  19.4 2.6 %collective-permute-start.1 = (bf16[1,64,128]{2,1,0:T(8,128)(2,1)S(1)}, bf16[1,64,128]{2,1,0:T(8,128)(2,1)S(1)}, u32[]{:S(2)}, u32[]{:S(2)}) collective-permute-start(bf16[1,64,128]{2,1,0:T(8,128)(2,1)S(1)} %get-tuple-element.22), channel_id=1, source_target_pairs={{0,64},{4,68},{8,72},{12,76},{16,80},{20,84},{24,88},{28,92},{32,9... | collective-permute-start | bytes 49160 | tf_op jit(solution)/shard_map/ppermute | solution.py:395
  22.0 1.3 %pick.1 = (bf16[8,4,64,128]{3,2,1,0:T(8,128)(2,1)S(1)}, bf16[8,4,16,128]{3,2,1,0:T(8,128)(2,1)S(1)}, bf16[8,16,128]{2,1,0:T(8,128)(2,1)S(1)}) custom-call(s32[1]{0:T(128)} %bitcast.first_ref, s32[128]{0:T(128)} %refs_0_.5, bf16[16,64,128]{2,1,0:T(8,128)(2,1)S(1)} %bitcast.4), custom_call_target="tpu_custom_call" | custom-call | bytes 1048576 | tf_op jit(solution)/shard_map/pick/pallas_call | solution.py:152
  23.3 2.5 %collective-permute-done.1.second_ref = bf16[1,64,128]{2,1,0:T(8,128)(2,1)S(1)} collective-permute-done((bf16[1,64,128]{2,1,0:T(8,128)(2,1)S(1)}, bf16[1,64,128]{2,1,0:T(8,128)(2,1)S(1)}, u32[]{:S(2)}, u32[]{:S(2)}) %collective-permute-start.1) | collective-permute-done | bytes 16416 | tf_op jit(solution)/shard_map/ppermute | solution.py:395
  25.9 0.0 collective-permute-done.next_ref
  25.9 0.1 merge.1
  26.0 17.6 %all_to_all.10.refs_4_ = bf16[8,4,64,128]{3,2,1,0:T(8,128)(2,1)S(1)} all-to-all(bf16[8,4,64,128]{3,2,1,0:T(8,128)(2,1)S(1)} %merge.1), channel_id=1, replica_groups={{28,12,24,8,20,4,16,0},{60,44,56,40,52,36,48,32},{92,76,88,72,84,68,80,..., dimensions={0} | all-to-all | bytes 1048576 | tf_op jit(solution)/shard_map/all_to_all | solution.py:390
  43.5 4.7 %attend.4.refs_0_ = bf16[512,384]{1,0:T(8,128)(2,1)S(1)} custom-call(s32[1]{0:T(128)} %bitcast.first_ref, s32[128]{0:T(128)} %refs_0_.5, bf16[512,1024]{1,0:T(8,128)(2,1)} %refs_1_.5, bf16[512,128]{1,0:T(8,128)(2,1)} %refs_2_.5, bf16[512,128]{1,0:T(8,128)(2,1)} %refs_3_.5, bf16[8,4,64,128]{3,2,1,0:T(8,128)(2,1)S(1)} %all_to_all.10.refs_4_), custom_call_target="tpu_custom_call" | custom-call | flops 2768240640 | bytes 1835008 | tf_op jit(solution)/shard_map/attend/pallas_call | solution.py:312
  48.3 1.3 %collective-permute-start.2 = (bf16[512,384]{1,0:T(8,128)(2,1)S(1)}, bf16[512,384]{1,0:T(8,128)(2,1)S(1)}, u32[]{:S(2)}, u32[]{:S(2)}) collective-permute-start(bf16[512,384]{1,0:T(8,128)(2,1)S(1)} %attend.4.refs_0_), channel_id=1, source_target_pairs={{0,2},{1,3},{2,0},{3,1},{4,6},{5,7},{6,4},{7,5},{8,10},{9,11},{10,... | collective-permute-start | bytes 1179656 | tf_op jit(solution)/shard_map/ppermute | solution.py:384
  49.5 5.5 %attend.3 = (bf16[512,384]{1,0:T(8,128)(2,1)S(1)}, bf16[2048,1280]{1,0:T(8,128)(2,1)S(1)}) custom-call(s32[1]{0:T(128)} %bitcast.first_ref, s32[128]{0:T(128)} %refs_0_.5, bf16[512,1024]{1,0:T(8,128)(2,1)} %refs_1_.5, bf16[512,128]{1,0:T(8,128)(2,1)} %refs_2_.5, bf16[512,128]{1,0:T(8,128)(2,1)} %refs_3_.5, bf16[8,4,64,128]{3,2,1,0:T(8,128)(2,1)S(1)} %all_to_all.10.refs_4_, ...), custom_call_target="tpu_custom_call" | custom-call | flops 2768240640 | bytes 1835008 | tf_op jit(solution)/shard_map/attend/pallas_call | solution.py:312
  55.1 5.1 %collective-permute-start.5 = (bf16[512,384]{1,0:T(8,128)(2,1)S(1)}, bf16[512,384]{1,0:T(8,128)(2,1)S(1)}, u32[]{:S(2)}, u32[]{:S(2)}) collective-permute-start(bf16[512,384]{1,0:T(8,128)(2,1)S(1)} %get-tuple-element.25.refs_1_), channel_id=1, source_target_pairs={{0,1},{1,0},{2,3},{3,2},{4,5},{5,4},{6,7},{7,6},{8,9},{9,8},{10,11... | collective-permute-start | bytes 1179656 | tf_op jit(solution)/shard_map/ppermute | solution.py:384
  60.1 0.1 collective-permute-start.4
  60.2 0.3 collective-permute-start.3
  60.5 0.7 collective-permute-start.7
  61.2 4.5 %attend.5 = (bf16[512,256]{1,0:T(8,128)(2,1)S(1)}, bf16[2048,1280]{1,0:T(8,128)(2,1)S(1)}) custom-call(s32[1]{0:T(128)} %bitcast.first_ref, s32[128]{0:T(128)} %refs_0_.5, bf16[512,1024]{1,0:T(8,128)(2,1)} %refs_1_.5, bf16[512,128]{1,0:T(8,128)(2,1)} %refs_2_.5, bf16[512,128]{1,0:T(8,128)(2,1)} %refs_3_.5, bf16[8,4,64,128]{3,2,1,0:T(8,128)(2,1)S(1)} %all_to_all.10.refs_4_, ...), custom_call_target="tpu_custom_call" | custom-call | flops 1845493760 | bytes 1572864 | tf_op jit(solution)/shard_map/attend/pallas_call | solution.py:312
  65.7 0.1 collective-permute-start.6
  65.8 0.0 collective-permute-done.5.refs_4_
  65.8 1.3 %collective-permute-start.8 = (bf16[512,256]{1,0:T(8,128)(2,1)S(1)}, bf16[512,256]{1,0:T(8,128)(2,1)S(1)}, u32[]{:S(2)}, u32[]{:S(2)}) collective-permute-start(bf16[512,256]{1,0:T(8,128)(2,1)S(1)} %get-tuple-element.26.refs_2_), channel_id=1, source_target_pairs={{0,2},{1,3},{2,0},{3,1},{4,6},{5,7},{6,4},{7,5},{8,10},{9,11},{10,... | collective-permute-start | bytes 786440 | tf_op jit(solution)/shard_map/ppermute | solution.py:384
  67.1 0.0 collective-permute-done.4.refs_3_
  67.1 0.2 collective-permute-done.6.refs_5_
  67.3 4.3 %project.2.refs_4_ = f32[512,1280]{1,0:T(8,128)S(1)} custom-call(bf16[2048,1280]{1,0:T(8,128)(2,1)S(1)} %get-tuple-element.23.near_ref, bf16[2048,1280]{1,0:T(8,128)(2,1)S(1)} %get-tuple-element.24.far_ref, bf16[512,384]{1,0:T(8,128)(2,1)S(1)} %attend.4.refs_0_, bf16[512,384]{1,0:T(8,128)(2,1)S(1)} %get-tuple-element.25.refs_1_, ...), custom_call_target="tpu_custom_call" | custom-call | flops 655360 | bytes 655360 | tf_op jit(solution)/shard_map/project/pallas_call | solution.py:366
  71.6 0.0 collective-permute-done.3.refs_0_
  71.6 1.0 %collective-permute-start.9 = (bf16[512,384]{1,0:T(8,128)(2,1)S(1)}, bf16[512,384]{1,0:T(8,128)(2,1)S(1)}, u32[]{:S(2)}, u32[]{:S(2)}) collective-permute-start(bf16[512,384]{1,0:T(8,128)(2,1)S(1)} %collective-permute-done.3.refs_0_), channel_id=1, source_target_pairs={{0,1},{1,0},{2,3},{3,2},{4,5},{5,4},{6,7},{7,6},{8,9},{9,8},{10,11... | collective-permute-start | bytes 1179656 | tf_op jit(solution)/shard_map/ppermute | solution.py:384
  72.6 3.5 %collective-permute-done.8.refs_1_ = bf16[512,256]{1,0:T(8,128)(2,1)S(1)} collective-permute-done((bf16[512,256]{1,0:T(8,128)(2,1)S(1)}, bf16[512,256]{1,0:T(8,128)(2,1)S(1)}, u32[]{:S(2)}, u32[]{:S(2)}) %collective-permute-start.8) | collective-permute-done | bytes 262176 | tf_op jit(solution)/shard_map/ppermute | solution.py:384
  76.1 1.2 %collective-permute-start.10 = (bf16[512,256]{1,0:T(8,128)(2,1)S(1)}, bf16[512,256]{1,0:T(8,128)(2,1)S(1)}, u32[]{:S(2)}, u32[]{:S(2)}) collective-permute-start(bf16[512,256]{1,0:T(8,128)(2,1)S(1)} %collective-permute-done.8.refs_1_), channel_id=1, source_target_pairs={{0,1},{1,0},{2,3},{3,2},{4,5},{5,4},{6,7},{7,6},{8,9},{9,8},{10,11... | collective-permute-start | bytes 786440 | tf_op jit(solution)/shard_map/ppermute | solution.py:384
  77.4 1.2 %collective-permute-done.10.refs_3_ = bf16[512,256]{1,0:T(8,128)(2,1)S(1)} collective-permute-done((bf16[512,256]{1,0:T(8,128)(2,1)S(1)}, bf16[512,256]{1,0:T(8,128)(2,1)S(1)}, u32[]{:S(2)}, u32[]{:S(2)}) %collective-permute-start.10) | collective-permute-done | bytes 262176 | tf_op jit(solution)/shard_map/ppermute | solution.py:384
  78.5 0.0 collective-permute-done.9.refs_2_
  78.5 3.3 %project.3 = bf16[512,1280]{1,0:T(8,128)(2,1)} custom-call(bf16[2048,1280]{1,0:T(8,128)(2,1)S(1)} %get-tuple-element.23.near_ref, bf16[2048,1280]{1,0:T(8,128)(2,1)S(1)} %get-tuple-element.24.far_ref, bf16[512,384]{1,0:T(8,128)(2,1)S(1)} %collective-permute-done.3.refs_0_, bf16[512,256]{1,0:T(8,128)(2,1)S(1)} %collective-permute-done.8.refs_1_, ...), custom_call_target="tpu_custom_call" | custom-call | flops 655360 | bytes 655360 | tf_op jit(solution)/shard_map/project/pallas_call | solution.py:366
  (2 shorter events, 0.0 us)
Async XLA Ops:
  1.7 15.5 %all-to-all-start = ((bf16[8,2,64,128]{3,2,1,0:T(8,128)(2,1)}), bf16[8,2,64,128]{3,2,1,0:T(8,128)(2,1)S(1)}, u32[]{:S(2)}, u32[]{:S(2)}) async-start(bf16[8,2,64,128]{3,2,1,0:T(8,128)(2,1)} %pack.1), calls=%async_computation | async-start | bytes 524288 | tf_op jit(solution)/shard_map/all_to_all | solution.py:390
  18.0 7.9 %collective-permute-start = (bf16[4,64,128]{2,1,0:T(8,128)(2,1)S(1)}, bf16[4,64,128]{2,1,0:T(8,128)(2,1)S(1)}, u32[]{:S(2)}, u32[]{:S(2)}) collective-permute-start(bf16[4,64,128]{2,1,0:T(8,128)(2,1)S(1)} %get-tuple-element.21), channel_id=1, source_target_pairs={{0,32},{4,36},{8,40},{12,44},{16,48},{20,52},{24,56},{28,60},{32,6... | collective-permute-start | bytes 196616 | tf_op jit(solution)/shard_map/ppermute | solution.py:395
  19.4 6.5 %collective-permute-start.1 = (bf16[1,64,128]{2,1,0:T(8,128)(2,1)S(1)}, bf16[1,64,128]{2,1,0:T(8,128)(2,1)S(1)}, u32[]{:S(2)}, u32[]{:S(2)}) collective-permute-start(bf16[1,64,128]{2,1,0:T(8,128)(2,1)S(1)} %get-tuple-element.22), channel_id=1, source_target_pairs={{0,64},{4,68},{8,72},{12,76},{16,80},{20,84},{24,88},{28,92},{32,9... | collective-permute-start | bytes 49160 | tf_op jit(solution)/shard_map/ppermute | solution.py:395
  48.3 12.2 %collective-permute-start.2 = (bf16[512,384]{1,0:T(8,128)(2,1)S(1)}, bf16[512,384]{1,0:T(8,128)(2,1)S(1)}, u32[]{:S(2)}, u32[]{:S(2)}) collective-permute-start(bf16[512,384]{1,0:T(8,128)(2,1)S(1)} %attend.4.refs_0_), channel_id=1, source_target_pairs={{0,2},{1,3},{2,0},{3,1},{4,6},{5,7},{6,4},{7,5},{8,10},{9,11},{10,... | collective-permute-start | bytes 1179656 | tf_op jit(solution)/shard_map/ppermute | solution.py:384
  55.1 10.7 %collective-permute-start.5 = (bf16[512,384]{1,0:T(8,128)(2,1)S(1)}, bf16[512,384]{1,0:T(8,128)(2,1)S(1)}, u32[]{:S(2)}, u32[]{:S(2)}) collective-permute-start(bf16[512,384]{1,0:T(8,128)(2,1)S(1)} %get-tuple-element.25.refs_1_), channel_id=1, source_target_pairs={{0,1},{1,0},{2,3},{3,2},{4,5},{5,4},{6,7},{7,6},{8,9},{9,8},{10,11... | collective-permute-start | bytes 1179656 | tf_op jit(solution)/shard_map/ppermute | solution.py:384
  60.1 7.0 %collective-permute-start.4 = (bf16[512,384]{1,0:T(8,128)(2,1)S(1)}, bf16[512,384]{1,0:T(8,128)(2,1)S(1)}, u32[]{:S(2)}, u32[]{:S(2)}) collective-permute-start(bf16[512,384]{1,0:T(8,128)(2,1)S(1)} %attend.4.refs_0_), channel_id=1, source_target_pairs={{0,1},{1,0},{2,3},{3,2},{4,5},{5,4},{6,7},{7,6},{8,9},{9,8},{10,11... | collective-permute-start | bytes 1179656 | tf_op jit(solution)/shard_map/ppermute | solution.py:384
  60.2 11.4 %collective-permute-start.3 = (bf16[512,384]{1,0:T(8,128)(2,1)S(1)}, bf16[512,384]{1,0:T(8,128)(2,1)S(1)}, u32[]{:S(2)}, u32[]{:S(2)}) collective-permute-start(bf16[512,384]{1,0:T(8,128)(2,1)S(1)} %get-tuple-element.25.refs_1_), channel_id=1, source_target_pairs={{0,2},{1,3},{2,0},{3,1},{4,6},{5,7},{6,4},{7,5},{8,10},{9,11},{10,... | collective-permute-start | bytes 1179656 | tf_op jit(solution)/shard_map/ppermute | solution.py:384
  60.5 6.8 %collective-permute-start.7 = (bf16[512,384]{1,0:T(8,128)(2,1)S(1)}, bf16[512,384]{1,0:T(8,128)(2,1)S(1)}, u32[]{:S(2)}, u32[]{:S(2)}) collective-permute-start(bf16[512,384]{1,0:T(8,128)(2,1)S(1)} %collective-permute-done.2.refs_7_.refs_6_), channel_id=1, source_target_pairs={{0,1},{1,0},{2,3},{3,2},{4,5},{5,4},{6,7},{7,6},{8,9},{9,8},{10,11... | collective-permute-start | bytes 1179656 | tf_op jit(solution)/shard_map/ppermute | solution.py:384
  65.7 1.6 %collective-permute-start.6 = (bf16[512,256]{1,0:T(8,128)(2,1)S(1)}, bf16[512,256]{1,0:T(8,128)(2,1)S(1)}, u32[]{:S(2)}, u32[]{:S(2)}) collective-permute-start(bf16[512,256]{1,0:T(8,128)(2,1)S(1)} %get-tuple-element.26.refs_2_), channel_id=1, source_target_pairs={{0,1},{1,0},{2,3},{3,2},{4,5},{5,4},{6,7},{7,6},{8,9},{9,8},{10,11... | collective-permute-start | bytes 786440 | tf_op jit(solution)/shard_map/ppermute | solution.py:384
  65.8 10.3 %collective-permute-start.8 = (bf16[512,256]{1,0:T(8,128)(2,1)S(1)}, bf16[512,256]{1,0:T(8,128)(2,1)S(1)}, u32[]{:S(2)}, u32[]{:S(2)}) collective-permute-start(bf16[512,256]{1,0:T(8,128)(2,1)S(1)} %get-tuple-element.26.refs_2_), channel_id=1, source_target_pairs={{0,2},{1,3},{2,0},{3,1},{4,6},{5,7},{6,4},{7,5},{8,10},{9,11},{10,... | collective-permute-start | bytes 786440 | tf_op jit(solution)/shard_map/ppermute | solution.py:384
  71.6 7.0 %collective-permute-start.9 = (bf16[512,384]{1,0:T(8,128)(2,1)S(1)}, bf16[512,384]{1,0:T(8,128)(2,1)S(1)}, u32[]{:S(2)}, u32[]{:S(2)}) collective-permute-start(bf16[512,384]{1,0:T(8,128)(2,1)S(1)} %collective-permute-done.3.refs_0_), channel_id=1, source_target_pairs={{0,1},{1,0},{2,3},{3,2},{4,5},{5,4},{6,7},{7,6},{8,9},{9,8},{10,11... | collective-permute-start | bytes 1179656 | tf_op jit(solution)/shard_map/ppermute | solution.py:384
  76.1 2.4 %collective-permute-start.10 = (bf16[512,256]{1,0:T(8,128)(2,1)S(1)}, bf16[512,256]{1,0:T(8,128)(2,1)S(1)}, u32[]{:S(2)}, u32[]{:S(2)}) collective-permute-start(bf16[512,256]{1,0:T(8,128)(2,1)S(1)} %collective-permute-done.8.refs_1_), channel_id=1, source_target_pairs={{0,1},{1,0},{2,3},{3,2},{4,5},{5,4},{6,7},{7,6},{8,9},{9,8},{10,11... | collective-permute-start | bytes 786440 | tf_op jit(solution)/shard_map/ppermute | solution.py:384

commit v14 on v7

--- a/solution.py
+++ b/solution.py
@@ -415,6 +415,7 @@
         own.append(part)
         across.append(swap(part, 2))
         head += size
+    own = lax.optimization_barrier(own)
     beside = [swap(part, 1) for part in own]
     corner = [swap(part, 1) for part in across[:-1]]
     near = project(

time: 82 us -> 82.3 us (level)
  blocking collectives: 17.6 us -> 0 us
  waiting for transfers between devices: 14.2 us -> 24.1 us
  starting transfers between devices: 24.1 us -> 31.3 us
    all_to_all x1 -> x0, blocking collectives: 17.6 us -> none  [trade(): lax.all_to_all(pieces, 'dp', 0, 0, tiled=True, axis_index_groups=rows)]
    all_to_all x1 -> x2, waiting for transfers between devices: 5.73 us -> 16.4 us  [trade(): lax.all_to_all(pieces, 'dp', 0, 0, tiled=True, axis_index_groups=rows)]
    all_to_all x1 -> x2, starting transfers between devices: 9.77 us -> 17.8 us  [trade(): lax.all_to_all(pieces, 'dp', 0, 0, tiled=True, axis_index_groups=rows)]
    ppermute x9, starting transfers between devices: 10.4 us -> 9.51 us  [swap(): return lax.ppermute(part, 'tensor', [(i, i ^ bit) for i in range(size)])]
  transfers between devices with their start and end apart: 12 -> 13, of which waited for: 5 -> 6; matrix products, arithmetic and copies ran while one was open for 0% -> 0% of each run, Pallas kernels for 20% -> 20%
where the time goes in v14:
time: 82.3 us; the launch traced here: 82 us
  starting transfers between devices  31.3 us (38%)
  Pallas kernels  26.6 us (32%)
  waiting for transfers between devices  24.1 us (29%)
    all_to_all x2, starting transfers between devices, trade(): lax.all_to_all(pieces, 'dp', 0, 0, tiled=True, axis_index_groups=rows)  17.8 us
    all_to_all x2, waiting for transfers between devices, trade(): lax.all_to_all(pieces, 'dp', 0, 0, tiled=True, axis_index_groups=rows)  16.4 us
    pallas_call x3, Pallas kernels, attend(): pl.pallas_call(functools.partial(attend_kernel, first_head, blocks), out_...  14.7 us
    ppermute x9, starting transfers between devices, swap(): return lax.ppermute(part, 'tensor', [(i, i ^ bit) for i in range(size)])  9.51 us
    pallas_call x2, Pallas kernels, project(): pl.pallas_call(functools.partial(project_kernel, [len(g) for g in groups]...  7.16 us
    ppermute x9, waiting for transfers between devices, swap(): return lax.ppermute(part, 'tensor', [(i, i ^ bit) for i in range(size)])  5.09 us
    ppermute x2, starting transfers between devices, onward(): lax.ppermute(piece, 'dp', [(i, (i + step) % devices) for i in range(devic...  3.99 us
    ppermute x2, waiting for transfers between devices, onward(): lax.ppermute(piece, 'dp', [(i, (i + step) % devices) for i in range(devic...  2.53 us
  transfers between devices with their start and end apart: 13, of which 6 were waited for; matrix products, arithmetic and copies ran while one was open for 0% of the time, Pallas kernels for 20%

profile of v14, /device:TPU:1, one launch (start us, length us, event | category | flops | bytes accessed | tf_op | source)
XLA Modules:
  0.0 82.0 jit_solution(9910926911387681827)
XLA Ops:
  0.0 1.7 %pack.1 = bf16[8,2,64,128]{3,2,1,0:T(8,128)(2,1)} custom-call(bf16[512,128]{1,0:T(8,128)(2,1)} %refs_2_.5, bf16[512,128]{1,0:T(8,128)(2,1)} %refs_3_.5), custom_call_target="tpu_custom_call" | custom-call | bytes 524288 | tf_op jit(solution)/shard_map/pack/pallas_call | solution.py:74
  1.7 9.8 %all-to-all-start = ((bf16[8,2,64,128]{3,2,1,0:T(8,128)(2,1)}), bf16[8,2,64,128]{3,2,1,0:T(8,128)(2,1)S(1)}, u32[]{:S(2)}, u32[]{:S(2)}) async-start(bf16[8,2,64,128]{3,2,1,0:T(8,128)(2,1)} %pack.1), calls=%async_computation | async-start | bytes 524288 | tf_op jit(solution)/shard_map/all_to_all | solution.py:390
  11.5 5.7 %all-to-all-done = bf16[8,2,64,128]{3,2,1,0:T(8,128)(2,1)S(1)} async-done(((bf16[8,2,64,128]{3,2,1,0:T(8,128)(2,1)}), bf16[8,2,64,128]{3,2,1,0:T(8,128)(2,1)S(1)}, u32[]{:S(2)}, u32[]{:S(2)}) %all-to-all-start) | async-done | bytes 262176 | tf_op jit(solution)/shard_map/all_to_all | solution.py:390
  17.2 0.8 carry_out.1
  18.0 1.4 %collective-permute-start = (bf16[4,64,128]{2,1,0:T(8,128)(2,1)S(1)}, bf16[4,64,128]{2,1,0:T(8,128)(2,1)S(1)}, u32[]{:S(2)}, u32[]{:S(2)}) collective-permute-start(bf16[4,64,128]{2,1,0:T(8,128)(2,1)S(1)} %get-tuple-element.22), channel_id=1, source_target_pairs={{0,32},{4,36},{8,40},{12,44},{16,48},{20,52},{24,56},{28,60},{32,6... | collective-permute-start | bytes 196616 | tf_op jit(solution)/shard_map/ppermute | solution.py:395
  19.4 2.6 %collective-permute-start.1 = (bf16[1,64,128]{2,1,0:T(8,128)(2,1)S(1)}, bf16[1,64,128]{2,1,0:T(8,128)(2,1)S(1)}, u32[]{:S(2)}, u32[]{:S(2)}) collective-permute-start(bf16[1,64,128]{2,1,0:T(8,128)(2,1)S(1)} %get-tuple-element.23), channel_id=1, source_target_pairs={{0,64},{4,68},{8,72},{12,76},{16,80},{20,84},{24,88},{28,92},{32,9... | collective-permute-start | bytes 49160 | tf_op jit(solution)/shard_map/ppermute | solution.py:395
  22.0 1.3 %pick.1 = (bf16[8,4,64,128]{3,2,1,0:T(8,128)(2,1)S(1)}, bf16[8,4,16,128]{3,2,1,0:T(8,128)(2,1)S(1)}, bf16[8,16,128]{2,1,0:T(8,128)(2,1)S(1)}) custom-call(s32[1]{0:T(128)} %bitcast.first_ref, s32[128]{0:T(128)} %refs_0_.5, bf16[16,64,128]{2,1,0:T(8,128)(2,1)S(1)} %bitcast.4), custom_call_target="tpu_custom_call" | custom-call | bytes 1048576 | tf_op jit(solution)/shard_map/pick/pallas_call | solution.py:152
  23.3 2.5 %collective-permute-done.1.second_ref = bf16[1,64,128]{2,1,0:T(8,128)(2,1)S(1)} collective-permute-done((bf16[1,64,128]{2,1,0:T(8,128)(2,1)S(1)}, bf16[1,64,128]{2,1,0:T(8,128)(2,1)S(1)}, u32[]{:S(2)}, u32[]{:S(2)}) %collective-permute-start.1) | collective-permute-done | bytes 16416 | tf_op jit(solution)/shard_map/ppermute | solution.py:395
  25.9 0.9 %merge.1 = bf16[8,4,64,128]{3,2,1,0:T(8,128)(2,1)} custom-call(bf16[8,4,64,128]{3,2,1,0:T(8,128)(2,1)S(1)} %get-tuple-element.19.inside_ref, bf16[8,4,16,128]{3,2,1,0:T(8,128)(2,1)S(1)} %get-tuple-element.20.on_next_ref, bf16[8,16,128]{2,1,0:T(8,128)(2,1)S(1)} %get-tuple-element.21.on_second_ref, bf16[4,64,128]{2,1,0:T(8,128)(2,1)S(1)} %collective-permute-done.next_ref, ...), custom_call_target="tpu_custom_call" | custom-call | bytes 1048576 | tf_op jit(solution)/shard_map/merge/pallas_call | solution.py:182
  26.8 8.0 %all-to-all-start.1 = ((bf16[8,4,64,128]{3,2,1,0:T(8,128)(2,1)}), bf16[8,4,64,128]{3,2,1,0:T(8,128)(2,1)S(1)}, u32[]{:S(2)}, u32[]{:S(2)}) async-start(bf16[8,4,64,128]{3,2,1,0:T(8,128)(2,1)} %merge.1), calls=%async_computation.1 | async-start | bytes 1048576 | tf_op jit(solution)/shard_map/all_to_all | solution.py:390
  34.8 10.7 %all-to-all-done.1.refs_4_ = bf16[8,4,64,128]{3,2,1,0:T(8,128)(2,1)S(1)} async-done(((bf16[8,4,64,128]{3,2,1,0:T(8,128)(2,1)}), bf16[8,4,64,128]{3,2,1,0:T(8,128)(2,1)S(1)}, u32[]{:S(2)}, u32[]{:S(2)}) %all-to-all-start.1) | async-done | bytes 524320 | tf_op jit(solution)/shard_map/all_to_all | solution.py:390
  45.5 3.7 %attend.4.refs_0_ = bf16[512,256]{1,0:T(8,128)(2,1)S(1)} custom-call(s32[1]{0:T(128)} %bitcast.first_ref, s32[128]{0:T(128)} %refs_0_.5, bf16[512,1024]{1,0:T(8,128)(2,1)} %refs_1_.5, bf16[512,128]{1,0:T(8,128)(2,1)} %refs_2_.5, bf16[512,128]{1,0:T(8,128)(2,1)} %refs_3_.5, bf16[8,4,64,128]{3,2,1,0:T(8,128)(2,1)S(1)} %all-to-all-done.1.refs_4_), custom_call_target="tpu_custom_call" | custom-call | flops 1845493760 | bytes 1572864 | tf_op jit(solution)/shard_map/attend/pallas_call | solution.py:312
  49.2 1.3 %collective-permute-start.2 = (bf16[512,256]{1,0:T(8,128)(2,1)S(1)}, bf16[512,256]{1,0:T(8,128)(2,1)S(1)}, u32[]{:S(2)}, u32[]{:S(2)}) collective-permute-start(bf16[512,256]{1,0:T(8,128)(2,1)S(1)} %attend.4.refs_0_), channel_id=1, source_target_pairs={{0,2},{1,3},{2,0},{3,1},{4,6},{5,7},{6,4},{7,5},{8,10},{9,11},{10,... | collective-permute-start | bytes 786440 | tf_op jit(solution)/shard_map/ppermute | solution.py:384
  50.5 5.5 %attend.3 = (bf16[512,384]{1,0:T(8,128)(2,1)S(1)}, bf16[2048,1280]{1,0:T(8,128)(2,1)S(1)}) custom-call(s32[1]{0:T(128)} %bitcast.first_ref, s32[128]{0:T(128)} %refs_0_.5, bf16[512,1024]{1,0:T(8,128)(2,1)} %refs_1_.5, bf16[512,128]{1,0:T(8,128)(2,1)} %refs_2_.5, bf16[512,128]{1,0:T(8,128)(2,1)} %refs_3_.5, ...), custom_call_target="tpu_custom_call" | custom-call | flops 2768240640 | bytes 1835008 | tf_op jit(solution)/shard_map/attend/pallas_call | solution.py:312
  56.0 0.5 collective-permute-start.7
  56.5 5.5 %attend.5 = (bf16[512,384]{1,0:T(8,128)(2,1)S(1)}, bf16[2048,1280]{1,0:T(8,128)(2,1)S(1)}) custom-call(s32[1]{0:T(128)} %bitcast.first_ref, s32[128]{0:T(128)} %refs_0_.5, bf16[512,1024]{1,0:T(8,128)(2,1)} %refs_1_.5, bf16[512,128]{1,0:T(8,128)(2,1)} %refs_2_.5, bf16[512,128]{1,0:T(8,128)(2,1)} %refs_3_.5, ...), custom_call_target="tpu_custom_call" | custom-call | flops 2768240640 | bytes 1835008 | tf_op jit(solution)/shard_map/attend/pallas_call | solution.py:312
  62.0 4.1 %collective-permute-start.5 = (bf16[512,384]{1,0:T(8,128)(2,1)S(1)}, bf16[512,384]{1,0:T(8,128)(2,1)S(1)}, u32[]{:S(2)}, u32[]{:S(2)}) collective-permute-start(bf16[512,384]{1,0:T(8,128)(2,1)S(1)} %get-tuple-element.29.refs_1_), channel_id=1, source_target_pairs={{0,1},{1,0},{2,3},{3,2},{4,5},{5,4},{6,7},{7,6},{8,9},{9,8},{10,11... | collective-permute-start | bytes 1179656 | tf_op jit(solution)/shard_map/ppermute | solution.py:384
  66.1 0.1 collective-permute-start.6
  66.2 1.2 %collective-permute-start.3 = (bf16[512,384]{1,0:T(8,128)(2,1)S(1)}, bf16[512,384]{1,0:T(8,128)(2,1)S(1)}, u32[]{:S(2)}, u32[]{:S(2)}) collective-permute-start(bf16[512,384]{1,0:T(8,128)(2,1)S(1)} %get-tuple-element.30.refs_2_), channel_id=1, source_target_pairs={{0,2},{1,3},{2,0},{3,1},{4,6},{5,7},{6,4},{7,5},{8,10},{9,11},{10,... | collective-permute-start | bytes 1179656 | tf_op jit(solution)/shard_map/ppermute | solution.py:384
  67.4 0.7 collective-permute-start.4
  68.1 0.0 collective-permute-done.7.refs_7_
  68.1 0.0 collective-permute-start.8
  68.1 1.2 %collective-permute-done.4.refs_3_ = bf16[512,256]{1,0:T(8,128)(2,1)S(1)} collective-permute-done((bf16[512,256]{1,0:T(8,128)(2,1)S(1)}, bf16[512,256]{1,0:T(8,128)(2,1)S(1)}, u32[]{:S(2)}, u32[]{:S(2)}) %collective-permute-start.4) | collective-permute-done | bytes 262176 | tf_op jit(solution)/shard_map/ppermute | solution.py:384
  69.2 0.4 collective-permute-start.9
  69.6 0.0 collective-permute-done.8.refs_8_
  69.6 0.0 collective-permute-done.5.refs_4_
  69.6 0.0 collective-permute-done.6.refs_5_
  69.6 4.3 %project.2.refs_3_ = f32[512,1280]{1,0:T(8,128)S(1)} custom-call(bf16[2048,1280]{1,0:T(8,128)(2,1)S(1)} %get-tuple-element.24.near_ref, bf16[2048,1280]{1,0:T(8,128)(2,1)S(1)} %get-tuple-element.25.far_ref, bf16[512,256]{1,0:T(8,128)(2,1)S(1)} %attend.4.refs_0_, bf16[512,384]{1,0:T(8,128)(2,1)S(1)} %get-tuple-element.29.refs_1_, ...), custom_call_target="tpu_custom_call" | custom-call | flops 655360 | bytes 655360 | tf_op jit(solution)/shard_map/project/pallas_call | solution.py:366
  73.9 2.6 %collective-permute-done.3.refs_0_ = bf16[512,384]{1,0:T(8,128)(2,1)S(1)} collective-permute-done((bf16[512,384]{1,0:T(8,128)(2,1)S(1)}, bf16[512,384]{1,0:T(8,128)(2,1)S(1)}, u32[]{:S(2)}, u32[]{:S(2)}) %collective-permute-start.3) | collective-permute-done | bytes 393248 | tf_op jit(solution)/shard_map/ppermute | solution.py:384
  76.5 1.2 %collective-permute-start.10 = (bf16[512,384]{1,0:T(8,128)(2,1)S(1)}, bf16[512,384]{1,0:T(8,128)(2,1)S(1)}, u32[]{:S(2)}, u32[]{:S(2)}) collective-permute-start(bf16[512,384]{1,0:T(8,128)(2,1)S(1)} %collective-permute-done.3.refs_0_), channel_id=1, source_target_pairs={{0,1},{1,0},{2,3},{3,2},{4,5},{5,4},{6,7},{7,6},{8,9},{9,8},{10,11... | collective-permute-start | bytes 1179656 | tf_op jit(solution)/shard_map/ppermute | solution.py:384
  77.7 1.3 %collective-permute-done.10.refs_2_ = bf16[512,384]{1,0:T(8,128)(2,1)S(1)} collective-permute-done((bf16[512,384]{1,0:T(8,128)(2,1)S(1)}, bf16[512,384]{1,0:T(8,128)(2,1)S(1)}, u32[]{:S(2)}, u32[]{:S(2)}) %collective-permute-start.10) | collective-permute-done | bytes 393248 | tf_op jit(solution)/shard_map/ppermute | solution.py:384
  79.1 2.9 %project.3 = bf16[512,1280]{1,0:T(8,128)(2,1)} custom-call(bf16[2048,1280]{1,0:T(8,128)(2,1)S(1)} %get-tuple-element.24.near_ref, bf16[2048,1280]{1,0:T(8,128)(2,1)S(1)} %get-tuple-element.25.far_ref, bf16[512,384]{1,0:T(8,128)(2,1)S(1)} %collective-permute-done.3.refs_0_, bf16[512,384]{1,0:T(8,128)(2,1)S(1)} %collective-permute-done.9.refs_1_, ...), custom_call_target="tpu_custom_call" | custom-call | flops 655360 | bytes 655360 | tf_op jit(solution)/shard_map/project/pallas_call | solution.py:366
  (3 shorter events, 0.0 us)
Async XLA Ops:
  1.7 15.5 %all-to-all-start = ((bf16[8,2,64,128]{3,2,1,0:T(8,128)(2,1)}), bf16[8,2,64,128]{3,2,1,0:T(8,128)(2,1)S(1)}, u32[]{:S(2)}, u32[]{:S(2)}) async-start(bf16[8,2,64,128]{3,2,1,0:T(8,128)(2,1)} %pack.1), calls=%async_computation | async-start | bytes 524288 | tf_op jit(solution)/shard_map/all_to_all | solution.py:390
  18.0 7.9 %collective-permute-start = (bf16[4,64,128]{2,1,0:T(8,128)(2,1)S(1)}, bf16[4,64,128]{2,1,0:T(8,128)(2,1)S(1)}, u32[]{:S(2)}, u32[]{:S(2)}) collective-permute-start(bf16[4,64,128]{2,1,0:T(8,128)(2,1)S(1)} %get-tuple-element.22), channel_id=1, source_target_pairs={{0,32},{4,36},{8,40},{12,44},{16,48},{20,52},{24,56},{28,60},{32,6... | collective-permute-start | bytes 196616 | tf_op jit(solution)/shard_map/ppermute | solution.py:395
  19.4 6.5 %collective-permute-start.1 = (bf16[1,64,128]{2,1,0:T(8,128)(2,1)S(1)}, bf16[1,64,128]{2,1,0:T(8,128)(2,1)S(1)}, u32[]{:S(2)}, u32[]{:S(2)}) collective-permute-start(bf16[1,64,128]{2,1,0:T(8,128)(2,1)S(1)} %get-tuple-element.23), channel_id=1, source_target_pairs={{0,64},{4,68},{8,72},{12,76},{16,80},{20,84},{24,88},{28,92},{32,9... | collective-permute-start | bytes 49160 | tf_op jit(solution)/shard_map/ppermute | solution.py:395
  26.8 18.7 %all-to-all-start.1 = ((bf16[8,4,64,128]{3,2,1,0:T(8,128)(2,1)}), bf16[8,4,64,128]{3,2,1,0:T(8,128)(2,1)S(1)}, u32[]{:S(2)}, u32[]{:S(2)}) async-start(bf16[8,4,64,128]{3,2,1,0:T(8,128)(2,1)} %merge.1), calls=%async_computation.1 | async-start | bytes 1048576 | tf_op jit(solution)/shard_map/all_to_all | solution.py:390
  49.2 7.3 %collective-permute-start.2 = (bf16[512,256]{1,0:T(8,128)(2,1)S(1)}, bf16[512,256]{1,0:T(8,128)(2,1)S(1)}, u32[]{:S(2)}, u32[]{:S(2)}) collective-permute-start(bf16[512,256]{1,0:T(8,128)(2,1)S(1)} %attend.4.refs_0_), channel_id=1, source_target_pairs={{0,2},{1,3},{2,0},{3,1},{4,6},{5,7},{6,4},{7,5},{8,10},{9,11},{10,... | collective-permute-start | bytes 786440 | tf_op jit(solution)/shard_map/ppermute | solution.py:384
  56.0 12.1 %collective-permute-start.7 = (bf16[512,384]{1,0:T(8,128)(2,1)S(1)}, bf16[512,384]{1,0:T(8,128)(2,1)S(1)}, u32[]{:S(2)}, u32[]{:S(2)}) collective-permute-start(bf16[512,384]{1,0:T(8,128)(2,1)S(1)} %get-tuple-element.29.refs_1_), channel_id=1, source_target_pairs={{0,2},{1,3},{2,0},{3,1},{4,6},{5,7},{6,4},{7,5},{8,10},{9,11},{10,... | collective-permute-start | bytes 1179656 | tf_op jit(solution)/shard_map/ppermute | solution.py:384
  62.0 7.6 %collective-permute-start.5 = (bf16[512,384]{1,0:T(8,128)(2,1)S(1)}, bf16[512,384]{1,0:T(8,128)(2,1)S(1)}, u32[]{:S(2)}, u32[]{:S(2)}) collective-permute-start(bf16[512,384]{1,0:T(8,128)(2,1)S(1)} %get-tuple-element.29.refs_1_), channel_id=1, source_target_pairs={{0,1},{1,0},{2,3},{3,2},{4,5},{5,4},{6,7},{7,6},{8,9},{9,8},{10,11... | collective-permute-start | bytes 1179656 | tf_op jit(solution)/shard_map/ppermute | solution.py:384
  66.1 3.5 %collective-permute-start.6 = (bf16[512,384]{1,0:T(8,128)(2,1)S(1)}, bf16[512,384]{1,0:T(8,128)(2,1)S(1)}, u32[]{:S(2)}, u32[]{:S(2)}) collective-permute-start(bf16[512,384]{1,0:T(8,128)(2,1)S(1)} %get-tuple-element.30.refs_2_), channel_id=1, source_target_pairs={{0,1},{1,0},{2,3},{3,2},{4,5},{5,4},{6,7},{7,6},{8,9},{9,8},{10,11... | collective-permute-start | bytes 1179656 | tf_op jit(solution)/shard_map/ppermute | solution.py:384
  66.2 10.3 %collective-permute-start.3 = (bf16[512,384]{1,0:T(8,128)(2,1)S(1)}, bf16[512,384]{1,0:T(8,128)(2,1)S(1)}, u32[]{:S(2)}, u32[]{:S(2)}) collective-permute-start(bf16[512,384]{1,0:T(8,128)(2,1)S(1)} %get-tuple-element.30.refs_2_), channel_id=1, source_target_pairs={{0,2},{1,3},{2,0},{3,1},{4,6},{5,7},{6,4},{7,5},{8,10},{9,11},{10,... | collective-permute-start | bytes 1179656 | tf_op jit(solution)/shard_map/ppermute | solution.py:384
  67.4 1.9 %collective-permute-start.4 = (bf16[512,256]{1,0:T(8,128)(2,1)S(1)}, bf16[512,256]{1,0:T(8,128)(2,1)S(1)}, u32[]{:S(2)}, u32[]{:S(2)}) collective-permute-start(bf16[512,256]{1,0:T(8,128)(2,1)S(1)} %attend.4.refs_0_), channel_id=1, source_target_pairs={{0,1},{1,0},{2,3},{3,2},{4,5},{5,4},{6,7},{7,6},{8,9},{9,8},{10,11... | collective-permute-start | bytes 786440 | tf_op jit(solution)/shard_map/ppermute | solution.py:384
  68.1 1.5 %collective-permute-start.8 = (bf16[512,256]{1,0:T(8,128)(2,1)S(1)}, bf16[512,256]{1,0:T(8,128)(2,1)S(1)}, u32[]{:S(2)}, u32[]{:S(2)}) collective-permute-start(bf16[512,256]{1,0:T(8,128)(2,1)S(1)} %collective-permute-done.2.refs_7_.refs_6_), channel_id=1, source_target_pairs={{0,1},{1,0},{2,3},{3,2},{4,5},{5,4},{6,7},{7,6},{8,9},{9,8},{10,11... | collective-permute-start | bytes 786440 | tf_op jit(solution)/shard_map/ppermute | solution.py:384
  69.2 8.5 %collective-permute-start.9 = (bf16[512,384]{1,0:T(8,128)(2,1)S(1)}, bf16[512,384]{1,0:T(8,128)(2,1)S(1)}, u32[]{:S(2)}, u32[]{:S(2)}) collective-permute-start(bf16[512,384]{1,0:T(8,128)(2,1)S(1)} %collective-permute-done.7.refs_7_), channel_id=1, source_target_pairs={{0,1},{1,0},{2,3},{3,2},{4,5},{5,4},{6,7},{7,6},{8,9},{9,8},{10,11... | collective-permute-start | bytes 1179656 | tf_op jit(solution)/shard_map/ppermute | solution.py:384
  76.5 2.6 %collective-permute-start.10 = (bf16[512,384]{1,0:T(8,128)(2,1)S(1)}, bf16[512,384]{1,0:T(8,128)(2,1)S(1)}, u32[]{:S(2)}, u32[]{:S(2)}) collective-permute-start(bf16[512,384]{1,0:T(8,128)(2,1)S(1)} %collective-permute-done.3.refs_0_), channel_id=1, source_target_pairs={{0,1},{1,0},{2,3},{3,2},{4,5},{5,4},{6,7},{7,6},{8,9},{9,8},{10,11... | collective-permute-start | bytes 1179656 | tf_op jit(solution)/shard_map/ppermute | solution.py:384

commit v15 on v12

--- a/solution.py
+++ b/solution.py
@@ -13,7 +13,7 @@
 LEVELS = 4
 ROW = 8
 ROW_SEGS = 2 * ROW
-LISTED = (7, 3, 6, 2, 5, 1, 4, 0)
+LISTED = (5, 4, 3, 2, 1, 0, 7, 6)
 PIECE = SEG_LEN // ROW
 PATH = LEVELS * SEG_LEN
 STACK = LEVELS * PIECE
@@ -88,8 +88,7 @@
 
 
 def slot_of(seg):
-    place = seg // 2
-    member = 2 * (ROW // 2 - 1 - place % (ROW // 2)) + 1 - place // (ROW // 2)
+    member = (LISTED[0] + ROW - seg // 2) % ROW
     return 2 * member + seg % 2
 
 

time: 82.2 us -> 82.3 us (level)
  starting transfers between devices: 34.4 us -> 36.7 us
  waiting for transfers between devices: 20.2 us -> 18.8 us
    all_to_all x2, waiting for transfers between devices: 16.4 us -> 14.8 us  [trade(): lax.all_to_all(pieces, 'dp', 0, 0, tiled=True, axis_index_groups=rows)]
    all_to_all x2, starting transfers between devices: 17.8 us -> 19.1 us  [trade(): lax.all_to_all(pieces, 'dp', 0, 0, tiled=True, axis_index_groups=rows)]
    ppermute x9, starting transfers between devices: 12.6 us -> 13.5 us  [swap(): return lax.ppermute(part, 'tensor', [(i, i ^ bit) for i in range(size)])]
  transfers between devices with their start and end apart: 13 -> 13, of which waited for: 4 -> 4; matrix products, arithmetic and copies ran while one was open for 0% -> 0% of each run, Pallas kernels for 20% -> 19%
where the time goes in v15:
time: 82.3 us; the launch traced here: 82 us
  starting transfers between devices  36.7 us (45%)
  Pallas kernels  26.5 us (32%)
  waiting for transfers between devices  18.8 us (23%)
    all_to_all x2, starting transfers between devices, trade(): lax.all_to_all(pieces, 'dp', 0, 0, tiled=True, axis_index_groups=rows)  19.1 us
    all_to_all x2, waiting for transfers between devices, trade(): lax.all_to_all(pieces, 'dp', 0, 0, tiled=True, axis_index_groups=rows)  14.8 us
    pallas_call x3, Pallas kernels, attend(): pl.pallas_call(functools.partial(attend_kernel, first_head, blocks), out_...  14.7 us
    ppermute x9, starting transfers between devices, swap(): return lax.ppermute(part, 'tensor', [(i, i ^ bit) for i in range(size)])  13.5 us
    pallas_call x2, Pallas kernels, project(): pl.pallas_call(functools.partial(project_kernel, [len(g) for g in groups]...  7.2 us
    ppermute x2, starting transfers between devices, onward(): lax.ppermute(piece, 'dp', [(i, (i + step) % devices) for i in range(devic...  3.99 us
    ppermute x2, waiting for transfers between devices, onward(): lax.ppermute(piece, 'dp', [(i, (i + step) % devices) for i in range(devic...  2.75 us
    pallas_call x1, Pallas kernels, pack(): pl.pallas_call(pack_kernel, out_shape=jax.ShapeDtypeStruct((ROW, 2, 2 * P...  1.69 us
  transfers between devices with their start and end apart: 13, of which 4 were waited for; matrix products, arithmetic and copies ran while one was open for 0% of the time, Pallas kernels for 19%

profile of v15, /device:TPU:1, one launch (start us, length us, event | category | flops | bytes accessed | tf_op | source)
XLA Modules:
  0.0 82.0 jit_solution(8369325542924607827)
XLA Ops:
  0.0 1.7 %pack.1 = bf16[8,2,64,128]{3,2,1,0:T(8,128)(2,1)} custom-call(bf16[512,128]{1,0:T(8,128)(2,1)} %refs_2_.5, bf16[512,128]{1,0:T(8,128)(2,1)} %refs_3_.5), custom_call_target="tpu_custom_call" | custom-call | bytes 524288 | tf_op jit(solution)/shard_map/pack/pallas_call | solution.py:74
  1.7 10.6 %all-to-all-start = ((bf16[8,2,64,128]{3,2,1,0:T(8,128)(2,1)}), bf16[8,2,64,128]{3,2,1,0:T(8,128)(2,1)S(1)}, u32[]{:S(2)}, u32[]{:S(2)}) async-start(bf16[8,2,64,128]{3,2,1,0:T(8,128)(2,1)} %pack.1), calls=%async_computation | async-start | bytes 524288 | tf_op jit(solution)/shard_map/all_to_all | solution.py:389
  12.3 6.1 %all-to-all-done = bf16[8,2,64,128]{3,2,1,0:T(8,128)(2,1)S(1)} async-done(((bf16[8,2,64,128]{3,2,1,0:T(8,128)(2,1)}), bf16[8,2,64,128]{3,2,1,0:T(8,128)(2,1)S(1)}, u32[]{:S(2)}, u32[]{:S(2)}) %all-to-all-start) | async-done | bytes 262176 | tf_op jit(solution)/shard_map/all_to_all | solution.py:389
  18.5 0.8 carry_out.1
  19.2 1.4 %collective-permute-start = (bf16[4,64,128]{2,1,0:T(8,128)(2,1)S(1)}, bf16[4,64,128]{2,1,0:T(8,128)(2,1)S(1)}, u32[]{:S(2)}, u32[]{:S(2)}) collective-permute-start(bf16[4,64,128]{2,1,0:T(8,128)(2,1)S(1)} %get-tuple-element.19), channel_id=1, source_target_pairs={{0,32},{4,36},{8,40},{12,44},{16,48},{20,52},{24,56},{28,60},{32,6... | collective-permute-start | bytes 196616 | tf_op jit(solution)/shard_map/ppermute | solution.py:394
  20.6 2.6 %collective-permute-start.1 = (bf16[1,64,128]{2,1,0:T(8,128)(2,1)S(1)}, bf16[1,64,128]{2,1,0:T(8,128)(2,1)S(1)}, u32[]{:S(2)}, u32[]{:S(2)}) collective-permute-start(bf16[1,64,128]{2,1,0:T(8,128)(2,1)S(1)} %get-tuple-element.20), channel_id=1, source_target_pairs={{0,64},{4,68},{8,72},{12,76},{16,80},{20,84},{24,88},{28,92},{32,9... | collective-permute-start | bytes 49160 | tf_op jit(solution)/shard_map/ppermute | solution.py:394
  23.2 1.2 %pick.1 = (bf16[8,4,64,128]{3,2,1,0:T(8,128)(2,1)S(1)}, bf16[8,4,16,128]{3,2,1,0:T(8,128)(2,1)S(1)}, bf16[8,16,128]{2,1,0:T(8,128)(2,1)S(1)}) custom-call(s32[1]{0:T(128)} %bitcast.first_ref, s32[128]{0:T(128)} %refs_0_.5, bf16[16,64,128]{2,1,0:T(8,128)(2,1)S(1)} %bitcast.4), custom_call_target="tpu_custom_call" | custom-call | bytes 1048576 | tf_op jit(solution)/shard_map/pick/pallas_call | solution.py:151
  24.5 2.7 %collective-permute-done.1.second_ref = bf16[1,64,128]{2,1,0:T(8,128)(2,1)S(1)} collective-permute-done((bf16[1,64,128]{2,1,0:T(8,128)(2,1)S(1)}, bf16[1,64,128]{2,1,0:T(8,128)(2,1)S(1)}, u32[]{:S(2)}, u32[]{:S(2)}) %collective-permute-start.1) | collective-permute-done | bytes 16416 | tf_op jit(solution)/shard_map/ppermute | solution.py:394
  27.2 0.0 collective-permute-done.next_ref
  27.2 0.9 %merge.1 = bf16[8,4,64,128]{3,2,1,0:T(8,128)(2,1)} custom-call(bf16[8,4,64,128]{3,2,1,0:T(8,128)(2,1)S(1)} %get-tuple-element.16.inside_ref, bf16[8,4,16,128]{3,2,1,0:T(8,128)(2,1)S(1)} %get-tuple-element.17.on_next_ref, bf16[8,16,128]{2,1,0:T(8,128)(2,1)S(1)} %get-tuple-element.18.on_second_ref, bf16[4,64,128]{2,1,0:T(8,128)(2,1)S(1)} %collective-permute-done.next_ref, ...), custom_call_target="tpu_custom_call" | custom-call | bytes 1048576 | tf_op jit(solution)/shard_map/merge/pallas_call | solution.py:181
  28.1 8.5 %all-to-all-start.1 = ((bf16[8,4,64,128]{3,2,1,0:T(8,128)(2,1)}), bf16[8,4,64,128]{3,2,1,0:T(8,128)(2,1)S(1)}, u32[]{:S(2)}, u32[]{:S(2)}) async-start(bf16[8,4,64,128]{3,2,1,0:T(8,128)(2,1)} %merge.1), calls=%async_computation.1 | async-start | bytes 1048576 | tf_op jit(solution)/shard_map/all_to_all | solution.py:389
  36.6 8.7 %all-to-all-done.1.refs_4_ = bf16[8,4,64,128]{3,2,1,0:T(8,128)(2,1)S(1)} async-done(((bf16[8,4,64,128]{3,2,1,0:T(8,128)(2,1)}), bf16[8,4,64,128]{3,2,1,0:T(8,128)(2,1)S(1)}, u32[]{:S(2)}, u32[]{:S(2)}) %all-to-all-start.1) | async-done | bytes 524320 | tf_op jit(solution)/shard_map/all_to_all | solution.py:389
  45.3 4.7 %attend.4.refs_0_ = bf16[512,384]{1,0:T(8,128)(2,1)S(1)} custom-call(s32[1]{0:T(128)} %bitcast.first_ref, s32[128]{0:T(128)} %refs_0_.5, bf16[512,1024]{1,0:T(8,128)(2,1)} %refs_1_.5, bf16[512,128]{1,0:T(8,128)(2,1)} %refs_2_.5, bf16[512,128]{1,0:T(8,128)(2,1)} %refs_3_.5, bf16[8,4,64,128]{3,2,1,0:T(8,128)(2,1)S(1)} %all-to-all-done.1.refs_4_), custom_call_target="tpu_custom_call" | custom-call | flops 2768240640 | bytes 1835008 | tf_op jit(solution)/shard_map/attend/pallas_call | solution.py:311
  50.0 1.3 %collective-permute-start.2 = (bf16[512,384]{1,0:T(8,128)(2,1)S(1)}, bf16[512,384]{1,0:T(8,128)(2,1)S(1)}, u32[]{:S(2)}, u32[]{:S(2)}) collective-permute-start(bf16[512,384]{1,0:T(8,128)(2,1)S(1)} %attend.4.refs_0_), channel_id=1, source_target_pairs={{0,2},{1,3},{2,0},{3,1},{4,6},{5,7},{6,4},{7,5},{8,10},{9,11},{10,... | collective-permute-start | bytes 1179656 | tf_op jit(solution)/shard_map/ppermute | solution.py:383
  51.3 5.5 %attend.3 = (bf16[512,384]{1,0:T(8,128)(2,1)S(1)}, bf16[2048,1280]{1,0:T(8,128)(2,1)S(1)}) custom-call(s32[1]{0:T(128)} %bitcast.first_ref, s32[128]{0:T(128)} %refs_0_.5, bf16[512,1024]{1,0:T(8,128)(2,1)} %refs_1_.5, bf16[512,128]{1,0:T(8,128)(2,1)} %refs_2_.5, bf16[512,128]{1,0:T(8,128)(2,1)} %refs_3_.5, ...), custom_call_target="tpu_custom_call" | custom-call | flops 2768240640 | bytes 1835008 | tf_op jit(solution)/shard_map/attend/pallas_call | solution.py:311
  56.9 0.3 collective-permute-start.7
  57.2 4.7 %collective-permute-start.5 = (bf16[512,384]{1,0:T(8,128)(2,1)S(1)}, bf16[512,384]{1,0:T(8,128)(2,1)S(1)}, u32[]{:S(2)}, u32[]{:S(2)}) collective-permute-start(bf16[512,384]{1,0:T(8,128)(2,1)S(1)} %get-tuple-element.24.refs_1_), channel_id=1, source_target_pairs={{0,1},{1,0},{2,3},{3,2},{4,5},{5,4},{6,7},{7,6},{8,9},{9,8},{10,11... | collective-permute-start | bytes 1179656 | tf_op jit(solution)/shard_map/ppermute | solution.py:383
  61.9 0.0 collective-permute-start.4
  62.0 2.1 %collective-permute-start.8 = (bf16[512,384]{1,0:T(8,128)(2,1)S(1)}, bf16[512,384]{1,0:T(8,128)(2,1)S(1)}, u32[]{:S(2)}, u32[]{:S(2)}) collective-permute-start(bf16[512,384]{1,0:T(8,128)(2,1)S(1)} %collective-permute-done.2.refs_7_.refs_6_), channel_id=1, source_target_pairs={{0,1},{1,0},{2,3},{3,2},{4,5},{5,4},{6,7},{7,6},{8,9},{9,8},{10,11... | collective-permute-start | bytes 1179656 | tf_op jit(solution)/shard_map/ppermute | solution.py:383
  64.1 4.5 %attend.5 = (bf16[512,256]{1,0:T(8,128)(2,1)S(1)}, bf16[2048,1280]{1,0:T(8,128)(2,1)S(1)}) custom-call(s32[1]{0:T(128)} %bitcast.first_ref, s32[128]{0:T(128)} %refs_0_.5, bf16[512,1024]{1,0:T(8,128)(2,1)} %refs_1_.5, bf16[512,128]{1,0:T(8,128)(2,1)} %refs_2_.5, bf16[512,128]{1,0:T(8,128)(2,1)} %refs_3_.5, ...), custom_call_target="tpu_custom_call" | custom-call | flops 1845493760 | bytes 1572864 | tf_op jit(solution)/shard_map/attend/pallas_call | solution.py:311
  68.6 0.1 collective-permute-start.6
  68.7 0.0 collective-permute-done.7.refs_7_
  68.7 2.3 %collective-permute-start.3 = (bf16[512,256]{1,0:T(8,128)(2,1)S(1)}, bf16[512,256]{1,0:T(8,128)(2,1)S(1)}, u32[]{:S(2)}, u32[]{:S(2)}) collective-permute-start(bf16[512,256]{1,0:T(8,128)(2,1)S(1)} %get-tuple-element.23.refs_2_), channel_id=1, source_target_pairs={{0,2},{1,3},{2,0},{3,1},{4,6},{5,7},{6,4},{7,5},{8,10},{9,11},{10,... | collective-permute-start | bytes 786440 | tf_op jit(solution)/shard_map/ppermute | solution.py:383
  71.0 0.0 collective-permute-done.5.refs_4_
  71.0 1.0 %collective-permute-start.9 = (bf16[512,384]{1,0:T(8,128)(2,1)S(1)}, bf16[512,384]{1,0:T(8,128)(2,1)S(1)}, u32[]{:S(2)}, u32[]{:S(2)}) collective-permute-start(bf16[512,384]{1,0:T(8,128)(2,1)S(1)} %collective-permute-done.7.refs_7_), channel_id=1, source_target_pairs={{0,1},{1,0},{2,3},{3,2},{4,5},{5,4},{6,7},{7,6},{8,9},{9,8},{10,11... | collective-permute-start | bytes 1179656 | tf_op jit(solution)/shard_map/ppermute | solution.py:383
  72.0 0.0 collective-permute-done.4.refs_3_
  72.0 0.0 collective-permute-done.6.refs_5_
  72.0 0.0 collective-permute-done.8.refs_8_
  72.0 4.6 %project.2.refs_3_ = f32[512,1280]{1,0:T(8,128)S(1)} custom-call(bf16[2048,1280]{1,0:T(8,128)(2,1)S(1)} %get-tuple-element.21.near_ref, bf16[2048,1280]{1,0:T(8,128)(2,1)S(1)} %get-tuple-element.22.far_ref, bf16[512,384]{1,0:T(8,128)(2,1)S(1)} %attend.4.refs_0_, bf16[512,384]{1,0:T(8,128)(2,1)S(1)} %get-tuple-element.24.refs_1_, ...), custom_call_target="tpu_custom_call" | custom-call | flops 655360 | bytes 655360 | tf_op jit(solution)/shard_map/project/pallas_call | solution.py:365
  76.7 1.6 %collective-permute-start.10 = (bf16[512,256]{1,0:T(8,128)(2,1)S(1)}, bf16[512,256]{1,0:T(8,128)(2,1)S(1)}, u32[]{:S(2)}, u32[]{:S(2)}) collective-permute-start(bf16[512,256]{1,0:T(8,128)(2,1)S(1)} %collective-permute-done.3.refs_0_), channel_id=1, source_target_pairs={{0,1},{1,0},{2,3},{3,2},{4,5},{5,4},{6,7},{7,6},{8,9},{9,8},{10,11... | collective-permute-start | bytes 786440 | tf_op jit(solution)/shard_map/ppermute | solution.py:383
  78.3 1.2 %collective-permute-done.10.refs_2_ = bf16[512,256]{1,0:T(8,128)(2,1)S(1)} collective-permute-done((bf16[512,256]{1,0:T(8,128)(2,1)S(1)}, bf16[512,256]{1,0:T(8,128)(2,1)S(1)}, u32[]{:S(2)}, u32[]{:S(2)}) %collective-permute-start.10) | collective-permute-done | bytes 262176 | tf_op jit(solution)/shard_map/ppermute | solution.py:383
  79.4 2.6 %project.3 = bf16[512,1280]{1,0:T(8,128)(2,1)} custom-call(bf16[2048,1280]{1,0:T(8,128)(2,1)S(1)} %get-tuple-element.21.near_ref, bf16[2048,1280]{1,0:T(8,128)(2,1)S(1)} %get-tuple-element.22.far_ref, bf16[512,256]{1,0:T(8,128)(2,1)S(1)} %collective-permute-done.3.refs_0_, bf16[512,384]{1,0:T(8,128)(2,1)S(1)} %collective-permute-done.9.refs_1_, ...), custom_call_target="tpu_custom_call" | custom-call | flops 655360 | bytes 655360 | tf_op jit(solution)/shard_map/project/pallas_call | solution.py:365
  (3 shorter events, 0.0 us)
Async XLA Ops:
  1.7 16.8 %all-to-all-start = ((bf16[8,2,64,128]{3,2,1,0:T(8,128)(2,1)}), bf16[8,2,64,128]{3,2,1,0:T(8,128)(2,1)S(1)}, u32[]{:S(2)}, u32[]{:S(2)}) async-start(bf16[8,2,64,128]{3,2,1,0:T(8,128)(2,1)} %pack.1), calls=%async_computation | async-start | bytes 524288 | tf_op jit(solution)/shard_map/all_to_all | solution.py:389
  19.2 8.0 %collective-permute-start = (bf16[4,64,128]{2,1,0:T(8,128)(2,1)S(1)}, bf16[4,64,128]{2,1,0:T(8,128)(2,1)S(1)}, u32[]{:S(2)}, u32[]{:S(2)}) collective-permute-start(bf16[4,64,128]{2,1,0:T(8,128)(2,1)S(1)} %get-tuple-element.19), channel_id=1, source_target_pairs={{0,32},{4,36},{8,40},{12,44},{16,48},{20,52},{24,56},{28,60},{32,6... | collective-permute-start | bytes 196616 | tf_op jit(solution)/shard_map/ppermute | solution.py:394
  20.6 6.6 %collective-permute-start.1 = (bf16[1,64,128]{2,1,0:T(8,128)(2,1)S(1)}, bf16[1,64,128]{2,1,0:T(8,128)(2,1)S(1)}, u32[]{:S(2)}, u32[]{:S(2)}) collective-permute-start(bf16[1,64,128]{2,1,0:T(8,128)(2,1)S(1)} %get-tuple-element.20), channel_id=1, source_target_pairs={{0,64},{4,68},{8,72},{12,76},{16,80},{20,84},{24,88},{28,92},{32,9... | collective-permute-start | bytes 49160 | tf_op jit(solution)/shard_map/ppermute | solution.py:394
  28.1 17.2 %all-to-all-start.1 = ((bf16[8,4,64,128]{3,2,1,0:T(8,128)(2,1)}), bf16[8,4,64,128]{3,2,1,0:T(8,128)(2,1)S(1)}, u32[]{:S(2)}, u32[]{:S(2)}) async-start(bf16[8,4,64,128]{3,2,1,0:T(8,128)(2,1)} %merge.1), calls=%async_computation.1 | async-start | bytes 1048576 | tf_op jit(solution)/shard_map/all_to_all | solution.py:389
  50.0 11.9 %collective-permute-start.2 = (bf16[512,384]{1,0:T(8,128)(2,1)S(1)}, bf16[512,384]{1,0:T(8,128)(2,1)S(1)}, u32[]{:S(2)}, u32[]{:S(2)}) collective-permute-start(bf16[512,384]{1,0:T(8,128)(2,1)S(1)} %attend.4.refs_0_), channel_id=1, source_target_pairs={{0,2},{1,3},{2,0},{3,1},{4,6},{5,7},{6,4},{7,5},{8,10},{9,11},{10,... | collective-permute-start | bytes 1179656 | tf_op jit(solution)/shard_map/ppermute | solution.py:383
  56.9 11.8 %collective-permute-start.7 = (bf16[512,384]{1,0:T(8,128)(2,1)S(1)}, bf16[512,384]{1,0:T(8,128)(2,1)S(1)}, u32[]{:S(2)}, u32[]{:S(2)}) collective-permute-start(bf16[512,384]{1,0:T(8,128)(2,1)S(1)} %get-tuple-element.24.refs_1_), channel_id=1, source_target_pairs={{0,2},{1,3},{2,0},{3,1},{4,6},{5,7},{6,4},{7,5},{8,10},{9,11},{10,... | collective-permute-start | bytes 1179656 | tf_op jit(solution)/shard_map/ppermute | solution.py:383
  57.2 13.8 %collective-permute-start.5 = (bf16[512,384]{1,0:T(8,128)(2,1)S(1)}, bf16[512,384]{1,0:T(8,128)(2,1)S(1)}, u32[]{:S(2)}, u32[]{:S(2)}) collective-permute-start(bf16[512,384]{1,0:T(8,128)(2,1)S(1)} %get-tuple-element.24.refs_1_), channel_id=1, source_target_pairs={{0,1},{1,0},{2,3},{3,2},{4,5},{5,4},{6,7},{7,6},{8,9},{9,8},{10,11... | collective-permute-start | bytes 1179656 | tf_op jit(solution)/shard_map/ppermute | solution.py:383
  61.9 10.1 %collective-permute-start.4 = (bf16[512,384]{1,0:T(8,128)(2,1)S(1)}, bf16[512,384]{1,0:T(8,128)(2,1)S(1)}, u32[]{:S(2)}, u32[]{:S(2)}) collective-permute-start(bf16[512,384]{1,0:T(8,128)(2,1)S(1)} %attend.4.refs_0_), channel_id=1, source_target_pairs={{0,1},{1,0},{2,3},{3,2},{4,5},{5,4},{6,7},{7,6},{8,9},{9,8},{10,11... | collective-permute-start | bytes 1179656 | tf_op jit(solution)/shard_map/ppermute | solution.py:383
  62.0 10.1 %collective-permute-start.8 = (bf16[512,384]{1,0:T(8,128)(2,1)S(1)}, bf16[512,384]{1,0:T(8,128)(2,1)S(1)}, u32[]{:S(2)}, u32[]{:S(2)}) collective-permute-start(bf16[512,384]{1,0:T(8,128)(2,1)S(1)} %collective-permute-done.2.refs_7_.refs_6_), channel_id=1, source_target_pairs={{0,1},{1,0},{2,3},{3,2},{4,5},{5,4},{6,7},{7,6},{8,9},{9,8},{10,11... | collective-permute-start | bytes 1179656 | tf_op jit(solution)/shard_map/ppermute | solution.py:383
  68.6 3.4 %collective-permute-start.6 = (bf16[512,256]{1,0:T(8,128)(2,1)S(1)}, bf16[512,256]{1,0:T(8,128)(2,1)S(1)}, u32[]{:S(2)}, u32[]{:S(2)}) collective-permute-start(bf16[512,256]{1,0:T(8,128)(2,1)S(1)} %get-tuple-element.23.refs_2_), channel_id=1, source_target_pairs={{0,1},{1,0},{2,3},{3,2},{4,5},{5,4},{6,7},{7,6},{8,9},{9,8},{10,11... | collective-permute-start | bytes 786440 | tf_op jit(solution)/shard_map/ppermute | solution.py:383
  68.7 8.0 %collective-permute-start.3 = (bf16[512,256]{1,0:T(8,128)(2,1)S(1)}, bf16[512,256]{1,0:T(8,128)(2,1)S(1)}, u32[]{:S(2)}, u32[]{:S(2)}) collective-permute-start(bf16[512,256]{1,0:T(8,128)(2,1)S(1)} %get-tuple-element.23.refs_2_), channel_id=1, source_target_pairs={{0,2},{1,3},{2,0},{3,1},{4,6},{5,7},{6,4},{7,5},{8,10},{9,11},{10,... | collective-permute-start | bytes 786440 | tf_op jit(solution)/shard_map/ppermute | solution.py:383
  71.0 7.3 %collective-permute-start.9 = (bf16[512,384]{1,0:T(8,128)(2,1)S(1)}, bf16[512,384]{1,0:T(8,128)(2,1)S(1)}, u32[]{:S(2)}, u32[]{:S(2)}) collective-permute-start(bf16[512,384]{1,0:T(8,128)(2,1)S(1)} %collective-permute-done.7.refs_7_), channel_id=1, source_target_pairs={{0,1},{1,0},{2,3},{3,2},{4,5},{5,4},{6,7},{7,6},{8,9},{9,8},{10,11... | collective-permute-start | bytes 1179656 | tf_op jit(solution)/shard_map/ppermute | solution.py:383
  76.7 2.7 %collective-permute-start.10 = (bf16[512,256]{1,0:T(8,128)(2,1)S(1)}, bf16[512,256]{1,0:T(8,128)(2,1)S(1)}, u32[]{:S(2)}, u32[]{:S(2)}) collective-permute-start(bf16[512,256]{1,0:T(8,128)(2,1)S(1)} %collective-permute-done.3.refs_0_), channel_id=1, source_target_pairs={{0,1},{1,0},{2,3},{3,2},{4,5},{5,4},{6,7},{7,6},{8,9},{9,8},{10,11... | collective-permute-start | bytes 786440 | tf_op jit(solution)/shard_map/ppermute | solution.py:383

commit v16 on v12

--- a/solution.py
+++ b/solution.py
@@ -222,8 +222,7 @@
             path_key_ref[rows, :HEAD_DIM] = far_ref[piece, level, :PIECE]
             path_value_ref[rows, :HEAD_DIM] = far_ref[piece, level, PIECE:]
     path_value_ref[:, HEAD_DIM:] = jnp.ones((PATH, HEAD_DIM), jnp.bfloat16)
-    for copy in fetches:
-        copy.wait()
+    fetches[0].wait()
     first = first_ref[0]
     _, depth0 = path_of(parents_ref, first)
     _, depth1 = path_of(parents_ref, first + 1)
@@ -233,6 +232,8 @@
     level = lax.rem(row // PIECE, LEVELS)
     limit = jnp.where(lane == 0, depth0, jnp.where(lane == 1, jnp.minimum(depth0, depth1), LEVELS))
     path_key_ref[:, HEAD_DIM:] = jnp.where(level < limit, 0.0, MASKED).astype(jnp.bfloat16)
+    for copy in fetches[1:]:
+        copy.wait()
     path_keys, path_values = path_key_ref[...], path_value_ref[...]
 
     rows = lax.broadcasted_iota(jnp.int32, (2 * SEG_LEN, HEAD_DIM), 0)

time: 82.2 us -> 82.1 us (level)
  transfers between devices with their start and end apart: 13 -> 13, of which waited for: 4 -> 4; matrix products, arithmetic and copies ran while one was open for 0% -> 0% of each run, Pallas kernels for 20% -> 19%
where the time goes in v16:
time: 82.1 us; the launch traced here: 81.2 us
  starting transfers between devices  34.5 us (42%)
  Pallas kernels  26.4 us (32%)
  waiting for transfers between devices  20.2 us (25%)
    all_to_all x2, starting transfers between devices, trade(): lax.all_to_all(pieces, 'dp', 0, 0, tiled=True, axis_index_groups=rows)  17.8 us
    all_to_all x2, waiting for transfers between devices, trade(): lax.all_to_all(pieces, 'dp', 0, 0, tiled=True, axis_index_groups=rows)  16.4 us
    pallas_call x3, Pallas kernels, attend(): pl.pallas_call(functools.partial(attend_kernel, first_head, blocks), out_...  14.5 us
    ppermute x9, starting transfers between devices, swap(): return lax.ppermute(part, 'tensor', [(i, i ^ bit) for i in range(size)])  12.7 us
    pallas_call x2, Pallas kernels, project(): pl.pallas_call(functools.partial(project_kernel, [len(g) for g in groups]...  7.2 us
    ppermute x2, starting transfers between devices, onward(): lax.ppermute(piece, 'dp', [(i, (i + step) % devices) for i in range(devic...  3.99 us
    ppermute x2, waiting for transfers between devices, onward(): lax.ppermute(piece, 'dp', [(i, (i + step) % devices) for i in range(devic...  2.53 us
    pallas_call x1, Pallas kernels, pack(): pl.pallas_call(pack_kernel, out_shape=jax.ShapeDtypeStruct((ROW, 2, 2 * P...  1.69 us
  transfers between devices with their start and end apart: 13, of which 4 were waited for; matrix products, arithmetic and copies ran while one was open for 0% of the time, Pallas kernels for 19%

profile of v16, /device:TPU:1, one launch (start us, length us, event | category | flops | bytes accessed | tf_op | source)
XLA Modules:
  0.0 81.2 jit_solution(4265887118083525564)
XLA Ops:
  0.0 1.7 %pack.1 = bf16[8,2,64,128]{3,2,1,0:T(8,128)(2,1)} custom-call(bf16[512,128]{1,0:T(8,128)(2,1)} %refs_2_.5, bf16[512,128]{1,0:T(8,128)(2,1)} %refs_3_.5), custom_call_target="tpu_custom_call" | custom-call | bytes 524288 | tf_op jit(solution)/shard_map/pack/pallas_call | solution.py:74
  1.7 9.8 %all-to-all-start = ((bf16[8,2,64,128]{3,2,1,0:T(8,128)(2,1)}), bf16[8,2,64,128]{3,2,1,0:T(8,128)(2,1)S(1)}, u32[]{:S(2)}, u32[]{:S(2)}) async-start(bf16[8,2,64,128]{3,2,1,0:T(8,128)(2,1)} %pack.1), calls=%async_computation | async-start | bytes 524288 | tf_op jit(solution)/shard_map/all_to_all | solution.py:391
  11.5 5.7 %all-to-all-done = bf16[8,2,64,128]{3,2,1,0:T(8,128)(2,1)S(1)} async-done(((bf16[8,2,64,128]{3,2,1,0:T(8,128)(2,1)}), bf16[8,2,64,128]{3,2,1,0:T(8,128)(2,1)S(1)}, u32[]{:S(2)}, u32[]{:S(2)}) %all-to-all-start) | async-done | bytes 262176 | tf_op jit(solution)/shard_map/all_to_all | solution.py:391
  17.2 0.8 carry_out.1
  18.0 1.4 %collective-permute-start = (bf16[4,64,128]{2,1,0:T(8,128)(2,1)S(1)}, bf16[4,64,128]{2,1,0:T(8,128)(2,1)S(1)}, u32[]{:S(2)}, u32[]{:S(2)}) collective-permute-start(bf16[4,64,128]{2,1,0:T(8,128)(2,1)S(1)} %get-tuple-element.19), channel_id=1, source_target_pairs={{0,32},{4,36},{8,40},{12,44},{16,48},{20,52},{24,56},{28,60},{32,6... | collective-permute-start | bytes 196616 | tf_op jit(solution)/shard_map/ppermute | solution.py:396
  19.4 2.6 %collective-permute-start.1 = (bf16[1,64,128]{2,1,0:T(8,128)(2,1)S(1)}, bf16[1,64,128]{2,1,0:T(8,128)(2,1)S(1)}, u32[]{:S(2)}, u32[]{:S(2)}) collective-permute-start(bf16[1,64,128]{2,1,0:T(8,128)(2,1)S(1)} %get-tuple-element.20), channel_id=1, source_target_pairs={{0,64},{4,68},{8,72},{12,76},{16,80},{20,84},{24,88},{28,92},{32,9... | collective-permute-start | bytes 49160 | tf_op jit(solution)/shard_map/ppermute | solution.py:396
  22.0 1.3 %pick.1 = (bf16[8,4,64,128]{3,2,1,0:T(8,128)(2,1)S(1)}, bf16[8,4,16,128]{3,2,1,0:T(8,128)(2,1)S(1)}, bf16[8,16,128]{2,1,0:T(8,128)(2,1)S(1)}) custom-call(s32[1]{0:T(128)} %bitcast.first_ref, s32[128]{0:T(128)} %refs_0_.5, bf16[16,64,128]{2,1,0:T(8,128)(2,1)S(1)} %bitcast.4), custom_call_target="tpu_custom_call" | custom-call | bytes 1048576 | tf_op jit(solution)/shard_map/pick/pallas_call | solution.py:152
  23.3 2.5 %collective-permute-done.1.second_ref = bf16[1,64,128]{2,1,0:T(8,128)(2,1)S(1)} collective-permute-done((bf16[1,64,128]{2,1,0:T(8,128)(2,1)S(1)}, bf16[1,64,128]{2,1,0:T(8,128)(2,1)S(1)}, u32[]{:S(2)}, u32[]{:S(2)}) %collective-permute-start.1) | collective-permute-done | bytes 16416 | tf_op jit(solution)/shard_map/ppermute | solution.py:396
  25.9 0.0 collective-permute-done.next_ref
  25.9 0.9 %merge.1 = bf16[8,4,64,128]{3,2,1,0:T(8,128)(2,1)} custom-call(bf16[8,4,64,128]{3,2,1,0:T(8,128)(2,1)S(1)} %get-tuple-element.16.inside_ref, bf16[8,4,16,128]{3,2,1,0:T(8,128)(2,1)S(1)} %get-tuple-element.17.on_next_ref, bf16[8,16,128]{2,1,0:T(8,128)(2,1)S(1)} %get-tuple-element.18.on_second_ref, bf16[4,64,128]{2,1,0:T(8,128)(2,1)S(1)} %collective-permute-done.next_ref, ...), custom_call_target="tpu_custom_call" | custom-call | bytes 1048576 | tf_op jit(solution)/shard_map/merge/pallas_call | solution.py:182
  26.8 8.0 %all-to-all-start.1 = ((bf16[8,4,64,128]{3,2,1,0:T(8,128)(2,1)}), bf16[8,4,64,128]{3,2,1,0:T(8,128)(2,1)S(1)}, u32[]{:S(2)}, u32[]{:S(2)}) async-start(bf16[8,4,64,128]{3,2,1,0:T(8,128)(2,1)} %merge.1), calls=%async_computation.1 | async-start | bytes 1048576 | tf_op jit(solution)/shard_map/all_to_all | solution.py:391
  34.8 10.7 %all-to-all-done.1.refs_4_ = bf16[8,4,64,128]{3,2,1,0:T(8,128)(2,1)S(1)} async-done(((bf16[8,4,64,128]{3,2,1,0:T(8,128)(2,1)}), bf16[8,4,64,128]{3,2,1,0:T(8,128)(2,1)S(1)}, u32[]{:S(2)}, u32[]{:S(2)}) %all-to-all-start.1) | async-done | bytes 524320 | tf_op jit(solution)/shard_map/all_to_all | solution.py:391
  45.5 4.6 %attend.4.refs_0_ = bf16[512,384]{1,0:T(8,128)(2,1)S(1)} custom-call(s32[1]{0:T(128)} %bitcast.first_ref, s32[128]{0:T(128)} %refs_0_.5, bf16[512,1024]{1,0:T(8,128)(2,1)} %refs_1_.5, bf16[512,128]{1,0:T(8,128)(2,1)} %refs_2_.5, bf16[512,128]{1,0:T(8,128)(2,1)} %refs_3_.5, bf16[8,4,64,128]{3,2,1,0:T(8,128)(2,1)S(1)} %all-to-all-done.1.refs_4_), custom_call_target="tpu_custom_call" | custom-call | flops 2768240640 | bytes 1835008 | tf_op jit(solution)/shard_map/attend/pallas_call | solution.py:313
  50.1 1.3 %collective-permute-start.2 = (bf16[512,384]{1,0:T(8,128)(2,1)S(1)}, bf16[512,384]{1,0:T(8,128)(2,1)S(1)}, u32[]{:S(2)}, u32[]{:S(2)}) collective-permute-start(bf16[512,384]{1,0:T(8,128)(2,1)S(1)} %attend.4.refs_0_), channel_id=1, source_target_pairs={{0,2},{1,3},{2,0},{3,1},{4,6},{5,7},{6,4},{7,5},{8,10},{9,11},{10,... | collective-permute-start | bytes 1179656 | tf_op jit(solution)/shard_map/ppermute | solution.py:385
  51.4 5.4 %attend.3 = (bf16[512,384]{1,0:T(8,128)(2,1)S(1)}, bf16[2048,1280]{1,0:T(8,128)(2,1)S(1)}) custom-call(s32[1]{0:T(128)} %bitcast.first_ref, s32[128]{0:T(128)} %refs_0_.5, bf16[512,1024]{1,0:T(8,128)(2,1)} %refs_1_.5, bf16[512,128]{1,0:T(8,128)(2,1)} %refs_2_.5, bf16[512,128]{1,0:T(8,128)(2,1)} %refs_3_.5, ...), custom_call_target="tpu_custom_call" | custom-call | flops 2768240640 | bytes 1835008 | tf_op jit(solution)/shard_map/attend/pallas_call | solution.py:313
  56.9 0.3 collective-permute-start.7
  57.2 4.0 %collective-permute-start.5 = (bf16[512,384]{1,0:T(8,128)(2,1)S(1)}, bf16[512,384]{1,0:T(8,128)(2,1)S(1)}, u32[]{:S(2)}, u32[]{:S(2)}) collective-permute-start(bf16[512,384]{1,0:T(8,128)(2,1)S(1)} %get-tuple-element.24.refs_1_), channel_id=1, source_target_pairs={{0,1},{1,0},{2,3},{3,2},{4,5},{5,4},{6,7},{7,6},{8,9},{9,8},{10,11... | collective-permute-start | bytes 1179656 | tf_op jit(solution)/shard_map/ppermute | solution.py:385
  61.2 0.0 collective-permute-start.4
  61.2 0.0 collective-permute-done.2.refs_7_.refs_6_
  61.2 2.1 %collective-permute-start.8 = (bf16[512,384]{1,0:T(8,128)(2,1)S(1)}, bf16[512,384]{1,0:T(8,128)(2,1)S(1)}, u32[]{:S(2)}, u32[]{:S(2)}) collective-permute-start(bf16[512,384]{1,0:T(8,128)(2,1)S(1)} %collective-permute-done.2.refs_7_.refs_6_), channel_id=1, source_target_pairs={{0,1},{1,0},{2,3},{3,2},{4,5},{5,4},{6,7},{7,6},{8,9},{9,8},{10,11... | collective-permute-start | bytes 1179656 | tf_op jit(solution)/shard_map/ppermute | solution.py:385
  63.3 4.4 %attend.5 = (bf16[512,256]{1,0:T(8,128)(2,1)S(1)}, bf16[2048,1280]{1,0:T(8,128)(2,1)S(1)}) custom-call(s32[1]{0:T(128)} %bitcast.first_ref, s32[128]{0:T(128)} %refs_0_.5, bf16[512,1024]{1,0:T(8,128)(2,1)} %refs_1_.5, bf16[512,128]{1,0:T(8,128)(2,1)} %refs_2_.5, bf16[512,128]{1,0:T(8,128)(2,1)} %refs_3_.5, ...), custom_call_target="tpu_custom_call" | custom-call | flops 1845493760 | bytes 1572864 | tf_op jit(solution)/shard_map/attend/pallas_call | solution.py:313
  67.8 0.1 collective-permute-start.6
  67.9 0.0 collective-permute-done.7.refs_7_
  67.9 2.3 %collective-permute-start.3 = (bf16[512,256]{1,0:T(8,128)(2,1)S(1)}, bf16[512,256]{1,0:T(8,128)(2,1)S(1)}, u32[]{:S(2)}, u32[]{:S(2)}) collective-permute-start(bf16[512,256]{1,0:T(8,128)(2,1)S(1)} %get-tuple-element.23.refs_2_), channel_id=1, source_target_pairs={{0,2},{1,3},{2,0},{3,1},{4,6},{5,7},{6,4},{7,5},{8,10},{9,11},{10,... | collective-permute-start | bytes 786440 | tf_op jit(solution)/shard_map/ppermute | solution.py:385
  70.1 0.0 collective-permute-done.5.refs_4_
  70.1 1.5 %collective-permute-start.9 = (bf16[512,384]{1,0:T(8,128)(2,1)S(1)}, bf16[512,384]{1,0:T(8,128)(2,1)S(1)}, u32[]{:S(2)}, u32[]{:S(2)}) collective-permute-start(bf16[512,384]{1,0:T(8,128)(2,1)S(1)} %collective-permute-done.7.refs_7_), channel_id=1, source_target_pairs={{0,1},{1,0},{2,3},{3,2},{4,5},{5,4},{6,7},{7,6},{8,9},{9,8},{10,11... | collective-permute-start | bytes 1179656 | tf_op jit(solution)/shard_map/ppermute | solution.py:385
  71.7 0.0 collective-permute-done.4.refs_3_
  71.7 0.0 collective-permute-done.6.refs_5_
  71.7 4.6 %project.2.refs_3_ = f32[512,1280]{1,0:T(8,128)S(1)} custom-call(bf16[2048,1280]{1,0:T(8,128)(2,1)S(1)} %get-tuple-element.21.near_ref, bf16[2048,1280]{1,0:T(8,128)(2,1)S(1)} %get-tuple-element.22.far_ref, bf16[512,384]{1,0:T(8,128)(2,1)S(1)} %attend.4.refs_0_, bf16[512,384]{1,0:T(8,128)(2,1)S(1)} %get-tuple-element.24.refs_1_, ...), custom_call_target="tpu_custom_call" | custom-call | flops 655360 | bytes 655360 | tf_op jit(solution)/shard_map/project/pallas_call | solution.py:367
  76.3 1.1 %collective-permute-start.10 = (bf16[512,256]{1,0:T(8,128)(2,1)S(1)}, bf16[512,256]{1,0:T(8,128)(2,1)S(1)}, u32[]{:S(2)}, u32[]{:S(2)}) collective-permute-start(bf16[512,256]{1,0:T(8,128)(2,1)S(1)} %collective-permute-done.3.refs_0_), channel_id=1, source_target_pairs={{0,1},{1,0},{2,3},{3,2},{4,5},{5,4},{6,7},{7,6},{8,9},{9,8},{10,11... | collective-permute-start | bytes 786440 | tf_op jit(solution)/shard_map/ppermute | solution.py:385
  77.4 1.2 %collective-permute-done.10.refs_2_ = bf16[512,256]{1,0:T(8,128)(2,1)S(1)} collective-permute-done((bf16[512,256]{1,0:T(8,128)(2,1)S(1)}, bf16[512,256]{1,0:T(8,128)(2,1)S(1)}, u32[]{:S(2)}, u32[]{:S(2)}) %collective-permute-start.10) | collective-permute-done | bytes 262176 | tf_op jit(solution)/shard_map/ppermute | solution.py:385
  78.6 2.6 %project.3 = bf16[512,1280]{1,0:T(8,128)(2,1)} custom-call(bf16[2048,1280]{1,0:T(8,128)(2,1)S(1)} %get-tuple-element.21.near_ref, bf16[2048,1280]{1,0:T(8,128)(2,1)S(1)} %get-tuple-element.22.far_ref, bf16[512,256]{1,0:T(8,128)(2,1)S(1)} %collective-permute-done.3.refs_0_, bf16[512,384]{1,0:T(8,128)(2,1)S(1)} %collective-permute-done.9.refs_1_, ...), custom_call_target="tpu_custom_call" | custom-call | flops 655360 | bytes 655360 | tf_op jit(solution)/shard_map/project/pallas_call | solution.py:367
  (3 shorter events, 0.0 us)
Async XLA Ops:
  1.7 15.5 %all-to-all-start = ((bf16[8,2,64,128]{3,2,1,0:T(8,128)(2,1)}), bf16[8,2,64,128]{3,2,1,0:T(8,128)(2,1)S(1)}, u32[]{:S(2)}, u32[]{:S(2)}) async-start(bf16[8,2,64,128]{3,2,1,0:T(8,128)(2,1)} %pack.1), calls=%async_computation | async-start | bytes 524288 | tf_op jit(solution)/shard_map/all_to_all | solution.py:391
  18.0 7.9 %collective-permute-start = (bf16[4,64,128]{2,1,0:T(8,128)(2,1)S(1)}, bf16[4,64,128]{2,1,0:T(8,128)(2,1)S(1)}, u32[]{:S(2)}, u32[]{:S(2)}) collective-permute-start(bf16[4,64,128]{2,1,0:T(8,128)(2,1)S(1)} %get-tuple-element.19), channel_id=1, source_target_pairs={{0,32},{4,36},{8,40},{12,44},{16,48},{20,52},{24,56},{28,60},{32,6... | collective-permute-start | bytes 196616 | tf_op jit(solution)/shard_map/ppermute | solution.py:396
  19.4 6.5 %collective-permute-start.1 = (bf16[1,64,128]{2,1,0:T(8,128)(2,1)S(1)}, bf16[1,64,128]{2,1,0:T(8,128)(2,1)S(1)}, u32[]{:S(2)}, u32[]{:S(2)}) collective-permute-start(bf16[1,64,128]{2,1,0:T(8,128)(2,1)S(1)} %get-tuple-element.20), channel_id=1, source_target_pairs={{0,64},{4,68},{8,72},{12,76},{16,80},{20,84},{24,88},{28,92},{32,9... | collective-permute-start | bytes 49160 | tf_op jit(solution)/shard_map/ppermute | solution.py:396
  26.8 18.7 %all-to-all-start.1 = ((bf16[8,4,64,128]{3,2,1,0:T(8,128)(2,1)}), bf16[8,4,64,128]{3,2,1,0:T(8,128)(2,1)S(1)}, u32[]{:S(2)}, u32[]{:S(2)}) async-start(bf16[8,4,64,128]{3,2,1,0:T(8,128)(2,1)} %merge.1), calls=%async_computation.1 | async-start | bytes 1048576 | tf_op jit(solution)/shard_map/all_to_all | solution.py:391
  50.1 11.1 %collective-permute-start.2 = (bf16[512,384]{1,0:T(8,128)(2,1)S(1)}, bf16[512,384]{1,0:T(8,128)(2,1)S(1)}, u32[]{:S(2)}, u32[]{:S(2)}) collective-permute-start(bf16[512,384]{1,0:T(8,128)(2,1)S(1)} %attend.4.refs_0_), channel_id=1, source_target_pairs={{0,2},{1,3},{2,0},{3,1},{4,6},{5,7},{6,4},{7,5},{8,10},{9,11},{10,... | collective-permute-start | bytes 1179656 | tf_op jit(solution)/shard_map/ppermute | solution.py:385
  56.9 11.0 %collective-permute-start.7 = (bf16[512,384]{1,0:T(8,128)(2,1)S(1)}, bf16[512,384]{1,0:T(8,128)(2,1)S(1)}, u32[]{:S(2)}, u32[]{:S(2)}) collective-permute-start(bf16[512,384]{1,0:T(8,128)(2,1)S(1)} %get-tuple-element.24.refs_1_), channel_id=1, source_target_pairs={{0,2},{1,3},{2,0},{3,1},{4,6},{5,7},{6,4},{7,5},{8,10},{9,11},{10,... | collective-permute-start | bytes 1179656 | tf_op jit(solution)/shard_map/ppermute | solution.py:385
  57.2 12.9 %collective-permute-start.5 = (bf16[512,384]{1,0:T(8,128)(2,1)S(1)}, bf16[512,384]{1,0:T(8,128)(2,1)S(1)}, u32[]{:S(2)}, u32[]{:S(2)}) collective-permute-start(bf16[512,384]{1,0:T(8,128)(2,1)S(1)} %get-tuple-element.24.refs_1_), channel_id=1, source_target_pairs={{0,1},{1,0},{2,3},{3,2},{4,5},{5,4},{6,7},{7,6},{8,9},{9,8},{10,11... | collective-permute-start | bytes 1179656 | tf_op jit(solution)/shard_map/ppermute | solution.py:385
  61.2 10.5 %collective-permute-start.4 = (bf16[512,384]{1,0:T(8,128)(2,1)S(1)}, bf16[512,384]{1,0:T(8,128)(2,1)S(1)}, u32[]{:S(2)}, u32[]{:S(2)}) collective-permute-start(bf16[512,384]{1,0:T(8,128)(2,1)S(1)} %attend.4.refs_0_), channel_id=1, source_target_pairs={{0,1},{1,0},{2,3},{3,2},{4,5},{5,4},{6,7},{7,6},{8,9},{9,8},{10,11... | collective-permute-start | bytes 1179656 | tf_op jit(solution)/shard_map/ppermute | solution.py:385
  61.2 10.5 %collective-permute-start.8 = (bf16[512,384]{1,0:T(8,128)(2,1)S(1)}, bf16[512,384]{1,0:T(8,128)(2,1)S(1)}, u32[]{:S(2)}, u32[]{:S(2)}) collective-permute-start(bf16[512,384]{1,0:T(8,128)(2,1)S(1)} %collective-permute-done.2.refs_7_.refs_6_), channel_id=1, source_target_pairs={{0,1},{1,0},{2,3},{3,2},{4,5},{5,4},{6,7},{7,6},{8,9},{9,8},{10,11... | collective-permute-start | bytes 1179656 | tf_op jit(solution)/shard_map/ppermute | solution.py:385
  67.8 3.9 %collective-permute-start.6 = (bf16[512,256]{1,0:T(8,128)(2,1)S(1)}, bf16[512,256]{1,0:T(8,128)(2,1)S(1)}, u32[]{:S(2)}, u32[]{:S(2)}) collective-permute-start(bf16[512,256]{1,0:T(8,128)(2,1)S(1)} %get-tuple-element.23.refs_2_), channel_id=1, source_target_pairs={{0,1},{1,0},{2,3},{3,2},{4,5},{5,4},{6,7},{7,6},{8,9},{9,8},{10,11... | collective-permute-start | bytes 786440 | tf_op jit(solution)/shard_map/ppermute | solution.py:385
  67.9 8.4 %collective-permute-start.3 = (bf16[512,256]{1,0:T(8,128)(2,1)S(1)}, bf16[512,256]{1,0:T(8,128)(2,1)S(1)}, u32[]{:S(2)}, u32[]{:S(2)}) collective-permute-start(bf16[512,256]{1,0:T(8,128)(2,1)S(1)} %get-tuple-element.23.refs_2_), channel_id=1, source_target_pairs={{0,2},{1,3},{2,0},{3,1},{4,6},{5,7},{6,4},{7,5},{8,10},{9,11},{10,... | collective-permute-start | bytes 786440 | tf_op jit(solution)/shard_map/ppermute | solution.py:385
  70.1 7.3 %collective-permute-start.9 = (bf16[512,384]{1,0:T(8,128)(2,1)S(1)}, bf16[512,384]{1,0:T(8,128)(2,1)S(1)}, u32[]{:S(2)}, u32[]{:S(2)}) collective-permute-start(bf16[512,384]{1,0:T(8,128)(2,1)S(1)} %collective-permute-done.7.refs_7_), channel_id=1, source_target_pairs={{0,1},{1,0},{2,3},{3,2},{4,5},{5,4},{6,7},{7,6},{8,9},{9,8},{10,11... | collective-permute-start | bytes 1179656 | tf_op jit(solution)/shard_map/ppermute | solution.py:385
  76.3 2.3 %collective-permute-start.10 = (bf16[512,256]{1,0:T(8,128)(2,1)S(1)}, bf16[512,256]{1,0:T(8,128)(2,1)S(1)}, u32[]{:S(2)}, u32[]{:S(2)}) collective-permute-start(bf16[512,256]{1,0:T(8,128)(2,1)S(1)} %collective-permute-done.3.refs_0_), channel_id=1, source_target_pairs={{0,1},{1,0},{2,3},{3,2},{4,5},{5,4},{6,7},{7,6},{8,9},{9,8},{10,11... | collective-permute-start | bytes 786440 | tf_op jit(solution)/shard_map/ppermute | solution.py:385
